TPU v7x, 512 devices: a whole 4x8x8 slice. The times are simulated.
512 devices in a mesh: rep: 32 (over y, z_lo, core), fsdp: 16 (over z_hi, x).
Axes of the slice: x: 4, y: 8, z: 8 (z_hi: 4, z_lo: 2; z = z_hi * 2 + z_lo), core: 2. Of those that a mesh axis runs over, the one named last changes fastest.
Arguments:
- tokens: bfloat16 [16384, 4096], P('rep', 'fsdp'), may hold values from -6 to 6
- gate_weight: bfloat16 [4096, 7168], P('rep', 'fsdp'), may hold values from -0.09375 to 0.09375
- up_act: bfloat16 [16384, 7168], P('rep', 'fsdp'), may hold values from -6 to 6
- cotangent: bfloat16 [16384, 7168], P('rep', 'fsdp'), may hold values from -0.099609375 to 0.099609375
Outputs:
- grad_sum: bfloat16 [4096, 7168], P('rep', 'fsdp')
- curvature: float32 [7168], P('fsdp')
- spread: float32 [7168], P('fsdp')
All inputs are finite; a program needn't handle non-finite values.
Results may differ from a plain program's by a relative error of at most 0.024.
Values may be sent and summed in bfloat16 or wider, within the bound.
No kernel may reach another device: no remote copies, remote signals or barrier semaphores. Data moves between devices by JAX's collectives and lax.ppermute only.
A program may use at most 64 MiB of HBM per device.

v0:
```python
import jax
import jax.numpy as jnp
from jax import lax
from jax.sharding import Mesh
from jax.sharding import PartitionSpec as P

REP = ("rep_0", "rep_1", "rep_2")


def copy_for_each(value, axis):
    count = lax.axis_size(axis)
    return lax.all_to_all(
        jnp.broadcast_to(value[None], (count, *value.shape)), axis, 0, 0, tiled=True
    )


def in_order(blocks, dim):
    blocks = jnp.moveaxis(blocks, 0, dim)
    lengths = blocks.shape
    return blocks.reshape(*lengths[:dim], lengths[dim] * lengths[dim + 1], *lengths[dim + 2 :])


def gathered_by_axis(value, axes, dim):
    far, near = axes
    blocks = copy_for_each(copy_for_each(value, far), near)
    return in_order(blocks.swapaxes(0, 1).reshape(-1, *value.shape), dim)


def padded_to(lines, count):
    spare = -len(lines) % count
    return jnp.pad(lines, [(0, spare)] + [(0, 0)] * (lines.ndim - 1))


def in_blocks(value, dim, count):
    lengths = value.shape
    blocks = value.reshape(*lengths[:dim], count, lengths[dim] // count, *lengths[dim + 1 :])
    return jnp.moveaxis(blocks, dim, 0)


def summed_on_arrival(value, axis, dim):
    count = lax.axis_size(axis)
    blocks = lax.all_to_all(in_blocks(value, dim, count), axis, 0, 0, tiled=True)
    return jnp.sum(blocks.astype(jnp.float32), axis=0)


def sum_in_two_steps(value, axes, dim):
    far, near = axes
    own = summed_on_arrival(in_blocks(value, dim, lax.axis_size(far)), near, dim + 1)
    return jnp.sum(
        lax.all_to_all(own.astype(jnp.bfloat16), far, 0, 0, tiled=True).astype(jnp.float32), axis=0
    )


def total_of(value, axes):
    lines = value.reshape(-1, value.shape[-1])
    padded = padded_to(lines, lax.axis_size(axes[0]) * lax.axis_size(axes[1]))
    whole = gathered_by_axis(sum_in_two_steps(padded, axes, 0).astype(jnp.bfloat16), axes, 0)
    return lax.slice_in_dim(whole, 0, len(lines)).reshape(value.shape).astype(jnp.float32)


def over_copies(value, axis):
    everything = copy_for_each(value, axis)
    return jnp.sum(everything, axis=0)


def in_one(arrays, axis):
    ravelled, at, outs = (jnp.concatenate([a.reshape(-1) for a in arrays]), 0, [])
    running = over_copies(ravelled, axis)
    for a in arrays:
        outs.append(running[at : at + a.size].reshape(a.shape))
        at += a.size
    return tuple(outs)


def shards(tokens, gate_weight, up_act, cotangent):
    features_all = lax.all_gather(tokens, "fsdp", axis=1, tiled=True)
    replicas = lax.axis_size(REP)
    gate_pre = jnp.dot(
        features_all,
        gathered_by_axis(gate_weight, (("rep_0", "rep_1"), "rep_2"), 0),
        preferred_element_type=jnp.float32,
    )
    sigmoid_gate = jax.nn.sigmoid(gate_pre)
    deriv_one = sigmoid_gate * (1.0 + gate_pre * (1.0 - sigmoid_gate))
    deriv_two = sigmoid_gate * (1.0 - sigmoid_gate) * (2.0 + gate_pre * (1.0 - 2.0 * sigmoid_gate))
    weighted = cotangent.astype(jnp.float32) * up_act.astype(jnp.float32)
    token_coeff = (weighted * deriv_one).astype(jnp.bfloat16)
    bend_weight = weighted * deriv_two
    rep_grad = lax.dot_general(
        features_all, token_coeff, (((0,), (0,)), ((), ())), preferred_element_type=jnp.float32
    ).astype(jnp.bfloat16)
    own_proj = jnp.dot(features_all, rep_grad, preferred_element_type=jnp.float32)
    grad_full = total_of(
        rep_grad.astype(jnp.float32).astype(jnp.bfloat16), (("rep_0", "rep_1"), "rep_2")
    ).astype(jnp.bfloat16)
    shard_rows = grad_full.shape[0] // replicas
    grad_shard = lax.dynamic_slice_in_dim(
        grad_full, lax.axis_index(REP) * shard_rows, shard_rows, 0
    )
    mean_proj = jnp.dot(features_all, grad_full, preferred_element_type=jnp.float32) / replicas
    deviate = own_proj - mean_proj
    curv_part = jnp.sum(bend_weight * mean_proj * mean_proj, axis=0)
    spread_part = jnp.sum(bend_weight * deviate * deviate, axis=0)
    curvature, spread_total = in_one((curv_part, spread_part), REP)
    return (grad_shard, curvature, spread_total / (replicas - 1))


def solution(mesh):
    torus = Mesh(
        mesh.devices.reshape(8, 2, 2, mesh.shape["fsdp"]), ("rep_0", "rep_1", "rep_2", "fsdp")
    )
    in_specs = (P(REP, "fsdp"), P(REP, "fsdp"), P(REP, "fsdp"), P(REP, "fsdp"))
    out_specs = (P(REP, "fsdp"), P("fsdp"), P("fsdp"))
    return jax.shard_map(
        shards, mesh=torus, in_specs=in_specs, out_specs=out_specs, check_vma=False
    )
```

profile of v0, /device:TPU:1, one launch (start us, length us, event | category | flops | bytes accessed | tf_op | source)
XLA Modules:
  0.0 298.9 jit_solution(17605486827183492126)
XLA Ops:
  7.2 0.0 all-gather.2.cloned.1.call-start
  7.2 0.7 all-gather.2.cloned.1.call-update
  7.9 1.2 broadcast_in_dim.10
  9.2 53.8 %all_to_all.36 = bf16[16,128,448]{1,2,0:T(8,128)(2,1)S(1)} all-to-all(bf16[16,128,448]{1,2,0:T(8,128)(2,1)S(1)} %broadcast_in_dim.10), channel_id=1, replica_groups=mesh['rep_0'=8,'rep_1'=2,'rep_2'=2,'fsdp'=16] {'rep_0','rep_1'}, dimensions={0} | all-to-all | bytes 3670016 | tf_op jit(solution)/shard_map/all_to_all | solution.py:12
  63.0 1.2 copy.28
  64.1 0.5 broadcast_in_dim.11
  64.6 8.7 %all_to_all.37 = bf16[2,16,128,448]{2,1,3,0:T(8,128)(2,1)S(1)} all-to-all(bf16[2,16,128,448]{2,1,3,0:T(8,128)(2,1)S(1)} %broadcast_in_dim.11), channel_id=1, replica_groups=mesh['rep_0'=8,'rep_1'=2,'rep_2'=2,'fsdp'=16] {'rep_2'}, dimensions={0} | all-to-all | bytes 7340032 | tf_op jit(solution)/shard_map/all_to_all | solution.py:12
  73.3 7.5 %copy.29 = bf16[16,2,128,448]{2,1,0,3:T(2,128)(2,1)} copy(bf16[16,2,128,448]{2,0,3,1:T(8,128)(2,1)S(1)} %bitcast.29) | data formatting | bytes 7340032 | tf_op jit(solution)/shard_map/transpose | solution.py:26
  80.8 7.2 %reshape_reshape.9 = bf16[4096,448]{0,1:T(8,128)(2,1)} reshape(bf16[16,2,128,448]{2,1,0,3:T(2,128)(2,1)} %copy.29) | data formatting | bytes 7340032 | tf_op jit(solution)/shard_map/reshape;reshape | solution.py:20
  88.0 0.0 copy-start.3
  88.0 0.0 copy-start.4
  88.0 24.2 %all-gather.2.cloned.1.call-done = bf16[512,4096]{1,0:T(8,128)(2,1)} async-done(((bf16[512,256]{1,0:T(8,128)(2,1)}), bf16[512,4096]{1,0:T(8,128)(2,1)}) %all-gather.2.cloned.1.call-update) | async-done | bytes 4194320 | tf_op jit(solution)/shard_map/all_gather | solution.py:76
  112.2 0.0 copy-start.1
  112.2 5.5 %fusion.13 = f32[512,448]{0,1:T(8,128)S(1)} fusion(bf16[512,4096]{1,0:T(8,128)(2,1)} %all-gather.2.cloned.1.call-done, bf16[4096,448]{0,1:T(8,128)(2,1)} %reshape_reshape.9), kind=kOutput, calls=%fused_computation.25 | convolution fusion | flops 1879048192 | bytes 8781824 | tf_op jit(solution)/shard_map/dot_general | solution.py:78
  117.8 0.0 copy-done.3
  117.8 0.0 copy-done.4
  117.8 0.0 copy-done.1
  117.8 0.0 copy-start.5
  117.8 4.1 %convolution_convert_fusion = bf16[448,4096]{1,0:T(8,128)(2,1)} fusion(bf16[512,4096]{1,0:T(8,128)(2,1)S(1)} %copy-done.1, f32[512,448]{0,1:T(8,128)S(1)} %fusion.13, bf16[512,448]{0,1:T(8,128)(2,1)S(1)} %copy-done.3, bf16[512,448]{0,1:T(8,128)(2,1)S(1)} %copy-done.4), kind=kOutput, calls=%fused_computation | convolution fusion | flops 1883635712 | bytes 9699328 | tf_op jit(solution)/shard_map/dot_general | solution.py:89
  121.9 0.0 copy-done.5
  121.9 7.1 %reshape_reshape.10 = bf16[16,2,128,448]{2,1,0,3:T(2,128)(2,1)} reshape(bf16[4096,448]{0,1:T(8,128)(2,1)} %bitcast.32) | data formatting | bytes 7340032 | tf_op jit(solution)/shard_map/reshape;reshape | solution.py:36
  129.0 2.5 copy.41
  131.5 7.9 %all_to_all.38 = bf16[2,16,128,448]{2,1,3,0:T(8,128)(2,1)} all-to-all(bf16[2,16,128,448]{2,1,3,0:T(8,128)(2,1)S(1)} %bitcast.30), channel_id=1, replica_groups=mesh['rep_0'=8,'rep_1'=2,'rep_2'=2,'fsdp'=16] {'rep_2'}, dimensions={0} | all-to-all | bytes 7340032 | tf_op jit(solution)/shard_map/all_to_all | solution.py:42
  139.5 4.0 %reduce_sum.51 = bf16[16,128,448]{1,0,2:T(8,128)(2,1)S(1)} reduce(bf16[2,16,128,448]{2,1,3,0:T(8,128)(2,1)} %all_to_all.38, bf16[]{:T(256)} %constant.11.clone.1), dimensions={0}, to_apply=%region_0.1 | reduce | flops 917504 | bytes 5505026 | tf_op jit(solution)/shard_map/reduce_sum | solution.py:43
  143.4 0.5 copy.32
  143.9 51.3 %all_to_all.39 = bf16[16,128,448]{1,2,0:T(8,128)(2,1)S(1)} all-to-all(bf16[16,128,448]{1,2,0:T(8,128)(2,1)S(1)} %copy.32), channel_id=1, replica_groups=mesh['rep_0'=8,'rep_1'=2,'rep_2'=2,'fsdp'=16] {'rep_0','rep_1'}, dimensions={0} | all-to-all | bytes 3670016 | tf_op jit(solution)/shard_map/all_to_all | solution.py:50
  195.2 0.3 reduce_sum.52
  195.5 0.3 broadcast_in_dim.12
  195.8 47.7 %all_to_all.40 = bf16[16,128,448]{1,2,0:T(8,128)(2,1)S(1)} all-to-all(bf16[16,128,448]{1,2,0:T(8,128)(2,1)S(1)} %broadcast_in_dim.12), channel_id=1, replica_groups=mesh['rep_0'=8,'rep_1'=2,'rep_2'=2,'fsdp'=16] {'rep_0','rep_1'}, dimensions={0} | all-to-all | bytes 3670016 | tf_op jit(solution)/shard_map/all_to_all | solution.py:12
  243.5 1.2 copy.33
  244.7 0.5 broadcast_in_dim.13
  245.2 8.8 %all_to_all.41 = bf16[2,16,128,448]{2,1,3,0:T(8,128)(2,1)S(1)} all-to-all(bf16[2,16,128,448]{2,1,3,0:T(8,128)(2,1)S(1)} %broadcast_in_dim.13), channel_id=1, replica_groups=mesh['rep_0'=8,'rep_1'=2,'rep_2'=2,'fsdp'=16] {'rep_2'}, dimensions={0} | all-to-all | bytes 7340032 | tf_op jit(solution)/shard_map/all_to_all | solution.py:12
  254.0 7.5 %copy.34 = bf16[16,2,128,448]{2,1,0,3:T(2,128)(2,1)} copy(bf16[16,2,128,448]{2,0,3,1:T(8,128)(2,1)S(1)} %bitcast.31) | data formatting | bytes 7340032 | tf_op jit(solution)/shard_map/transpose | solution.py:26
  261.5 0.0 copy-start.6
  261.5 7.2 %reshape_reshape.11 = bf16[4096,448]{0,1:T(8,128)(2,1)} reshape(bf16[16,2,128,448]{2,1,0,3:T(2,128)(2,1)} %copy.34) | data formatting | bytes 7340032 | tf_op jit(solution)/shard_map/reshape;reshape | solution.py:20
  268.8 0.0 copy-done.6
  268.8 0.0 copy-start
  268.8 6.0 %fusion.9 = (f32[448]{0:T(512)S(1)}, f32[512,448]{0,1:T(8,128)S(1)}) fusion(f32[512,448]{0,1:T(8,128)S(1)} %copy-done.6, bf16[512,448]{0,1:T(8,128)(2,1)S(1)} %copy-done.3, bf16[512,448]{0,1:T(8,128)(2,1)S(1)} %copy-done.4, bf16[4096,448]{0,1:T(8,128)(2,1)} %reshape_reshape.11, bf16[512,4096]{1,0:T(8,128)(2,1)} %all-gather.2.cloned.1.call-done), kind=kOutput, calls=%fused_computation.17 | convolution fusion | flops 1883176448 | bytes 10618624 | tf_op jit(solution)/shard_map/dot_general | solution.py:100
  274.8 0.0 copy-done
  274.8 0.0 copy-done.2
  274.8 2.6 fusion.2
  277.5 0.1 pad_maximum_fusion
  277.5 0.7 broadcast_in_dim.14
  278.2 3.9 %all-to-all-start.6 = ((f32[32,1,896]{2,1,0:T(1,128)}), f32[32,1,896]{2,1,0:T(1,128)S(1)}, u32[]{:S(2)}, u32[]{:S(2)}) async-start(f32[32,1,896]{2,1,0:T(1,128)} %broadcast_in_dim.14), calls=%async_computation.6 | async-start | bytes 229376 | tf_op jit(solution)/shard_map/all_to_all | solution.py:12
  282.1 1.6 constant_dynamic-slice_fusion
  283.7 7.6 %all-to-all-done.6 = f32[32,1,896]{2,1,0:T(1,128)S(1)} async-done(((f32[32,1,896]{2,1,0:T(1,128)}), f32[32,1,896]{2,1,0:T(1,128)S(1)}, u32[]{:S(2)}, u32[]{:S(2)}) %all-to-all-start.6) | async-done | bytes 114720 | tf_op jit(solution)/shard_map/all_to_all | solution.py:12
  291.3 0.1 reduce_sum.55
  291.4 0.7 slice_multiply_fusion
  (1 shorter events, 0.0 us)
Async XLA Ops:
  7.2 105.0 %all-gather.2.cloned.1.call-start = ((), (), s32[]{:S(2)}) async-start(), calls=%async_computation.7 | async-start | bytes 4456448 | tf_op jit(solution)/shard_map/all_gather | solution.py:76
  88.0 29.8 %copy-start.3 = (bf16[512,448]{0,1:T(8,128)(2,1)S(1)}, bf16[512,448]{0,1:T(8,128)(2,1)}, u32[]{:S(2)}) copy-start(bf16[512,448]{0,1:T(8,128)(2,1)} %param.6) | copy-start | bytes 1376260
  88.0 29.8 %copy-start.4 = (bf16[512,448]{0,1:T(8,128)(2,1)S(1)}, bf16[512,448]{0,1:T(8,128)(2,1)}, u32[]{:S(2)}) copy-start(bf16[512,448]{0,1:T(8,128)(2,1)} %param.7) | copy-start | bytes 1376260
  112.2 5.6 %copy-start.1 = (bf16[512,4096]{1,0:T(8,128)(2,1)S(1)}, bf16[512,4096]{1,0:T(8,128)(2,1)}, u32[]{:S(2)}) copy-start(bf16[512,4096]{1,0:T(8,128)(2,1)} %all-gather.2.cloned.1.call-done) | copy-start | bytes 12582916
  117.8 4.1 %copy-start.5 = (f32[512,448]{0,1:T(8,128)}, f32[512,448]{0,1:T(8,128)S(1)}, u32[]{:S(2)}) copy-start(f32[512,448]{0,1:T(8,128)S(1)} %fusion.13) | copy-start | bytes 2752516
  261.5 7.2 %copy-start.6 = (f32[512,448]{0,1:T(8,128)S(1)}, f32[512,448]{0,1:T(8,128)}, u32[]{:S(2)}) copy-start(f32[512,448]{0,1:T(8,128)} %copy-done.5) | copy-start | bytes 2752516
  268.8 6.0 %copy-start = (bf16[448,4096]{1,0:T(8,128)(2,1)S(1)}, bf16[448,4096]{1,0:T(8,128)(2,1)}, u32[]{:S(2)}) copy-start(bf16[448,4096]{1,0:T(8,128)(2,1)} %convolution_convert_fusion) | copy-start | bytes 11010052
  268.8 6.1 %copy-start.2 = (bf16[512,4096]{1,0:T(8,128)(2,1)S(1)}, bf16[512,4096]{1,0:T(8,128)(2,1)}, u32[]{:S(2)}) copy-start(bf16[512,4096]{1,0:T(8,128)(2,1)} %all-gather.2.cloned.1.call-done) | copy-start | bytes 12582916
  278.2 13.1 %all-to-all-start.6 = ((f32[32,1,896]{2,1,0:T(1,128)}), f32[32,1,896]{2,1,0:T(1,128)S(1)}, u32[]{:S(2)}, u32[]{:S(2)}) async-start(f32[32,1,896]{2,1,0:T(1,128)} %broadcast_in_dim.14), calls=%async_computation.6 | async-start | bytes 229376 | tf_op jit(solution)/shard_map/all_to_all | solution.py:12
Sparse Core Ops, SparseCore 0:
  11.0 101.1 all-gather.1
where the time goes:
time: 300 us; the launch traced here: 299 us
  blocking collectives  178 us (59%)
  local copies, waits for them, and re-layouts  46.7 us (16%)
  waiting for transfers between devices  32.5 us (11%)
  matrix products  18.3 us (6%)
  between operations  14.2 us (5%)
  other arithmetic  5.04 us (2%)
  starting transfers between devices  3.92 us (1%)
    all_to_all x4, blocking collectives, copy_for_each(): lax.all_to_all(jnp.broadcast_to(value[None], (count, *value.shape)), axis...  119 us
    all_to_all x1, blocking collectives, sum_in_two_steps(): lax.all_to_all(own.astype(jnp.bfloat16), far, 0, 0, tiled=True)  51.3 us
    all_gather x1, waiting for transfers between devices, shards(): features_all = lax.all_gather(tokens, 'fsdp', axis=1, tiled=True)  24.2 us
    transpose x2, local copies, waits for them, and re-layouts, gathered_by_axis(): return in_order(blocks.swapaxes(0, 1).reshape(-1, *value.shape), dim)  15 us
    another operation x2, local copies, waits for them, and re-layouts, in_order(): blocks.reshape(*lengths[:dim], lengths[dim] * lengths[dim + 1], *lengths[...  14.4 us
    another operation x2, local copies, waits for them, and re-layouts, in_blocks(): value.reshape(*lengths[:dim], count, lengths[dim] // count, *lengths[dim...  9.59 us
    all_to_all x1, blocking collectives, summed_on_arrival(): lax.all_to_all(in_blocks(value, dim, count), axis, 0, 0, tiled=True)  7.95 us
    all_to_all x1, waiting for transfers between devices, copy_for_each(): lax.all_to_all(jnp.broadcast_to(value[None], (count, *value.shape)), axis...  7.6 us
  transfers between devices with their start and end apart: 2, of which 2 were waited for; matrix products, arithmetic and copies ran while one was open for 6% of the time, Pallas kernels for 0%

commit v1 on v0

v1 whole, which is shorter than its diff:
```python
import functools

import jax
import jax.numpy as jnp
from jax import lax
from jax.experimental import pallas as pl
from jax.experimental.pallas import tpu as pltpu
from jax.sharding import Mesh
from jax.sharding import PartitionSpec as P

REP = ("y", "zl", "c")
F32, BF = jnp.float32, jnp.bfloat16
NT = (((1,), (1,)), ((), ()))
CUT = 288
VM = pl.BlockSpec(memory_space=pltpu.VMEM)
SM = pl.BlockSpec(memory_space=pltpu.SMEM)


def call(kernel, outs, operands, flops, scratch=()):
    moved = sum(a.size * a.dtype.itemsize for a in operands) + sum(
        o.size * o.dtype.itemsize for o in outs
    )
    return pl.pallas_call(
        kernel,
        out_shape=outs,
        in_specs=[SM] + [VM] * (len(operands) - 1),
        out_specs=[VM] * len(outs),
        scratch_shapes=list(scratch),
        cost_estimate=pl.CostEstimate(flops=flops, bytes_accessed=moved, transcendentals=0),
        compiler_params=pltpu.CompilerParams(vmem_limit_bytes=40 * 1024 * 1024),
    )(*operands)


def piece(tok, y, zl):
    f = 2 * y + zl
    return tok[f % 4, f // 4]


def block_of(refs, y, rel):
    if len(refs) == 4:
        return refs[rel][y], refs[2 + rel][y]
    return refs[0][y, rel], refs[1][y, rel]


def project(me, tok, refs, acc):
    mine, first = me[0], me[1] == 0
    acc[...] = jnp.zeros_like(acc)

    def step(y, unused):
        rows, cols = [], []
        for rel in (0, 1):
            own, other = block_of(refs, y, rel)
            rows += [jnp.where(first, own, other), jnp.where(first, other, own)]
            cols.append(piece(tok, y, jnp.bitwise_xor(mine, rel)))
        acc[...] += lax.dot_general(
            jnp.concatenate(rows, 1), jnp.concatenate(cols, 1), NT, preferred_element_type=F32
        )
        return unused

    lax.fori_loop(0, 8, step, 0)


def gate_kernel(me, tok, up, cot, w0, w1, w2, w3, coeff, bend, acc):
    project(me, tok, (w0, w1, w2, w3), acc)

    def part(i, unused):
        at = pl.ds(pl.multiple_of(i * 32, 32), 32)
        pre = acc[at, :]
        s = jax.nn.sigmoid(pre)
        one = s * (1.0 + pre * (1.0 - s))
        two = s * (1.0 - s) * (2.0 + pre * (1.0 - 2.0 * s))
        weighted = cot[at, :].astype(F32) * up[at, :].astype(F32)
        coeff[at, :] = (weighted * one).astype(BF)
        bend[at, :] = weighted * two
        return unused

    lax.fori_loop(0, 448 // 32, part, 0)


def grad_kernel(start, rows, me, tok, coeff, own0, own1, snd0, snd1):
    mine, first = me[0], me[1] == 0

    def step(y, unused):
        for rel, own, snd in ((0, own0, snd0), (1, own1, snd1)):
            tile = piece(tok, y, jnp.bitwise_xor(mine, rel))
            got = jnp.dot(coeff[start : start + rows, :], tile, preferred_element_type=F32)
            got = got.astype(BF)
            low, high = got[:, :128], got[:, 128:]
            own[y] = jnp.where(first, low, high)
            snd[y] = jnp.where(first, high, low)
        return unused

    lax.fori_loop(0, 8, step, 0)


def own_kernel(n, me, tok, *refs):
    project(me, tok, refs[:n], refs[n])


def mean_kernel(n, start, rows, me, tok, bend, own, *refs):
    curv, spread, acc = refs[n:]
    project(me, tok, refs[:n], acc)
    c = jnp.zeros((rows, 128), F32)
    s = jnp.zeros((rows, 128), F32)
    for k in range(4):
        lanes = slice(128 * k, 128 * k + 128)
        mean = acc[:, lanes] / 32.0
        b = bend[start : start + rows, lanes]
        off = own[:, lanes] - mean
        c += b * mean * mean
        s += b * off * off
    curv[...] = jnp.sum(c.T, axis=0, keepdims=True)
    spread[...] = jnp.sum(s.T, axis=0, keepdims=True)


def swap(value, axis):
    return lax.ppermute(value, axis, ((0, 1), (1, 0)))


def to_all(value, axis):
    count = lax.axis_size(axis)
    return lax.all_to_all(
        jnp.broadcast_to(value[None], (count, *value.shape)), axis, 0, 0, tiled=True
    )


def total(*values):
    return functools.reduce(jnp.add, [v.astype(F32) for v in values])


def shape(*lengths, dtype=BF):
    return jax.ShapeDtypeStruct(lengths, dtype)


def grads(me, tok, coeff, start, rows):
    return call(
        functools.partial(grad_kernel, start, rows),
        [shape(8, rows, 128)] * 4,
        (me, tok, coeff),
        2 * rows * 512 * 4096,
    )


def projected(me, tok, refs, rows):
    return call(
        functools.partial(own_kernel, len(refs)),
        [shape(rows, 512, dtype=F32)],
        (me, tok, *refs),
        2 * rows * 512 * 4096,
    )[0]


def terms(me, tok, bend, own, refs, start, rows):
    return call(
        functools.partial(mean_kernel, len(refs), start, rows),
        [shape(1, rows, dtype=F32)] * 2,
        (me, tok, bend, own, *refs),
        2 * rows * 512 * 4096,
        [pltpu.VMEM((rows, 512), F32)],
    )


def shards(tokens, gate_weight, up_act, cotangent):
    me = jnp.stack([lax.axis_index("zl"), lax.axis_index("c")]).astype(jnp.int32)
    tok = to_all(to_all(tokens, "zh"), "x")
    w0 = lax.all_gather(gate_weight.T, "y", axis=0)
    w1 = swap(w0, "zl")
    w2, w3 = swap(w0, "c"), swap(w1, "c")
    coeff, bend = call(
        gate_kernel,
        [shape(448, 512), shape(448, 512, dtype=F32)],
        (me, tok, up_act.T, cotangent.T, w0, w1, w2, w3),
        2 * 448 * 512 * 4096,
        [pltpu.VMEM((448, 512), F32)],
    )
    b0, b1, p0, p1 = grads(me, tok, coeff, CUT, 448 - CUT)
    sums_b = jnp.stack(
        [total(b0, swap(p0, "c")).astype(BF), total(b1, swap(p1, "c")).astype(BF)], axis=1
    )
    across_b = lax.all_to_all(sums_b, "y", 0, 0, tiled=True)
    a0, a1, q0, q1 = grads(me, tok, coeff, 0, CUT)
    sent = swap(total(a1, swap(q1, "c")).astype(BF), "zl")
    sums_a = total(a0, swap(q0, "c"), sent).astype(BF)
    own_b = projected(me, tok, (b0, b1, p0, p1), 448 - CUT)
    own_a = projected(me, tok, (a0, a1, q0, q1), CUT)
    part_b = jnp.sum(across_b.astype(F32), axis=0)
    grad_b = total(part_b[0], swap(part_b[1].astype(BF), "zl")).astype(BF)
    across_a = lax.all_to_all(sums_a, "y", 0, 0, tiled=True)
    grad_a = jnp.sum(across_a.astype(F32), axis=0).astype(BF)
    u0 = to_all(grad_a, "y")
    u1 = swap(u0, "zl")
    v0 = to_all(jnp.stack([grad_b, swap(grad_b, "zl")]), "y")
    u2, u3 = swap(u0, "c"), swap(u1, "c")
    v1 = swap(v0, "c")
    curv_a, spread_a = terms(me, tok, bend, own_a, (u0, u1, u2, u3), 0, CUT)
    curv_b, spread_b = terms(me, tok, bend, own_b, (v0, v1), CUT, 448 - CUT)
    line = jnp.concatenate([curv_a, curv_b, spread_a, spread_b], axis=1)
    whole = jnp.sum(to_all(line, REP), axis=(0, 1))
    grad = jnp.concatenate([grad_a, grad_b], axis=0).T
    return grad, whole[:448], whole[448:] / 31


def solution(mesh):
    torus = Mesh(mesh.devices.reshape(8, 2, 2, 4, 4), ("y", "zl", "c", "zh", "x"))
    fsdp = ("zh", "x")
    return jax.shard_map(
        shards,
        mesh=torus,
        in_specs=(P(REP, fsdp),) * 4,
        out_specs=(P(REP, fsdp), P(fsdp), P(fsdp)),
        check_vma=False,
    )
```

time: 300 us -> 278 us (0.927)
  blocking collectives: 178 us -> 55.4 us
  starting transfers between devices: 3.92 us -> 80.9 us
  waiting for transfers between devices: 32.5 us -> 83.1 us
  Pallas kernels: 0 us -> 36.5 us
  local copies, waits for them, and re-layouts: 46.7 us -> 16.6 us
  matrix products: 18.3 us -> 0 us
  between operations: 14.2 us -> 1.06 us
    all_to_all x6 -> x1, blocking collectives: 178 us -> 32.2 us  [to_all(): lax.all_to_all(jnp.broadcast_to(value[None], (count, *value.shape)), axis...]
    ppermute x0 -> x14, starting transfers between devices: none -> 57 us  [swap(): return lax.ppermute(value, axis, ((0, 1), (1, 0)))]
    all_to_all x1 -> x6, waiting for transfers between devices: 7.6 us -> 55.1 us  [the longest x4 30.3 us: to_all(): lax.all_to_all(jnp.broadcast_to(value[None], (count, *value.shape)), axis...]
    pallas_call x0 -> x7, Pallas kernels: none -> 36.5 us  [call(): pl.pallas_call(kernel, out_shape=outs, in_specs=[SM] + [VM] * (len(operan...]
    ppermute x0 -> x14, waiting for transfers between devices: none -> 28.1 us  [swap(): return lax.ppermute(value, axis, ((0, 1), (1, 0)))]
    all_gather x1 -> x0, waiting for transfers between devices: 24.2 us -> none  [shards(): features_all = lax.all_gather(tokens, 'fsdp', axis=1, tiled=True)]
    all_gather x0 -> x1, blocking collectives: none -> 23.2 us  [shards(): w0 = lax.all_gather(gate_weight.T, 'y', axis=0)]
    another operation x4 -> x1, local copies, waits for them, and re-layouts: 24 us -> 0.89 us  [shards(): jnp.stack([total(b0, swap(p0, 'c')).astype(BF), total(b1, swap(p1, 'c'))....]
  transfers between devices with their start and end apart: 2 -> 20, of which waited for: 2 -> 11; matrix products, arithmetic and copies ran while one was open for 6% -> 1% of each run, Pallas kernels for 0% -> 7%
where the time goes in v1:
time: 278 us; the launch traced here: 277 us
  waiting for transfers between devices  83.1 us (30%)
  starting transfers between devices  80.9 us (29%)
  blocking collectives  55.4 us (20%)
  Pallas kernels  36.5 us (13%)
  local copies, waits for them, and re-layouts  16.6 us (6%)
  other arithmetic  3.22 us (1%)
    ppermute x14, starting transfers between devices, swap(): return lax.ppermute(value, axis, ((0, 1), (1, 0)))  57 us
    pallas_call x7, Pallas kernels, call(): pl.pallas_call(kernel, out_shape=outs, in_specs=[SM] + [VM] * (len(operan...  36.5 us
    all_to_all x1, blocking collectives, to_all(): lax.all_to_all(jnp.broadcast_to(value[None], (count, *value.shape)), axis...  32.2 us
    all_to_all x4, waiting for transfers between devices, to_all(): lax.all_to_all(jnp.broadcast_to(value[None], (count, *value.shape)), axis...  30.3 us
    ppermute x14, waiting for transfers between devices, swap(): return lax.ppermute(value, axis, ((0, 1), (1, 0)))  28.1 us
    all_gather x1, blocking collectives, shards(): w0 = lax.all_gather(gate_weight.T, 'y', axis=0)  23.2 us
    all_to_all x1, waiting for transfers between devices, shards(): across_b = lax.all_to_all(sums_b, 'y', 0, 0, tiled=True)  19 us
    all_to_all x4, starting transfers between devices, to_all(): lax.all_to_all(jnp.broadcast_to(value[None], (count, *value.shape)), axis...  15.7 us
  transfers between devices with their start and end apart: 20, of which 11 were waited for; matrix products, arithmetic and copies ran while one was open for 1% of the time, Pallas kernels for 7%

profile of v1, /device:TPU:1, one launch (start us, length us, event | category | flops | bytes accessed | tf_op | source)
XLA Modules:
  0.0 276.8 jit_solution(16977254779085025383)
XLA Ops:
  0.6 1.0 broadcast_in_dim.12
  1.7 32.2 %all_to_all.35 = bf16[4,512,256]{2,1,0:T(8,128)(2,1)S(1)} all-to-all(bf16[4,512,256]{2,1,0:T(8,128)(2,1)S(1)} %broadcast_in_dim.12), channel_id=1, replica_groups=mesh['y'=8,'zl'=2,'c'=2,'zh'=4,'x'=4] {'zh'}, dimensions={0} | all-to-all | bytes 2097152 | tf_op jit(solution)/shard_map/all_to_all | solution.py:122
  33.8 2.5 broadcast_in_dim.13
  36.3 5.0 %all-to-all-start.1 = ((bf16[4,4,512,256]{3,2,1,0:T(8,128)(2,1)}), bf16[4,4,512,256]{3,2,1,0:T(8,128)(2,1)}, u32[]{:S(2)}, u32[]{:S(2)}) async-start(bf16[4,4,512,256]{3,2,1,0:T(8,128)(2,1)} %broadcast_in_dim.13), calls=%async_computation.1 | async-start | bytes 8388608 | tf_op jit(solution)/shard_map/all_to_all | solution.py:122
  41.3 23.2 %all-gather = bf16[3584,128]{1,0:T(8,128)(2,1)S(1)} all-gather(bf16[448,128]{1,0:T(8,128)(2,1)S(1)} %bitcast.28), channel_id=2, replica_groups=mesh['y'=8,'zl'=2,'c'=2,'zh'=4,'x'=4] {'y'}, dimensions={0}, use_global_device_ids=true | all-gather | bytes 1032192 | tf_op jit(solution)/shard_map/all_gather | solution.py:166
  64.5 10.6 %collective-permute-start = (bf16[8,448,128]{2,1,0:T(8,128)(2,1)S(1)}, bf16[8,448,128]{2,1,0:T(8,128)(2,1)S(1)}, u32[]{:S(2)}, u32[]{:S(2)}) collective-permute-start(bf16[8,448,128]{2,1,0:T(8,128)(2,1)S(1)} %bitcast.22), channel_id=1, source_target_pairs={{0,32},{32,0},{1,33},{33,1},{2,34},{34,2},{3,35},{35,3},{4,36},{36... | collective-permute-start | bytes 2752520 | tf_op jit(solution)/shard_map/ppermute | solution.py:117
  75.1 6.8 %collective-permute-start.1 = (bf16[8,448,128]{2,1,0:T(8,128)(2,1)S(1)}, bf16[8,448,128]{2,1,0:T(8,128)(2,1)S(1)}, u32[]{:S(2)}, u32[]{:S(2)}) collective-permute-start(bf16[8,448,128]{2,1,0:T(8,128)(2,1)S(1)} %bitcast.23), channel_id=1, source_target_pairs={{0,16},{16,0},{1,17},{17,1},{2,18},{18,2},{3,19},{19,3},{4,20},{20... | collective-permute-start | bytes 2752520 | tf_op jit(solution)/shard_map/ppermute | solution.py:117
  81.8 9.3 %collective-permute-done.w1 = bf16[8,448,128]{2,1,0:T(8,128)(2,1)S(1)} collective-permute-done((bf16[8,448,128]{2,1,0:T(8,128)(2,1)S(1)}, bf16[8,448,128]{2,1,0:T(8,128)(2,1)S(1)}, u32[]{:S(2)}, u32[]{:S(2)}) %collective-permute-start) | collective-permute-done | bytes 917536 | tf_op jit(solution)/shard_map/ppermute | solution.py:117
  91.1 7.1 %collective-permute-start.2 = (bf16[8,448,128]{2,1,0:T(8,128)(2,1)S(1)}, bf16[8,448,128]{2,1,0:T(8,128)(2,1)}, u32[]{:S(2)}, u32[]{:S(2)}) collective-permute-start(bf16[8,448,128]{2,1,0:T(8,128)(2,1)S(1)} %collective-permute-done.w1), channel_id=1, source_target_pairs={{0,16},{16,0},{1,17},{17,1},{2,18},{18,2},{3,19},{19,3},{4,20},{20... | collective-permute-start | bytes 2752520 | tf_op jit(solution)/shard_map/ppermute | solution.py:117
  99.3 1.2 collective-permute-done.2.w3
  100.5 1.2 copy-done.5
  101.7 1.0 copy-done.10
  102.7 1.0 copy-done.11
  103.7 6.7 %shard_map.67 = (bf16[448,512]{1,0:T(8,128)(2,1)S(1)}, f32[448,512]{1,0:T(8,128)S(1)}) custom-call(s32[2]{0:T(128)S(1)} %pad_add_fusion.me, bf16[4,4,512,256]{3,2,1,0:T(8,128)(2,1)} %all-to-all-done.1.tok, bf16[448,512]{1,0:T(8,128)(2,1)S(1)} %bitcast.25, bf16[448,512]{1,0:T(8,128)(2,1)S(1)} %bitcast.26, bf16[8,448,128]{2,1,0:T(8,128)(2,1)S(1)} %bitcast.24, ...), custom_call_target="tpu_custom_call" | custom-call | flops 1879048192 | bytes 10158088 | tf_op jit(solution)/shard_map/pallas_call | solution.py:23
  110.4 4.8 %shard_map.68 = (bf16[8,288,128]{2,1,0:T(8,128)(2,1)S(1)}, bf16[8,288,128]{2,1,0:T(8,128)(2,1)S(1)}, bf16[8,288,128]{2,1,0:T(8,128)(2,1)S(1)}, bf16[8,288,128]{2,1,0:T(8,128)(2,1)S(1)}) custom-call(s32[2]{0:T(128)S(1)} %pad_add_fusion.me, bf16[4,4,512,256]{3,2,1,0:T(8,128)(2,1)} %all-to-all-done.1.tok, bf16[448,512]{1,0:T(8,128)(2,1)S(1)} %get-tuple-element.17.coeff), custom_call_target="tpu_custom_call" | custom-call | flops 1207959552 | bytes 7012360 | tf_op jit(solution)/shard_map/pallas_call | solution.py:23
  115.3 2.3 collective-permute-start.4
  118.4 2.0 collective-permute-start.3
  121.5 3.4 %collective-permute-start.5 = (bf16[8,288,128]{2,1,0:T(8,128)(2,1)S(1)}, bf16[8,288,128]{2,1,0:T(8,128)(2,1)S(1)}, u32[]{:S(2)}, u32[]{:S(2)}) collective-permute-start(bf16[8,288,128]{2,1,0:T(8,128)(2,1)S(1)} %add_convert_fusion.1), channel_id=1, source_target_pairs={{0,32},{32,0},{1,33},{33,1},{2,34},{34,2},{3,35},{35,3},{4,36},{36... | collective-permute-start | bytes 1769480 | tf_op jit(solution)/shard_map/ppermute | solution.py:117
  124.9 13.0 %collective-permute-done.5 = bf16[8,288,128]{2,1,0:T(8,128)(2,1)S(1)} collective-permute-done((bf16[8,288,128]{2,1,0:T(8,128)(2,1)S(1)}, bf16[8,288,128]{2,1,0:T(8,128)(2,1)S(1)}, u32[]{:S(2)}, u32[]{:S(2)}) %collective-permute-start.5) | collective-permute-done | bytes 589856 | tf_op jit(solution)/shard_map/ppermute | solution.py:117
  137.9 1.1 add_convert_fusion
  139.0 4.7 %all-to-all-start.2 = ((bf16[8,288,128]{2,1,0:T(8,128)(2,1)}), bf16[8,288,128]{2,1,0:T(8,128)(2,1)S(1)}, u32[]{:S(2)}, u32[]{:S(2)}) async-start(bf16[8,288,128]{2,1,0:T(8,128)(2,1)} %add_convert_fusion), calls=%async_computation.2 | async-start | bytes 1179648 | tf_op jit(solution)/shard_map/all_to_all | solution.py:188
  143.7 4.3 %shard_map.69 = (bf16[8,160,128]{2,1,0:T(8,128)(2,1)S(1)}, bf16[8,160,128]{2,1,0:T(8,128)(2,1)S(1)}, bf16[8,160,128]{2,1,0:T(8,128)(2,1)S(1)}, bf16[8,160,128]{2,1,0:T(8,128)(2,1)S(1)}) custom-call(s32[2]{0:T(128)S(1)} %pad_add_fusion.me, bf16[4,4,512,256]{3,2,1,0:T(8,128)(2,1)} %all-to-all-done.1.tok, bf16[448,512]{1,0:T(8,128)(2,1)S(1)} %get-tuple-element.17.coeff), custom_call_target="tpu_custom_call" | custom-call | flops 671088640 | bytes 5963784 | tf_op jit(solution)/shard_map/pallas_call | solution.py:23
  148.0 3.4 %collective-permute-start.6 = (bf16[8,160,128]{2,1,0:T(8,128)(2,1)S(1)}, bf16[8,160,128]{2,1,0:T(8,128)(2,1)S(1)}, u32[]{:S(2)}, u32[]{:S(2)}) collective-permute-start(bf16[8,160,128]{2,1,0:T(8,128)(2,1)S(1)} %get-tuple-element.23.refs_2_), channel_id=1, source_target_pairs={{0,16},{16,0},{1,17},{17,1},{2,18},{18,2},{3,19},{19,3},{4,20},{20... | collective-permute-start | bytes 983048 | tf_op jit(solution)/shard_map/ppermute | solution.py:117
  151.4 1.9 collective-permute-start.7
  153.5 1.5 collective-permute-done.7
  156.0 5.7 %all-to-all-done.2 = bf16[8,288,128]{2,1,0:T(8,128)(2,1)S(1)} async-done(((bf16[8,288,128]{2,1,0:T(8,128)(2,1)}), bf16[8,288,128]{2,1,0:T(8,128)(2,1)S(1)}, u32[]{:S(2)}, u32[]{:S(2)}) %all-to-all-start.2) | async-done | bytes 589856 | tf_op jit(solution)/shard_map/all_to_all | solution.py:188
  161.8 3.5 %all-to-all-start.3 = ((bf16[8,2,160,128]{3,2,1,0:T(8,128)(2,1)}), bf16[8,2,160,128]{3,2,1,0:T(8,128)(2,1)S(1)}, u32[]{:S(2)}, u32[]{:S(2)}) async-start(bf16[8,2,160,128]{3,2,1,0:T(8,128)(2,1)} %copy.9), calls=%async_computation.3 | async-start | bytes 1310720 | tf_op jit(solution)/shard_map/all_to_all | solution.py:180
  165.4 19.0 %all-to-all-done.3 = bf16[8,2,160,128]{3,2,1,0:T(8,128)(2,1)S(1)} async-done(((bf16[8,2,160,128]{3,2,1,0:T(8,128)(2,1)}), bf16[8,2,160,128]{3,2,1,0:T(8,128)(2,1)S(1)}, u32[]{:S(2)}, u32[]{:S(2)}) %all-to-all-start.3) | async-done | bytes 655392 | tf_op jit(solution)/shard_map/all_to_all | solution.py:180
  185.4 3.5 %all-to-all-start.4 = ((bf16[8,288,128]{2,1,0:T(8,128)(2,1)}), bf16[8,288,128]{2,1,0:T(8,128)(2,1)S(1)}, u32[]{:S(2)}, u32[]{:S(2)}) async-start(bf16[8,288,128]{2,1,0:T(8,128)(2,1)} %broadcast_in_dim.14), calls=%async_computation.4 | async-start | bytes 1179648 | tf_op jit(solution)/shard_map/all_to_all | solution.py:122
  189.0 3.4 %collective-permute-start.8 = (bf16[160,128]{1,0:T(8,128)(2,1)S(1)}, bf16[160,128]{1,0:T(8,128)(2,1)S(1)}, u32[]{:S(2)}, u32[]{:S(2)}) collective-permute-start(bf16[160,128]{1,0:T(8,128)(2,1)S(1)} %fusion.4), channel_id=1, source_target_pairs={{0,32},{32,0},{1,33},{33,1},{2,34},{34,2},{3,35},{35,3},{4,36},{36... | collective-permute-start | bytes 122888 | tf_op jit(solution)/shard_map/ppermute | solution.py:117
  192.4 1.4 collective-permute-done.8
  193.8 3.4 %collective-permute-start.12 = (bf16[160,128]{1,0:T(8,128)(2,1)S(1)}, bf16[160,128]{1,0:T(8,128)(2,1)S(1)}, u32[]{:S(2)}, u32[]{:S(2)}) collective-permute-start(bf16[160,128]{1,0:T(8,128)(2,1)S(1)} %fusion.3), channel_id=1, source_target_pairs={{0,32},{32,0},{1,33},{33,1},{2,34},{34,2},{3,35},{35,3},{4,36},{36... | collective-permute-start | bytes 122888 | tf_op jit(solution)/shard_map/ppermute | solution.py:117
  197.1 1.7 collective-permute-done.12
  198.8 7.2 %all-to-all-done.4.refs_0_ = bf16[8,288,128]{2,1,0:T(8,128)(2,1)S(1)} async-done(((bf16[8,288,128]{2,1,0:T(8,128)(2,1)}), bf16[8,288,128]{2,1,0:T(8,128)(2,1)S(1)}, u32[]{:S(2)}, u32[]{:S(2)}) %all-to-all-start.4) | async-done | bytes 589856 | tf_op jit(solution)/shard_map/all_to_all | solution.py:122
  206.9 3.5 %all-to-all-start.5 = ((bf16[8,2,160,128]{3,2,1,0:T(8,128)(2,1)}), bf16[8,2,160,128]{3,2,1,0:T(8,128)(2,1)S(1)}, u32[]{:S(2)}, u32[]{:S(2)}) async-start(bf16[8,2,160,128]{3,2,1,0:T(8,128)(2,1)} %broadcast_in_dim.15), calls=%async_computation.5 | async-start | bytes 1310720 | tf_op jit(solution)/shard_map/all_to_all | solution.py:122
  210.5 3.4 %collective-permute-start.9 = (bf16[8,288,128]{2,1,0:T(8,128)(2,1)S(1)}, bf16[8,288,128]{2,1,0:T(8,128)(2,1)}, u32[]{:S(2)}, u32[]{:S(2)}) collective-permute-start(bf16[8,288,128]{2,1,0:T(8,128)(2,1)S(1)} %all-to-all-done.4.refs_0_), channel_id=1, source_target_pairs={{0,32},{32,0},{1,33},{33,1},{2,34},{34,2},{3,35},{35,3},{4,36},{36... | collective-permute-start | bytes 1769480 | tf_op jit(solution)/shard_map/ppermute | solution.py:117
  213.9 14.7 %all-to-all-done.5.refs_0_ = bf16[8,2,160,128]{3,2,1,0:T(8,128)(2,1)S(1)} async-done(((bf16[8,2,160,128]{3,2,1,0:T(8,128)(2,1)}), bf16[8,2,160,128]{3,2,1,0:T(8,128)(2,1)S(1)}, u32[]{:S(2)}, u32[]{:S(2)}) %all-to-all-start.5) | async-done | bytes 655392 | tf_op jit(solution)/shard_map/all_to_all | solution.py:122
  228.5 5.1 %collective-permute-start.13 = (bf16[8,2,160,128]{3,2,1,0:T(8,128)(2,1)S(1)}, bf16[8,2,160,128]{3,2,1,0:T(8,128)(2,1)S(1)}, u32[]{:S(2)}, u32[]{:S(2)}) collective-permute-start(bf16[8,2,160,128]{3,2,1,0:T(8,128)(2,1)S(1)} %all-to-all-done.5.refs_0_), channel_id=1, source_target_pairs={{0,16},{16,0},{1,17},{17,1},{2,18},{18,2},{3,19},{19,3},{4,20},{20... | collective-permute-start | bytes 1966088 | tf_op jit(solution)/shard_map/ppermute | solution.py:117
  233.6 1.9 collective-permute-start.10
  235.6 2.4 collective-permute-start.11
  238.9 1.0 copy-done.3
  240.9 1.0 copy-done.15
  241.9 4.9 %shard_map.72.own = f32[160,512]{1,0:T(8,128)S(1)} custom-call(s32[2]{0:T(128)S(1)} %pad_add_fusion.me, bf16[4,4,512,256]{3,2,1,0:T(8,128)(2,1)} %all-to-all-done.1.tok, bf16[8,160,128]{2,1,0:T(8,128)(2,1)S(1)} %copy-done.1, bf16[8,160,128]{2,1,0:T(8,128)(2,1)S(1)} %copy-done.3, bf16[8,160,128]{2,1,0:T(8,128)(2,1)S(1)} %copy-done.13, ...), custom_call_target="tpu_custom_call" | custom-call | flops 671088640 | bytes 5832712 | tf_op jit(solution)/shard_map/pallas_call | solution.py:23
  246.8 5.1 %shard_map.70.own = f32[288,512]{1,0:T(8,128)S(1)} custom-call(s32[2]{0:T(128)S(1)} %pad_add_fusion.me, bf16[4,4,512,256]{3,2,1,0:T(8,128)(2,1)} %all-to-all-done.1.tok, bf16[8,288,128]{2,1,0:T(8,128)(2,1)S(1)} %get-tuple-element.18.refs_0_, bf16[8,288,128]{2,1,0:T(8,128)(2,1)S(1)} %get-tuple-element.20.refs_1_, bf16[8,288,128]{2,1,0:T(8,128)(2,1)S(1)} %copy-done.7, ...), custom_call_target="tpu_custom_call" | custom-call | flops 1207959552 | bytes 7143432 | tf_op jit(solution)/shard_map/pallas_call | solution.py:23
  252.0 5.0 %shard_map.73 = (f32[1,160]{1,0:T(1,128)S(1)}, f32[1,160]{1,0:T(1,128)S(1)}) custom-call(s32[2]{0:T(128)S(1)} %pad_add_fusion.me, bf16[4,4,512,256]{3,2,1,0:T(8,128)(2,1)} %all-to-all-done.1.tok, f32[448,512]{1,0:T(8,128)S(1)} %get-tuple-element.26.bend, f32[160,512]{1,0:T(8,128)S(1)} %shard_map.72.own, bf16[8,2,160,128]{3,2,1,0:T(8,128)(2,1)S(1)} %all-to-all-done.5.refs_0_, ...), custom_call_target="tpu_custom_call" | custom-call | flops 671088640 | bytes 6751496 | tf_op jit(solution)/shard_map/pallas_call | solution.py:23
  257.0 5.5 %shard_map.71 = (f32[1,288]{1,0:T(1,128)S(1)}, f32[1,288]{1,0:T(1,128)S(1)}) custom-call(s32[2]{0:T(128)S(1)} %pad_add_fusion.me, bf16[4,4,512,256]{3,2,1,0:T(8,128)(2,1)} %all-to-all-done.1.tok, f32[448,512]{1,0:T(8,128)S(1)} %get-tuple-element.26.bend, f32[288,512]{1,0:T(8,128)S(1)} %shard_map.70.own, bf16[8,288,128]{2,1,0:T(8,128)(2,1)S(1)} %all-to-all-done.4.refs_0_, ...), custom_call_target="tpu_custom_call" | custom-call | flops 1207959552 | bytes 8063240 | tf_op jit(solution)/shard_map/pallas_call | solution.py:23
  263.3 3.6 %all-to-all-start.6 = ((f32[32,1,896]{2,1,0:T(1,128)}), f32[32,1,896]{2,1,0:T(1,128)S(1)}, u32[]{:S(2)}, u32[]{:S(2)}) async-start(f32[32,1,896]{2,1,0:T(1,128)} %broadcast_in_dim.17), calls=%async_computation.6 | async-start | bytes 229376 | tf_op jit(solution)/shard_map/all_to_all | solution.py:122
  267.6 8.4 %all-to-all-done.6 = f32[32,1,896]{2,1,0:T(1,128)S(1)} async-done(((f32[32,1,896]{2,1,0:T(1,128)}), f32[32,1,896]{2,1,0:T(1,128)S(1)}, u32[]{:S(2)}, u32[]{:S(2)}) %all-to-all-start.6) | async-done | bytes 114720 | tf_op jit(solution)/shard_map/all_to_all | solution.py:122
  (56 shorter events, 10.2 us)
Async XLA Ops:
  36.3 5.0 %copy-start.16 = (bf16[128,448]{0,1:T(8,128)(2,1)S(1)}, bf16[128,448]{0,1:T(8,128)(2,1)}, u32[]{:S(2)}) copy-start(bf16[128,448]{0,1:T(8,128)(2,1)} %param.5) | copy-start | bytes 344068
  36.3 64.2 %all-to-all-start.1 = ((bf16[4,4,512,256]{3,2,1,0:T(8,128)(2,1)}), bf16[4,4,512,256]{3,2,1,0:T(8,128)(2,1)}, u32[]{:S(2)}, u32[]{:S(2)}) async-start(bf16[4,4,512,256]{3,2,1,0:T(8,128)(2,1)} %broadcast_in_dim.13), calls=%async_computation.1 | async-start | bytes 8388608 | tf_op jit(solution)/shard_map/all_to_all | solution.py:122
  64.5 26.7 %collective-permute-start = (bf16[8,448,128]{2,1,0:T(8,128)(2,1)S(1)}, bf16[8,448,128]{2,1,0:T(8,128)(2,1)S(1)}, u32[]{:S(2)}, u32[]{:S(2)}) collective-permute-start(bf16[8,448,128]{2,1,0:T(8,128)(2,1)S(1)} %bitcast.22), channel_id=1, source_target_pairs={{0,32},{32,0},{1,33},{33,1},{2,34},{34,2},{3,35},{35,3},{4,36},{36... | collective-permute-start | bytes 2752520 | tf_op jit(solution)/shard_map/ppermute | solution.py:117
  75.1 23.3 %collective-permute-start.1 = (bf16[8,448,128]{2,1,0:T(8,128)(2,1)S(1)}, bf16[8,448,128]{2,1,0:T(8,128)(2,1)S(1)}, u32[]{:S(2)}, u32[]{:S(2)}) collective-permute-start(bf16[8,448,128]{2,1,0:T(8,128)(2,1)S(1)} %bitcast.23), channel_id=1, source_target_pairs={{0,16},{16,0},{1,17},{17,1},{2,18},{18,2},{3,19},{19,3},{4,20},{20... | collective-permute-start | bytes 2752520 | tf_op jit(solution)/shard_map/ppermute | solution.py:117
  91.1 9.3 %collective-permute-start.2 = (bf16[8,448,128]{2,1,0:T(8,128)(2,1)S(1)}, bf16[8,448,128]{2,1,0:T(8,128)(2,1)}, u32[]{:S(2)}, u32[]{:S(2)}) collective-permute-start(bf16[8,448,128]{2,1,0:T(8,128)(2,1)S(1)} %collective-permute-done.w1), channel_id=1, source_target_pairs={{0,16},{16,0},{1,17},{17,1},{2,18},{18,2},{3,19},{19,3},{4,20},{20... | collective-permute-start | bytes 2752520 | tf_op jit(solution)/shard_map/ppermute | solution.py:117
  98.3 0.9 copy-start.4
  100.5 1.2 copy-start.5
  101.7 1.0 copy-start.10
  102.7 1.0 copy-start.11
  115.3 6.0 %collective-permute-start.4 = (bf16[8,288,128]{2,1,0:T(8,128)(2,1)S(1)}, bf16[8,288,128]{2,1,0:T(8,128)(2,1)S(1)}, u32[]{:S(2)}, u32[]{:S(2)}) collective-permute-start(bf16[8,288,128]{2,1,0:T(8,128)(2,1)S(1)} %get-tuple-element.21.refs_3_), channel_id=1, source_target_pairs={{0,16},{16,0},{1,17},{17,1},{2,18},{18,2},{3,19},{19,3},{4,20},{20... | collective-permute-start | bytes 1769480 | tf_op jit(solution)/shard_map/ppermute | solution.py:117
  117.6 0.9 copy-start.8
  118.4 6.4 %collective-permute-start.3 = (bf16[8,288,128]{2,1,0:T(8,128)(2,1)S(1)}, bf16[8,288,128]{2,1,0:T(8,128)(2,1)S(1)}, u32[]{:S(2)}, u32[]{:S(2)}) collective-permute-start(bf16[8,288,128]{2,1,0:T(8,128)(2,1)S(1)} %get-tuple-element.19.refs_2_), channel_id=1, source_target_pairs={{0,16},{16,0},{1,17},{17,1},{2,18},{18,2},{3,19},{19,3},{4,20},{20... | collective-permute-start | bytes 1769480 | tf_op jit(solution)/shard_map/ppermute | solution.py:117
  120.5 0.8 copy-start.6
  121.5 16.4 %collective-permute-start.5 = (bf16[8,288,128]{2,1,0:T(8,128)(2,1)S(1)}, bf16[8,288,128]{2,1,0:T(8,128)(2,1)S(1)}, u32[]{:S(2)}, u32[]{:S(2)}) collective-permute-start(bf16[8,288,128]{2,1,0:T(8,128)(2,1)S(1)} %add_convert_fusion.1), channel_id=1, source_target_pairs={{0,32},{32,0},{1,33},{33,1},{2,34},{34,2},{3,35},{35,3},{4,36},{36... | collective-permute-start | bytes 1769480 | tf_op jit(solution)/shard_map/ppermute | solution.py:117
  139.0 22.8 %all-to-all-start.2 = ((bf16[8,288,128]{2,1,0:T(8,128)(2,1)}), bf16[8,288,128]{2,1,0:T(8,128)(2,1)S(1)}, u32[]{:S(2)}, u32[]{:S(2)}) async-start(bf16[8,288,128]{2,1,0:T(8,128)(2,1)} %add_convert_fusion), calls=%async_computation.2 | async-start | bytes 1179648 | tf_op jit(solution)/shard_map/all_to_all | solution.py:188
  148.0 7.1 %copy-start = (bf16[8,160,128]{2,1,0:T(8,128)(2,1)}, bf16[8,160,128]{2,1,0:T(8,128)(2,1)S(1)}, u32[]{:S(2)}) copy-start(bf16[8,160,128]{2,1,0:T(8,128)(2,1)S(1)} %get-tuple-element.22.refs_0_) | copy-start | bytes 983044
  148.0 7.1 %copy-start.2 = (bf16[8,160,128]{2,1,0:T(8,128)(2,1)}, bf16[8,160,128]{2,1,0:T(8,128)(2,1)S(1)}, u32[]{:S(2)}) copy-start(bf16[8,160,128]{2,1,0:T(8,128)(2,1)S(1)} %get-tuple-element.24.refs_1_) | copy-start | bytes 983044
  148.0 7.1 %copy-start.12 = (bf16[8,160,128]{2,1,0:T(8,128)(2,1)}, bf16[8,160,128]{2,1,0:T(8,128)(2,1)S(1)}, u32[]{:S(2)}) copy-start(bf16[8,160,128]{2,1,0:T(8,128)(2,1)S(1)} %get-tuple-element.23.refs_2_) | copy-start | bytes 983044
  148.0 7.1 %copy-start.14 = (bf16[8,160,128]{2,1,0:T(8,128)(2,1)}, bf16[8,160,128]{2,1,0:T(8,128)(2,1)S(1)}, u32[]{:S(2)}) copy-start(bf16[8,160,128]{2,1,0:T(8,128)(2,1)S(1)} %get-tuple-element.25.refs_3_) | copy-start | bytes 983044
  148.0 5.3 %collective-permute-start.6 = (bf16[8,160,128]{2,1,0:T(8,128)(2,1)S(1)}, bf16[8,160,128]{2,1,0:T(8,128)(2,1)S(1)}, u32[]{:S(2)}, u32[]{:S(2)}) collective-permute-start(bf16[8,160,128]{2,1,0:T(8,128)(2,1)S(1)} %get-tuple-element.23.refs_2_), channel_id=1, source_target_pairs={{0,16},{16,0},{1,17},{17,1},{2,18},{18,2},{3,19},{19,3},{4,20},{20... | collective-permute-start | bytes 983048 | tf_op jit(solution)/shard_map/ppermute | solution.py:117
  151.4 3.5 %collective-permute-start.7 = (bf16[8,160,128]{2,1,0:T(8,128)(2,1)S(1)}, bf16[8,160,128]{2,1,0:T(8,128)(2,1)S(1)}, u32[]{:S(2)}, u32[]{:S(2)}) collective-permute-start(bf16[8,160,128]{2,1,0:T(8,128)(2,1)S(1)} %get-tuple-element.25.refs_3_), channel_id=1, source_target_pairs={{0,16},{16,0},{1,17},{17,1},{2,18},{18,2},{3,19},{19,3},{4,20},{20... | collective-permute-start | bytes 983048 | tf_op jit(solution)/shard_map/ppermute | solution.py:117
  161.8 22.7 %all-to-all-start.3 = ((bf16[8,2,160,128]{3,2,1,0:T(8,128)(2,1)}), bf16[8,2,160,128]{3,2,1,0:T(8,128)(2,1)S(1)}, u32[]{:S(2)}, u32[]{:S(2)}) async-start(bf16[8,2,160,128]{3,2,1,0:T(8,128)(2,1)} %copy.9), calls=%async_computation.3 | async-start | bytes 1310720 | tf_op jit(solution)/shard_map/all_to_all | solution.py:180
  185.4 20.7 %all-to-all-start.4 = ((bf16[8,288,128]{2,1,0:T(8,128)(2,1)}), bf16[8,288,128]{2,1,0:T(8,128)(2,1)S(1)}, u32[]{:S(2)}, u32[]{:S(2)}) async-start(bf16[8,288,128]{2,1,0:T(8,128)(2,1)} %broadcast_in_dim.14), calls=%async_computation.4 | async-start | bytes 1179648 | tf_op jit(solution)/shard_map/all_to_all | solution.py:122
  189.0 4.7 %collective-permute-start.8 = (bf16[160,128]{1,0:T(8,128)(2,1)S(1)}, bf16[160,128]{1,0:T(8,128)(2,1)S(1)}, u32[]{:S(2)}, u32[]{:S(2)}) collective-permute-start(bf16[160,128]{1,0:T(8,128)(2,1)S(1)} %fusion.4), channel_id=1, source_target_pairs={{0,32},{32,0},{1,33},{33,1},{2,34},{34,2},{3,35},{35,3},{4,36},{36... | collective-permute-start | bytes 122888 | tf_op jit(solution)/shard_map/ppermute | solution.py:117
  193.8 5.0 %collective-permute-start.12 = (bf16[160,128]{1,0:T(8,128)(2,1)S(1)}, bf16[160,128]{1,0:T(8,128)(2,1)S(1)}, u32[]{:S(2)}, u32[]{:S(2)}) collective-permute-start(bf16[160,128]{1,0:T(8,128)(2,1)S(1)} %fusion.3), channel_id=1, source_target_pairs={{0,32},{32,0},{1,33},{33,1},{2,34},{34,2},{3,35},{35,3},{4,36},{36... | collective-permute-start | bytes 122888 | tf_op jit(solution)/shard_map/ppermute | solution.py:117
  206.9 21.6 %all-to-all-start.5 = ((bf16[8,2,160,128]{3,2,1,0:T(8,128)(2,1)}), bf16[8,2,160,128]{3,2,1,0:T(8,128)(2,1)S(1)}, u32[]{:S(2)}, u32[]{:S(2)}) async-start(bf16[8,2,160,128]{3,2,1,0:T(8,128)(2,1)} %broadcast_in_dim.15), calls=%async_computation.5 | async-start | bytes 1310720 | tf_op jit(solution)/shard_map/all_to_all | solution.py:122
  210.5 25.1 %collective-permute-start.9 = (bf16[8,288,128]{2,1,0:T(8,128)(2,1)S(1)}, bf16[8,288,128]{2,1,0:T(8,128)(2,1)}, u32[]{:S(2)}, u32[]{:S(2)}) collective-permute-start(bf16[8,288,128]{2,1,0:T(8,128)(2,1)S(1)} %all-to-all-done.4.refs_0_), channel_id=1, source_target_pairs={{0,32},{32,0},{1,33},{33,1},{2,34},{34,2},{3,35},{35,3},{4,36},{36... | collective-permute-start | bytes 1769480 | tf_op jit(solution)/shard_map/ppermute | solution.py:117
  228.5 23.4 %collective-permute-start.13 = (bf16[8,2,160,128]{3,2,1,0:T(8,128)(2,1)S(1)}, bf16[8,2,160,128]{3,2,1,0:T(8,128)(2,1)S(1)}, u32[]{:S(2)}, u32[]{:S(2)}) collective-permute-start(bf16[8,2,160,128]{3,2,1,0:T(8,128)(2,1)S(1)} %all-to-all-done.5.refs_0_), channel_id=1, source_target_pairs={{0,16},{16,0},{1,17},{17,1},{2,18},{18,2},{3,19},{19,3},{4,20},{20... | collective-permute-start | bytes 1966088 | tf_op jit(solution)/shard_map/ppermute | solution.py:117
  233.6 23.4 %collective-permute-start.10 = (bf16[8,288,128]{2,1,0:T(8,128)(2,1)S(1)}, bf16[8,288,128]{2,1,0:T(8,128)(2,1)S(1)}, u32[]{:S(2)}, u32[]{:S(2)}) collective-permute-start(bf16[8,288,128]{2,1,0:T(8,128)(2,1)S(1)} %all-to-all-done.4.refs_0_), channel_id=1, source_target_pairs={{0,16},{16,0},{1,17},{17,1},{2,18},{18,2},{3,19},{19,3},{4,20},{20... | collective-permute-start | bytes 1769480 | tf_op jit(solution)/shard_map/ppermute | solution.py:117
  235.6 21.5 %collective-permute-start.11 = (bf16[8,288,128]{2,1,0:T(8,128)(2,1)}, bf16[8,288,128]{2,1,0:T(8,128)(2,1)S(1)}, u32[]{:S(2)}, u32[]{:S(2)}) collective-permute-start(bf16[8,288,128]{2,1,0:T(8,128)(2,1)} %collective-permute-done.9.refs_1_), channel_id=1, source_target_pairs={{0,16},{16,0},{1,17},{17,1},{2,18},{18,2},{3,19},{19,3},{4,20},{20... | collective-permute-start | bytes 1769480 | tf_op jit(solution)/shard_map/ppermute | solution.py:117
  238.0 1.0 copy-start.1
  238.9 1.0 copy-start.3
  239.9 1.0 copy-start.13
  240.9 1.0 copy-start.15
  241.9 5.0 %copy-start.7 = (bf16[8,288,128]{2,1,0:T(8,128)(2,1)S(1)}, bf16[8,288,128]{2,1,0:T(8,128)(2,1)}, u32[]{:S(2)}) copy-start(bf16[8,288,128]{2,1,0:T(8,128)(2,1)} %copy-done.6) | copy-start | bytes 1769476
  241.9 5.0 %copy-start.9 = (bf16[8,288,128]{2,1,0:T(8,128)(2,1)S(1)}, bf16[8,288,128]{2,1,0:T(8,128)(2,1)}, u32[]{:S(2)}) copy-start(bf16[8,288,128]{2,1,0:T(8,128)(2,1)} %copy-done.8) | copy-start | bytes 1769476
  263.3 12.7 %all-to-all-start.6 = ((f32[32,1,896]{2,1,0:T(1,128)}), f32[32,1,896]{2,1,0:T(1,128)S(1)}, u32[]{:S(2)}, u32[]{:S(2)}) async-start(f32[32,1,896]{2,1,0:T(1,128)} %broadcast_in_dim.17), calls=%async_computation.6 | async-start | bytes 229376 | tf_op jit(solution)/shard_map/all_to_all | solution.py:122

commit v2 on v1

v2 whole, which is shorter than its diff:
```python
import functools

import jax
import jax.numpy as jnp
from jax import lax
from jax.experimental import pallas as pl
from jax.experimental.pallas import tpu as pltpu
from jax.sharding import Mesh
from jax.sharding import PartitionSpec as P

REP = ("y", "zl", "c")
F32, BF = jnp.float32, jnp.bfloat16
NT = (((1,), (1,)), ((), ()))
CUT = 336
VM = pl.BlockSpec(memory_space=pltpu.VMEM)
SM = pl.BlockSpec(memory_space=pltpu.SMEM)


def call(kernel, outs, operands, flops, scratch=()):
    moved = sum(a.size * a.dtype.itemsize for a in operands) + sum(
        o.size * o.dtype.itemsize for o in outs
    )
    return pl.pallas_call(
        kernel,
        out_shape=outs,
        in_specs=[SM] + [VM] * (len(operands) - 1),
        out_specs=[VM] * len(outs),
        scratch_shapes=list(scratch),
        cost_estimate=pl.CostEstimate(flops=flops, bytes_accessed=moved, transcendentals=0),
        compiler_params=pltpu.CompilerParams(vmem_limit_bytes=24 * 1024 * 1024),
    )(*operands)


def block_of(refs, y, rel):
    a0, a1, a2, a3, b0, b1 = refs
    own, other = ((a0, a2), (a1, a3))[rel]
    return (
        jnp.concatenate([own[y], b0[y, rel]], 0),
        jnp.concatenate([other[y], b1[y, rel]], 0),
    )


def project(me, tok, block, acc):
    mine, first = me[0], me[1] == 0
    acc[...] = jnp.zeros_like(acc)

    def step(y, unused):
        rows, cols = [], []
        for rel in (0, 1):
            own, other = block(y, rel)
            rows += [jnp.where(first, own, other), jnp.where(first, other, own)]
            cols.append(tok[2 * y + jnp.bitwise_xor(mine, rel)])
        acc[...] += lax.dot_general(
            jnp.concatenate(rows, 1), jnp.concatenate(cols, 1), NT, preferred_element_type=F32
        )
        return unused

    lax.fori_loop(0, 8, step, 0)


def gate_kernel(me, t0, t1, t3, t2a, t2b, up, cot, w0, w1, w2, w3, tok, coeff, bend, acc):
    for d in range(4):
        x = lax.rem(me[2] + d, 4)
        for z in range(4):
            tok[4 * z + x] = (t0[z], t1[z], (t2a, t2b)[z // 2][z % 2], t3[z])[d]
    project(me, tok, lambda y, rel: ((w0[y], w2[y]), (w1[y], w3[y]))[rel], acc)

    def part(i, unused):
        at = pl.ds(pl.multiple_of(i * 32, 32), 32)
        pre = acc[at, :]
        s = jax.nn.sigmoid(pre)
        one = s * (1.0 + pre * (1.0 - s))
        two = s * (1.0 - s) * (2.0 + pre * (1.0 - 2.0 * s))
        weighted = cot[at, :].astype(F32) * up[at, :].astype(F32)
        coeff[at, :] = (weighted * one).astype(BF)
        bend[at, :] = weighted * two
        return unused

    lax.fori_loop(0, 448 // 32, part, 0)


def grad_kernel(me, tok, coeff, own0, own1, sent, own_b, sent_b):
    mine, first = me[0], me[1] == 0

    def step(y, unused):
        for rel, own in ((0, own0), (1, own1)):
            tile = tok[2 * y + jnp.bitwise_xor(mine, rel)]
            got = jnp.dot(coeff[...], tile, preferred_element_type=F32).astype(BF)
            low, high = got[:, :128], got[:, 128:]
            keep, give = jnp.where(first, low, high), jnp.where(first, high, low)
            own[y] = keep[:CUT]
            own_b[y, rel] = keep[CUT:]
            sent[rel, y] = give[:CUT]
            sent_b[y, rel] = give[CUT:]
        return unused

    lax.fori_loop(0, 8, step, 0)


def own_kernel(me, tok, a0, a1, sent, b0, b1, acc):
    project(me, tok, functools.partial(block_of, (a0, a1, sent.at[0], sent.at[1], b0, b1)), acc)


def mean_kernel(me, tok, bend, own, a0, a1, a2, a3, b0, b1, sums, acc):
    project(me, tok, functools.partial(block_of, (a0, a1, a2, a3, b0, b1)), acc)
    c = jnp.zeros((448, 128), F32)
    s = jnp.zeros((448, 128), F32)
    for k in range(4):
        lanes = slice(128 * k, 128 * k + 128)
        mean = acc[:, lanes] / 32.0
        b = bend[:, lanes]
        off = own[:, lanes] - mean
        c += b * mean * mean
        s += b * off * off
    sums[0:1, :] = jnp.sum(c.T, axis=0, keepdims=True)
    sums[1:2, :] = jnp.sum(s.T, axis=0, keepdims=True)


def swap(value, axis):
    return lax.ppermute(value, axis, ((0, 1), (1, 0)))


def to_all(value, axis):
    count = lax.axis_size(axis)
    return lax.all_to_all(
        jnp.broadcast_to(value[None], (count, *value.shape)), axis, 0, 0, tiled=True
    )


def total(*values):
    return functools.reduce(jnp.add, [v.astype(F32) for v in values])


def shape(*lengths, dtype=BF):
    return jax.ShapeDtypeStruct(lengths, dtype)


def along_x(value, by):
    return lax.ppermute(value, "x", [(i, (i + by) % 4) for i in range(4)])


def shards(tokens, gate_weight, up_act, cotangent):
    me = jnp.stack([lax.axis_index("zl"), lax.axis_index("c"), lax.axis_index("x")])
    me = me.astype(jnp.int32)
    flops = 2 * 448 * 512 * 4096
    rest = 448 - CUT
    w0 = lax.all_gather(gate_weight.T, "y", axis=0)
    t0, w0 = lax.optimization_barrier((to_all(tokens, "zh"), w0))
    t3, t1 = along_x(t0, 1), along_x(t0, -1)
    w1 = swap(w0, "zl")
    t2a, t2b = along_x(t3[:2], 1), along_x(t1[2:], -1)
    w2, w3 = swap(w0, "c"), swap(w1, "c")
    tok, coeff, bend = call(
        gate_kernel,
        [shape(16, 512, 256), shape(448, 512), shape(448, 512, dtype=F32)],
        (me, t0, t1, t3, t2a, t2b, up_act.T, cotangent.T, w0, w1, w2, w3),
        flops,
        [pltpu.VMEM((448, 512), F32)],
    )
    a0, a1, sent, b0, sent_b = call(
        grad_kernel,
        [shape(8, CUT, 128)] * 2
        + [shape(2, 8, CUT, 128)]
        + [shape(8, 2, rest, 128)] * 2,
        (me, tok, coeff),
        flops,
    )
    across_b = lax.all_to_all(total(b0, swap(sent_b, "c")).astype(BF), "y", 0, 0, tiled=True)
    came = swap(sent, "c")
    came_1 = swap(total(a1, came[1]).astype(BF), "zl")
    sums_a = total(a0, came[0], came_1).astype(BF)
    own = call(
        own_kernel, [shape(448, 512, dtype=F32)], (me, tok, a0, a1, sent, b0, sent_b), flops
    )[0]
    sums_a, across_b, own = lax.optimization_barrier((sums_a, across_b, own))
    across_a = lax.all_to_all(sums_a, "y", 0, 0, tiled=True)
    part_b = jnp.sum(across_b.astype(F32), axis=0).astype(BF)
    other_b = swap(part_b, "zl")
    both_b = total(part_b, other_b[::-1]).astype(BF)
    grad_a = jnp.sum(across_a.astype(F32), axis=0).astype(BF)
    u0, both_b = lax.optimization_barrier((to_all(grad_a, "y"), both_b))
    v0 = to_all(both_b, "y")
    u1 = swap(u0, "zl")
    u2, u3 = swap(u0, "c"), swap(u1, "c")
    v1 = swap(v0, "c")
    line = call(
        mean_kernel,
        [shape(2, 448, dtype=F32)],
        (me, tok, bend, own, u0, u1, u2, u3, v0, v1),
        flops,
        [pltpu.VMEM((448, 512), F32)],
    )[0]
    whole = jnp.sum(to_all(line, REP), axis=0)
    grad = jnp.concatenate([grad_a, both_b[0]], axis=0).T
    return grad, whole[0], whole[1] / 31


def solution(mesh):
    torus = Mesh(mesh.devices.reshape(8, 2, 2, 4, 4), ("y", "zl", "c", "zh", "x"))
    fsdp = ("zh", "x")
    return jax.shard_map(
        shards,
        mesh=torus,
        in_specs=(P(REP, fsdp),) * 4,
        out_specs=(P(REP, fsdp), P(fsdp), P(fsdp)),
        check_vma=False,
    )
```

time: 278 us -> 235 us (0.85)
  waiting for transfers between devices: 83.1 us -> 54.4 us
  Pallas kernels: 36.5 us -> 19.8 us
  blocking collectives: 55.4 us -> 45.3 us
  starting transfers between devices: 80.9 us -> 89.1 us
  other arithmetic: 3.22 us -> 6.25 us
    all_to_all x2 -> x1, waiting for transfers between devices: 24.8 us -> 5.79 us  [shards(): lax.all_to_all(total(b0, swap(sent_b, 'c')).astype(BF), 'y', 0, 0, tiled=...]
    pallas_call x7 -> x4, Pallas kernels: 36.5 us -> 19.8 us  [call(): pl.pallas_call(kernel, out_shape=outs, in_specs=[SM] + [VM] * (len(operan...]
    ppermute x0 -> x4, starting transfers between devices: none -> 13 us  [along_x(): return lax.ppermute(value, 'x', [(i, (i + by) % 4) for i in range(4)])]
    ppermute x14 -> x11, waiting for transfers between devices: 28.1 us -> 16.1 us  [swap(): return lax.ppermute(value, axis, ((0, 1), (1, 0)))]
    ppermute x0 -> x4, waiting for transfers between devices: none -> 11.1 us  [along_x(): return lax.ppermute(value, 'x', [(i, (i + by) % 4) for i in range(4)])]
    all_to_all x1, blocking collectives: 32.2 us -> 22 us  [shards(): across_a = lax.all_to_all(sums_a, 'y', 0, 0, tiled=True)]
    ppermute x14 -> x11, starting transfers between devices: 57 us -> 47 us  [swap(): return lax.ppermute(value, axis, ((0, 1), (1, 0)))]
    all_to_all x4, waiting for transfers between devices: 30.3 us -> 21.4 us  [to_all(): lax.all_to_all(jnp.broadcast_to(value[None], (count, *value.shape)), axis...]
  transfers between devices with their start and end apart: 20 -> 20, of which waited for: 11 -> 11; matrix products, arithmetic and copies ran while one was open for 1% -> 3% of each run, Pallas kernels for 7% -> 2%
where the time goes in v2:
time: 235 us; the launch traced here: 234 us
  starting transfers between devices  89.1 us (38%)
  waiting for transfers between devices  54.4 us (23%)
  blocking collectives  45.3 us (19%)
  Pallas kernels  19.8 us (8%)
  local copies, waits for them, and re-layouts  18.2 us (8%)
  other arithmetic  6.25 us (3%)
    ppermute x11, starting transfers between devices, swap(): return lax.ppermute(value, axis, ((0, 1), (1, 0)))  47 us
    all_gather x1, blocking collectives, shards(): w0 = lax.all_gather(gate_weight.T, 'y', axis=0)  23.3 us
    all_to_all x1, blocking collectives, shards(): across_a = lax.all_to_all(sums_a, 'y', 0, 0, tiled=True)  22 us
    all_to_all x4, starting transfers between devices, to_all(): lax.all_to_all(jnp.broadcast_to(value[None], (count, *value.shape)), axis...  21.9 us
    all_to_all x4, waiting for transfers between devices, to_all(): lax.all_to_all(jnp.broadcast_to(value[None], (count, *value.shape)), axis...  21.4 us
    pallas_call x4, Pallas kernels, call(): pl.pallas_call(kernel, out_shape=outs, in_specs=[SM] + [VM] * (len(operan...  19.8 us
    ppermute x11, waiting for transfers between devices, swap(): return lax.ppermute(value, axis, ((0, 1), (1, 0)))  16.1 us
    ppermute x4, starting transfers between devices, along_x(): return lax.ppermute(value, 'x', [(i, (i + by) % 4) for i in range(4)])  13 us
  transfers between devices with their start and end apart: 20, of which 11 were waited for; matrix products, arithmetic and copies ran while one was open for 3% of the time, Pallas kernels for 2%

profile of v2, /device:TPU:1, one launch (start us, length us, event | category | flops | bytes accessed | tf_op | source)
XLA Modules:
  0.0 233.9 jit_solution(14586062825313601288)
XLA Ops:
  0.6 2.0 broadcast_in_dim.8
  2.6 11.0 %all-to-all-start = ((bf16[4,512,256]{2,1,0:T(8,128)(2,1)}), bf16[4,512,256]{2,1,0:T(8,128)(2,1)S(1)}, u32[]{:S(2)}, u32[]{:S(2)}) async-start(bf16[4,512,256]{2,1,0:T(8,128)(2,1)} %broadcast_in_dim.8), calls=%async_computation | async-start | bytes 2097152 | tf_op jit(solution)/shard_map/all_to_all | solution.py:125
  13.6 23.3 %all-gather = bf16[3584,128]{1,0:T(8,128)(2,1)S(1)} all-gather(bf16[448,128]{1,0:T(8,128)(2,1)S(1)} %bitcast.28), channel_id=2, replica_groups=mesh['y'=8,'zl'=2,'c'=2,'zh'=4,'x'=4] {'y'}, dimensions={0}, use_global_device_ids=true | all-gather | bytes 1032192 | tf_op jit(solution)/shard_map/all_gather | solution.py:147
  36.9 7.2 %collective-permute-start.4 = (bf16[8,448,128]{2,1,0:T(8,128)(2,1)S(1)}, bf16[8,448,128]{2,1,0:T(8,128)(2,1)}, u32[]{:S(2)}, u32[]{:S(2)}) collective-permute-start(bf16[8,448,128]{2,1,0:T(8,128)(2,1)S(1)} %bitcast.23), channel_id=1, source_target_pairs={{0,32},{32,0},{1,33},{33,1},{2,34},{34,2},{3,35},{35,3},{4,36},{36... | collective-permute-start | bytes 2752520 | tf_op jit(solution)/shard_map/ppermute | solution.py:120
  44.1 3.1 %collective-permute-start.1 = (bf16[4,512,256]{2,1,0:T(8,128)(2,1)S(1)}, bf16[4,512,256]{2,1,0:T(8,128)(2,1)S(1)}, u32[]{:S(2)}, u32[]{:S(2)}) collective-permute-start(bf16[4,512,256]{2,1,0:T(8,128)(2,1)S(1)} %all-to-all-done.t0), channel_id=1, source_target_pairs={{0,1},{1,2},{2,3},{3,0},{4,5},{5,6},{6,7},{7,4},{8,9},{9,10},{10,1... | collective-permute-start | bytes 3145736 | tf_op jit(solution)/shard_map/ppermute | solution.py:139
  47.2 3.4 %collective-permute-start = (bf16[4,512,256]{2,1,0:T(8,128)(2,1)S(1)}, bf16[4,512,256]{2,1,0:T(8,128)(2,1)S(1)}, u32[]{:S(2)}, u32[]{:S(2)}) collective-permute-start(bf16[4,512,256]{2,1,0:T(8,128)(2,1)S(1)} %all-to-all-done.t0), channel_id=1, source_target_pairs={{0,3},{1,0},{2,1},{3,2},{4,7},{5,4},{6,5},{7,6},{8,11},{9,8},{10,9... | collective-permute-start | bytes 3145736 | tf_op jit(solution)/shard_map/ppermute | solution.py:139
  50.6 4.2 %collective-permute-start.5 = (bf16[8,448,128]{2,1,0:T(8,128)(2,1)S(1)}, bf16[8,448,128]{2,1,0:T(8,128)(2,1)}, u32[]{:S(2)}, u32[]{:S(2)}) collective-permute-start(bf16[8,448,128]{2,1,0:T(8,128)(2,1)S(1)} %bitcast.24), channel_id=1, source_target_pairs={{0,16},{16,0},{1,17},{17,1},{2,18},{18,2},{3,19},{19,3},{4,20},{20... | collective-permute-start | bytes 2752520 | tf_op jit(solution)/shard_map/ppermute | solution.py:120
  54.9 7.9 %collective-permute-done.4.w1 = bf16[8,448,128]{2,1,0:T(8,128)(2,1)} collective-permute-done((bf16[8,448,128]{2,1,0:T(8,128)(2,1)S(1)}, bf16[8,448,128]{2,1,0:T(8,128)(2,1)}, u32[]{:S(2)}, u32[]{:S(2)}) %collective-permute-start.4) | collective-permute-done | bytes 917536 | tf_op jit(solution)/shard_map/ppermute | solution.py:120
  62.8 4.6 %collective-permute-start.6 = (bf16[8,448,128]{2,1,0:T(8,128)(2,1)}, bf16[8,448,128]{2,1,0:T(8,128)(2,1)}, u32[]{:S(2)}, u32[]{:S(2)}) collective-permute-start(bf16[8,448,128]{2,1,0:T(8,128)(2,1)} %collective-permute-done.4.w1), channel_id=1, source_target_pairs={{0,16},{16,0},{1,17},{17,1},{2,18},{18,2},{3,19},{19,3},{4,20},{20... | collective-permute-start | bytes 2752520 | tf_op jit(solution)/shard_map/ppermute | solution.py:120
  67.4 2.7 %collective-permute-done.1.t3 = bf16[4,512,256]{2,1,0:T(8,128)(2,1)S(1)} collective-permute-done((bf16[4,512,256]{2,1,0:T(8,128)(2,1)S(1)}, bf16[4,512,256]{2,1,0:T(8,128)(2,1)S(1)}, u32[]{:S(2)}, u32[]{:S(2)}) %collective-permute-start.1) | collective-permute-done | bytes 1048608 | tf_op jit(solution)/shard_map/ppermute | solution.py:139
  70.9 1.9 collective-permute-start.2
  74.7 4.6 %collective-permute-start.3 = (bf16[2,512,256]{2,1,0:T(8,128)(2,1)}, bf16[2,512,256]{2,1,0:T(8,128)(2,1)}, u32[]{:S(2)}, u32[]{:S(2)}) collective-permute-start(bf16[2,512,256]{2,1,0:T(8,128)(2,1)} %slice.29), channel_id=1, source_target_pairs={{0,3},{1,0},{2,1},{3,2},{4,7},{5,4},{6,5},{7,6},{8,11},{9,8},{10,9... | collective-permute-start | bytes 1572872 | tf_op jit(solution)/shard_map/ppermute | solution.py:139
  79.3 5.6 %collective-permute-done.2.t2a = bf16[2,512,256]{2,1,0:T(8,128)(2,1)S(1)} collective-permute-done((bf16[2,512,256]{2,1,0:T(8,128)(2,1)}, bf16[2,512,256]{2,1,0:T(8,128)(2,1)S(1)}, u32[]{:S(2)}, u32[]{:S(2)}) %collective-permute-start.2) | collective-permute-done | bytes 524320 | tf_op jit(solution)/shard_map/ppermute | solution.py:139
  84.9 2.8 %collective-permute-done.3.t2b = bf16[2,512,256]{2,1,0:T(8,128)(2,1)} collective-permute-done((bf16[2,512,256]{2,1,0:T(8,128)(2,1)}, bf16[2,512,256]{2,1,0:T(8,128)(2,1)}, u32[]{:S(2)}, u32[]{:S(2)}) %collective-permute-start.3) | collective-permute-done | bytes 524320 | tf_op jit(solution)/shard_map/ppermute | solution.py:139
  87.8 1.2 copy-done.4
  89.0 1.0 copy-done.9
  90.0 1.0 copy-done.10
  91.0 6.4 %shard_map.67 = (bf16[16,512,256]{2,1,0:T(8,128)(2,1)S(1)}, bf16[448,512]{1,0:T(8,128)(2,1)S(1)}, f32[448,512]{1,0:T(8,128)S(1)}) custom-call(s32[3]{0:T(128)S(1)} %pad_add_fusion.me, bf16[4,512,256]{2,1,0:T(8,128)(2,1)S(1)} %all-to-all-done.t0, bf16[4,512,256]{2,1,0:T(8,128)(2,1)S(1)} %copy-done.4, bf16[4,512,256]{2,1,0:T(8,128)(2,1)S(1)} %collective-permute-done.1.t3, ...), custom_call_target="tpu_custom_call" | custom-call | flops 1879048192 | bytes 14352396 | tf_op jit(solution)/shard_map/pallas_call | solution.py:23
  98.4 3.8 %shard_map.68 = (bf16[8,336,128]{2,1,0:T(8,128)(2,1)S(1)}, bf16[8,336,128]{2,1,0:T(8,128)(2,1)S(1)}, bf16[2,8,336,128]{3,2,1,0:T(8,128)(2,1)S(1)}, bf16[8,2,112,...) custom-call(s32[3]{0:T(128)S(1)} %pad_add_fusion.me, bf16[16,512,256]{2,1,0:T(8,128)(2,1)S(1)} %get-tuple-element.20.tok, ...), custom_call_target="tpu_custom_call" | custom-call | flops 1879048192 | bytes 8323084 | tf_op jit(solution)/shard_map/pallas_call | solution.py:23
  102.2 5.8 %collective-permute-start.7 = (bf16[2,8,336,128]{3,2,1,0:T(8,128)(2,1)S(1)}, bf16[2,8,336,128]{3,2,1,0:T(8,128)(2,1)S(1)}, u32[]{:S(2)}, u32[]{:S(2)}) collective-permute-start(bf16[2,8,336,128]{3,2,1,0:T(8,128)(2,1)S(1)} %get-tuple-element.23.sent), channel_id=1, source_target_pairs={{0,16},{16,0},{1,17},{17,1},{2,18},{18,2},{3,19},{19,3},{4,20},{20... | collective-permute-start | bytes 4128776 | tf_op jit(solution)/shard_map/ppermute | solution.py:120
  108.1 1.1 copy-done.5
  109.2 1.9 collective-permute-start.9
  111.1 1.3 fusion
  112.4 1.9 collective-permute-start.8
  115.2 7.2 %all-to-all-start.1 = ((bf16[8,2,112,128]{3,2,1,0:T(8,128)(2,1)}), bf16[8,2,112,128]{3,2,1,0:T(8,128)(2,1)}, u32[]{:S(2)}, u32[]{:S(2)}) async-start(bf16[8,2,112,128]{3,2,1,0:T(8,128)(2,1)} %add_convert_fusion), calls=%async_computation.1 | async-start | bytes 917504 | tf_op jit(solution)/shard_map/all_to_all | solution.py:168
  122.4 2.2 copy-done.1
  124.6 1.3 copy-done.6
  126.0 4.1 %shard_map.69.own = f32[448,512]{1,0:T(8,128)S(1)} custom-call(s32[3]{0:T(128)S(1)} %pad_add_fusion.me, bf16[16,512,256]{2,1,0:T(8,128)(2,1)S(1)} %copy-done.1, bf16[8,336,128]{2,1,0:T(8,128)(2,1)S(1)} %get-tuple-element.22.a0, bf16[8,336,128]{2,1,0:T(8,128)(2,1)S(1)} %get-tuple-element.24.a1, bf16[2,8,336,128]{3,2,1,0:T(8,128)(2,1)S(1)} %copy-done.6, ...), custom_call_target="tpu_custom_call" | custom-call | flops 1879048192 | bytes 8781836 | tf_op jit(solution)/shard_map/pallas_call | solution.py:23
  130.1 1.0 collective-permute-done.8
  131.1 1.4 fusion.2
  132.5 5.8 %all-to-all-done.1 = bf16[8,2,112,128]{3,2,1,0:T(8,128)(2,1)} async-done(((bf16[8,2,112,128]{3,2,1,0:T(8,128)(2,1)}), bf16[8,2,112,128]{3,2,1,0:T(8,128)(2,1)}, u32[]{:S(2)}, u32[]{:S(2)}) %all-to-all-start.1) | async-done | bytes 458784 | tf_op jit(solution)/shard_map/all_to_all | solution.py:168
  138.3 22.0 %all_to_all.30 = bf16[8,336,128]{2,1,0:T(8,128)(2,1)S(1)} all-to-all(bf16[8,336,128]{2,1,0:T(8,128)(2,1)S(1)} %fusion.2), channel_id=1, replica_groups=mesh['y'=8,'zl'=2,'c'=2,'zh'=4,'x'=4] {'y'}, dimensions={0} | all-to-all | bytes 1376256 | tf_op jit(solution)/shard_map/all_to_all | solution.py:176
  161.3 3.5 %all-to-all-start.3 = ((bf16[8,336,128]{2,1,0:T(8,128)(2,1)}), bf16[8,336,128]{2,1,0:T(8,128)(2,1)S(1)}, u32[]{:S(2)}, u32[]{:S(2)}) async-start(bf16[8,336,128]{2,1,0:T(8,128)(2,1)} %broadcast_in_dim.9), calls=%async_computation.3 | async-start | bytes 1376256 | tf_op jit(solution)/shard_map/all_to_all | solution.py:125
  164.8 1.2 reduce_sum.34
  166.0 3.1 %collective-permute-start.10 = (bf16[2,112,128]{2,1,0:T(8,128)(2,1)S(1)}, bf16[2,112,128]{2,1,0:T(8,128)(2,1)S(1)}, u32[]{:S(2)}, u32[]{:S(2)}) collective-permute-start(bf16[2,112,128]{2,1,0:T(8,128)(2,1)S(1)} %reduce_sum.34), channel_id=1, source_target_pairs={{0,32},{32,0},{1,33},{33,1},{2,34},{34,2},{3,35},{35,3},{4,36},{36... | collective-permute-start | bytes 172040 | tf_op jit(solution)/shard_map/ppermute | solution.py:120
  169.1 2.1 collective-permute-done.10
  171.3 12.6 %all-to-all-done.3.a0 = bf16[8,336,128]{2,1,0:T(8,128)(2,1)S(1)} async-done(((bf16[8,336,128]{2,1,0:T(8,128)(2,1)}), bf16[8,336,128]{2,1,0:T(8,128)(2,1)S(1)}, u32[]{:S(2)}, u32[]{:S(2)}) %all-to-all-start.3) | async-done | bytes 688160 | tf_op jit(solution)/shard_map/all_to_all | solution.py:125
  183.9 3.1 %collective-permute-start.11 = (bf16[8,336,128]{2,1,0:T(8,128)(2,1)S(1)}, bf16[8,336,128]{2,1,0:T(8,128)(2,1)}, u32[]{:S(2)}, u32[]{:S(2)}) collective-permute-start(bf16[8,336,128]{2,1,0:T(8,128)(2,1)S(1)} %all-to-all-done.3.a0), channel_id=1, source_target_pairs={{0,32},{32,0},{1,33},{33,1},{2,34},{34,2},{3,35},{35,3},{4,36},{36... | collective-permute-start | bytes 2064392 | tf_op jit(solution)/shard_map/ppermute | solution.py:120
  187.8 3.5 %all-to-all-start.4 = ((bf16[8,2,112,128]{3,2,1,0:T(8,128)(2,1)}), bf16[8,2,112,128]{3,2,1,0:T(8,128)(2,1)S(1)}, u32[]{:S(2)}, u32[]{:S(2)}) async-start(bf16[8,2,112,128]{3,2,1,0:T(8,128)(2,1)} %broadcast_in_dim.10), calls=%async_computation.4 | async-start | bytes 917504 | tf_op jit(solution)/shard_map/all_to_all | solution.py:125
  191.3 5.1 %collective-permute-start.12 = (bf16[8,336,128]{2,1,0:T(8,128)(2,1)S(1)}, bf16[8,336,128]{2,1,0:T(8,128)(2,1)}, u32[]{:S(2)}, u32[]{:S(2)}) collective-permute-start(bf16[8,336,128]{2,1,0:T(8,128)(2,1)S(1)} %all-to-all-done.3.a0), channel_id=1, source_target_pairs={{0,16},{16,0},{1,17},{17,1},{2,18},{18,2},{3,19},{19,3},{4,20},{20... | collective-permute-start | bytes 2064392 | tf_op jit(solution)/shard_map/ppermute | solution.py:120
  196.4 3.6 %collective-permute-done.11.a1 = bf16[8,336,128]{2,1,0:T(8,128)(2,1)} collective-permute-done((bf16[8,336,128]{2,1,0:T(8,128)(2,1)S(1)}, bf16[8,336,128]{2,1,0:T(8,128)(2,1)}, u32[]{:S(2)}, u32[]{:S(2)}) %collective-permute-start.11) | collective-permute-done | bytes 688160 | tf_op jit(solution)/shard_map/ppermute | solution.py:120
  199.9 5.7 %collective-permute-start.13 = (bf16[8,336,128]{2,1,0:T(8,128)(2,1)}, bf16[8,336,128]{2,1,0:T(8,128)(2,1)}, u32[]{:S(2)}, u32[]{:S(2)}) collective-permute-start(bf16[8,336,128]{2,1,0:T(8,128)(2,1)} %collective-permute-done.11.a1), channel_id=1, source_target_pairs={{0,16},{16,0},{1,17},{17,1},{2,18},{18,2},{3,19},{19,3},{4,20},{20... | collective-permute-start | bytes 2064392 | tf_op jit(solution)/shard_map/ppermute | solution.py:120
  205.6 4.5 %collective-permute-start.14 = (bf16[8,2,112,128]{3,2,1,0:T(8,128)(2,1)S(1)}, bf16[8,2,112,128]{3,2,1,0:T(8,128)(2,1)S(1)}, u32[]{:S(2)}, u32[]{:S(2)}) collective-permute-start(bf16[8,2,112,128]{3,2,1,0:T(8,128)(2,1)S(1)} %all-to-all-done.4.b0), channel_id=1, source_target_pairs={{0,16},{16,0},{1,17},{17,1},{2,18},{18,2},{3,19},{19,3},{4,20},{20... | collective-permute-start | bytes 1376264 | tf_op jit(solution)/shard_map/ppermute | solution.py:120
  210.2 1.4 collective-permute-done.14.b1
  211.6 2.2 copy-done.2
  213.8 5.4 %shard_map.70 = f32[2,448]{1,0:T(2,128)S(1)} custom-call(s32[3]{0:T(128)S(1)} %pad_add_fusion.me, bf16[16,512,256]{2,1,0:T(8,128)(2,1)S(1)} %copy-done.2, f32[448,512]{1,0:T(8,128)S(1)} %copy-done.8, f32[448,512]{1,0:T(8,128)S(1)} %shard_map.69.own, bf16[8,336,128]{2,1,0:T(8,128)(2,1)S(1)} %all-to-all-done.3.a0, ...), custom_call_target="tpu_custom_call" | custom-call | flops 1879048192 | bytes 9702924 | tf_op jit(solution)/shard_map/pallas_call | solution.py:23
  219.9 3.9 %all-to-all-start.5 = ((f32[32,2,448]{2,1,0:T(2,128)}), f32[32,2,448]{2,1,0:T(2,128)S(1)}, u32[]{:S(2)}, u32[]{:S(2)}) async-start(f32[32,2,448]{2,1,0:T(2,128)} %broadcast_in_dim.11), calls=%async_computation.5 | async-start | bytes 262144 | tf_op jit(solution)/shard_map/all_to_all | solution.py:125
  224.4 8.8 %all-to-all-done.5 = f32[32,2,448]{2,1,0:T(2,128)S(1)} async-done(((f32[32,2,448]{2,1,0:T(2,128)}), f32[32,2,448]{2,1,0:T(2,128)S(1)}, u32[]{:S(2)}, u32[]{:S(2)}) %all-to-all-start.5) | async-done | bytes 114720 | tf_op jit(solution)/shard_map/all_to_all | solution.py:125
  (43 shorter events, 8.5 us)
Async XLA Ops:
  2.6 11.0 %copy-start.13 = (bf16[128,448]{0,1:T(8,128)(2,1)S(1)}, bf16[128,448]{0,1:T(8,128)(2,1)}, u32[]{:S(2)}) copy-start(bf16[128,448]{0,1:T(8,128)(2,1)} %param.5) | copy-start | bytes 344068
  2.6 34.3 %all-to-all-start = ((bf16[4,512,256]{2,1,0:T(8,128)(2,1)}), bf16[4,512,256]{2,1,0:T(8,128)(2,1)S(1)}, u32[]{:S(2)}, u32[]{:S(2)}) async-start(bf16[4,512,256]{2,1,0:T(8,128)(2,1)} %broadcast_in_dim.8), calls=%async_computation | async-start | bytes 2097152 | tf_op jit(solution)/shard_map/all_to_all | solution.py:125
  36.9 25.9 %collective-permute-start.4 = (bf16[8,448,128]{2,1,0:T(8,128)(2,1)S(1)}, bf16[8,448,128]{2,1,0:T(8,128)(2,1)}, u32[]{:S(2)}, u32[]{:S(2)}) collective-permute-start(bf16[8,448,128]{2,1,0:T(8,128)(2,1)S(1)} %bitcast.23), channel_id=1, source_target_pairs={{0,32},{32,0},{1,33},{33,1},{2,34},{34,2},{3,35},{35,3},{4,36},{36... | collective-permute-start | bytes 2752520 | tf_op jit(solution)/shard_map/ppermute | solution.py:120
  44.1 26.0 %collective-permute-start.1 = (bf16[4,512,256]{2,1,0:T(8,128)(2,1)S(1)}, bf16[4,512,256]{2,1,0:T(8,128)(2,1)S(1)}, u32[]{:S(2)}, u32[]{:S(2)}) collective-permute-start(bf16[4,512,256]{2,1,0:T(8,128)(2,1)S(1)} %all-to-all-done.t0), channel_id=1, source_target_pairs={{0,1},{1,2},{2,3},{3,0},{4,5},{5,6},{6,7},{7,4},{8,9},{9,10},{10,1... | collective-permute-start | bytes 3145736 | tf_op jit(solution)/shard_map/ppermute | solution.py:139
  47.2 25.6 %collective-permute-start = (bf16[4,512,256]{2,1,0:T(8,128)(2,1)S(1)}, bf16[4,512,256]{2,1,0:T(8,128)(2,1)S(1)}, u32[]{:S(2)}, u32[]{:S(2)}) collective-permute-start(bf16[4,512,256]{2,1,0:T(8,128)(2,1)S(1)} %all-to-all-done.t0), channel_id=1, source_target_pairs={{0,3},{1,0},{2,1},{3,2},{4,7},{5,4},{6,5},{7,6},{8,11},{9,8},{10,9... | collective-permute-start | bytes 3145736 | tf_op jit(solution)/shard_map/ppermute | solution.py:139
  50.6 28.7 %collective-permute-start.5 = (bf16[8,448,128]{2,1,0:T(8,128)(2,1)S(1)}, bf16[8,448,128]{2,1,0:T(8,128)(2,1)}, u32[]{:S(2)}, u32[]{:S(2)}) collective-permute-start(bf16[8,448,128]{2,1,0:T(8,128)(2,1)S(1)} %bitcast.24), channel_id=1, source_target_pairs={{0,16},{16,0},{1,17},{17,1},{2,18},{18,2},{3,19},{19,3},{4,20},{20... | collective-permute-start | bytes 2752520 | tf_op jit(solution)/shard_map/ppermute | solution.py:120
  62.8 25.0 %collective-permute-start.6 = (bf16[8,448,128]{2,1,0:T(8,128)(2,1)}, bf16[8,448,128]{2,1,0:T(8,128)(2,1)}, u32[]{:S(2)}, u32[]{:S(2)}) collective-permute-start(bf16[8,448,128]{2,1,0:T(8,128)(2,1)} %collective-permute-done.4.w1), channel_id=1, source_target_pairs={{0,16},{16,0},{1,17},{17,1},{2,18},{18,2},{3,19},{19,3},{4,20},{20... | collective-permute-start | bytes 2752520 | tf_op jit(solution)/shard_map/ppermute | solution.py:120
  70.9 14.0 %collective-permute-start.2 = (bf16[2,512,256]{2,1,0:T(8,128)(2,1)}, bf16[2,512,256]{2,1,0:T(8,128)(2,1)S(1)}, u32[]{:S(2)}, u32[]{:S(2)}) collective-permute-start(bf16[2,512,256]{2,1,0:T(8,128)(2,1)} %slice.28), channel_id=1, source_target_pairs={{0,1},{1,2},{2,3},{3,0},{4,5},{5,6},{6,7},{7,4},{8,9},{9,10},{10,1... | collective-permute-start | bytes 1572872 | tf_op jit(solution)/shard_map/ppermute | solution.py:139
  73.7 1.0 copy-start.3
  74.7 13.1 %collective-permute-start.3 = (bf16[2,512,256]{2,1,0:T(8,128)(2,1)}, bf16[2,512,256]{2,1,0:T(8,128)(2,1)}, u32[]{:S(2)}, u32[]{:S(2)}) collective-permute-start(bf16[2,512,256]{2,1,0:T(8,128)(2,1)} %slice.29), channel_id=1, source_target_pairs={{0,3},{1,0},{2,1},{3,2},{4,7},{5,4},{6,5},{7,6},{8,11},{9,8},{10,9... | collective-permute-start | bytes 1572872 | tf_op jit(solution)/shard_map/ppermute | solution.py:139
  87.8 1.2 copy-start.4
  89.0 1.0 copy-start.9
  90.0 1.0 copy-start.10
  97.5 0.9 copy-start.7
  98.4 3.8 %copy-start = (bf16[16,512,256]{2,1,0:T(8,128)(2,1)}, bf16[16,512,256]{2,1,0:T(8,128)(2,1)S(1)}, u32[]{:S(2)}) copy-start(bf16[16,512,256]{2,1,0:T(8,128)(2,1)S(1)} %get-tuple-element.20.tok) | copy-start | bytes 12582916
  102.2 8.8 %collective-permute-start.7 = (bf16[2,8,336,128]{3,2,1,0:T(8,128)(2,1)S(1)}, bf16[2,8,336,128]{3,2,1,0:T(8,128)(2,1)S(1)}, u32[]{:S(2)}, u32[]{:S(2)}) collective-permute-start(bf16[2,8,336,128]{3,2,1,0:T(8,128)(2,1)S(1)} %get-tuple-element.23.sent), channel_id=1, source_target_pairs={{0,16},{16,0},{1,17},{17,1},{2,18},{18,2},{3,19},{19,3},{4,20},{20... | collective-permute-start | bytes 4128776 | tf_op jit(solution)/shard_map/ppermute | solution.py:120
  108.1 1.1 copy-start.5
  109.2 5.1 %collective-permute-start.9 = (bf16[8,2,112,128]{3,2,1,0:T(8,128)(2,1)S(1)}, bf16[8,2,112,128]{3,2,1,0:T(8,128)(2,1)S(1)}, u32[]{:S(2)}, u32[]{:S(2)}) collective-permute-start(bf16[8,2,112,128]{3,2,1,0:T(8,128)(2,1)S(1)} %get-tuple-element.26.b1), channel_id=1, source_target_pairs={{0,16},{16,0},{1,17},{17,1},{2,18},{18,2},{3,19},{19,3},{4,20},{20... | collective-permute-start | bytes 1376264 | tf_op jit(solution)/shard_map/ppermute | solution.py:120
  111.1 3.2 %copy-start.11 = (bf16[2,8,336,128]{3,2,1,0:T(8,128)(2,1)}, bf16[2,8,336,128]{3,2,1,0:T(8,128)(2,1)S(1)}, u32[]{:S(2)}) copy-start(bf16[2,8,336,128]{3,2,1,0:T(8,128)(2,1)S(1)} %collective-permute-done.7) | copy-start | bytes 4128772
  112.4 18.7 %collective-permute-start.8 = (bf16[8,336,128]{2,1,0:T(8,128)(2,1)}, bf16[8,336,128]{2,1,0:T(8,128)(2,1)}, u32[]{:S(2)}, u32[]{:S(2)}) collective-permute-start(bf16[8,336,128]{2,1,0:T(8,128)(2,1)} %fusion), channel_id=1, source_target_pairs={{0,32},{32,0},{1,33},{33,1},{2,34},{34,2},{3,35},{35,3},{4,36},{36... | collective-permute-start | bytes 2064392 | tf_op jit(solution)/shard_map/ppermute | solution.py:120
  115.2 23.1 %all-to-all-start.1 = ((bf16[8,2,112,128]{3,2,1,0:T(8,128)(2,1)}), bf16[8,2,112,128]{3,2,1,0:T(8,128)(2,1)}, u32[]{:S(2)}, u32[]{:S(2)}) async-start(bf16[8,2,112,128]{3,2,1,0:T(8,128)(2,1)} %add_convert_fusion), calls=%async_computation.1 | async-start | bytes 917504 | tf_op jit(solution)/shard_map/all_to_all | solution.py:168
  122.4 2.2 copy-start.1
  124.6 1.3 copy-start.6
  125.9 5.1 %copy-start.12 = (bf16[2,8,336,128]{3,2,1,0:T(8,128)(2,1)S(1)}, bf16[2,8,336,128]{3,2,1,0:T(8,128)(2,1)}, u32[]{:S(2)}) copy-start(bf16[2,8,336,128]{3,2,1,0:T(8,128)(2,1)} %copy-done.11) | copy-start | bytes 4128772
  161.3 22.6 %all-to-all-start.3 = ((bf16[8,336,128]{2,1,0:T(8,128)(2,1)}), bf16[8,336,128]{2,1,0:T(8,128)(2,1)S(1)}, u32[]{:S(2)}, u32[]{:S(2)}) async-start(bf16[8,336,128]{2,1,0:T(8,128)(2,1)} %broadcast_in_dim.9), calls=%async_computation.3 | async-start | bytes 1376256 | tf_op jit(solution)/shard_map/all_to_all | solution.py:125
  164.8 46.8 %copy-start.8 = (f32[448,512]{1,0:T(8,128)S(1)}, f32[448,512]{1,0:T(8,128)}, u32[]{:S(2)}) copy-start(f32[448,512]{1,0:T(8,128)} %copy-done.7) | copy-start | bytes 2752516
  166.0 5.2 %collective-permute-start.10 = (bf16[2,112,128]{2,1,0:T(8,128)(2,1)S(1)}, bf16[2,112,128]{2,1,0:T(8,128)(2,1)S(1)}, u32[]{:S(2)}, u32[]{:S(2)}) collective-permute-start(bf16[2,112,128]{2,1,0:T(8,128)(2,1)S(1)} %reduce_sum.34), channel_id=1, source_target_pairs={{0,32},{32,0},{1,33},{33,1},{2,34},{34,2},{3,35},{35,3},{4,36},{36... | collective-permute-start | bytes 172040 | tf_op jit(solution)/shard_map/ppermute | solution.py:120
  183.9 16.1 %collective-permute-start.11 = (bf16[8,336,128]{2,1,0:T(8,128)(2,1)S(1)}, bf16[8,336,128]{2,1,0:T(8,128)(2,1)}, u32[]{:S(2)}, u32[]{:S(2)}) collective-permute-start(bf16[8,336,128]{2,1,0:T(8,128)(2,1)S(1)} %all-to-all-done.3.a0), channel_id=1, source_target_pairs={{0,32},{32,0},{1,33},{33,1},{2,34},{34,2},{3,35},{35,3},{4,36},{36... | collective-permute-start | bytes 2064392 | tf_op jit(solution)/shard_map/ppermute | solution.py:120
  187.8 17.8 %all-to-all-start.4 = ((bf16[8,2,112,128]{3,2,1,0:T(8,128)(2,1)}), bf16[8,2,112,128]{3,2,1,0:T(8,128)(2,1)S(1)}, u32[]{:S(2)}, u32[]{:S(2)}) async-start(bf16[8,2,112,128]{3,2,1,0:T(8,128)(2,1)} %broadcast_in_dim.10), calls=%async_computation.4 | async-start | bytes 917504 | tf_op jit(solution)/shard_map/all_to_all | solution.py:125
  191.3 18.9 %collective-permute-start.12 = (bf16[8,336,128]{2,1,0:T(8,128)(2,1)S(1)}, bf16[8,336,128]{2,1,0:T(8,128)(2,1)}, u32[]{:S(2)}, u32[]{:S(2)}) collective-permute-start(bf16[8,336,128]{2,1,0:T(8,128)(2,1)S(1)} %all-to-all-done.3.a0), channel_id=1, source_target_pairs={{0,16},{16,0},{1,17},{17,1},{2,18},{18,2},{3,19},{19,3},{4,20},{20... | collective-permute-start | bytes 2064392 | tf_op jit(solution)/shard_map/ppermute | solution.py:120
  199.9 11.6 %collective-permute-start.13 = (bf16[8,336,128]{2,1,0:T(8,128)(2,1)}, bf16[8,336,128]{2,1,0:T(8,128)(2,1)}, u32[]{:S(2)}, u32[]{:S(2)}) collective-permute-start(bf16[8,336,128]{2,1,0:T(8,128)(2,1)} %collective-permute-done.11.a1), channel_id=1, source_target_pairs={{0,16},{16,0},{1,17},{17,1},{2,18},{18,2},{3,19},{19,3},{4,20},{20... | collective-permute-start | bytes 2064392 | tf_op jit(solution)/shard_map/ppermute | solution.py:120
  205.6 5.9 %collective-permute-start.14 = (bf16[8,2,112,128]{3,2,1,0:T(8,128)(2,1)S(1)}, bf16[8,2,112,128]{3,2,1,0:T(8,128)(2,1)S(1)}, u32[]{:S(2)}, u32[]{:S(2)}) collective-permute-start(bf16[8,2,112,128]{3,2,1,0:T(8,128)(2,1)S(1)} %all-to-all-done.4.b0), channel_id=1, source_target_pairs={{0,16},{16,0},{1,17},{17,1},{2,18},{18,2},{3,19},{19,3},{4,20},{20... | collective-permute-start | bytes 1376264 | tf_op jit(solution)/shard_map/ppermute | solution.py:120
  211.6 2.2 copy-start.2
  219.9 13.4 %all-to-all-start.5 = ((f32[32,2,448]{2,1,0:T(2,128)}), f32[32,2,448]{2,1,0:T(2,128)S(1)}, u32[]{:S(2)}, u32[]{:S(2)}) async-start(f32[32,2,448]{2,1,0:T(2,128)} %broadcast_in_dim.11), calls=%async_computation.5 | async-start | bytes 262144 | tf_op jit(solution)/shard_map/all_to_all | solution.py:125

commit v3 on v2

v3 whole, which is shorter than its diff:
```python
import functools

import jax
import jax.numpy as jnp
from jax import lax
from jax.experimental import pallas as pl
from jax.experimental.pallas import tpu as pltpu
from jax.sharding import Mesh
from jax.sharding import PartitionSpec as P

REP = ("y", "zl", "c")
F32, BF = jnp.float32, jnp.bfloat16
NT = (((1,), (1,)), ((), ()))
CUT = 336
VMEM_LIMIT = 60 * 1024 * 1024
TOK = pltpu.VMEM((16, 512, 256), BF)
ACC = pltpu.VMEM((448, 512), F32)
VM = pl.BlockSpec(memory_space=pltpu.VMEM)
ANY = pl.BlockSpec(memory_space=pltpu.HBM)
SM = pl.BlockSpec(memory_space=pltpu.SMEM)


def call(kernel, outs, operands, flops, scratch, anywhere=(), out_anywhere=()):
    moved = sum(a.size * a.dtype.itemsize for a in operands) + sum(
        o.size * o.dtype.itemsize for o in outs
    )
    ins = [SM] + [ANY if i in anywhere else VM for i in range(1, len(operands))]
    return pl.pallas_call(
        kernel,
        out_shape=outs,
        in_specs=ins,
        out_specs=[ANY if i in out_anywhere else VM for i in range(len(outs))],
        scratch_shapes=list(scratch),
        cost_estimate=pl.CostEstimate(flops=flops, bytes_accessed=moved, transcendentals=0),
        compiler_params=pltpu.CompilerParams(vmem_limit_bytes=VMEM_LIMIT),
    )(*operands)


def block_of(refs, y, rel):
    a0, a1, a2, a3, b0, b1 = refs
    own, other = ((a0, a2), (a1, a3))[rel]
    return (
        jnp.concatenate([own[y], b0[y, rel]], 0),
        jnp.concatenate([other[y], b1[y, rel]], 0),
    )


def project(me, tok, block, acc, ready=None):
    mine, first = me[0], me[1] == 0
    acc[...] = jnp.zeros_like(acc)

    def step(y, unused):
        if ready is not None:
            ready(y)
        rows, cols = [], []
        for rel in (0, 1):
            own, other = block(y, rel)
            rows += [jnp.where(first, own, other), jnp.where(first, other, own)]
            cols.append(tok[2 * y + jnp.bitwise_xor(mine, rel)])
        acc[...] += lax.dot_general(
            jnp.concatenate(rows, 1), jnp.concatenate(cols, 1), NT, preferred_element_type=F32
        )
        return unused

    lax.fori_loop(0, 8, step, 0)


def fetch(source, tok, sems):
    def part(y):
        at = pl.ds(2 * y, 2)
        return pltpu.make_async_copy(source.at[at], tok.at[at], sems.at[y])

    for y in range(8):
        part(y).start()
    return lambda y: part(y).wait()


def first_kernel(*refs):
    me, t, zp, zm, z2a, z2b, x3, x1, o3, o1, fa, fb, up, cot, a0, a1, a2, a3, b0, b1 = refs[:20]
    tok_out, bend_out, own0, own1, sent, own_b, sent_b = refs[20:27]
    tok, coeff, bend, acc, sems, out_sems = refs[27:]
    mine, first = me[0], me[1] == 0
    copies = []

    def put(dx, dz, half, value):
        f = 4 * lax.rem(me[3] + dz, 4) + lax.rem(me[2] + dx, 4)
        there = tok.at[f, pl.ds(256 * half, 256), :]
        copies.append(pltpu.make_async_copy(value, there, sems.at[len(copies)]))

    for half in (0, 1):
        own = pl.ds(256 * half, 256)
        put(0, 0, half, t.at[own])
        put(0, 3, half, zp.at[own])
        put(0, 1, half, zm.at[own])
        put(0, 2, half, (z2a, z2b)[half])
        for dx, near, far in ((3, x3, o3), (1, x1, o1)):
            for i, dz in enumerate((0, 3, 1)):
                put(dx, dz, half, near.at[pl.ds(768 * half + 256 * i, 256)])
            put(dx, 2, half, far.at[own])
        for i, dz in enumerate((0, 3, 1, 2)):
            put(2, dz, half, (fa, fb)[half].at[pl.ds(256 * i, 256)])
    for copy in copies:
        copy.start()
    for copy in copies:
        copy.wait()
    keep_tok = pltpu.make_async_copy(tok, tok_out, out_sems.at[0])
    keep_tok.start()
    project(me, tok, functools.partial(block_of, (a0, a1, a2, a3, b0, b1)), acc)

    def part(i, unused):
        at = pl.ds(pl.multiple_of(i * 32, 32), 32)
        pre = acc[at, :]
        s = jax.nn.sigmoid(pre)
        one = s * (1.0 + pre * (1.0 - s))
        two = s * (1.0 - s) * (2.0 + pre * (1.0 - 2.0 * s))
        weighted = cot[at, :].astype(F32) * up[at, :].astype(F32)
        coeff[at, :] = (weighted * one).astype(BF)
        bend[at, :] = weighted * two
        return unused

    lax.fori_loop(0, 448 // 32, part, 0)
    keep_bend = pltpu.make_async_copy(bend, bend_out, out_sems.at[1])
    keep_bend.start()

    def step(y, unused):
        for rel, own in ((0, own0), (1, own1)):
            tile = tok[2 * y + jnp.bitwise_xor(mine, rel)]
            got = jnp.dot(coeff[...], tile, preferred_element_type=F32).astype(BF)
            low, high = got[:, :128], got[:, 128:]
            keep, give = jnp.where(first, low, high), jnp.where(first, high, low)
            own[y] = keep[:CUT]
            own_b[y, rel] = keep[CUT:]
            sent[rel, y] = give[:CUT]
            sent_b[y, rel] = give[CUT:]
        return unused

    lax.fori_loop(0, 8, step, 0)
    keep_tok.wait()
    keep_bend.wait()


def own_kernel(me, source, a0, a1, sent, b0, b1, acc, tok, sems):
    blocks = (a0, a1, sent.at[0], sent.at[1], b0, b1)
    project(me, tok, functools.partial(block_of, blocks), acc, fetch(source, tok, sems))


def mean_kernel(me, source, bend_in, own_in, a0, a1, a2, a3, b0, b1, sums, acc, bend, own, tok, sems):
    ready = fetch(source, tok, sems)
    get_bend = pltpu.make_async_copy(bend_in, bend, sems.at[8])
    get_own = pltpu.make_async_copy(own_in, own, sems.at[9])
    get_bend.start()
    get_own.start()
    project(me, tok, functools.partial(block_of, (a0, a1, a2, a3, b0, b1)), acc, ready)
    get_bend.wait()
    get_own.wait()
    c = jnp.zeros((448, 128), F32)
    s = jnp.zeros((448, 128), F32)
    for k in range(4):
        lanes = slice(128 * k, 128 * k + 128)
        mean = acc[:, lanes] / 32.0
        b = bend[:, lanes]
        off = own[:, lanes] - mean
        c += b * mean * mean
        s += b * off * off
    sums[0:1, :] = jnp.sum(c.T, axis=0, keepdims=True)
    sums[1:2, :] = jnp.sum(s.T, axis=0, keepdims=True)


def swap(value, axis):
    return lax.ppermute(value, axis, ((0, 1), (1, 0)))


def to_all(value, axis):
    count = lax.axis_size(axis)
    return lax.all_to_all(
        jnp.broadcast_to(value[None], (count, *value.shape)), axis, 0, 0, tiled=True
    )


def total(*values):
    return functools.reduce(jnp.add, [v.astype(F32) for v in values])


def shape(*lengths, dtype=BF):
    return jax.ShapeDtypeStruct(lengths, dtype)


def turn(value, axis, by):
    return lax.ppermute(value, axis, [(i, (i + by) % 4) for i in range(4)])


def all_features(t, weight_a, weight_b):
    zp, zm = turn(t, "zh", 1), turn(t, "zh", -1)
    three = (t, zp, zm)
    near = jnp.concatenate([v[:256] for v in three] + [v[256:] for v in three])
    x3, x1 = turn(near, "x", 1), turn(near, "x", -1)
    z2a, z2b = turn(zp[:256], "zh", 1), turn(zm[256:], "zh", -1)
    weights, (z2a, z2b) = all_rows(weight_a, weight_b, z2a, z2b)
    far = jnp.concatenate([z2a, z2b])
    o3, o1 = turn(far, "x", 1), turn(far, "x", -1)
    fa = turn(jnp.concatenate([x3[:768], o3[:256]]), "x", 1)
    fb = turn(jnp.concatenate([x1[768:], o1[256:]]), "x", -1)
    return (t, zp, zm, z2a, z2b, x3, x1, o3, o1, fa, fb), weights


def all_rows(part_a, part_b, *after):
    a0, part_b, *after = lax.optimization_barrier((to_all(part_a, "y"), part_b, *after))
    b0 = to_all(part_b, "y")
    a1 = swap(a0, "zl")
    return (a0, a1, swap(a0, "c"), swap(a1, "c"), b0, swap(b0, "c")), after


def shards(tokens, gate_weight, up_act, cotangent):
    me = jnp.stack([lax.axis_index(axis) for axis in ("zl", "c", "x", "zh")]).astype(jnp.int32)
    flops = 2 * 448 * 512 * 4096
    rest = 448 - CUT
    weight = gate_weight.T
    weight_b = jnp.stack([weight[CUT:], swap(weight[CUT:], "zl")])
    pieces, weights = all_features(tokens, weight[:CUT], weight_b)
    tok, bend, a0, a1, sent, b0, sent_b = call(
        first_kernel,
        [
            shape(16, 512, 256),
            shape(448, 512, dtype=F32),
            *[shape(8, CUT, 128)] * 2,
            shape(2, 8, CUT, 128),
            *[shape(8, 2, rest, 128)] * 2,
        ],
        (me, *pieces, up_act.T, cotangent.T, *weights),
        2 * flops,
        [TOK, pltpu.VMEM((448, 512), BF), *[ACC] * 2, *map(pltpu.SemaphoreType.DMA, ((32,), (2,)))],
        range(1, 12),
        (0, 1),
    )
    came_b = swap(sent_b, "c")
    sent, came_b = lax.optimization_barrier((sent, came_b))
    came = swap(sent, "c")
    across_b = lax.all_to_all(total(b0, came_b).astype(BF), "y", 0, 0, tiled=True)
    came_1 = swap(total(a1, came[1]).astype(BF), "zl")
    sums_a = total(a0, came[0], came_1).astype(BF)
    own = call(
        own_kernel,
        [shape(448, 512, dtype=F32)],
        (me, tok, a0, a1, sent, b0, sent_b),
        flops,
        [TOK, pltpu.SemaphoreType.DMA((8,))],
        (1,),
    )[0]
    sums_a, across_b, own = lax.optimization_barrier((sums_a, across_b, own))
    across_a = lax.all_to_all(sums_a, "y", 0, 0, tiled=True)
    part_b = jnp.sum(across_b.astype(F32), axis=0).astype(BF)
    other_b = swap(part_b, "zl")
    both_b = total(part_b, other_b[::-1]).astype(BF)
    grad_a = jnp.sum(across_a.astype(F32), axis=0).astype(BF)
    rows, _ = all_rows(grad_a, both_b)
    line = call(
        mean_kernel,
        [shape(2, 448, dtype=F32)],
        (me, tok, bend, own, *rows),
        flops,
        [*[ACC] * 3, TOK, pltpu.SemaphoreType.DMA((10,))],
        (1, 2, 3),
    )[0]
    whole = jnp.sum(to_all(line, REP), axis=0)
    grad = jnp.concatenate([grad_a, both_b[0]], axis=0).T
    return grad, whole[0], whole[1] / 31


def solution(mesh):
    torus = Mesh(mesh.devices.reshape(8, 2, 2, 4, 4), ("y", "zl", "c", "zh", "x"))
    fsdp = ("zh", "x")
    return jax.shard_map(
        shards,
        mesh=torus,
        in_specs=(P(REP, fsdp),) * 4,
        out_specs=(P(REP, fsdp), P(fsdp), P(fsdp)),
        check_vma=False,
    )
```

time: 235 us -> 249 us (1.060)
  starting transfers between devices: 89.1 us -> 113 us
  blocking collectives: 45.3 us -> 22.8 us
  Pallas kernels: 19.8 us -> 29.3 us
  waiting for transfers between devices: 54.4 us -> 59.9 us
  local copies, waits for them, and re-layouts: 18.2 us -> 14.6 us
    ppermute x4 -> x10, starting transfers between devices: 13 us -> 40.3 us  [turn(): return lax.ppermute(value, axis, [(i, (i + by) % 4) for i in range(4)])]
    all_gather x1 -> x0, blocking collectives: 23.3 us -> none  [shards(): w0 = lax.all_gather(gate_weight.T, 'y', axis=0)]
    pallas_call x4 -> x3, Pallas kernels: 19.8 us -> 29.3 us  [call(): pl.pallas_call(kernel, out_shape=outs, in_specs=ins, out_specs=[ANY if i...]
    unnamed x28 -> x46, local copies, waits for them, and re-layouts: 12 us -> 5.95 us
    ppermute x11 -> x13, starting transfers between devices: 47 us -> 41.4 us  [swap(): return lax.ppermute(value, axis, ((0, 1), (1, 0)))]
    all_to_all x4 -> x5, waiting for transfers between devices: 21.4 us -> 24.9 us  [to_all(): lax.all_to_all(jnp.broadcast_to(value[None], (count, *value.shape)), axis...]
    all_to_all x4 -> x5, starting transfers between devices: 21.9 us -> 24.2 us  [to_all(): lax.all_to_all(jnp.broadcast_to(value[None], (count, *value.shape)), axis...]
    ppermute x4 -> x10, waiting for transfers between devices: 11.1 us -> 13.4 us  [turn(): return lax.ppermute(value, axis, [(i, (i + by) % 4) for i in range(4)])]
  transfers between devices with their start and end apart: 20 -> 29, of which waited for: 11 -> 14; matrix products, arithmetic and copies ran while one was open for 3% -> 5% of each run, Pallas kernels for 2% -> 3%
where the time goes in v3:
time: 249 us; the launch traced here: 247 us
  starting transfers between devices  113 us (45%)
  waiting for transfers between devices  59.9 us (24%)
  Pallas kernels  29.3 us (12%)
  blocking collectives  22.8 us (9%)
  local copies, waits for them, and re-layouts  14.6 us (6%)
  other arithmetic  6.7 us (3%)
    ppermute x13, starting transfers between devices, swap(): return lax.ppermute(value, axis, ((0, 1), (1, 0)))  41.4 us
    ppermute x10, starting transfers between devices, turn(): return lax.ppermute(value, axis, [(i, (i + by) % 4) for i in range(4)])  40.3 us
    pallas_call x3, Pallas kernels, call(): pl.pallas_call(kernel, out_shape=outs, in_specs=ins, out_specs=[ANY if i...  29.3 us
    all_to_all x5, waiting for transfers between devices, to_all(): lax.all_to_all(jnp.broadcast_to(value[None], (count, *value.shape)), axis...  24.9 us
    all_to_all x5, starting transfers between devices, to_all(): lax.all_to_all(jnp.broadcast_to(value[None], (count, *value.shape)), axis...  24.2 us
    all_to_all x1, blocking collectives, shards(): across_a = lax.all_to_all(sums_a, 'y', 0, 0, tiled=True)  22.8 us
    ppermute x13, waiting for transfers between devices, swap(): return lax.ppermute(value, axis, ((0, 1), (1, 0)))  15.5 us
    ppermute x10, waiting for transfers between devices, turn(): return lax.ppermute(value, axis, [(i, (i + by) % 4) for i in range(4)])  13.4 us
  transfers between devices with their start and end apart: 29, of which 14 were waited for; matrix products, arithmetic and copies ran while one was open for 5% of the time, Pallas kernels for 3%

profile of v3, /device:TPU:1, one launch (start us, length us, event | category | flops | bytes accessed | tf_op | source)
XLA Modules:
  0.0 247.4 jit_solution(14838965553834520336)
XLA Ops:
  0.6 11.6 %collective-permute-start.1 = (bf16[512,256]{1,0:T(8,128)(2,1)}, bf16[512,256]{1,0:T(8,128)(2,1)S(1)}, u32[]{:S(2)}, u32[]{:S(2)}) collective-permute-start(bf16[512,256]{1,0:T(8,128)(2,1)} %refs_1_.1), channel_id=1, source_target_pairs={{0,12},{4,0},{8,4},{12,8},{1,13},{5,1},{9,5},{13,9},{2,14},{6,2},{... | collective-permute-start | bytes 786440 | tf_op jit(solution)/shard_map/ppermute | solution.py:189
  12.3 1.9 collective-permute-start
  15.0 3.1 %collective-permute-start.2 = (bf16[112,128]{1,0:T(8,128)(2,1)S(1)}, bf16[112,128]{1,0:T(8,128)(2,1)S(1)}, u32[]{:S(2)}, u32[]{:S(2)}) collective-permute-start(bf16[112,128]{1,0:T(8,128)(2,1)S(1)} %get-tuple-element.44), channel_id=1, source_target_pairs={{0,32},{32,0},{1,33},{33,1},{2,34},{34,2},{3,35},{35,3},{4,36},{36... | collective-permute-start | bytes 86024 | tf_op jit(solution)/shard_map/ppermute | solution.py:170
  19.9 6.8 %all-to-all-start = ((bf16[8,336,128]{2,1,0:T(8,128)(2,1)}), bf16[8,336,128]{2,1,0:T(8,128)(2,1)S(1)}, u32[]{:S(2)}, u32[]{:S(2)}) async-start(bf16[8,336,128]{2,1,0:T(8,128)(2,1)} %broadcast_in_dim.10), calls=%async_computation | async-start | bytes 1376256 | tf_op jit(solution)/shard_map/all_to_all | solution.py:175
  30.8 5.5 %collective-permute-start.4 = (bf16[256,256]{1,0:T(8,128)(2,1)S(1)}, bf16[256,256]{1,0:T(8,128)(2,1)S(1)}, u32[]{:S(2)}, u32[]{:S(2)}) collective-permute-start(bf16[256,256]{1,0:T(8,128)(2,1)S(1)} %get-tuple-element.40), channel_id=1, source_target_pairs={{0,12},{4,0},{8,4},{12,8},{1,13},{5,1},{9,5},{13,9},{2,14},{6,2},{... | collective-permute-start | bytes 393224 | tf_op jit(solution)/shard_map/ppermute | solution.py:189
  36.2 1.9 collective-permute-start.3
  38.2 4.4 %collective-permute-start.6 = (bf16[1536,256]{1,0:T(8,128)(2,1)}, bf16[1536,256]{1,0:T(8,128)(2,1)S(1)}, u32[]{:S(2)}, u32[]{:S(2)}) collective-permute-start(bf16[1536,256]{1,0:T(8,128)(2,1)} %get-tuple-element.39), channel_id=1, source_target_pairs={{0,3},{1,0},{2,1},{3,2},{4,7},{5,4},{6,5},{7,6},{8,11},{9,8},{10,9... | collective-permute-start | bytes 2359304 | tf_op jit(solution)/shard_map/ppermute | solution.py:189
  42.6 1.9 collective-permute-start.5
  44.5 3.0 %collective-permute-done.3.refs_4_ = bf16[256,256]{1,0:T(8,128)(2,1)S(1)} collective-permute-done((bf16[256,256]{1,0:T(8,128)(2,1)S(1)}, bf16[256,256]{1,0:T(8,128)(2,1)S(1)}, u32[]{:S(2)}, u32[]{:S(2)}) %collective-permute-start.3) | collective-permute-done | bytes 131104 | tf_op jit(solution)/shard_map/ppermute | solution.py:189
  47.6 2.2 collective-permute-start.11
  50.6 6.5 %all-to-all-start.1 = ((bf16[8,2,112,128]{3,2,1,0:T(8,128)(2,1)}), bf16[8,2,112,128]{3,2,1,0:T(8,128)(2,1)S(1)}, u32[]{:S(2)}, u32[]{:S(2)}) async-start(bf16[8,2,112,128]{3,2,1,0:T(8,128)(2,1)} %broadcast_in_dim.11), calls=%async_computation.1 | async-start | bytes 917504 | tf_op jit(solution)/shard_map/all_to_all | solution.py:175
  57.2 4.4 %collective-permute-start.8 = (bf16[512,256]{1,0:T(8,128)(2,1)S(1)}, bf16[512,256]{1,0:T(8,128)(2,1)S(1)}, u32[]{:S(2)}, u32[]{:S(2)}) collective-permute-start(bf16[512,256]{1,0:T(8,128)(2,1)S(1)} %constant_dynamic-update-slice_fusion.2), channel_id=1, source_target_pairs={{0,3},{1,0},{2,1},{3,2},{4,7},{5,4},{6,5},{7,6},{8,11},{9,8},{10,9... | collective-permute-start | bytes 786440 | tf_op jit(solution)/shard_map/ppermute | solution.py:189
  61.6 1.9 collective-permute-start.7
  64.9 5.2 %collective-permute-start.12 = (bf16[8,336,128]{2,1,0:T(8,128)(2,1)S(1)}, bf16[8,336,128]{2,1,0:T(8,128)(2,1)}, u32[]{:S(2)}, u32[]{:S(2)}) collective-permute-start(bf16[8,336,128]{2,1,0:T(8,128)(2,1)S(1)} %all-to-all-done.refs_14_), channel_id=1, source_target_pairs={{0,16},{16,0},{1,17},{17,1},{2,18},{18,2},{3,19},{19,3},{4,20},{20... | collective-permute-start | bytes 2064392 | tf_op jit(solution)/shard_map/ppermute | solution.py:170
  70.1 1.9 collective-permute-start.13
  72.1 4.9 %collective-permute-start.10 = (bf16[1024,256]{1,0:T(8,128)(2,1)S(1)}, bf16[1024,256]{1,0:T(8,128)(2,1)S(1)}, u32[]{:S(2)}, u32[]{:S(2)}) collective-permute-start(bf16[1024,256]{1,0:T(8,128)(2,1)S(1)} %pad_maximum_fusion.1), channel_id=1, source_target_pairs={{0,3},{1,0},{2,1},{3,2},{4,7},{5,4},{6,5},{7,6},{8,11},{9,8},{10,9... | collective-permute-start | bytes 1572872 | tf_op jit(solution)/shard_map/ppermute | solution.py:189
  77.7 1.9 collective-permute-start.9
  79.7 2.7 %collective-permute-start.14 = (bf16[8,2,112,128]{3,2,1,0:T(8,128)(2,1)S(1)}, bf16[8,2,112,128]{3,2,1,0:T(8,128)(2,1)}, u32[]{:S(2)}, u32[]{:S(2)}) collective-permute-start(bf16[8,2,112,128]{3,2,1,0:T(8,128)(2,1)S(1)} %all-to-all-done.1.refs_18_), channel_id=1, source_target_pairs={{0,16},{16,0},{1,17},{17,1},{2,18},{18,2},{3,19},{19,3},{4,20},{20... | collective-permute-start | bytes 1376264 | tf_op jit(solution)/shard_map/ppermute | solution.py:170
  83.0 4.7 %collective-permute-done.10.refs_11_ = bf16[1024,256]{1,0:T(8,128)(2,1)S(1)} collective-permute-done((bf16[1024,256]{1,0:T(8,128)(2,1)S(1)}, bf16[1024,256]{1,0:T(8,128)(2,1)S(1)}, u32[]{:S(2)}, u32[]{:S(2)}) %collective-permute-start.10) | collective-permute-done | bytes 524320 | tf_op jit(solution)/shard_map/ppermute | solution.py:189
  87.7 5.8 %collective-permute-done.9.refs_10_ = bf16[1024,256]{1,0:T(8,128)(2,1)S(1)} collective-permute-done((bf16[1024,256]{1,0:T(8,128)(2,1)S(1)}, bf16[1024,256]{1,0:T(8,128)(2,1)S(1)}, u32[]{:S(2)}, u32[]{:S(2)}) %collective-permute-start.9) | collective-permute-done | bytes 524320 | tf_op jit(solution)/shard_map/ppermute | solution.py:189
  94.3 14.2 %shard_map.67 = (bf16[16,512,256]{2,1,0:T(8,128)(2,1)}, f32[448,512]{1,0:T(8,128)}, bf16[8,336,128]{2,1,0:T(8,128)(2,1)}, bf16[8,336,128]{2,1,0:T(8,128)(2,1)}, ...) custom-call(s32[4]{0:T(128)} %pad_add_fusion.refs_0_.me, ...), custom_call_target="tpu_custom_call" | custom-call | flops 3758096384 | bytes 17563664 | tf_op jit(solution)/shard_map/pallas_call | solution.py:28
  108.5 3.7 %collective-permute-start.15 = (bf16[8,2,112,128]{3,2,1,0:T(8,128)(2,1)}, bf16[8,2,112,128]{3,2,1,0:T(8,128)(2,1)S(1)}, u32[]{:S(2)}, u32[]{:S(2)}) collective-permute-start(bf16[8,2,112,128]{3,2,1,0:T(8,128)(2,1)} %get-tuple-element.27.b1), channel_id=1, source_target_pairs={{0,16},{16,0},{1,17},{17,1},{2,18},{18,2},{3,19},{19,3},{4,20},{20... | collective-permute-start | bytes 1376264 | tf_op jit(solution)/shard_map/ppermute | solution.py:170
  112.2 1.6 collective-permute-done.15
  113.9 2.3 collective-permute-start.16
  116.2 2.9 %collective-permute-done.16 = bf16[2,8,336,128]{3,2,1,0:T(8,128)(2,1)S(1)} collective-permute-done((bf16[2,8,336,128]{3,2,1,0:T(8,128)(2,1)}, bf16[2,8,336,128]{3,2,1,0:T(8,128)(2,1)S(1)}, u32[]{:S(2)}, u32[]{:S(2)}) %collective-permute-start.16) | collective-permute-done | bytes 1376288 | tf_op jit(solution)/shard_map/ppermute | solution.py:170
  119.1 2.1 fusion
  121.2 1.9 collective-permute-start.17
  124.1 6.9 %all-to-all-start.2 = ((bf16[8,2,112,128]{3,2,1,0:T(8,128)(2,1)}), bf16[8,2,112,128]{3,2,1,0:T(8,128)(2,1)S(1)}, u32[]{:S(2)}, u32[]{:S(2)}) async-start(bf16[8,2,112,128]{3,2,1,0:T(8,128)(2,1)} %add_convert_fusion), calls=%async_computation.2 | async-start | bytes 917504 | tf_op jit(solution)/shard_map/all_to_all | solution.py:238
  131.0 7.6 %shard_map.68.own_in = f32[448,512]{1,0:T(8,128)} custom-call(s32[4]{0:T(128)} %pad_add_fusion.refs_0_.me, bf16[16,512,256]{2,1,0:T(8,128)(2,1)} %get-tuple-element.32.source, bf16[8,336,128]{2,1,0:T(8,128)(2,1)} %get-tuple-element.25.a0, bf16[8,336,128]{2,1,0:T(8,128)(2,1)} %get-tuple-element.29.a1, bf16[2,8,336,128]{3,2,1,0:T(8,128)(2,1)} %get-tuple-element.28.sent, ...), custom_call_target="tpu_custom_call" | custom-call | flops 1879048192 | bytes 8781840 | tf_op jit(solution)/shard_map/pallas_call | solution.py:28
  138.6 1.4 collective-permute-done.17
  140.1 1.4 fusion.2
  141.5 6.1 %all-to-all-done.2 = bf16[8,2,112,128]{3,2,1,0:T(8,128)(2,1)S(1)} async-done(((bf16[8,2,112,128]{3,2,1,0:T(8,128)(2,1)}), bf16[8,2,112,128]{3,2,1,0:T(8,128)(2,1)S(1)}, u32[]{:S(2)}, u32[]{:S(2)}) %all-to-all-start.2) | async-done | bytes 458784 | tf_op jit(solution)/shard_map/all_to_all | solution.py:238
  147.5 22.8 %all_to_all.35 = bf16[8,336,128]{2,1,0:T(8,128)(2,1)S(1)} all-to-all(bf16[8,336,128]{2,1,0:T(8,128)(2,1)S(1)} %fusion.2), channel_id=1, replica_groups=mesh['y'=8,'zl'=2,'c'=2,'zh'=4,'x'=4] {'y'}, dimensions={0} | all-to-all | bytes 1376256 | tf_op jit(solution)/shard_map/all_to_all | solution.py:250
  171.4 3.5 %all-to-all-start.4 = ((bf16[8,336,128]{2,1,0:T(8,128)(2,1)}), bf16[8,336,128]{2,1,0:T(8,128)(2,1)S(1)}, u32[]{:S(2)}, u32[]{:S(2)}) async-start(bf16[8,336,128]{2,1,0:T(8,128)(2,1)} %broadcast_in_dim.12), calls=%async_computation.4 | async-start | bytes 1376256 | tf_op jit(solution)/shard_map/all_to_all | solution.py:175
  175.0 3.3 %collective-permute-start.18 = (bf16[2,112,128]{2,1,0:T(8,128)(2,1)S(1)}, bf16[2,112,128]{2,1,0:T(8,128)(2,1)S(1)}, u32[]{:S(2)}, u32[]{:S(2)}) collective-permute-start(bf16[2,112,128]{2,1,0:T(8,128)(2,1)S(1)} %reduce_sum.34), channel_id=1, source_target_pairs={{0,32},{32,0},{1,33},{33,1},{2,34},{34,2},{3,35},{35,3},{4,36},{36... | collective-permute-start | bytes 172040 | tf_op jit(solution)/shard_map/ppermute | solution.py:170
  178.4 1.6 collective-permute-done.18
  180.0 15.6 %all-to-all-done.4.a0 = bf16[8,336,128]{2,1,0:T(8,128)(2,1)S(1)} async-done(((bf16[8,336,128]{2,1,0:T(8,128)(2,1)}), bf16[8,336,128]{2,1,0:T(8,128)(2,1)S(1)}, u32[]{:S(2)}, u32[]{:S(2)}) %all-to-all-start.4) | async-done | bytes 688160 | tf_op jit(solution)/shard_map/all_to_all | solution.py:175
  195.6 3.2 %collective-permute-start.19 = (bf16[8,336,128]{2,1,0:T(8,128)(2,1)S(1)}, bf16[8,336,128]{2,1,0:T(8,128)(2,1)S(1)}, u32[]{:S(2)}, u32[]{:S(2)}) collective-permute-start(bf16[8,336,128]{2,1,0:T(8,128)(2,1)S(1)} %all-to-all-done.4.a0), channel_id=1, source_target_pairs={{0,32},{32,0},{1,33},{33,1},{2,34},{34,2},{3,35},{35,3},{4,36},{36... | collective-permute-start | bytes 2064392 | tf_op jit(solution)/shard_map/ppermute | solution.py:170
  199.7 3.5 %all-to-all-start.5 = ((bf16[8,2,112,128]{3,2,1,0:T(8,128)(2,1)}), bf16[8,2,112,128]{3,2,1,0:T(8,128)(2,1)S(1)}, u32[]{:S(2)}, u32[]{:S(2)}) async-start(bf16[8,2,112,128]{3,2,1,0:T(8,128)(2,1)} %broadcast_in_dim.13), calls=%async_computation.5 | async-start | bytes 917504 | tf_op jit(solution)/shard_map/all_to_all | solution.py:175
  203.1 3.6 %collective-permute-start.20 = (bf16[8,336,128]{2,1,0:T(8,128)(2,1)S(1)}, bf16[8,336,128]{2,1,0:T(8,128)(2,1)S(1)}, u32[]{:S(2)}, u32[]{:S(2)}) collective-permute-start(bf16[8,336,128]{2,1,0:T(8,128)(2,1)S(1)} %all-to-all-done.4.a0), channel_id=1, source_target_pairs={{0,16},{16,0},{1,17},{17,1},{2,18},{18,2},{3,19},{19,3},{4,20},{20... | collective-permute-start | bytes 2064392 | tf_op jit(solution)/shard_map/ppermute | solution.py:170
  206.7 6.5 %collective-permute-done.19.a1 = bf16[8,336,128]{2,1,0:T(8,128)(2,1)S(1)} collective-permute-done((bf16[8,336,128]{2,1,0:T(8,128)(2,1)S(1)}, bf16[8,336,128]{2,1,0:T(8,128)(2,1)S(1)}, u32[]{:S(2)}, u32[]{:S(2)}) %collective-permute-start.19) | collective-permute-done | bytes 688160 | tf_op jit(solution)/shard_map/ppermute | solution.py:170
  213.2 4.0 %collective-permute-start.21 = (bf16[8,336,128]{2,1,0:T(8,128)(2,1)S(1)}, bf16[8,336,128]{2,1,0:T(8,128)(2,1)S(1)}, u32[]{:S(2)}, u32[]{:S(2)}) collective-permute-start(bf16[8,336,128]{2,1,0:T(8,128)(2,1)S(1)} %collective-permute-done.19.a1), channel_id=1, source_target_pairs={{0,16},{16,0},{1,17},{17,1},{2,18},{18,2},{3,19},{19,3},{4,20},{20... | collective-permute-start | bytes 2064392 | tf_op jit(solution)/shard_map/ppermute | solution.py:170
  217.6 4.4 %collective-permute-start.22 = (bf16[8,2,112,128]{3,2,1,0:T(8,128)(2,1)S(1)}, bf16[8,2,112,128]{3,2,1,0:T(8,128)(2,1)S(1)}, u32[]{:S(2)}, u32[]{:S(2)}) collective-permute-start(bf16[8,2,112,128]{3,2,1,0:T(8,128)(2,1)S(1)} %all-to-all-done.5.b0), channel_id=1, source_target_pairs={{0,16},{16,0},{1,17},{17,1},{2,18},{18,2},{3,19},{19,3},{4,20},{20... | collective-permute-start | bytes 1376264 | tf_op jit(solution)/shard_map/ppermute | solution.py:170
  222.0 1.4 collective-permute-done.22.b1
  224.5 7.6 %shard_map.69 = f32[2,448]{1,0:T(2,128)} custom-call(s32[4]{0:T(128)} %pad_add_fusion.refs_0_.me, bf16[16,512,256]{2,1,0:T(8,128)(2,1)} %get-tuple-element.32.source, f32[448,512]{1,0:T(8,128)} %get-tuple-element.35.bend_in, f32[448,512]{1,0:T(8,128)} %shard_map.68.own_in, bf16[8,336,128]{2,1,0:T(8,128)(2,1)} %copy-done, bf16[8,336,128]{2,1,0:T(8,128)(2,1)} %copy-done.5, ...), custom_call_target="tpu_custom_call" | custom-call | flops 1879048192 | bytes 9702928 | tf_op jit(solution)/shard_map/pallas_call | solution.py:28
  232.0 1.4 broadcast_in_dim.14
  233.4 3.9 %all-to-all-start.6 = ((f32[32,2,448]{2,1,0:T(2,128)}), f32[32,2,448]{2,1,0:T(2,128)S(1)}, u32[]{:S(2)}, u32[]{:S(2)}) async-start(f32[32,2,448]{2,1,0:T(2,128)} %broadcast_in_dim.14), calls=%async_computation.6 | async-start | bytes 262144 | tf_op jit(solution)/shard_map/all_to_all | solution.py:175
  238.0 8.8 %all-to-all-done.6 = f32[32,2,448]{2,1,0:T(2,128)S(1)} async-done(((f32[32,2,448]{2,1,0:T(2,128)}), f32[32,2,448]{2,1,0:T(2,128)S(1)}, u32[]{:S(2)}, u32[]{:S(2)}) %all-to-all-start.6) | async-done | bytes 114720 | tf_op jit(solution)/shard_map/all_to_all | solution.py:175
  (87 shorter events, 16.9 us)
Async XLA Ops:
  0.6 26.1 %copy-start.12 = (bf16[512,256]{1,0:T(8,128)(2,1)S(1)}, bf16[512,256]{1,0:T(8,128)(2,1)}, u32[]{:S(2)}) copy-start(bf16[512,256]{1,0:T(8,128)(2,1)} %refs_1_.1) | copy-start | bytes 786436
  0.6 27.5 %collective-permute-start.1 = (bf16[512,256]{1,0:T(8,128)(2,1)}, bf16[512,256]{1,0:T(8,128)(2,1)S(1)}, u32[]{:S(2)}, u32[]{:S(2)}) collective-permute-start(bf16[512,256]{1,0:T(8,128)(2,1)} %refs_1_.1), channel_id=1, source_target_pairs={{0,12},{4,0},{8,4},{12,8},{1,13},{5,1},{9,5},{13,9},{2,14},{6,2},{... | collective-permute-start | bytes 786440 | tf_op jit(solution)/shard_map/ppermute | solution.py:189
  12.3 15.1 %collective-permute-start = (bf16[512,256]{1,0:T(8,128)(2,1)}, bf16[512,256]{1,0:T(8,128)(2,1)S(1)}, u32[]{:S(2)}, u32[]{:S(2)}) collective-permute-start(bf16[512,256]{1,0:T(8,128)(2,1)} %refs_1_.1), channel_id=1, source_target_pairs={{0,4},{4,8},{8,12},{12,0},{1,5},{5,9},{9,13},{13,1},{2,6},{6,10},{... | collective-permute-start | bytes 786440 | tf_op jit(solution)/shard_map/ppermute | solution.py:189
  15.0 29.5 %collective-permute-start.2 = (bf16[112,128]{1,0:T(8,128)(2,1)S(1)}, bf16[112,128]{1,0:T(8,128)(2,1)S(1)}, u32[]{:S(2)}, u32[]{:S(2)}) collective-permute-start(bf16[112,128]{1,0:T(8,128)(2,1)S(1)} %get-tuple-element.44), channel_id=1, source_target_pairs={{0,32},{32,0},{1,33},{33,1},{2,34},{34,2},{3,35},{35,3},{4,36},{36... | collective-permute-start | bytes 86024 | tf_op jit(solution)/shard_map/ppermute | solution.py:170
  19.9 27.7 %all-to-all-start = ((bf16[8,336,128]{2,1,0:T(8,128)(2,1)}), bf16[8,336,128]{2,1,0:T(8,128)(2,1)S(1)}, u32[]{:S(2)}, u32[]{:S(2)}) async-start(bf16[8,336,128]{2,1,0:T(8,128)(2,1)} %broadcast_in_dim.10), calls=%async_computation | async-start | bytes 1376256 | tf_op jit(solution)/shard_map/all_to_all | solution.py:175
  27.4 23.2 %copy-start.8 = (bf16[512,256]{1,0:T(8,128)(2,1)}, bf16[512,256]{1,0:T(8,128)(2,1)S(1)}, u32[]{:S(2)}) copy-start(bf16[512,256]{1,0:T(8,128)(2,1)S(1)} %collective-permute-done.refs_2_) | copy-start | bytes 786436
  28.1 22.5 %copy-start.11 = (bf16[512,256]{1,0:T(8,128)(2,1)}, bf16[512,256]{1,0:T(8,128)(2,1)S(1)}, u32[]{:S(2)}) copy-start(bf16[512,256]{1,0:T(8,128)(2,1)S(1)} %collective-permute-done.1.refs_3_) | copy-start | bytes 786436
  30.8 13.7 %collective-permute-start.4 = (bf16[256,256]{1,0:T(8,128)(2,1)S(1)}, bf16[256,256]{1,0:T(8,128)(2,1)S(1)}, u32[]{:S(2)}, u32[]{:S(2)}) collective-permute-start(bf16[256,256]{1,0:T(8,128)(2,1)S(1)} %get-tuple-element.40), channel_id=1, source_target_pairs={{0,12},{4,0},{8,4},{12,8},{1,13},{5,1},{9,5},{13,9},{2,14},{6,2},{... | collective-permute-start | bytes 393224 | tf_op jit(solution)/shard_map/ppermute | solution.py:189
  36.2 11.3 %collective-permute-start.3 = (bf16[256,256]{1,0:T(8,128)(2,1)S(1)}, bf16[256,256]{1,0:T(8,128)(2,1)S(1)}, u32[]{:S(2)}, u32[]{:S(2)}) collective-permute-start(bf16[256,256]{1,0:T(8,128)(2,1)S(1)} %get-tuple-element.42), channel_id=1, source_target_pairs={{0,4},{4,8},{8,12},{12,0},{1,5},{5,9},{9,13},{13,1},{2,6},{6,10},{... | collective-permute-start | bytes 393224 | tf_op jit(solution)/shard_map/ppermute | solution.py:189
  38.2 25.3 %collective-permute-start.6 = (bf16[1536,256]{1,0:T(8,128)(2,1)}, bf16[1536,256]{1,0:T(8,128)(2,1)S(1)}, u32[]{:S(2)}, u32[]{:S(2)}) collective-permute-start(bf16[1536,256]{1,0:T(8,128)(2,1)} %get-tuple-element.39), channel_id=1, source_target_pairs={{0,3},{1,0},{2,1},{3,2},{4,7},{5,4},{6,5},{7,6},{8,11},{9,8},{10,9... | collective-permute-start | bytes 2359304 | tf_op jit(solution)/shard_map/ppermute | solution.py:189
  42.6 21.0 %collective-permute-start.5 = (bf16[1536,256]{1,0:T(8,128)(2,1)}, bf16[1536,256]{1,0:T(8,128)(2,1)}, u32[]{:S(2)}, u32[]{:S(2)}) collective-permute-start(bf16[1536,256]{1,0:T(8,128)(2,1)} %get-tuple-element.39), channel_id=1, source_target_pairs={{0,1},{1,2},{2,3},{3,0},{4,5},{5,6},{6,7},{7,4},{8,9},{9,10},{10,1... | collective-permute-start | bytes 2359304 | tf_op jit(solution)/shard_map/ppermute | solution.py:189
  44.5 20.3 %copy-start.14 = (bf16[256,256]{1,0:T(8,128)(2,1)}, bf16[256,256]{1,0:T(8,128)(2,1)S(1)}, u32[]{:S(2)}) copy-start(bf16[256,256]{1,0:T(8,128)(2,1)S(1)} %collective-permute-done.4.refs_5_) | copy-start | bytes 393220
  47.5 17.4 %copy-start.15 = (bf16[256,256]{1,0:T(8,128)(2,1)}, bf16[256,256]{1,0:T(8,128)(2,1)S(1)}, u32[]{:S(2)}) copy-start(bf16[256,256]{1,0:T(8,128)(2,1)S(1)} %collective-permute-done.3.refs_4_) | copy-start | bytes 393220
  47.6 17.3 %copy-start.4 = (bf16[8,336,128]{2,1,0:T(8,128)(2,1)}, bf16[8,336,128]{2,1,0:T(8,128)(2,1)S(1)}, u32[]{:S(2)}) copy-start(bf16[8,336,128]{2,1,0:T(8,128)(2,1)S(1)} %all-to-all-done.refs_14_) | copy-start | bytes 2064388
  47.6 22.5 %collective-permute-start.11 = (bf16[8,336,128]{2,1,0:T(8,128)(2,1)S(1)}, bf16[8,336,128]{2,1,0:T(8,128)(2,1)}, u32[]{:S(2)}, u32[]{:S(2)}) collective-permute-start(bf16[8,336,128]{2,1,0:T(8,128)(2,1)S(1)} %all-to-all-done.refs_14_), channel_id=1, source_target_pairs={{0,32},{32,0},{1,33},{33,1},{2,34},{34,2},{3,35},{35,3},{4,36},{36... | collective-permute-start | bytes 2064392 | tf_op jit(solution)/shard_map/ppermute | solution.py:170
  50.6 29.0 %all-to-all-start.1 = ((bf16[8,2,112,128]{3,2,1,0:T(8,128)(2,1)}), bf16[8,2,112,128]{3,2,1,0:T(8,128)(2,1)S(1)}, u32[]{:S(2)}, u32[]{:S(2)}) async-start(bf16[8,2,112,128]{3,2,1,0:T(8,128)(2,1)} %broadcast_in_dim.11), calls=%async_computation.1 | async-start | bytes 917504 | tf_op jit(solution)/shard_map/all_to_all | solution.py:175
  57.2 12.9 %collective-permute-start.8 = (bf16[512,256]{1,0:T(8,128)(2,1)S(1)}, bf16[512,256]{1,0:T(8,128)(2,1)S(1)}, u32[]{:S(2)}, u32[]{:S(2)}) collective-permute-start(bf16[512,256]{1,0:T(8,128)(2,1)S(1)} %constant_dynamic-update-slice_fusion.2), channel_id=1, source_target_pairs={{0,3},{1,0},{2,1},{3,2},{4,7},{5,4},{6,5},{7,6},{8,11},{9,8},{10,9... | collective-permute-start | bytes 786440 | tf_op jit(solution)/shard_map/ppermute | solution.py:189
  61.6 15.4 %collective-permute-start.7 = (bf16[512,256]{1,0:T(8,128)(2,1)S(1)}, bf16[512,256]{1,0:T(8,128)(2,1)S(1)}, u32[]{:S(2)}, u32[]{:S(2)}) collective-permute-start(bf16[512,256]{1,0:T(8,128)(2,1)S(1)} %constant_dynamic-update-slice_fusion.2), channel_id=1, source_target_pairs={{0,1},{1,2},{2,3},{3,0},{4,5},{5,6},{6,7},{7,4},{8,9},{9,10},{10,1... | collective-permute-start | bytes 786440 | tf_op jit(solution)/shard_map/ppermute | solution.py:189
  63.5 8.6 %copy-start.13 = (bf16[1536,256]{1,0:T(8,128)(2,1)}, bf16[1536,256]{1,0:T(8,128)(2,1)S(1)}, u32[]{:S(2)}) copy-start(bf16[1536,256]{1,0:T(8,128)(2,1)S(1)} %collective-permute-done.6.refs_7_) | copy-start | bytes 2359300
  64.9 18.2 %collective-permute-start.12 = (bf16[8,336,128]{2,1,0:T(8,128)(2,1)S(1)}, bf16[8,336,128]{2,1,0:T(8,128)(2,1)}, u32[]{:S(2)}, u32[]{:S(2)}) collective-permute-start(bf16[8,336,128]{2,1,0:T(8,128)(2,1)S(1)} %all-to-all-done.refs_14_), channel_id=1, source_target_pairs={{0,16},{16,0},{1,17},{17,1},{2,18},{18,2},{3,19},{19,3},{4,20},{20... | collective-permute-start | bytes 2064392 | tf_op jit(solution)/shard_map/ppermute | solution.py:170
  70.1 23.4 %copy-start.16 = (bf16[512,256]{1,0:T(8,128)(2,1)}, bf16[512,256]{1,0:T(8,128)(2,1)S(1)}, u32[]{:S(2)}) copy-start(bf16[512,256]{1,0:T(8,128)(2,1)S(1)} %collective-permute-done.8.refs_9_) | copy-start | bytes 786436
  70.1 23.4 %collective-permute-start.13 = (bf16[8,336,128]{2,1,0:T(8,128)(2,1)}, bf16[8,336,128]{2,1,0:T(8,128)(2,1)}, u32[]{:S(2)}, u32[]{:S(2)}) collective-permute-start(bf16[8,336,128]{2,1,0:T(8,128)(2,1)} %collective-permute-done.11.refs_15_), channel_id=1, source_target_pairs={{0,16},{16,0},{1,17},{17,1},{2,18},{18,2},{3,19},{19,3},{4,20},{20... | collective-permute-start | bytes 2064392 | tf_op jit(solution)/shard_map/ppermute | solution.py:170
  72.1 15.6 %collective-permute-start.10 = (bf16[1024,256]{1,0:T(8,128)(2,1)S(1)}, bf16[1024,256]{1,0:T(8,128)(2,1)S(1)}, u32[]{:S(2)}, u32[]{:S(2)}) collective-permute-start(bf16[1024,256]{1,0:T(8,128)(2,1)S(1)} %pad_maximum_fusion.1), channel_id=1, source_target_pairs={{0,3},{1,0},{2,1},{3,2},{4,7},{5,4},{6,5},{7,6},{8,11},{9,8},{10,9... | collective-permute-start | bytes 1572872 | tf_op jit(solution)/shard_map/ppermute | solution.py:189
  77.7 15.8 %collective-permute-start.9 = (bf16[1024,256]{1,0:T(8,128)(2,1)S(1)}, bf16[1024,256]{1,0:T(8,128)(2,1)S(1)}, u32[]{:S(2)}, u32[]{:S(2)}) collective-permute-start(bf16[1024,256]{1,0:T(8,128)(2,1)S(1)} %pad_maximum_fusion), channel_id=1, source_target_pairs={{0,1},{1,2},{2,3},{3,0},{4,5},{5,6},{6,7},{7,4},{8,9},{9,10},{10,1... | collective-permute-start | bytes 1572872 | tf_op jit(solution)/shard_map/ppermute | solution.py:189
  79.7 13.9 %copy-start.9 = (bf16[8,2,112,128]{3,2,1,0:T(8,128)(2,1)}, bf16[8,2,112,128]{3,2,1,0:T(8,128)(2,1)S(1)}, u32[]{:S(2)}) copy-start(bf16[8,2,112,128]{3,2,1,0:T(8,128)(2,1)S(1)} %all-to-all-done.1.refs_18_) | copy-start | bytes 1376260
  79.7 13.8 %collective-permute-start.14 = (bf16[8,2,112,128]{3,2,1,0:T(8,128)(2,1)S(1)}, bf16[8,2,112,128]{3,2,1,0:T(8,128)(2,1)}, u32[]{:S(2)}, u32[]{:S(2)}) collective-permute-start(bf16[8,2,112,128]{3,2,1,0:T(8,128)(2,1)S(1)} %all-to-all-done.1.refs_18_), channel_id=1, source_target_pairs={{0,16},{16,0},{1,17},{17,1},{2,18},{18,2},{3,19},{19,3},{4,20},{20... | collective-permute-start | bytes 1376264 | tf_op jit(solution)/shard_map/ppermute | solution.py:170
  87.7 5.8 %copy-start.18 = (bf16[1024,256]{1,0:T(8,128)(2,1)}, bf16[1024,256]{1,0:T(8,128)(2,1)S(1)}, u32[]{:S(2)}) copy-start(bf16[1024,256]{1,0:T(8,128)(2,1)S(1)} %collective-permute-done.10.refs_11_) | copy-start | bytes 1572868
  93.5 0.8 copy-start.19
  108.5 14.6 %copy-start.3 = (bf16[8,2,112,128]{3,2,1,0:T(8,128)(2,1)S(1)}, bf16[8,2,112,128]{3,2,1,0:T(8,128)(2,1)}, u32[]{:S(2)}) copy-start(bf16[8,2,112,128]{3,2,1,0:T(8,128)(2,1)} %get-tuple-element.30.b0) | copy-start | bytes 1376260
  108.5 5.3 %collective-permute-start.15 = (bf16[8,2,112,128]{3,2,1,0:T(8,128)(2,1)}, bf16[8,2,112,128]{3,2,1,0:T(8,128)(2,1)S(1)}, u32[]{:S(2)}, u32[]{:S(2)}) collective-permute-start(bf16[8,2,112,128]{3,2,1,0:T(8,128)(2,1)} %get-tuple-element.27.b1), channel_id=1, source_target_pairs={{0,16},{16,0},{1,17},{17,1},{2,18},{18,2},{3,19},{19,3},{4,20},{20... | collective-permute-start | bytes 1376264 | tf_op jit(solution)/shard_map/ppermute | solution.py:170
  113.9 5.2 %collective-permute-start.16 = (bf16[2,8,336,128]{3,2,1,0:T(8,128)(2,1)}, bf16[2,8,336,128]{3,2,1,0:T(8,128)(2,1)S(1)}, u32[]{:S(2)}, u32[]{:S(2)}) collective-permute-start(bf16[2,8,336,128]{3,2,1,0:T(8,128)(2,1)} %get-tuple-element.28.sent), channel_id=1, source_target_pairs={{0,16},{16,0},{1,17},{17,1},{2,18},{18,2},{3,19},{19,3},{4,20},{20... | collective-permute-start | bytes 4128776 | tf_op jit(solution)/shard_map/ppermute | solution.py:170
  121.2 18.8 %collective-permute-start.17 = (bf16[8,336,128]{2,1,0:T(8,128)(2,1)}, bf16[8,336,128]{2,1,0:T(8,128)(2,1)}, u32[]{:S(2)}, u32[]{:S(2)}) collective-permute-start(bf16[8,336,128]{2,1,0:T(8,128)(2,1)} %fusion), channel_id=1, source_target_pairs={{0,32},{32,0},{1,33},{33,1},{2,34},{34,2},{3,35},{35,3},{4,36},{36... | collective-permute-start | bytes 2064392 | tf_op jit(solution)/shard_map/ppermute | solution.py:170
  124.1 23.4 %all-to-all-start.2 = ((bf16[8,2,112,128]{3,2,1,0:T(8,128)(2,1)}), bf16[8,2,112,128]{3,2,1,0:T(8,128)(2,1)S(1)}, u32[]{:S(2)}, u32[]{:S(2)}) async-start(bf16[8,2,112,128]{3,2,1,0:T(8,128)(2,1)} %add_convert_fusion), calls=%async_computation.2 | async-start | bytes 917504 | tf_op jit(solution)/shard_map/all_to_all | solution.py:238
  131.0 9.0 %copy-start.1 = (bf16[8,336,128]{2,1,0:T(8,128)(2,1)S(1)}, bf16[8,336,128]{2,1,0:T(8,128)(2,1)}, u32[]{:S(2)}) copy-start(bf16[8,336,128]{2,1,0:T(8,128)(2,1)} %get-tuple-element.25.a0) | copy-start | bytes 2064388
  171.4 24.2 %all-to-all-start.4 = ((bf16[8,336,128]{2,1,0:T(8,128)(2,1)}), bf16[8,336,128]{2,1,0:T(8,128)(2,1)S(1)}, u32[]{:S(2)}, u32[]{:S(2)}) async-start(bf16[8,336,128]{2,1,0:T(8,128)(2,1)} %broadcast_in_dim.12), calls=%async_computation.4 | async-start | bytes 1376256 | tf_op jit(solution)/shard_map/all_to_all | solution.py:175
  175.0 4.9 %collective-permute-start.18 = (bf16[2,112,128]{2,1,0:T(8,128)(2,1)S(1)}, bf16[2,112,128]{2,1,0:T(8,128)(2,1)S(1)}, u32[]{:S(2)}, u32[]{:S(2)}) collective-permute-start(bf16[2,112,128]{2,1,0:T(8,128)(2,1)S(1)} %reduce_sum.34), channel_id=1, source_target_pairs={{0,32},{32,0},{1,33},{33,1},{2,34},{34,2},{3,35},{35,3},{4,36},{36... | collective-permute-start | bytes 172040 | tf_op jit(solution)/shard_map/ppermute | solution.py:170
  195.6 27.8 %copy-start = (bf16[8,336,128]{2,1,0:T(8,128)(2,1)}, bf16[8,336,128]{2,1,0:T(8,128)(2,1)S(1)}, u32[]{:S(2)}) copy-start(bf16[8,336,128]{2,1,0:T(8,128)(2,1)S(1)} %all-to-all-done.4.a0) | copy-start | bytes 2064388
  195.6 17.6 %collective-permute-start.19 = (bf16[8,336,128]{2,1,0:T(8,128)(2,1)S(1)}, bf16[8,336,128]{2,1,0:T(8,128)(2,1)S(1)}, u32[]{:S(2)}, u32[]{:S(2)}) collective-permute-start(bf16[8,336,128]{2,1,0:T(8,128)(2,1)S(1)} %all-to-all-done.4.a0), channel_id=1, source_target_pairs={{0,32},{32,0},{1,33},{33,1},{2,34},{34,2},{3,35},{35,3},{4,36},{36... | collective-permute-start | bytes 2064392 | tf_op jit(solution)/shard_map/ppermute | solution.py:170
  199.7 18.0 %all-to-all-start.5 = ((bf16[8,2,112,128]{3,2,1,0:T(8,128)(2,1)}), bf16[8,2,112,128]{3,2,1,0:T(8,128)(2,1)S(1)}, u32[]{:S(2)}, u32[]{:S(2)}) async-start(bf16[8,2,112,128]{3,2,1,0:T(8,128)(2,1)} %broadcast_in_dim.13), calls=%async_computation.5 | async-start | bytes 917504 | tf_op jit(solution)/shard_map/all_to_all | solution.py:175
  203.1 18.9 %collective-permute-start.20 = (bf16[8,336,128]{2,1,0:T(8,128)(2,1)S(1)}, bf16[8,336,128]{2,1,0:T(8,128)(2,1)S(1)}, u32[]{:S(2)}, u32[]{:S(2)}) collective-permute-start(bf16[8,336,128]{2,1,0:T(8,128)(2,1)S(1)} %all-to-all-done.4.a0), channel_id=1, source_target_pairs={{0,16},{16,0},{1,17},{17,1},{2,18},{18,2},{3,19},{19,3},{4,20},{20... | collective-permute-start | bytes 2064392 | tf_op jit(solution)/shard_map/ppermute | solution.py:170
  213.2 10.2 %copy-start.5 = (bf16[8,336,128]{2,1,0:T(8,128)(2,1)}, bf16[8,336,128]{2,1,0:T(8,128)(2,1)S(1)}, u32[]{:S(2)}) copy-start(bf16[8,336,128]{2,1,0:T(8,128)(2,1)S(1)} %collective-permute-done.19.a1) | copy-start | bytes 2064388
  213.2 10.2 %collective-permute-start.21 = (bf16[8,336,128]{2,1,0:T(8,128)(2,1)S(1)}, bf16[8,336,128]{2,1,0:T(8,128)(2,1)S(1)}, u32[]{:S(2)}, u32[]{:S(2)}) collective-permute-start(bf16[8,336,128]{2,1,0:T(8,128)(2,1)S(1)} %collective-permute-done.19.a1), channel_id=1, source_target_pairs={{0,16},{16,0},{1,17},{17,1},{2,18},{18,2},{3,19},{19,3},{4,20},{20... | collective-permute-start | bytes 2064392 | tf_op jit(solution)/shard_map/ppermute | solution.py:170
  217.6 5.8 %copy-start.2 = (bf16[8,2,112,128]{3,2,1,0:T(8,128)(2,1)}, bf16[8,2,112,128]{3,2,1,0:T(8,128)(2,1)S(1)}, u32[]{:S(2)}) copy-start(bf16[8,2,112,128]{3,2,1,0:T(8,128)(2,1)S(1)} %all-to-all-done.5.b0) | copy-start | bytes 1376260
  217.6 5.8 %collective-permute-start.22 = (bf16[8,2,112,128]{3,2,1,0:T(8,128)(2,1)S(1)}, bf16[8,2,112,128]{3,2,1,0:T(8,128)(2,1)S(1)}, u32[]{:S(2)}, u32[]{:S(2)}) collective-permute-start(bf16[8,2,112,128]{3,2,1,0:T(8,128)(2,1)S(1)} %all-to-all-done.5.b0), channel_id=1, source_target_pairs={{0,16},{16,0},{1,17},{17,1},{2,18},{18,2},{3,19},{19,3},{4,20},{20... | collective-permute-start | bytes 1376264 | tf_op jit(solution)/shard_map/ppermute | solution.py:170
  222.0 1.4 copy-start.6
  223.4 0.8 copy-start.10
  223.4 1.1 copy-start.7
  233.4 13.3 %all-to-all-start.6 = ((f32[32,2,448]{2,1,0:T(2,128)}), f32[32,2,448]{2,1,0:T(2,128)S(1)}, u32[]{:S(2)}, u32[]{:S(2)}) async-start(f32[32,2,448]{2,1,0:T(2,128)} %broadcast_in_dim.14), calls=%async_computation.6 | async-start | bytes 262144 | tf_op jit(solution)/shard_map/all_to_all | solution.py:175
  (1 other events, 0.7 us)

commit v4 on v2

v4 whole, which is shorter than its diff:
```python
import functools

import jax
import jax.numpy as jnp
from jax import lax
from jax.experimental import pallas as pl
from jax.experimental.pallas import tpu as pltpu
from jax.sharding import Mesh
from jax.sharding import PartitionSpec as P

REP = ("y", "zl", "c")
F32, BF = jnp.float32, jnp.bfloat16
NT = (((1,), (1,)), ((), ()))
CUT = 336
VMEM_LIMIT = 60 * 1024 * 1024
TOK = pltpu.VMEM((16, 512, 256), BF)
ACC = pltpu.VMEM((448, 512), F32)
VM = pl.BlockSpec(memory_space=pltpu.VMEM)
ANY = pl.BlockSpec(memory_space=pltpu.HBM)
SM = pl.BlockSpec(memory_space=pltpu.SMEM)


def call(kernel, outs, operands, flops, scratch, near=False):
    moved = sum(a.size * a.dtype.itemsize for a in operands) + sum(
        o.size * o.dtype.itemsize for o in outs
    )
    return pl.pallas_call(
        kernel,
        out_shape=outs,
        in_specs=[SM] + [ANY] * (len(operands) - 1),
        out_specs=[VM if near else ANY] * len(outs),
        scratch_shapes=list(scratch),
        cost_estimate=pl.CostEstimate(flops=flops, bytes_accessed=moved, transcendentals=0),
        compiler_params=pltpu.CompilerParams(vmem_limit_bytes=VMEM_LIMIT),
    )(*operands)


def fetched(pairs, sems):
    def part(i, y):
        source, there = pairs[i]
        return pltpu.make_async_copy(source.at[y], there.at[y], sems.at[i, y])

    for y in range(8):
        for i in range(len(pairs)):
            part(i, y).start()

    def ready(y):
        for i in range(len(pairs)):
            part(i, y).wait()

    return ready


def rows_of(held, held_b, y, rel):
    own, other = held[rel, y], held[2 + rel, y]
    if held_b is None:
        return own, other
    return (
        jnp.concatenate([own, held_b[0, y, rel]], 0),
        jnp.concatenate([other, held_b[1, y, rel]], 0),
    )


def project(me, tok, held, held_b, acc, ready):
    mine, first = me[0], me[1] == 0

    def product(y):
        ready(y)
        rows, cols = [], []
        for rel in (0, 1):
            own, other = rows_of(held, held_b, y, rel)
            rows += [jnp.where(first, own, other), jnp.where(first, other, own)]
            cols.append(tok[2 * y + jnp.bitwise_xor(mine, rel)])
        return lax.dot_general(
            jnp.concatenate(rows, 1), jnp.concatenate(cols, 1), NT, preferred_element_type=F32
        )

    acc[...] = product(0)

    def step(y, unused):
        acc[...] += product(y)
        return unused

    lax.fori_loop(1, 8, step, 0)


def first_kernel(*refs):
    me, t0, p1, p2, m1, m2, f1, f2, up_in, cot_in, w0, w1, w2, w3 = refs[:14]
    tok_out, bend_out, *outs = refs[14:21]
    tok, held, up, cot, coeff, bend, acc, own, own_b, tok_sems, w_sems, in_sems, out_sems, sems = refs[21:]
    mine, first = me[0], me[1] == 0
    sources = ((t0.at[0:2], t0.at[2:4]), (m2, m1), (f1, f2), (p1, p2))

    def token_copy(d, z):
        there = tok.at[4 * z + lax.rem(me[2] + d, 4)]
        return pltpu.make_async_copy(sources[d][z // 2].at[z % 2], there, tok_sems.at[d, z])

    for d in (0, 1, 3, 2):
        for z in range(4):
            token_copy(d, z).start()
    w_ready = fetched([(w, held.at[i]) for i, w in enumerate((w0, w1, w2, w3))], w_sems)
    get_up = pltpu.make_async_copy(up_in, up, in_sems.at[0])
    get_cot = pltpu.make_async_copy(cot_in, cot, in_sems.at[1])
    get_up.start()
    get_cot.start()
    for d in (0, 1, 3, 2):
        for z in range(4):
            token_copy(d, z).wait()
    keep_tok = pltpu.make_async_copy(tok, tok_out, sems.at[0])
    keep_tok.start()
    project(me, tok, held, None, acc, w_ready)
    get_up.wait()
    get_cot.wait()

    def part(i, unused):
        at = pl.ds(pl.multiple_of(i * 32, 32), 32)
        pre = acc[at, :]
        s = jax.nn.sigmoid(pre)
        one = s * (1.0 + pre * (1.0 - s))
        two = s * (1.0 - s) * (2.0 + pre * (1.0 - 2.0 * s))
        weighted = cot[at, :].astype(F32) * up[at, :].astype(F32)
        coeff[at, :] = (weighted * one).astype(BF)
        bend[at, :] = weighted * two
        return unused

    lax.fori_loop(0, 448 // 32, part, 0)
    keep_bend = pltpu.make_async_copy(bend, bend_out, sems.at[1])
    keep_bend.start()

    def out_copies(y):
        pairs = [(own.at[k, y], out) for k, out in enumerate((outs[0].at[y], outs[1].at[y]))]
        pairs += [(own.at[2 + k, y], outs[2].at[k, y]) for k in range(2)]
        pairs += [(own_b.at[k, y], outs[3 + k].at[y]) for k in range(2)]
        return [
            pltpu.make_async_copy(here, there, out_sems.at[k, y])
            for k, (here, there) in enumerate(pairs)
        ]

    def step(y, unused):
        for rel in (0, 1):
            tile = tok[2 * y + jnp.bitwise_xor(mine, rel)]
            got = jnp.dot(coeff[...], tile, preferred_element_type=F32).astype(BF)
            low, high = got[:, :128], got[:, 128:]
            keep, give = jnp.where(first, low, high), jnp.where(first, high, low)
            own[rel, y] = keep[:CUT]
            own_b[0, y, rel] = keep[CUT:]
            own[2 + rel, y] = give[:CUT]
            own_b[1, y, rel] = give[CUT:]
        for copy in out_copies(y):
            copy.start()
        return unused

    lax.fori_loop(0, 8, step, 0)
    for y in range(8):
        for copy in out_copies(y):
            copy.wait()
    keep_tok.wait()
    keep_bend.wait()


def fetch_all(source, arrays, tok, held, held_b, tok_sems, sems):
    pairs = [(a, held.at[i]) for i, a in enumerate(arrays[:4])]
    pairs += [(b, held_b.at[i]) for i, b in enumerate(arrays[4:])]

    def part(y):
        at = pl.ds(2 * y, 2)
        return pltpu.make_async_copy(source.at[at], tok.at[at], tok_sems.at[y])

    for y in range(8):
        part(y).start()
    rows_ready = fetched(pairs, sems)

    def ready(y):
        part(y).wait()
        rows_ready(y)

    return ready


def own_kernel(me, source, a0, a1, sent, b0, b1, acc, tok, held, held_b, tok_sems, sems):
    arrays = (a0, a1, sent.at[0], sent.at[1], b0, b1)
    ready = fetch_all(source, arrays, tok, held, held_b, tok_sems, sems)
    project(me, tok, held, held_b, acc, ready)


def mean_kernel(me, source, bend_in, own_in, *refs):
    sums, acc, bend, own, tok, held, held_b, tok_sems, sems, in_sems = refs[6:]
    ready = fetch_all(source, refs[:6], tok, held, held_b, tok_sems, sems)
    get_bend = pltpu.make_async_copy(bend_in, bend, in_sems.at[0])
    get_own = pltpu.make_async_copy(own_in, own, in_sems.at[1])
    get_bend.start()
    get_own.start()
    project(me, tok, held, held_b, acc, ready)
    get_bend.wait()
    get_own.wait()
    c = jnp.zeros((448, 128), F32)
    s = jnp.zeros((448, 128), F32)
    for k in range(4):
        lanes = slice(128 * k, 128 * k + 128)
        mean = acc[:, lanes] / 32.0
        b = bend[:, lanes]
        off = own[:, lanes] - mean
        c += b * mean * mean
        s += b * off * off
    sums[0:1, :] = jnp.sum(c.T, axis=0, keepdims=True)
    sums[1:2, :] = jnp.sum(s.T, axis=0, keepdims=True)


def swap(value, axis):
    return lax.ppermute(value, axis, ((0, 1), (1, 0)))


def to_all(value, axis):
    count = lax.axis_size(axis)
    return lax.all_to_all(
        jnp.broadcast_to(value[None], (count, *value.shape)), axis, 0, 0, tiled=True
    )


def total(*values):
    return functools.reduce(jnp.add, [v.astype(F32) for v in values])


def shape(*lengths, dtype=BF):
    return jax.ShapeDtypeStruct(lengths, dtype)


def along_x(value, by):
    return lax.ppermute(value, "x", [(i, (i + by) % 4) for i in range(4)])


def all_rows(part_a, part_b):
    a0, part_b = lax.optimization_barrier((to_all(part_a, "y"), part_b))
    b0 = to_all(part_b, "y")
    a1 = swap(a0, "zl")
    return a0, a1, swap(a0, "c"), swap(a1, "c"), b0, swap(b0, "c")


def shards(tokens, gate_weight, up_act, cotangent):
    me = jnp.stack([lax.axis_index(axis) for axis in ("zl", "c", "x")]).astype(jnp.int32)
    flops = 2 * 448 * 512 * 4096
    rest = 448 - CUT
    dma = pltpu.SemaphoreType.DMA
    held = [pltpu.VMEM((4, 8, CUT, 128), BF), pltpu.VMEM((2, 8, 2, rest, 128), BF)]
    w0 = lax.all_gather(gate_weight.T, "y", axis=0)
    t0, w0 = lax.optimization_barrier((to_all(tokens, "zh"), w0))
    low, high = t0[:2], t0[2:]
    p1, m1 = along_x(low, 1), along_x(high, -1)
    p2, m2 = along_x(high, 1), along_x(low, -1)
    f1, f2 = along_x(p1, 1), along_x(m1, -1)
    w1, f1, f2 = lax.optimization_barrier((swap(w0, "zl"), f1, f2))
    w0, p2, m2 = lax.optimization_barrier((w0, p2, m2))
    w2, w3 = swap(w0, "c"), swap(w1, "c")
    tok, bend, a0, a1, sent, b0, sent_b = call(
        first_kernel,
        [
            shape(16, 512, 256),
            shape(448, 512, dtype=F32),
            *[shape(8, CUT, 128)] * 2,
            shape(2, 8, CUT, 128),
            *[shape(8, 2, rest, 128)] * 2,
        ],
        (me, t0, p1, p2, m1, m2, f1, f2, up_act.T, cotangent.T, w0, w1, w2, w3),
        2 * flops,
        [
            TOK,
            pltpu.VMEM((4, 8, 448, 128), BF),
            *[pltpu.VMEM((448, 512), BF)] * 3,
            *[ACC] * 2,
            *held,
            *map(dma, ((4, 4), (4, 8), (2,), (6, 8), (2,))),
        ],
    )
    came_b = swap(sent_b, "c")
    came = swap(sent, "c")
    across_b = lax.all_to_all(total(b0, came_b).astype(BF), "y", 0, 0, tiled=True)
    came_1 = swap(total(a1, came[1]).astype(BF), "zl")
    sums_a = total(a0, came[0], came_1).astype(BF)
    own = call(
        own_kernel,
        [shape(448, 512, dtype=F32)],
        (me, tok, a0, a1, sent, b0, sent_b),
        flops,
        [TOK, *held, dma((8,)), dma((6, 8))],
        True,
    )[0]
    sums_a, across_b, own = lax.optimization_barrier((sums_a, across_b, own))
    across_a = lax.all_to_all(sums_a, "y", 0, 0, tiled=True)
    part_b = jnp.sum(across_b.astype(F32), axis=0).astype(BF)
    other_b = swap(part_b, "zl")
    both_b = total(part_b, other_b[::-1]).astype(BF)
    grad_a = jnp.sum(across_a.astype(F32), axis=0).astype(BF)
    line = call(
        mean_kernel,
        [shape(2, 448, dtype=F32)],
        (me, tok, bend, own, *all_rows(grad_a, both_b)),
        flops,
        [*[ACC] * 3, TOK, *held, dma((8,)), dma((6, 8)), dma((2,))],
        True,
    )[0]
    whole = jnp.sum(to_all(line, REP), axis=0)
    grad = jnp.concatenate([grad_a, both_b[0]], axis=0).T
    return grad, whole[0], whole[1] / 31


def solution(mesh):
    torus = Mesh(mesh.devices.reshape(8, 2, 2, 4, 4), ("y", "zl", "c", "zh", "x"))
    fsdp = ("zh", "x")
    return jax.shard_map(
        shards,
        mesh=torus,
        in_specs=(P(REP, fsdp),) * 4,
        out_specs=(P(REP, fsdp), P(fsdp), P(fsdp)),
        check_vma=False,
    )
```

time: 235 us -> 238 us (1.013)
  local copies, waits for them, and re-layouts: 18.2 us -> 6.36 us
  Pallas kernels: 19.8 us -> 30 us
  starting transfers between devices: 89.1 us -> 94.5 us
    unnamed x28 -> x36, local copies, waits for them, and re-layouts: 12 us -> 1.1 us
    pallas_call x4 -> x3, Pallas kernels: 19.8 us -> 30 us  [call(): pl.pallas_call(kernel, out_shape=outs, in_specs=[SM] + [ANY] * (len(opera...]
    ppermute x4 -> x6, starting transfers between devices: 13 us -> 18.1 us  [along_x(): return lax.ppermute(value, 'x', [(i, (i + by) % 4) for i in range(4)])]
    ppermute x11, waiting for transfers between devices: 16.1 us -> 12.7 us  [swap(): return lax.ppermute(value, axis, ((0, 1), (1, 0)))]
    all_to_all x4, waiting for transfers between devices: 21.4 us -> 24.4 us  [to_all(): lax.all_to_all(jnp.broadcast_to(value[None], (count, *value.shape)), axis...]
    ppermute x4 -> x6, waiting for transfers between devices: 11.1 us -> 8.64 us  [along_x(): return lax.ppermute(value, 'x', [(i, (i + by) % 4) for i in range(4)])]
  transfers between devices with their start and end apart: 20 -> 22, of which waited for: 11 -> 11; matrix products, arithmetic and copies ran while one was open for 3% -> 3% of each run, Pallas kernels for 2% -> 3%
where the time goes in v4:
time: 238 us; the launch traced here: 237 us
  starting transfers between devices  94.5 us (40%)
  waiting for transfers between devices  52.6 us (22%)
  blocking collectives  46.1 us (19%)
  Pallas kernels  30 us (13%)
  other arithmetic  6.52 us (3%)
  local copies, waits for them, and re-layouts  6.36 us (3%)
    ppermute x11, starting transfers between devices, swap(): return lax.ppermute(value, axis, ((0, 1), (1, 0)))  47.8 us
    pallas_call x3, Pallas kernels, call(): pl.pallas_call(kernel, out_shape=outs, in_specs=[SM] + [ANY] * (len(opera...  30 us
    all_to_all x4, waiting for transfers between devices, to_all(): lax.all_to_all(jnp.broadcast_to(value[None], (count, *value.shape)), axis...  24.4 us
    all_gather x1, blocking collectives, shards(): w0 = lax.all_gather(gate_weight.T, 'y', axis=0)  23.3 us
    all_to_all x1, blocking collectives, shards(): across_a = lax.all_to_all(sums_a, 'y', 0, 0, tiled=True)  22.8 us
    all_to_all x4, starting transfers between devices, to_all(): lax.all_to_all(jnp.broadcast_to(value[None], (count, *value.shape)), axis...  21.9 us
    ppermute x6, starting transfers between devices, along_x(): return lax.ppermute(value, 'x', [(i, (i + by) % 4) for i in range(4)])  18.1 us
    ppermute x11, waiting for transfers between devices, swap(): return lax.ppermute(value, axis, ((0, 1), (1, 0)))  12.7 us
  transfers between devices with their start and end apart: 22, of which 11 were waited for; matrix products, arithmetic and copies ran while one was open for 3% of the time, Pallas kernels for 3%

profile of v4, /device:TPU:1, one launch (start us, length us, event | category | flops | bytes accessed | tf_op | source)
XLA Modules:
  0.0 237.2 jit_solution(1639956512692672265)
XLA Ops:
  0.6 2.0 broadcast_in_dim.8
  2.6 11.0 %all-to-all-start = ((bf16[4,512,256]{2,1,0:T(8,128)(2,1)}), bf16[4,512,256]{2,1,0:T(8,128)(2,1)S(1)}, u32[]{:S(2)}, u32[]{:S(2)}) async-start(bf16[4,512,256]{2,1,0:T(8,128)(2,1)} %broadcast_in_dim.8), calls=%async_computation | async-start | bytes 2097152 | tf_op jit(solution)/shard_map/all_to_all | solution.py:215
  13.6 23.3 %all-gather = bf16[3584,128]{1,0:T(8,128)(2,1)S(1)} all-gather(bf16[448,128]{1,0:T(8,128)(2,1)S(1)} %bitcast.26), channel_id=2, replica_groups=mesh['y'=8,'zl'=2,'c'=2,'zh'=4,'x'=4] {'y'}, dimensions={0}, use_global_device_ids=true | all-gather | bytes 1032192 | tf_op jit(solution)/shard_map/all_gather | solution.py:245
  37.0 4.4 %collective-permute-start.3 = (bf16[2,512,256]{2,1,0:T(8,128)(2,1)S(1)}, bf16[2,512,256]{2,1,0:T(8,128)(2,1)S(1)}, u32[]{:S(2)}, u32[]{:S(2)}) collective-permute-start(bf16[2,512,256]{2,1,0:T(8,128)(2,1)S(1)} %get-tuple-element.43), channel_id=1, source_target_pairs={{0,3},{1,0},{2,1},{3,2},{4,7},{5,4},{6,5},{7,6},{8,11},{9,8},{10,9... | collective-permute-start | bytes 1572872 | tf_op jit(solution)/shard_map/ppermute | solution.py:229
  41.4 1.9 collective-permute-start
  43.3 7.2 %collective-permute-start.4 = (bf16[8,448,128]{2,1,0:T(8,128)(2,1)S(1)}, bf16[8,448,128]{2,1,0:T(8,128)(2,1)S(1)}, u32[]{:S(2)}, u32[]{:S(2)}) collective-permute-start(bf16[8,448,128]{2,1,0:T(8,128)(2,1)S(1)} %bitcast.23), channel_id=1, source_target_pairs={{0,32},{32,0},{1,33},{33,1},{2,34},{34,2},{3,35},{35,3},{4,36},{36... | collective-permute-start | bytes 2752520 | tf_op jit(solution)/shard_map/ppermute | solution.py:210
  50.5 2.1 collective-permute-start.1
  52.6 4.4 %collective-permute-start.2 = (bf16[2,512,256]{2,1,0:T(8,128)(2,1)S(1)}, bf16[2,512,256]{2,1,0:T(8,128)(2,1)S(1)}, u32[]{:S(2)}, u32[]{:S(2)}) collective-permute-start(bf16[2,512,256]{2,1,0:T(8,128)(2,1)S(1)} %get-tuple-element.44), channel_id=1, source_target_pairs={{0,3},{1,0},{2,1},{3,2},{4,7},{5,4},{6,5},{7,6},{8,11},{9,8},{10,9... | collective-permute-start | bytes 1572872 | tf_op jit(solution)/shard_map/ppermute | solution.py:229
  57.0 3.4 %collective-permute-start.6 = (bf16[2,512,256]{2,1,0:T(8,128)(2,1)S(1)}, bf16[2,512,256]{2,1,0:T(8,128)(2,1)S(1)}, u32[]{:S(2)}, u32[]{:S(2)}) collective-permute-start(bf16[2,512,256]{2,1,0:T(8,128)(2,1)S(1)} %collective-permute-done.3.refs_4_), channel_id=1, source_target_pairs={{0,3},{1,0},{2,1},{3,2},{4,7},{5,4},{6,5},{7,6},{8,11},{9,8},{10,9... | collective-permute-start | bytes 1572872 | tf_op jit(solution)/shard_map/ppermute | solution.py:229
  60.4 1.9 collective-permute-start.5
  62.4 5.3 %collective-permute-done.1.refs_3_ = bf16[2,512,256]{2,1,0:T(8,128)(2,1)S(1)} collective-permute-done((bf16[2,512,256]{2,1,0:T(8,128)(2,1)S(1)}, bf16[2,512,256]{2,1,0:T(8,128)(2,1)S(1)}, u32[]{:S(2)}, u32[]{:S(2)}) %collective-permute-start.1) | collective-permute-done | bytes 524320 | tf_op jit(solution)/shard_map/ppermute | solution.py:229
  67.6 7.8 %collective-permute-start.7 = (bf16[8,448,128]{2,1,0:T(8,128)(2,1)S(1)}, bf16[8,448,128]{2,1,0:T(8,128)(2,1)}, u32[]{:S(2)}, u32[]{:S(2)}) collective-permute-start(bf16[8,448,128]{2,1,0:T(8,128)(2,1)S(1)} %bitcast.24), channel_id=1, source_target_pairs={{0,16},{16,0},{1,17},{17,1},{2,18},{18,2},{3,19},{19,3},{4,20},{20... | collective-permute-start | bytes 2752520 | tf_op jit(solution)/shard_map/ppermute | solution.py:210
  75.5 1.6 collective-permute-done.6.refs_7_
  77.1 1.8 collective-permute-done.5.refs_6_
  78.9 5.1 %collective-permute-start.8 = (bf16[8,448,128]{2,1,0:T(8,128)(2,1)S(1)}, bf16[8,448,128]{2,1,0:T(8,128)(2,1)}, u32[]{:S(2)}, u32[]{:S(2)}) collective-permute-start(bf16[8,448,128]{2,1,0:T(8,128)(2,1)S(1)} %collective-permute-done.4.refs_11_), channel_id=1, source_target_pairs={{0,16},{16,0},{1,17},{17,1},{2,18},{18,2},{3,19},{19,3},{4,20},{20... | collective-permute-start | bytes 2752520 | tf_op jit(solution)/shard_map/ppermute | solution.py:210
  84.5 1.6 collective-permute-done.8.refs_13_
  86.1 13.6 %shard_map.67 = (bf16[16,512,256]{2,1,0:T(8,128)(2,1)}, f32[448,512]{1,0:T(8,128)}, bf16[8,336,128]{2,1,0:T(8,128)(2,1)}, bf16[8,336,128]{2,1,0:T(8,128)(2,1)}, ...) custom-call(s32[3]{0:T(128)} %pad_add_fusion.refs_0_.me, ...), custom_call_target="tpu_custom_call" | custom-call | flops 3758096384 | bytes 17563660 | tf_op jit(solution)/shard_map/pallas_call | solution.py:27
  99.8 2.4 %collective-permute-start.9 = (bf16[2,8,336,128]{3,2,1,0:T(8,128)(2,1)}, bf16[2,8,336,128]{3,2,1,0:T(8,128)(2,1)S(1)}, u32[]{:S(2)}, u32[]{:S(2)}) collective-permute-start(bf16[2,8,336,128]{3,2,1,0:T(8,128)(2,1)} %get-tuple-element.32.sent), channel_id=1, source_target_pairs={{0,16},{16,0},{1,17},{17,1},{2,18},{18,2},{3,19},{19,3},{4,20},{20... | collective-permute-start | bytes 4128776 | tf_op jit(solution)/shard_map/ppermute | solution.py:210
  102.2 2.0 collective-permute-start.11
  104.3 0.9 collective-permute-done.9
  105.2 2.2 fusion
  107.4 6.5 %collective-permute-start.10 = (bf16[8,336,128]{2,1,0:T(8,128)(2,1)}, bf16[8,336,128]{2,1,0:T(8,128)(2,1)}, u32[]{:S(2)}, u32[]{:S(2)}) collective-permute-start(bf16[8,336,128]{2,1,0:T(8,128)(2,1)} %fusion), channel_id=1, source_target_pairs={{0,32},{32,0},{1,33},{33,1},{2,34},{34,2},{3,35},{35,3},{4,36},{36... | collective-permute-start | bytes 2064392 | tf_op jit(solution)/shard_map/ppermute | solution.py:210
  113.8 0.9 add_convert_fusion
  114.7 6.8 %all-to-all-start.1 = ((bf16[8,2,112,128]{3,2,1,0:T(8,128)(2,1)}), bf16[8,2,112,128]{3,2,1,0:T(8,128)(2,1)S(1)}, u32[]{:S(2)}, u32[]{:S(2)}) async-start(bf16[8,2,112,128]{3,2,1,0:T(8,128)(2,1)} %add_convert_fusion), calls=%async_computation.1 | async-start | bytes 917504 | tf_op jit(solution)/shard_map/all_to_all | solution.py:276
  121.6 8.3 %shard_map.68.own_in = f32[448,512]{1,0:T(8,128)} custom-call(s32[3]{0:T(128)} %pad_add_fusion.refs_0_.me, bf16[16,512,256]{2,1,0:T(8,128)(2,1)} %get-tuple-element.36.source, bf16[8,336,128]{2,1,0:T(8,128)(2,1)} %get-tuple-element.31.a0, bf16[8,336,128]{2,1,0:T(8,128)(2,1)} %get-tuple-element.33.a1, bf16[2,8,336,128]{3,2,1,0:T(8,128)(2,1)} %get-tuple-element.32.sent, ...), custom_call_target="tpu_custom_call" | custom-call | flops 1879048192 | bytes 8781836 | tf_op jit(solution)/shard_map/pallas_call | solution.py:27
  129.8 1.4 fusion.2
  131.2 6.8 %all-to-all-done.1 = bf16[8,2,112,128]{3,2,1,0:T(8,128)(2,1)S(1)} async-done(((bf16[8,2,112,128]{3,2,1,0:T(8,128)(2,1)}), bf16[8,2,112,128]{3,2,1,0:T(8,128)(2,1)S(1)}, u32[]{:S(2)}, u32[]{:S(2)}) %all-to-all-start.1) | async-done | bytes 458784 | tf_op jit(solution)/shard_map/all_to_all | solution.py:276
  138.0 22.8 %all_to_all.30 = bf16[8,336,128]{2,1,0:T(8,128)(2,1)S(1)} all-to-all(bf16[8,336,128]{2,1,0:T(8,128)(2,1)S(1)} %fusion.2), channel_id=1, replica_groups=mesh['y'=8,'zl'=2,'c'=2,'zh'=4,'x'=4] {'y'}, dimensions={0} | all-to-all | bytes 1376256 | tf_op jit(solution)/shard_map/all_to_all | solution.py:288
  161.0 0.9 broadcast_in_dim.9
  161.9 3.5 %all-to-all-start.3 = ((bf16[8,336,128]{2,1,0:T(8,128)(2,1)}), bf16[8,336,128]{2,1,0:T(8,128)(2,1)S(1)}, u32[]{:S(2)}, u32[]{:S(2)}) async-start(bf16[8,336,128]{2,1,0:T(8,128)(2,1)} %broadcast_in_dim.9), calls=%async_computation.3 | async-start | bytes 1376256 | tf_op jit(solution)/shard_map/all_to_all | solution.py:215
  165.5 2.9 %collective-permute-start.12 = (bf16[2,112,128]{2,1,0:T(8,128)(2,1)S(1)}, bf16[2,112,128]{2,1,0:T(8,128)(2,1)S(1)}, u32[]{:S(2)}, u32[]{:S(2)}) collective-permute-start(bf16[2,112,128]{2,1,0:T(8,128)(2,1)S(1)} %reduce_sum.34), channel_id=1, source_target_pairs={{0,32},{32,0},{1,33},{33,1},{2,34},{34,2},{3,35},{35,3},{4,36},{36... | collective-permute-start | bytes 172040 | tf_op jit(solution)/shard_map/ppermute | solution.py:210
  168.4 2.0 collective-permute-done.12
  170.5 15.6 %all-to-all-done.3.refs_0_ = bf16[8,336,128]{2,1,0:T(8,128)(2,1)S(1)} async-done(((bf16[8,336,128]{2,1,0:T(8,128)(2,1)}), bf16[8,336,128]{2,1,0:T(8,128)(2,1)S(1)}, u32[]{:S(2)}, u32[]{:S(2)}) %all-to-all-start.3) | async-done | bytes 688160 | tf_op jit(solution)/shard_map/all_to_all | solution.py:215
  186.1 1.9 collective-permute-start.13
  188.0 0.9 broadcast_in_dim.10
  188.9 3.5 %all-to-all-start.4 = ((bf16[8,2,112,128]{3,2,1,0:T(8,128)(2,1)}), bf16[8,2,112,128]{3,2,1,0:T(8,128)(2,1)S(1)}, u32[]{:S(2)}, u32[]{:S(2)}) async-start(bf16[8,2,112,128]{3,2,1,0:T(8,128)(2,1)} %broadcast_in_dim.10), calls=%async_computation.4 | async-start | bytes 917504 | tf_op jit(solution)/shard_map/all_to_all | solution.py:215
  192.4 4.4 %collective-permute-start.14 = (bf16[8,336,128]{2,1,0:T(8,128)(2,1)S(1)}, bf16[8,336,128]{2,1,0:T(8,128)(2,1)S(1)}, u32[]{:S(2)}, u32[]{:S(2)}) collective-permute-start(bf16[8,336,128]{2,1,0:T(8,128)(2,1)S(1)} %all-to-all-done.3.refs_0_), channel_id=1, source_target_pairs={{0,16},{16,0},{1,17},{17,1},{2,18},{18,2},{3,19},{19,3},{4,20},{20... | collective-permute-start | bytes 2064392 | tf_op jit(solution)/shard_map/ppermute | solution.py:210
  196.8 6.8 %collective-permute-done.13.refs_1_ = bf16[8,336,128]{2,1,0:T(8,128)(2,1)S(1)} collective-permute-done((bf16[8,336,128]{2,1,0:T(8,128)(2,1)S(1)}, bf16[8,336,128]{2,1,0:T(8,128)(2,1)S(1)}, u32[]{:S(2)}, u32[]{:S(2)}) %collective-permute-start.13) | collective-permute-done | bytes 688160 | tf_op jit(solution)/shard_map/ppermute | solution.py:210
  203.6 4.1 %collective-permute-start.15 = (bf16[8,336,128]{2,1,0:T(8,128)(2,1)S(1)}, bf16[8,336,128]{2,1,0:T(8,128)(2,1)S(1)}, u32[]{:S(2)}, u32[]{:S(2)}) collective-permute-start(bf16[8,336,128]{2,1,0:T(8,128)(2,1)S(1)} %collective-permute-done.13.refs_1_), channel_id=1, source_target_pairs={{0,16},{16,0},{1,17},{17,1},{2,18},{18,2},{3,19},{19,3},{4,20},{20... | collective-permute-start | bytes 2064392 | tf_op jit(solution)/shard_map/ppermute | solution.py:210
  207.7 3.5 %collective-permute-start.16 = (bf16[8,2,112,128]{3,2,1,0:T(8,128)(2,1)S(1)}, bf16[8,2,112,128]{3,2,1,0:T(8,128)(2,1)S(1)}, u32[]{:S(2)}, u32[]{:S(2)}) collective-permute-start(bf16[8,2,112,128]{3,2,1,0:T(8,128)(2,1)S(1)} %all-to-all-done.4.refs_4_), channel_id=1, source_target_pairs={{0,16},{16,0},{1,17},{17,1},{2,18},{18,2},{3,19},{19,3},{4,20},{20... | collective-permute-start | bytes 1376264 | tf_op jit(solution)/shard_map/ppermute | solution.py:210
  211.2 1.4 collective-permute-done.16.refs_5_
  212.7 0.7 copy-done.9
  213.7 8.2 %shard_map.69 = f32[2,448]{1,0:T(2,128)} custom-call(s32[3]{0:T(128)} %pad_add_fusion.refs_0_.me, bf16[16,512,256]{2,1,0:T(8,128)(2,1)} %get-tuple-element.36.source, f32[448,512]{1,0:T(8,128)} %get-tuple-element.39.bend_in, f32[448,512]{1,0:T(8,128)} %shard_map.68.own_in, bf16[8,336,128]{2,1,0:T(8,128)(2,1)} %copy-done.1, bf16[8,336,128]{2,1,0:T(8,128)(2,1)} %copy-done.6, ...), custom_call_target="tpu_custom_call" | custom-call | flops 1879048192 | bytes 9702924 | tf_op jit(solution)/shard_map/pallas_call | solution.py:27
  221.9 1.4 broadcast_in_dim.11
  223.2 3.9 %all-to-all-start.5 = ((f32[32,2,448]{2,1,0:T(2,128)}), f32[32,2,448]{2,1,0:T(2,128)S(1)}, u32[]{:S(2)}, u32[]{:S(2)}) async-start(f32[32,2,448]{2,1,0:T(2,128)} %broadcast_in_dim.11), calls=%async_computation.5 | async-start | bytes 262144 | tf_op jit(solution)/shard_map/all_to_all | solution.py:215
  227.1 0.7 maximum_bitcast_fusion
  227.8 8.8 %all-to-all-done.5 = f32[32,2,448]{2,1,0:T(2,128)S(1)} async-done(((f32[32,2,448]{2,1,0:T(2,128)}), f32[32,2,448]{2,1,0:T(2,128)S(1)}, u32[]{:S(2)}, u32[]{:S(2)}) %all-to-all-start.5) | async-done | bytes 114720 | tf_op jit(solution)/shard_map/all_to_all | solution.py:215
  236.7 0.6 slice_multiply_fusion
  (53 shorter events, 1.3 us)
Async XLA Ops:
  2.6 11.0 %copy-start.10 = (bf16[128,448]{0,1:T(8,128)(2,1)S(1)}, bf16[128,448]{0,1:T(8,128)(2,1)}, u32[]{:S(2)}) copy-start(bf16[128,448]{0,1:T(8,128)(2,1)} %param.5) | copy-start | bytes 344068
  2.6 34.3 %all-to-all-start = ((bf16[4,512,256]{2,1,0:T(8,128)(2,1)}), bf16[4,512,256]{2,1,0:T(8,128)(2,1)S(1)}, u32[]{:S(2)}, u32[]{:S(2)}) async-start(bf16[4,512,256]{2,1,0:T(8,128)(2,1)} %broadcast_in_dim.8), calls=%async_computation | async-start | bytes 2097152 | tf_op jit(solution)/shard_map/all_to_all | solution.py:215
  36.9 49.2 %copy-start.5 = (bf16[3584,128]{1,0:T(8,128)(2,1)}, bf16[3584,128]{1,0:T(8,128)(2,1)S(1)}, u32[]{:S(2)}) copy-start(bf16[3584,128]{1,0:T(8,128)(2,1)S(1)} %all-gather) | copy-start | bytes 2752516
  36.9 49.2 %copy-start = (bf16[4,512,256]{2,1,0:T(8,128)(2,1)}, bf16[4,512,256]{2,1,0:T(8,128)(2,1)S(1)}, u32[]{:S(2)}) copy-start(bf16[4,512,256]{2,1,0:T(8,128)(2,1)S(1)} %all-to-all-done.refs_1_) | copy-start | bytes 3145732
  37.0 20.0 %collective-permute-start.3 = (bf16[2,512,256]{2,1,0:T(8,128)(2,1)S(1)}, bf16[2,512,256]{2,1,0:T(8,128)(2,1)S(1)}, u32[]{:S(2)}, u32[]{:S(2)}) collective-permute-start(bf16[2,512,256]{2,1,0:T(8,128)(2,1)S(1)} %get-tuple-element.43), channel_id=1, source_target_pairs={{0,3},{1,0},{2,1},{3,2},{4,7},{5,4},{6,5},{7,6},{8,11},{9,8},{10,9... | collective-permute-start | bytes 1572872 | tf_op jit(solution)/shard_map/ppermute | solution.py:229
  41.4 19.0 %collective-permute-start = (bf16[2,512,256]{2,1,0:T(8,128)(2,1)S(1)}, bf16[2,512,256]{2,1,0:T(8,128)(2,1)S(1)}, u32[]{:S(2)}, u32[]{:S(2)}) collective-permute-start(bf16[2,512,256]{2,1,0:T(8,128)(2,1)S(1)} %get-tuple-element.44), channel_id=1, source_target_pairs={{0,1},{1,2},{2,3},{3,0},{4,5},{5,6},{6,7},{7,4},{8,9},{9,10},{10,1... | collective-permute-start | bytes 1572872 | tf_op jit(solution)/shard_map/ppermute | solution.py:229
  43.3 32.1 %collective-permute-start.4 = (bf16[8,448,128]{2,1,0:T(8,128)(2,1)S(1)}, bf16[8,448,128]{2,1,0:T(8,128)(2,1)S(1)}, u32[]{:S(2)}, u32[]{:S(2)}) collective-permute-start(bf16[8,448,128]{2,1,0:T(8,128)(2,1)S(1)} %bitcast.23), channel_id=1, source_target_pairs={{0,32},{32,0},{1,33},{33,1},{2,34},{34,2},{3,35},{35,3},{4,36},{36... | collective-permute-start | bytes 2752520 | tf_op jit(solution)/shard_map/ppermute | solution.py:210
  50.5 17.1 %collective-permute-start.1 = (bf16[2,512,256]{2,1,0:T(8,128)(2,1)S(1)}, bf16[2,512,256]{2,1,0:T(8,128)(2,1)S(1)}, u32[]{:S(2)}, u32[]{:S(2)}) collective-permute-start(bf16[2,512,256]{2,1,0:T(8,128)(2,1)S(1)} %get-tuple-element.43), channel_id=1, source_target_pairs={{0,1},{1,2},{2,3},{3,0},{4,5},{5,6},{6,7},{7,4},{8,9},{9,10},{10,1... | collective-permute-start | bytes 1572872 | tf_op jit(solution)/shard_map/ppermute | solution.py:229
  52.6 15.0 %collective-permute-start.2 = (bf16[2,512,256]{2,1,0:T(8,128)(2,1)S(1)}, bf16[2,512,256]{2,1,0:T(8,128)(2,1)S(1)}, u32[]{:S(2)}, u32[]{:S(2)}) collective-permute-start(bf16[2,512,256]{2,1,0:T(8,128)(2,1)S(1)} %get-tuple-element.44), channel_id=1, source_target_pairs={{0,3},{1,0},{2,1},{3,2},{4,7},{5,4},{6,5},{7,6},{8,11},{9,8},{10,9... | collective-permute-start | bytes 1572872 | tf_op jit(solution)/shard_map/ppermute | solution.py:229
  57.0 29.1 %copy-start.12 = (bf16[2,512,256]{2,1,0:T(8,128)(2,1)}, bf16[2,512,256]{2,1,0:T(8,128)(2,1)S(1)}, u32[]{:S(2)}) copy-start(bf16[2,512,256]{2,1,0:T(8,128)(2,1)S(1)} %collective-permute-done.3.refs_4_) | copy-start | bytes 1572868
  57.0 20.1 %collective-permute-start.6 = (bf16[2,512,256]{2,1,0:T(8,128)(2,1)S(1)}, bf16[2,512,256]{2,1,0:T(8,128)(2,1)S(1)}, u32[]{:S(2)}, u32[]{:S(2)}) collective-permute-start(bf16[2,512,256]{2,1,0:T(8,128)(2,1)S(1)} %collective-permute-done.3.refs_4_), channel_id=1, source_target_pairs={{0,3},{1,0},{2,1},{3,2},{4,7},{5,4},{6,5},{7,6},{8,11},{9,8},{10,9... | collective-permute-start | bytes 1572872 | tf_op jit(solution)/shard_map/ppermute | solution.py:229
  60.4 16.7 %copy-start.13 = (bf16[2,512,256]{2,1,0:T(8,128)(2,1)}, bf16[2,512,256]{2,1,0:T(8,128)(2,1)S(1)}, u32[]{:S(2)}) copy-start(bf16[2,512,256]{2,1,0:T(8,128)(2,1)S(1)} %collective-permute-done.refs_2_) | copy-start | bytes 1572868
  60.4 18.4 %collective-permute-start.5 = (bf16[2,512,256]{2,1,0:T(8,128)(2,1)S(1)}, bf16[2,512,256]{2,1,0:T(8,128)(2,1)S(1)}, u32[]{:S(2)}, u32[]{:S(2)}) collective-permute-start(bf16[2,512,256]{2,1,0:T(8,128)(2,1)S(1)} %collective-permute-done.refs_2_), channel_id=1, source_target_pairs={{0,1},{1,2},{2,3},{3,0},{4,5},{5,6},{6,7},{7,4},{8,9},{9,10},{10,1... | collective-permute-start | bytes 1572872 | tf_op jit(solution)/shard_map/ppermute | solution.py:229
  67.6 11.2 %copy-start.14 = (bf16[2,512,256]{2,1,0:T(8,128)(2,1)}, bf16[2,512,256]{2,1,0:T(8,128)(2,1)S(1)}, u32[]{:S(2)}) copy-start(bf16[2,512,256]{2,1,0:T(8,128)(2,1)S(1)} %collective-permute-done.1.refs_3_) | copy-start | bytes 1572868
  67.6 16.3 %copy-start.15 = (bf16[2,512,256]{2,1,0:T(8,128)(2,1)}, bf16[2,512,256]{2,1,0:T(8,128)(2,1)S(1)}, u32[]{:S(2)}) copy-start(bf16[2,512,256]{2,1,0:T(8,128)(2,1)S(1)} %collective-permute-done.2.refs_5_) | copy-start | bytes 1572868
  67.6 16.9 %collective-permute-start.7 = (bf16[8,448,128]{2,1,0:T(8,128)(2,1)S(1)}, bf16[8,448,128]{2,1,0:T(8,128)(2,1)}, u32[]{:S(2)}, u32[]{:S(2)}) collective-permute-start(bf16[8,448,128]{2,1,0:T(8,128)(2,1)S(1)} %bitcast.24), channel_id=1, source_target_pairs={{0,16},{16,0},{1,17},{17,1},{2,18},{18,2},{3,19},{19,3},{4,20},{20... | collective-permute-start | bytes 2752520 | tf_op jit(solution)/shard_map/ppermute | solution.py:210
  75.5 10.7 %copy-start.11 = (bf16[8,448,128]{2,1,0:T(8,128)(2,1)}, bf16[8,448,128]{2,1,0:T(8,128)(2,1)S(1)}, u32[]{:S(2)}) copy-start(bf16[8,448,128]{2,1,0:T(8,128)(2,1)S(1)} %collective-permute-done.4.refs_11_) | copy-start | bytes 2752516
  77.1 6.8 %copy-start.16 = (bf16[2,512,256]{2,1,0:T(8,128)(2,1)}, bf16[2,512,256]{2,1,0:T(8,128)(2,1)S(1)}, u32[]{:S(2)}) copy-start(bf16[2,512,256]{2,1,0:T(8,128)(2,1)S(1)} %collective-permute-done.6.refs_7_) | copy-start | bytes 1572868
  78.9 5.1 %copy-start.17 = (bf16[2,512,256]{2,1,0:T(8,128)(2,1)}, bf16[2,512,256]{2,1,0:T(8,128)(2,1)S(1)}, u32[]{:S(2)}) copy-start(bf16[2,512,256]{2,1,0:T(8,128)(2,1)S(1)} %collective-permute-done.5.refs_6_) | copy-start | bytes 1572868
  78.9 7.3 %collective-permute-start.8 = (bf16[8,448,128]{2,1,0:T(8,128)(2,1)S(1)}, bf16[8,448,128]{2,1,0:T(8,128)(2,1)}, u32[]{:S(2)}, u32[]{:S(2)}) collective-permute-start(bf16[8,448,128]{2,1,0:T(8,128)(2,1)S(1)} %collective-permute-done.4.refs_11_), channel_id=1, source_target_pairs={{0,16},{16,0},{1,17},{17,1},{2,18},{18,2},{3,19},{19,3},{4,20},{20... | collective-permute-start | bytes 2752520 | tf_op jit(solution)/shard_map/ppermute | solution.py:210
  99.8 14.0 %copy-start.4 = (bf16[8,2,112,128]{3,2,1,0:T(8,128)(2,1)S(1)}, bf16[8,2,112,128]{3,2,1,0:T(8,128)(2,1)}, u32[]{:S(2)}) copy-start(bf16[8,2,112,128]{3,2,1,0:T(8,128)(2,1)} %get-tuple-element.34.b0) | copy-start | bytes 1376260
  99.8 5.4 %collective-permute-start.9 = (bf16[2,8,336,128]{3,2,1,0:T(8,128)(2,1)}, bf16[2,8,336,128]{3,2,1,0:T(8,128)(2,1)S(1)}, u32[]{:S(2)}, u32[]{:S(2)}) collective-permute-start(bf16[2,8,336,128]{3,2,1,0:T(8,128)(2,1)} %get-tuple-element.32.sent), channel_id=1, source_target_pairs={{0,16},{16,0},{1,17},{17,1},{2,18},{18,2},{3,19},{19,3},{4,20},{20... | collective-permute-start | bytes 4128776 | tf_op jit(solution)/shard_map/ppermute | solution.py:210
  102.2 11.6 %collective-permute-start.11 = (bf16[8,2,112,128]{3,2,1,0:T(8,128)(2,1)}, bf16[8,2,112,128]{3,2,1,0:T(8,128)(2,1)S(1)}, u32[]{:S(2)}, u32[]{:S(2)}) collective-permute-start(bf16[8,2,112,128]{3,2,1,0:T(8,128)(2,1)} %get-tuple-element.35.b1), channel_id=1, source_target_pairs={{0,16},{16,0},{1,17},{17,1},{2,18},{18,2},{3,19},{19,3},{4,20},{20... | collective-permute-start | bytes 1376264 | tf_op jit(solution)/shard_map/ppermute | solution.py:210
  107.4 22.5 %collective-permute-start.10 = (bf16[8,336,128]{2,1,0:T(8,128)(2,1)}, bf16[8,336,128]{2,1,0:T(8,128)(2,1)}, u32[]{:S(2)}, u32[]{:S(2)}) collective-permute-start(bf16[8,336,128]{2,1,0:T(8,128)(2,1)} %fusion), channel_id=1, source_target_pairs={{0,32},{32,0},{1,33},{33,1},{2,34},{34,2},{3,35},{35,3},{4,36},{36... | collective-permute-start | bytes 2064392 | tf_op jit(solution)/shard_map/ppermute | solution.py:210
  114.7 23.3 %all-to-all-start.1 = ((bf16[8,2,112,128]{3,2,1,0:T(8,128)(2,1)}), bf16[8,2,112,128]{3,2,1,0:T(8,128)(2,1)S(1)}, u32[]{:S(2)}, u32[]{:S(2)}) async-start(bf16[8,2,112,128]{3,2,1,0:T(8,128)(2,1)} %add_convert_fusion), calls=%async_computation.1 | async-start | bytes 917504 | tf_op jit(solution)/shard_map/all_to_all | solution.py:276
  121.5 8.3 %copy-start.2 = (bf16[8,336,128]{2,1,0:T(8,128)(2,1)S(1)}, bf16[8,336,128]{2,1,0:T(8,128)(2,1)}, u32[]{:S(2)}) copy-start(bf16[8,336,128]{2,1,0:T(8,128)(2,1)} %get-tuple-element.31.a0) | copy-start | bytes 2064388
  161.9 24.1 %all-to-all-start.3 = ((bf16[8,336,128]{2,1,0:T(8,128)(2,1)}), bf16[8,336,128]{2,1,0:T(8,128)(2,1)S(1)}, u32[]{:S(2)}, u32[]{:S(2)}) async-start(bf16[8,336,128]{2,1,0:T(8,128)(2,1)} %broadcast_in_dim.9), calls=%async_computation.3 | async-start | bytes 1376256 | tf_op jit(solution)/shard_map/all_to_all | solution.py:215
  165.5 4.9 %collective-permute-start.12 = (bf16[2,112,128]{2,1,0:T(8,128)(2,1)S(1)}, bf16[2,112,128]{2,1,0:T(8,128)(2,1)S(1)}, u32[]{:S(2)}, u32[]{:S(2)}) collective-permute-start(bf16[2,112,128]{2,1,0:T(8,128)(2,1)S(1)} %reduce_sum.34), channel_id=1, source_target_pairs={{0,32},{32,0},{1,33},{33,1},{2,34},{34,2},{3,35},{35,3},{4,36},{36... | collective-permute-start | bytes 172040 | tf_op jit(solution)/shard_map/ppermute | solution.py:210
  186.1 26.6 %copy-start.1 = (bf16[8,336,128]{2,1,0:T(8,128)(2,1)}, bf16[8,336,128]{2,1,0:T(8,128)(2,1)S(1)}, u32[]{:S(2)}) copy-start(bf16[8,336,128]{2,1,0:T(8,128)(2,1)S(1)} %all-to-all-done.3.refs_0_) | copy-start | bytes 2064388
  186.1 17.5 %collective-permute-start.13 = (bf16[8,336,128]{2,1,0:T(8,128)(2,1)S(1)}, bf16[8,336,128]{2,1,0:T(8,128)(2,1)S(1)}, u32[]{:S(2)}, u32[]{:S(2)}) collective-permute-start(bf16[8,336,128]{2,1,0:T(8,128)(2,1)S(1)} %all-to-all-done.3.refs_0_), channel_id=1, source_target_pairs={{0,32},{32,0},{1,33},{33,1},{2,34},{34,2},{3,35},{35,3},{4,36},{36... | collective-permute-start | bytes 2064392 | tf_op jit(solution)/shard_map/ppermute | solution.py:210
  188.9 18.8 %all-to-all-start.4 = ((bf16[8,2,112,128]{3,2,1,0:T(8,128)(2,1)}), bf16[8,2,112,128]{3,2,1,0:T(8,128)(2,1)S(1)}, u32[]{:S(2)}, u32[]{:S(2)}) async-start(bf16[8,2,112,128]{3,2,1,0:T(8,128)(2,1)} %broadcast_in_dim.10), calls=%async_computation.4 | async-start | bytes 917504 | tf_op jit(solution)/shard_map/all_to_all | solution.py:215
  192.4 18.9 %collective-permute-start.14 = (bf16[8,336,128]{2,1,0:T(8,128)(2,1)S(1)}, bf16[8,336,128]{2,1,0:T(8,128)(2,1)S(1)}, u32[]{:S(2)}, u32[]{:S(2)}) collective-permute-start(bf16[8,336,128]{2,1,0:T(8,128)(2,1)S(1)} %all-to-all-done.3.refs_0_), channel_id=1, source_target_pairs={{0,16},{16,0},{1,17},{17,1},{2,18},{18,2},{3,19},{19,3},{4,20},{20... | collective-permute-start | bytes 2064392 | tf_op jit(solution)/shard_map/ppermute | solution.py:210
  203.6 9.1 %copy-start.6 = (bf16[8,336,128]{2,1,0:T(8,128)(2,1)}, bf16[8,336,128]{2,1,0:T(8,128)(2,1)S(1)}, u32[]{:S(2)}) copy-start(bf16[8,336,128]{2,1,0:T(8,128)(2,1)S(1)} %collective-permute-done.13.refs_1_) | copy-start | bytes 2064388
  203.6 9.0 %collective-permute-start.15 = (bf16[8,336,128]{2,1,0:T(8,128)(2,1)S(1)}, bf16[8,336,128]{2,1,0:T(8,128)(2,1)S(1)}, u32[]{:S(2)}, u32[]{:S(2)}) collective-permute-start(bf16[8,336,128]{2,1,0:T(8,128)(2,1)S(1)} %collective-permute-done.13.refs_1_), channel_id=1, source_target_pairs={{0,16},{16,0},{1,17},{17,1},{2,18},{18,2},{3,19},{19,3},{4,20},{20... | collective-permute-start | bytes 2064392 | tf_op jit(solution)/shard_map/ppermute | solution.py:210
  207.7 5.0 %copy-start.3 = (bf16[8,2,112,128]{3,2,1,0:T(8,128)(2,1)}, bf16[8,2,112,128]{3,2,1,0:T(8,128)(2,1)S(1)}, u32[]{:S(2)}) copy-start(bf16[8,2,112,128]{3,2,1,0:T(8,128)(2,1)S(1)} %all-to-all-done.4.refs_4_) | copy-start | bytes 1376260
  207.7 4.9 %collective-permute-start.16 = (bf16[8,2,112,128]{3,2,1,0:T(8,128)(2,1)S(1)}, bf16[8,2,112,128]{3,2,1,0:T(8,128)(2,1)S(1)}, u32[]{:S(2)}, u32[]{:S(2)}) collective-permute-start(bf16[8,2,112,128]{3,2,1,0:T(8,128)(2,1)S(1)} %all-to-all-done.4.refs_4_), channel_id=1, source_target_pairs={{0,16},{16,0},{1,17},{17,1},{2,18},{18,2},{3,19},{19,3},{4,20},{20... | collective-permute-start | bytes 1376264 | tf_op jit(solution)/shard_map/ppermute | solution.py:210
  211.2 1.4 copy-start.7
  212.6 0.8 copy-start.9
  212.7 1.1 copy-start.8
  223.2 13.3 %all-to-all-start.5 = ((f32[32,2,448]{2,1,0:T(2,128)}), f32[32,2,448]{2,1,0:T(2,128)S(1)}, u32[]{:S(2)}, u32[]{:S(2)}) async-start(f32[32,2,448]{2,1,0:T(2,128)} %broadcast_in_dim.11), calls=%async_computation.5 | async-start | bytes 262144 | tf_op jit(solution)/shard_map/all_to_all | solution.py:215

commit v5 on v4

--- a/solution.py
+++ b/solution.py
@@ -12,6 +12,7 @@
 F32, BF = jnp.float32, jnp.bfloat16
 NT = (((1,), (1,)), ((), ()))
 CUT = 336
+RING = 240
 VMEM_LIMIT = 60 * 1024 * 1024
 TOK = pltpu.VMEM((16, 512, 256), BF)
 ACC = pltpu.VMEM((448, 512), F32)
@@ -36,52 +37,37 @@
 
 
 def fetched(pairs, sems):
-    def part(i, y):
+    def part(i, half):
         source, there = pairs[i]
-        return pltpu.make_async_copy(source.at[y], there.at[y], sems.at[i, y])
-
-    for y in range(8):
+        count = source.shape[0] // 2
+        at = pl.ds(count * half, count)
+        return pltpu.make_async_copy(source.at[at], there.at[at], sems.at[i, half])
+
+    for half in (0, 1):
         for i in range(len(pairs)):
-            part(i, y).start()
-
-    def ready(y):
+            part(i, half).start()
+
+    def ready(half):
         for i in range(len(pairs)):
-            part(i, y).wait()
+            part(i, half).wait()
 
     return ready
 
 
-def rows_of(held, held_b, y, rel):
-    own, other = held[rel, y], held[2 + rel, y]
-    if held_b is None:
-        return own, other
-    return (
-        jnp.concatenate([own, held_b[0, y, rel]], 0),
-        jnp.concatenate([other, held_b[1, y, rel]], 0),
-    )
-
-
-def project(me, tok, held, held_b, acc, ready):
+def project(me, tok, rows_of, acc, ready):
     mine, first = me[0], me[1] == 0
-
-    def product(y):
-        ready(y)
+    for half in (0, 1):
+        ready(half)
         rows, cols = [], []
-        for rel in (0, 1):
-            own, other = rows_of(held, held_b, y, rel)
-            rows += [jnp.where(first, own, other), jnp.where(first, other, own)]
-            cols.append(tok[2 * y + jnp.bitwise_xor(mine, rel)])
-        return lax.dot_general(
+        for y in range(4 * half, 4 * half + 4):
+            for rel in (0, 1):
+                own, other = rows_of(y, rel)
+                rows += [jnp.where(first, own, other), jnp.where(first, other, own)]
+                cols.append(tok[2 * y + jnp.bitwise_xor(mine, rel)])
+        part = lax.dot_general(
             jnp.concatenate(rows, 1), jnp.concatenate(cols, 1), NT, preferred_element_type=F32
         )
-
-    acc[...] = product(0)
-
-    def step(y, unused):
-        acc[...] += product(y)
-        return unused
-
-    lax.fori_loop(1, 8, step, 0)
+        acc[...] = part if half == 0 else acc[...] + part
 
 
 def first_kernel(*refs):
@@ -95,20 +81,26 @@
         there = tok.at[4 * z + lax.rem(me[2] + d, 4)]
         return pltpu.make_async_copy(sources[d][z // 2].at[z % 2], there, tok_sems.at[d, z])
 
-    for d in (0, 1, 3, 2):
-        for z in range(4):
+    for z in range(4):
+        for d in range(4):
             token_copy(d, z).start()
     w_ready = fetched([(w, held.at[i]) for i, w in enumerate((w0, w1, w2, w3))], w_sems)
     get_up = pltpu.make_async_copy(up_in, up, in_sems.at[0])
     get_cot = pltpu.make_async_copy(cot_in, cot, in_sems.at[1])
     get_up.start()
     get_cot.start()
-    for d in (0, 1, 3, 2):
-        for z in range(4):
-            token_copy(d, z).wait()
+
+    def ready(half):
+        for z in (2 * half, 2 * half + 1):
+            for d in range(4):
+                token_copy(d, z).wait()
+        w_ready(half)
+
+    project(
+        me, tok, lambda y, rel: (held[rel, y], held[2 + rel, y]), acc, ready
+    )
     keep_tok = pltpu.make_async_copy(tok, tok_out, sems.at[0])
     keep_tok.start()
-    project(me, tok, held, None, acc, w_ready)
     get_up.wait()
     get_cot.wait()
 
@@ -127,70 +119,76 @@
     keep_bend = pltpu.make_async_copy(bend, bend_out, sems.at[1])
     keep_bend.start()
 
-    def out_copies(y):
-        pairs = [(own.at[k, y], out) for k, out in enumerate((outs[0].at[y], outs[1].at[y]))]
-        pairs += [(own.at[2 + k, y], outs[2].at[k, y]) for k in range(2)]
-        pairs += [(own_b.at[k, y], outs[3 + k].at[y]) for k in range(2)]
+    def out_copies(i):
+        at = pl.ds(2 * i, 2)
+        pairs = [(own.at[k, at], outs[k].at[at]) for k in range(2)]
+        pairs += [(own.at[2 + k, at], outs[2].at[k, at]) for k in range(2)]
+        pairs += [(own_b.at[k, at], outs[3 + k].at[at]) for k in range(2)]
         return [
-            pltpu.make_async_copy(here, there, out_sems.at[k, y])
+            pltpu.make_async_copy(here, there, out_sems.at[k, i])
             for k, (here, there) in enumerate(pairs)
         ]
 
-    def step(y, unused):
-        for rel in (0, 1):
-            tile = tok[2 * y + jnp.bitwise_xor(mine, rel)]
-            got = jnp.dot(coeff[...], tile, preferred_element_type=F32).astype(BF)
-            low, high = got[:, :128], got[:, 128:]
+    for i in range(4):
+        order = [(y, rel) for y in (2 * i, 2 * i + 1) for rel in (0, 1)]
+        tiles = [tok[2 * y + jnp.bitwise_xor(mine, rel)] for y, rel in order]
+        got = jnp.dot(
+            coeff[...], jnp.concatenate(tiles, 1), preferred_element_type=F32
+        ).astype(BF)
+        for k, (y, rel) in enumerate(order):
+            low, high = got[:, 256 * k : 256 * k + 128], got[:, 256 * k + 128 : 256 * k + 256]
             keep, give = jnp.where(first, low, high), jnp.where(first, high, low)
             own[rel, y] = keep[:CUT]
             own_b[0, y, rel] = keep[CUT:]
             own[2 + rel, y] = give[:CUT]
             own_b[1, y, rel] = give[CUT:]
-        for copy in out_copies(y):
+        for copy in out_copies(i):
             copy.start()
-        return unused
-
-    lax.fori_loop(0, 8, step, 0)
-    for y in range(8):
-        for copy in out_copies(y):
+    for i in range(4):
+        for copy in out_copies(i):
             copy.wait()
     keep_tok.wait()
     keep_bend.wait()
 
 
-def fetch_all(source, arrays, tok, held, held_b, tok_sems, sems):
-    pairs = [(a, held.at[i]) for i, a in enumerate(arrays[:4])]
-    pairs += [(b, held_b.at[i]) for i, b in enumerate(arrays[4:])]
-
-    def part(y):
-        at = pl.ds(2 * y, 2)
-        return pltpu.make_async_copy(source.at[at], tok.at[at], tok_sems.at[y])
-
-    for y in range(8):
-        part(y).start()
+def own_kernel(me, source, a0, a1, sent, b0, b1, acc, tok, held, held_b, tok_sems, sems):
+    tok_ready = fetched([(source, tok)], tok_sems)
+    pairs = [(a, held.at[i]) for i, a in enumerate((a0, a1, sent.at[0], sent.at[1]))]
+    pairs += [(b, held_b.at[i]) for i, b in enumerate((b0, b1))]
     rows_ready = fetched(pairs, sems)
 
-    def ready(y):
-        part(y).wait()
-        rows_ready(y)
-
-    return ready
-
-
-def own_kernel(me, source, a0, a1, sent, b0, b1, acc, tok, held, held_b, tok_sems, sems):
-    arrays = (a0, a1, sent.at[0], sent.at[1], b0, b1)
-    ready = fetch_all(source, arrays, tok, held, held_b, tok_sems, sems)
-    project(me, tok, held, held_b, acc, ready)
+    def ready(half):
+        tok_ready(half)
+        rows_ready(half)
+
+    def rows_of(y, rel):
+        return [
+            jnp.concatenate([held[2 * core + rel, y], held_b[core, y, rel]], 0) for core in (0, 1)
+        ]
+
+    project(me, tok, rows_of, acc, ready)
 
 
 def mean_kernel(me, source, bend_in, own_in, *refs):
-    sums, acc, bend, own, tok, held, held_b, tok_sems, sems, in_sems = refs[6:]
-    ready = fetch_all(source, refs[:6], tok, held, held_b, tok_sems, sems)
+    sums, acc, bend, own, tok, held, held_b, tok_sems, sems, in_sems = refs[4:]
+    tok_ready = fetched([(source, tok)], tok_sems)
     get_bend = pltpu.make_async_copy(bend_in, bend, in_sems.at[0])
     get_own = pltpu.make_async_copy(own_in, own, in_sems.at[1])
+    pairs = [(a, (held, held_b)[i % 2].at[i // 2]) for i, a in enumerate(refs[:4])]
+    rows_ready = fetched(pairs, sems)
     get_bend.start()
     get_own.start()
-    project(me, tok, held, held_b, acc, ready)
+
+    def ready(half):
+        tok_ready(half)
+        rows_ready(half)
+
+    def rows_of(y, rel):
+        return [
+            jnp.concatenate([held[core, y, rel], held_b[core, y, rel]], 0) for core in (0, 1)
+        ]
+
+    project(me, tok, rows_of, acc, ready)
     get_bend.wait()
     get_own.wait()
     c = jnp.zeros((448, 128), F32)
@@ -227,13 +225,6 @@
 
 def along_x(value, by):
     return lax.ppermute(value, "x", [(i, (i + by) % 4) for i in range(4)])
-
-
-def all_rows(part_a, part_b):
-    a0, part_b = lax.optimization_barrier((to_all(part_a, "y"), part_b))
-    b0 = to_all(part_b, "y")
-    a1 = swap(a0, "zl")
-    return a0, a1, swap(a0, "c"), swap(a1, "c"), b0, swap(b0, "c")
 
 
 def shards(tokens, gate_weight, up_act, cotangent):
@@ -268,12 +259,12 @@
             *[pltpu.VMEM((448, 512), BF)] * 3,
             *[ACC] * 2,
             *held,
-            *map(dma, ((4, 4), (4, 8), (2,), (6, 8), (2,))),
+            *map(dma, ((4, 4), (4, 2), (2,), (6, 4), (2,))),
         ],
     )
-    came_b = swap(sent_b, "c")
-    came = swap(sent, "c")
-    across_b = lax.all_to_all(total(b0, came_b).astype(BF), "y", 0, 0, tiled=True)
+    came_b, came = swap(sent_b, "c"), swap(sent, "c")
+    sums_b, came = lax.optimization_barrier((total(b0, came_b).astype(BF), came))
+    across_b = lax.all_to_all(sums_b, "y", 0, 0, tiled=True)
     came_1 = swap(total(a1, came[1]).astype(BF), "zl")
     sums_a = total(a0, came[0], came_1).astype(BF)
     own = call(
@@ -281,7 +272,7 @@
         [shape(448, 512, dtype=F32)],
         (me, tok, a0, a1, sent, b0, sent_b),
         flops,
-        [TOK, *held, dma((8,)), dma((6, 8))],
+        [TOK, *held, dma((1, 2)), dma((6, 2))],
         True,
     )[0]
     sums_a, across_b, own = lax.optimization_barrier((sums_a, across_b, own))
@@ -290,16 +281,26 @@
     other_b = swap(part_b, "zl")
     both_b = total(part_b, other_b[::-1]).astype(BF)
     grad_a = jnp.sum(across_a.astype(F32), axis=0).astype(BF)
+    both_a = jnp.stack([grad_a, swap(grad_a, "zl")])
+    both = jnp.concatenate([both_a, both_b], axis=1)
+    g1 = to_all(both[:, RING:], "y")
+    g0 = lax.all_gather(both[:, :RING], "y", axis=0)
     line = call(
         mean_kernel,
         [shape(2, 448, dtype=F32)],
-        (me, tok, bend, own, *all_rows(grad_a, both_b)),
+        (me, tok, bend, own, g0, g1, swap(g0, "c"), swap(g1, "c")),
         flops,
-        [*[ACC] * 3, TOK, *held, dma((8,)), dma((6, 8)), dma((2,))],
+        [
+            *[ACC] * 3,
+            TOK,
+            pltpu.VMEM((2, 8, 2, RING, 128), BF),
+            pltpu.VMEM((2, 8, 2, 448 - RING, 128), BF),
+            *map(dma, ((1, 2), (4, 2), (2,))),
+        ],
         True,
     )[0]
     whole = jnp.sum(to_all(line, REP), axis=0)
-    grad = jnp.concatenate([grad_a, both_b[0]], axis=0).T
+    grad = both[0].T
     return grad, whole[0], whole[1] / 31
 
 

time: 238 us -> 246 us (1.034)
  blocking collectives: 46.1 us -> 60.7 us
  Pallas kernels: 30 us -> 22.6 us
    all_gather x0 -> x1, blocking collectives: none -> 37.3 us  [shards(): g0 = lax.all_gather(both[:, :RING], 'y', axis=0)]
    all_to_all x1 -> x0, blocking collectives: 22.8 us -> none  [shards(): across_a = lax.all_to_all(sums_a, 'y', 0, 0, tiled=True)]
    all_to_all x1 -> x2, waiting for transfers between devices: 6.82 us -> 25.7 us  [the longest x1 19.4 us: shards(): across_a = lax.all_to_all(sums_a, 'y', 0, 0, tiled=True)]
    all_to_all x4 -> x3, waiting for transfers between devices: 24.4 us -> 8.61 us  [to_all(): lax.all_to_all(jnp.broadcast_to(value[None], (count, *value.shape)), axis...]
    pallas_call x3, Pallas kernels: 30 us -> 22.6 us  [call(): pl.pallas_call(kernel, out_shape=outs, in_specs=[SM] + [ANY] * (len(opera...]
    all_to_all x1 -> x2, starting transfers between devices: 6.83 us -> 10.4 us  [the longest x1 6.83 us: shards(): across_b = lax.all_to_all(sums_b, 'y', 0, 0, tiled=True)]
    ppermute x11 -> x10, starting transfers between devices: 47.8 us -> 45.7 us  [swap(): return lax.ppermute(value, axis, ((0, 1), (1, 0)))]
    all_to_all x4 -> x3, starting transfers between devices: 21.9 us -> 20 us  [to_all(): lax.all_to_all(jnp.broadcast_to(value[None], (count, *value.shape)), axis...]
  transfers between devices with their start and end apart: 22 -> 21, of which waited for: 11 -> 12; matrix products, arithmetic and copies ran while one was open for 3% -> 2% of each run, Pallas kernels for 3% -> 3%
where the time goes in v5:
time: 246 us; the launch traced here: 244 us
  starting transfers between devices  94.1 us (38%)
  blocking collectives  60.7 us (25%)
  waiting for transfers between devices  54.4 us (22%)
  Pallas kernels  22.6 us (9%)
  local copies, waits for them, and re-layouts  6.1 us (2%)
  other arithmetic  5.61 us (2%)
    ppermute x10, starting transfers between devices, swap(): return lax.ppermute(value, axis, ((0, 1), (1, 0)))  45.7 us
    all_gather x1, blocking collectives, shards(): g0 = lax.all_gather(both[:, :RING], 'y', axis=0)  37.3 us
    all_gather x1, blocking collectives, shards(): w0 = lax.all_gather(gate_weight.T, 'y', axis=0)  23.3 us
    pallas_call x3, Pallas kernels, call(): pl.pallas_call(kernel, out_shape=outs, in_specs=[SM] + [ANY] * (len(opera...  22.6 us
    all_to_all x3, starting transfers between devices, to_all(): lax.all_to_all(jnp.broadcast_to(value[None], (count, *value.shape)), axis...  20 us
    all_to_all x1, waiting for transfers between devices, shards(): across_a = lax.all_to_all(sums_a, 'y', 0, 0, tiled=True)  19.4 us
    ppermute x6, starting transfers between devices, along_x(): return lax.ppermute(value, 'x', [(i, (i + by) % 4) for i in range(4)])  18.1 us
    ppermute x10, waiting for transfers between devices, swap(): return lax.ppermute(value, axis, ((0, 1), (1, 0)))  11.4 us
  transfers between devices with their start and end apart: 21, of which 12 were waited for; matrix products, arithmetic and copies ran while one was open for 2% of the time, Pallas kernels for 3%

profile of v5, /device:TPU:1, one launch (start us, length us, event | category | flops | bytes accessed | tf_op | source)
XLA Modules:
  0.0 244.4 jit_solution(7705364162710994318)
XLA Ops:
  0.6 2.0 broadcast_in_dim.6
  2.6 11.0 %all-to-all-start = ((bf16[4,512,256]{2,1,0:T(8,128)(2,1)}), bf16[4,512,256]{2,1,0:T(8,128)(2,1)S(1)}, u32[]{:S(2)}, u32[]{:S(2)}) async-start(bf16[4,512,256]{2,1,0:T(8,128)(2,1)} %broadcast_in_dim.6), calls=%async_computation | async-start | bytes 2097152 | tf_op jit(solution)/shard_map/all_to_all | solution.py:213
  13.6 23.3 %all-gather = bf16[3584,128]{1,0:T(8,128)(2,1)S(1)} all-gather(bf16[448,128]{1,0:T(8,128)(2,1)S(1)} %bitcast.33), channel_id=2, replica_groups=mesh['y'=8,'zl'=2,'c'=2,'zh'=4,'x'=4] {'y'}, dimensions={0}, use_global_device_ids=true | all-gather | bytes 1032192 | tf_op jit(solution)/shard_map/all_gather | solution.py:236
  37.0 4.4 %collective-permute-start.3 = (bf16[2,512,256]{2,1,0:T(8,128)(2,1)S(1)}, bf16[2,512,256]{2,1,0:T(8,128)(2,1)S(1)}, u32[]{:S(2)}, u32[]{:S(2)}) collective-permute-start(bf16[2,512,256]{2,1,0:T(8,128)(2,1)S(1)} %get-tuple-element.43), channel_id=1, source_target_pairs={{0,3},{1,0},{2,1},{3,2},{4,7},{5,4},{6,5},{7,6},{8,11},{9,8},{10,9... | collective-permute-start | bytes 1572872 | tf_op jit(solution)/shard_map/ppermute | solution.py:227
  41.4 1.9 collective-permute-start
  43.3 7.2 %collective-permute-start.4 = (bf16[8,448,128]{2,1,0:T(8,128)(2,1)S(1)}, bf16[8,448,128]{2,1,0:T(8,128)(2,1)S(1)}, u32[]{:S(2)}, u32[]{:S(2)}) collective-permute-start(bf16[8,448,128]{2,1,0:T(8,128)(2,1)S(1)} %bitcast.27), channel_id=1, source_target_pairs={{0,32},{32,0},{1,33},{33,1},{2,34},{34,2},{3,35},{35,3},{4,36},{36... | collective-permute-start | bytes 2752520 | tf_op jit(solution)/shard_map/ppermute | solution.py:208
  50.5 2.1 collective-permute-start.1
  52.6 4.4 %collective-permute-start.2 = (bf16[2,512,256]{2,1,0:T(8,128)(2,1)S(1)}, bf16[2,512,256]{2,1,0:T(8,128)(2,1)S(1)}, u32[]{:S(2)}, u32[]{:S(2)}) collective-permute-start(bf16[2,512,256]{2,1,0:T(8,128)(2,1)S(1)} %get-tuple-element.44), channel_id=1, source_target_pairs={{0,3},{1,0},{2,1},{3,2},{4,7},{5,4},{6,5},{7,6},{8,11},{9,8},{10,9... | collective-permute-start | bytes 1572872 | tf_op jit(solution)/shard_map/ppermute | solution.py:227
  57.0 3.4 %collective-permute-start.6 = (bf16[2,512,256]{2,1,0:T(8,128)(2,1)S(1)}, bf16[2,512,256]{2,1,0:T(8,128)(2,1)S(1)}, u32[]{:S(2)}, u32[]{:S(2)}) collective-permute-start(bf16[2,512,256]{2,1,0:T(8,128)(2,1)S(1)} %collective-permute-done.3.refs_4_), channel_id=1, source_target_pairs={{0,3},{1,0},{2,1},{3,2},{4,7},{5,4},{6,5},{7,6},{8,11},{9,8},{10,9... | collective-permute-start | bytes 1572872 | tf_op jit(solution)/shard_map/ppermute | solution.py:227
  60.4 1.9 collective-permute-start.5
  62.3 5.3 %collective-permute-done.1.refs_3_ = bf16[2,512,256]{2,1,0:T(8,128)(2,1)S(1)} collective-permute-done((bf16[2,512,256]{2,1,0:T(8,128)(2,1)S(1)}, bf16[2,512,256]{2,1,0:T(8,128)(2,1)S(1)}, u32[]{:S(2)}, u32[]{:S(2)}) %collective-permute-start.1) | collective-permute-done | bytes 524320 | tf_op jit(solution)/shard_map/ppermute | solution.py:227
  67.6 7.8 %collective-permute-start.7 = (bf16[8,448,128]{2,1,0:T(8,128)(2,1)S(1)}, bf16[8,448,128]{2,1,0:T(8,128)(2,1)}, u32[]{:S(2)}, u32[]{:S(2)}) collective-permute-start(bf16[8,448,128]{2,1,0:T(8,128)(2,1)S(1)} %bitcast.28), channel_id=1, source_target_pairs={{0,16},{16,0},{1,17},{17,1},{2,18},{18,2},{3,19},{19,3},{4,20},{20... | collective-permute-start | bytes 2752520 | tf_op jit(solution)/shard_map/ppermute | solution.py:208
  75.5 1.6 collective-permute-done.6.refs_7_
  77.1 1.8 collective-permute-done.5.refs_6_
  78.9 5.1 %collective-permute-start.8 = (bf16[8,448,128]{2,1,0:T(8,128)(2,1)S(1)}, bf16[8,448,128]{2,1,0:T(8,128)(2,1)}, u32[]{:S(2)}, u32[]{:S(2)}) collective-permute-start(bf16[8,448,128]{2,1,0:T(8,128)(2,1)S(1)} %collective-permute-done.4.refs_11_), channel_id=1, source_target_pairs={{0,16},{16,0},{1,17},{17,1},{2,18},{18,2},{3,19},{19,3},{4,20},{20... | collective-permute-start | bytes 2752520 | tf_op jit(solution)/shard_map/ppermute | solution.py:208
  84.0 0.6 pad_add_fusion.refs_0_.me
  84.6 1.6 collective-permute-done.8.refs_13_
  86.1 9.6 %shard_map.67 = (bf16[16,512,256]{2,1,0:T(8,128)(2,1)}, f32[448,512]{1,0:T(8,128)}, bf16[8,336,128]{2,1,0:T(8,128)(2,1)}, bf16[8,336,128]{2,1,0:T(8,128)(2,1)}, ...) custom-call(s32[3]{0:T(128)} %pad_add_fusion.refs_0_.me, ...), custom_call_target="tpu_custom_call" | custom-call | flops 3758096384 | bytes 17563660 | tf_op jit(solution)/shard_map/pallas_call | solution.py:28
  95.8 2.4 collective-permute-start.10
  98.2 2.0 collective-permute-start.9
  100.2 1.9 collective-permute-done.9
  102.1 1.9 add_convert_fusion
  104.1 1.0 fusion
  105.1 6.5 %collective-permute-start.11 = (bf16[8,336,128]{2,1,0:T(8,128)(2,1)}, bf16[8,336,128]{2,1,0:T(8,128)(2,1)S(1)}, u32[]{:S(2)}, u32[]{:S(2)}) collective-permute-start(bf16[8,336,128]{2,1,0:T(8,128)(2,1)} %fusion), channel_id=1, source_target_pairs={{0,32},{32,0},{1,33},{33,1},{2,34},{34,2},{3,35},{35,3},{4,36},{36... | collective-permute-start | bytes 2064392 | tf_op jit(solution)/shard_map/ppermute | solution.py:208
  111.6 6.8 %all-to-all-start.1 = ((bf16[8,2,112,128]{3,2,1,0:T(8,128)(2,1)}), bf16[8,2,112,128]{3,2,1,0:T(8,128)(2,1)S(1)}, u32[]{:S(2)}, u32[]{:S(2)}) async-start(bf16[8,2,112,128]{3,2,1,0:T(8,128)(2,1)} %add_convert_fusion), calls=%async_computation.1 | async-start | bytes 917504 | tf_op jit(solution)/shard_map/all_to_all | solution.py:267
  118.4 6.7 %shard_map.68.own_in = f32[448,512]{1,0:T(8,128)} custom-call(s32[3]{0:T(128)} %pad_add_fusion.refs_0_.me, bf16[16,512,256]{2,1,0:T(8,128)(2,1)} %get-tuple-element.38.source, bf16[8,336,128]{2,1,0:T(8,128)(2,1)} %get-tuple-element.31.a0, bf16[8,336,128]{2,1,0:T(8,128)(2,1)} %get-tuple-element.36.a1, bf16[2,8,336,128]{3,2,1,0:T(8,128)(2,1)} %get-tuple-element.34.sent, ...), custom_call_target="tpu_custom_call" | custom-call | flops 1879048192 | bytes 8781836 | tf_op jit(solution)/shard_map/pallas_call | solution.py:28
  125.1 2.3 collective-permute-done.11
  127.4 1.1 fusion.2
  128.6 6.4 %all-to-all-done.1 = bf16[8,2,112,128]{3,2,1,0:T(8,128)(2,1)S(1)} async-done(((bf16[8,2,112,128]{3,2,1,0:T(8,128)(2,1)}), bf16[8,2,112,128]{3,2,1,0:T(8,128)(2,1)S(1)}, u32[]{:S(2)}, u32[]{:S(2)}) %all-to-all-start.1) | async-done | bytes 458784 | tf_op jit(solution)/shard_map/all_to_all | solution.py:267
  134.9 3.5 %all-to-all-start.2 = ((bf16[8,336,128]{2,1,0:T(8,128)(2,1)}), bf16[8,336,128]{2,1,0:T(8,128)(2,1)S(1)}, u32[]{:S(2)}, u32[]{:S(2)}) async-start(bf16[8,336,128]{2,1,0:T(8,128)(2,1)} %fusion.2), calls=%async_computation.2 | async-start | bytes 1376256 | tf_op jit(solution)/shard_map/all_to_all | solution.py:279
  138.6 1.9 collective-permute-start.13
  140.5 19.4 %all-to-all-done.2 = bf16[8,336,128]{2,1,0:T(8,128)(2,1)S(1)} async-done(((bf16[8,336,128]{2,1,0:T(8,128)(2,1)}), bf16[8,336,128]{2,1,0:T(8,128)(2,1)S(1)}, u32[]{:S(2)}, u32[]{:S(2)}) %all-to-all-start.2) | async-done | bytes 688160 | tf_op jit(solution)/shard_map/all_to_all | solution.py:279
  160.0 1.9 collective-permute-start.12
  162.0 3.3 %collective-permute-done.12 = bf16[336,128]{1,0:T(8,128)(2,1)S(1)} collective-permute-done((bf16[336,128]{1,0:T(8,128)(2,1)S(1)}, bf16[336,128]{1,0:T(8,128)(2,1)S(1)}, u32[]{:S(2)}, u32[]{:S(2)}) %collective-permute-start.12) | collective-permute-done | bytes 86048 | tf_op jit(solution)/shard_map/ppermute | solution.py:208
  165.2 1.0 broadcast_in_dim.7
  166.2 3.5 %all-to-all-start.3 = ((bf16[8,2,208,128]{3,2,1,0:T(8,128)(2,1)}), bf16[8,2,208,128]{3,2,1,0:T(8,128)(2,1)S(1)}, u32[]{:S(2)}, u32[]{:S(2)}) async-start(bf16[8,2,208,128]{3,2,1,0:T(8,128)(2,1)} %broadcast_in_dim.7), calls=%async_computation.3 | async-start | bytes 1703936 | tf_op jit(solution)/shard_map/all_to_all | solution.py:213
  169.8 37.3 %all-gather.1 = bf16[16,240,128]{2,1,0:T(8,128)(2,1)S(1)} all-gather(bf16[2,240,128]{2,1,0:T(8,128)(2,1)S(1)} %pad_maximum_fusion.1), channel_id=3, replica_groups=mesh['y'=8,'zl'=2,'c'=2,'zh'=4,'x'=4] {'y'}, dimensions={0}, use_global_device_ids=true | all-gather | bytes 1105920 | tf_op jit(solution)/shard_map/all_gather | solution.py:287
  207.2 8.9 %collective-permute-start.14 = (bf16[8,2,240,128]{3,2,1,0:T(8,128)(2,1)S(1)}, bf16[8,2,240,128]{3,2,1,0:T(8,128)(2,1)S(1)}, u32[]{:S(2)}, u32[]{:S(2)}) collective-permute-start(bf16[8,2,240,128]{3,2,1,0:T(8,128)(2,1)S(1)} %bitcast.22), channel_id=1, source_target_pairs={{0,16},{16,0},{1,17},{17,1},{2,18},{18,2},{3,19},{19,3},{4,20},{20... | collective-permute-start | bytes 2949128 | tf_op jit(solution)/shard_map/ppermute | solution.py:208
  216.1 1.9 collective-permute-start.15
  218.1 0.2 collective-permute-done.14.refs_2_
  218.3 2.1 collective-permute-done.15.refs_3_
  220.4 0.9 copy-done.7
  221.3 6.3 %shard_map.69 = f32[2,448]{1,0:T(2,128)} custom-call(s32[3]{0:T(128)} %pad_add_fusion.refs_0_.me, bf16[16,512,256]{2,1,0:T(8,128)(2,1)} %get-tuple-element.38.source, f32[448,512]{1,0:T(8,128)} %get-tuple-element.41.bend_in, f32[448,512]{1,0:T(8,128)} %shard_map.68.own_in, bf16[8,2,240,128]{3,2,1,0:T(8,128)(2,1)} %bitcast.23, ...), custom_call_target="tpu_custom_call" | custom-call | flops 1879048192 | bytes 9702924 | tf_op jit(solution)/shard_map/pallas_call | solution.py:28
  227.7 1.4 broadcast_in_dim.8
  229.0 5.5 %all-to-all-start.4 = ((f32[32,2,448]{2,1,0:T(2,128)}), f32[32,2,448]{2,1,0:T(2,128)S(1)}, u32[]{:S(2)}, u32[]{:S(2)}) async-start(f32[32,2,448]{2,1,0:T(2,128)} %broadcast_in_dim.8), calls=%async_computation.4 | async-start | bytes 262144 | tf_op jit(solution)/shard_map/all_to_all | solution.py:213
  234.5 0.7 slice_bitcast_fusion
  235.1 8.6 %all-to-all-done.4 = f32[32,2,448]{2,1,0:T(2,128)S(1)} async-done(((f32[32,2,448]{2,1,0:T(2,128)}), f32[32,2,448]{2,1,0:T(2,128)S(1)}, u32[]{:S(2)}, u32[]{:S(2)}) %all-to-all-start.4) | async-done | bytes 114720 | tf_op jit(solution)/shard_map/all_to_all | solution.py:213
  243.8 0.6 slice_multiply_fusion
  (48 shorter events, 0.5 us)
Async XLA Ops:
  2.6 11.0 %copy-start.8 = (bf16[128,448]{0,1:T(8,128)(2,1)S(1)}, bf16[128,448]{0,1:T(8,128)(2,1)}, u32[]{:S(2)}) copy-start(bf16[128,448]{0,1:T(8,128)(2,1)} %param.5) | copy-start | bytes 344068
  2.6 34.3 %all-to-all-start = ((bf16[4,512,256]{2,1,0:T(8,128)(2,1)}), bf16[4,512,256]{2,1,0:T(8,128)(2,1)S(1)}, u32[]{:S(2)}, u32[]{:S(2)}) async-start(bf16[4,512,256]{2,1,0:T(8,128)(2,1)} %broadcast_in_dim.6), calls=%async_computation | async-start | bytes 2097152 | tf_op jit(solution)/shard_map/all_to_all | solution.py:213
  36.9 49.2 %copy-start.6 = (bf16[3584,128]{1,0:T(8,128)(2,1)}, bf16[3584,128]{1,0:T(8,128)(2,1)S(1)}, u32[]{:S(2)}) copy-start(bf16[3584,128]{1,0:T(8,128)(2,1)S(1)} %all-gather) | copy-start | bytes 2752516
  36.9 49.2 %copy-start = (bf16[4,512,256]{2,1,0:T(8,128)(2,1)}, bf16[4,512,256]{2,1,0:T(8,128)(2,1)S(1)}, u32[]{:S(2)}) copy-start(bf16[4,512,256]{2,1,0:T(8,128)(2,1)S(1)} %all-to-all-done.refs_1_) | copy-start | bytes 3145732
  37.0 20.0 %collective-permute-start.3 = (bf16[2,512,256]{2,1,0:T(8,128)(2,1)S(1)}, bf16[2,512,256]{2,1,0:T(8,128)(2,1)S(1)}, u32[]{:S(2)}, u32[]{:S(2)}) collective-permute-start(bf16[2,512,256]{2,1,0:T(8,128)(2,1)S(1)} %get-tuple-element.43), channel_id=1, source_target_pairs={{0,3},{1,0},{2,1},{3,2},{4,7},{5,4},{6,5},{7,6},{8,11},{9,8},{10,9... | collective-permute-start | bytes 1572872 | tf_op jit(solution)/shard_map/ppermute | solution.py:227
  41.4 19.0 %collective-permute-start = (bf16[2,512,256]{2,1,0:T(8,128)(2,1)S(1)}, bf16[2,512,256]{2,1,0:T(8,128)(2,1)S(1)}, u32[]{:S(2)}, u32[]{:S(2)}) collective-permute-start(bf16[2,512,256]{2,1,0:T(8,128)(2,1)S(1)} %get-tuple-element.44), channel_id=1, source_target_pairs={{0,1},{1,2},{2,3},{3,0},{4,5},{5,6},{6,7},{7,4},{8,9},{9,10},{10,1... | collective-permute-start | bytes 1572872 | tf_op jit(solution)/shard_map/ppermute | solution.py:227
  43.3 32.1 %collective-permute-start.4 = (bf16[8,448,128]{2,1,0:T(8,128)(2,1)S(1)}, bf16[8,448,128]{2,1,0:T(8,128)(2,1)S(1)}, u32[]{:S(2)}, u32[]{:S(2)}) collective-permute-start(bf16[8,448,128]{2,1,0:T(8,128)(2,1)S(1)} %bitcast.27), channel_id=1, source_target_pairs={{0,32},{32,0},{1,33},{33,1},{2,34},{34,2},{3,35},{35,3},{4,36},{36... | collective-permute-start | bytes 2752520 | tf_op jit(solution)/shard_map/ppermute | solution.py:208
  50.5 17.1 %collective-permute-start.1 = (bf16[2,512,256]{2,1,0:T(8,128)(2,1)S(1)}, bf16[2,512,256]{2,1,0:T(8,128)(2,1)S(1)}, u32[]{:S(2)}, u32[]{:S(2)}) collective-permute-start(bf16[2,512,256]{2,1,0:T(8,128)(2,1)S(1)} %get-tuple-element.43), channel_id=1, source_target_pairs={{0,1},{1,2},{2,3},{3,0},{4,5},{5,6},{6,7},{7,4},{8,9},{9,10},{10,1... | collective-permute-start | bytes 1572872 | tf_op jit(solution)/shard_map/ppermute | solution.py:227
  52.6 15.0 %collective-permute-start.2 = (bf16[2,512,256]{2,1,0:T(8,128)(2,1)S(1)}, bf16[2,512,256]{2,1,0:T(8,128)(2,1)S(1)}, u32[]{:S(2)}, u32[]{:S(2)}) collective-permute-start(bf16[2,512,256]{2,1,0:T(8,128)(2,1)S(1)} %get-tuple-element.44), channel_id=1, source_target_pairs={{0,3},{1,0},{2,1},{3,2},{4,7},{5,4},{6,5},{7,6},{8,11},{9,8},{10,9... | collective-permute-start | bytes 1572872 | tf_op jit(solution)/shard_map/ppermute | solution.py:227
  57.0 29.1 %copy-start.10 = (bf16[2,512,256]{2,1,0:T(8,128)(2,1)}, bf16[2,512,256]{2,1,0:T(8,128)(2,1)S(1)}, u32[]{:S(2)}) copy-start(bf16[2,512,256]{2,1,0:T(8,128)(2,1)S(1)} %collective-permute-done.3.refs_4_) | copy-start | bytes 1572868
  57.0 20.1 %collective-permute-start.6 = (bf16[2,512,256]{2,1,0:T(8,128)(2,1)S(1)}, bf16[2,512,256]{2,1,0:T(8,128)(2,1)S(1)}, u32[]{:S(2)}, u32[]{:S(2)}) collective-permute-start(bf16[2,512,256]{2,1,0:T(8,128)(2,1)S(1)} %collective-permute-done.3.refs_4_), channel_id=1, source_target_pairs={{0,3},{1,0},{2,1},{3,2},{4,7},{5,4},{6,5},{7,6},{8,11},{9,8},{10,9... | collective-permute-start | bytes 1572872 | tf_op jit(solution)/shard_map/ppermute | solution.py:227
  60.4 16.7 %copy-start.11 = (bf16[2,512,256]{2,1,0:T(8,128)(2,1)}, bf16[2,512,256]{2,1,0:T(8,128)(2,1)S(1)}, u32[]{:S(2)}) copy-start(bf16[2,512,256]{2,1,0:T(8,128)(2,1)S(1)} %collective-permute-done.refs_2_) | copy-start | bytes 1572868
  60.4 18.4 %collective-permute-start.5 = (bf16[2,512,256]{2,1,0:T(8,128)(2,1)S(1)}, bf16[2,512,256]{2,1,0:T(8,128)(2,1)S(1)}, u32[]{:S(2)}, u32[]{:S(2)}) collective-permute-start(bf16[2,512,256]{2,1,0:T(8,128)(2,1)S(1)} %collective-permute-done.refs_2_), channel_id=1, source_target_pairs={{0,1},{1,2},{2,3},{3,0},{4,5},{5,6},{6,7},{7,4},{8,9},{9,10},{10,1... | collective-permute-start | bytes 1572872 | tf_op jit(solution)/shard_map/ppermute | solution.py:227
  67.6 11.2 %copy-start.12 = (bf16[2,512,256]{2,1,0:T(8,128)(2,1)}, bf16[2,512,256]{2,1,0:T(8,128)(2,1)S(1)}, u32[]{:S(2)}) copy-start(bf16[2,512,256]{2,1,0:T(8,128)(2,1)S(1)} %collective-permute-done.1.refs_3_) | copy-start | bytes 1572868
  67.6 16.3 %copy-start.13 = (bf16[2,512,256]{2,1,0:T(8,128)(2,1)}, bf16[2,512,256]{2,1,0:T(8,128)(2,1)S(1)}, u32[]{:S(2)}) copy-start(bf16[2,512,256]{2,1,0:T(8,128)(2,1)S(1)} %collective-permute-done.2.refs_5_) | copy-start | bytes 1572868
  67.6 16.9 %collective-permute-start.7 = (bf16[8,448,128]{2,1,0:T(8,128)(2,1)S(1)}, bf16[8,448,128]{2,1,0:T(8,128)(2,1)}, u32[]{:S(2)}, u32[]{:S(2)}) collective-permute-start(bf16[8,448,128]{2,1,0:T(8,128)(2,1)S(1)} %bitcast.28), channel_id=1, source_target_pairs={{0,16},{16,0},{1,17},{17,1},{2,18},{18,2},{3,19},{19,3},{4,20},{20... | collective-permute-start | bytes 2752520 | tf_op jit(solution)/shard_map/ppermute | solution.py:208
  75.5 10.7 %copy-start.9 = (bf16[8,448,128]{2,1,0:T(8,128)(2,1)}, bf16[8,448,128]{2,1,0:T(8,128)(2,1)S(1)}, u32[]{:S(2)}) copy-start(bf16[8,448,128]{2,1,0:T(8,128)(2,1)S(1)} %collective-permute-done.4.refs_11_) | copy-start | bytes 2752516
  77.1 6.8 %copy-start.14 = (bf16[2,512,256]{2,1,0:T(8,128)(2,1)}, bf16[2,512,256]{2,1,0:T(8,128)(2,1)S(1)}, u32[]{:S(2)}) copy-start(bf16[2,512,256]{2,1,0:T(8,128)(2,1)S(1)} %collective-permute-done.6.refs_7_) | copy-start | bytes 1572868
  78.9 5.1 %copy-start.15 = (bf16[2,512,256]{2,1,0:T(8,128)(2,1)}, bf16[2,512,256]{2,1,0:T(8,128)(2,1)S(1)}, u32[]{:S(2)}) copy-start(bf16[2,512,256]{2,1,0:T(8,128)(2,1)S(1)} %collective-permute-done.5.refs_6_) | copy-start | bytes 1572868
  78.9 7.3 %collective-permute-start.8 = (bf16[8,448,128]{2,1,0:T(8,128)(2,1)S(1)}, bf16[8,448,128]{2,1,0:T(8,128)(2,1)}, u32[]{:S(2)}, u32[]{:S(2)}) collective-permute-start(bf16[8,448,128]{2,1,0:T(8,128)(2,1)S(1)} %collective-permute-done.4.refs_11_), channel_id=1, source_target_pairs={{0,16},{16,0},{1,17},{17,1},{2,18},{18,2},{3,19},{19,3},{4,20},{20... | collective-permute-start | bytes 2752520 | tf_op jit(solution)/shard_map/ppermute | solution.py:208
  95.7 8.3 %copy-start.4 = (bf16[8,336,128]{2,1,0:T(8,128)(2,1)S(1)}, bf16[8,336,128]{2,1,0:T(8,128)(2,1)}, u32[]{:S(2)}) copy-start(bf16[8,336,128]{2,1,0:T(8,128)(2,1)} %get-tuple-element.36.a1) | copy-start | bytes 2064388
  95.8 8.3 %collective-permute-start.10 = (bf16[2,8,336,128]{3,2,1,0:T(8,128)(2,1)}, bf16[2,8,336,128]{3,2,1,0:T(8,128)(2,1)S(1)}, u32[]{:S(2)}, u32[]{:S(2)}) collective-permute-start(bf16[2,8,336,128]{3,2,1,0:T(8,128)(2,1)} %get-tuple-element.34.sent), channel_id=1, source_target_pairs={{0,16},{16,0},{1,17},{17,1},{2,18},{18,2},{3,19},{19,3},{4,20},{20... | collective-permute-start | bytes 4128776 | tf_op jit(solution)/shard_map/ppermute | solution.py:208
  98.2 3.9 %collective-permute-start.9 = (bf16[8,2,112,128]{3,2,1,0:T(8,128)(2,1)}, bf16[8,2,112,128]{3,2,1,0:T(8,128)(2,1)S(1)}, u32[]{:S(2)}, u32[]{:S(2)}) collective-permute-start(bf16[8,2,112,128]{3,2,1,0:T(8,128)(2,1)} %get-tuple-element.33.b1), channel_id=1, source_target_pairs={{0,16},{16,0},{1,17},{17,1},{2,18},{18,2},{3,19},{19,3},{4,20},{20... | collective-permute-start | bytes 1376264 | tf_op jit(solution)/shard_map/ppermute | solution.py:208
  105.1 22.3 %collective-permute-start.11 = (bf16[8,336,128]{2,1,0:T(8,128)(2,1)}, bf16[8,336,128]{2,1,0:T(8,128)(2,1)S(1)}, u32[]{:S(2)}, u32[]{:S(2)}) collective-permute-start(bf16[8,336,128]{2,1,0:T(8,128)(2,1)} %fusion), channel_id=1, source_target_pairs={{0,32},{32,0},{1,33},{33,1},{2,34},{34,2},{3,35},{35,3},{4,36},{36... | collective-permute-start | bytes 2064392 | tf_op jit(solution)/shard_map/ppermute | solution.py:208
  111.6 23.4 %all-to-all-start.1 = ((bf16[8,2,112,128]{3,2,1,0:T(8,128)(2,1)}), bf16[8,2,112,128]{3,2,1,0:T(8,128)(2,1)S(1)}, u32[]{:S(2)}, u32[]{:S(2)}) async-start(bf16[8,2,112,128]{3,2,1,0:T(8,128)(2,1)} %add_convert_fusion), calls=%async_computation.1 | async-start | bytes 917504 | tf_op jit(solution)/shard_map/all_to_all | solution.py:267
  118.4 9.0 %copy-start.3 = (bf16[8,336,128]{2,1,0:T(8,128)(2,1)S(1)}, bf16[8,336,128]{2,1,0:T(8,128)(2,1)}, u32[]{:S(2)}) copy-start(bf16[8,336,128]{2,1,0:T(8,128)(2,1)} %get-tuple-element.31.a0) | copy-start | bytes 2064388
  134.9 24.9 %all-to-all-start.2 = ((bf16[8,336,128]{2,1,0:T(8,128)(2,1)}), bf16[8,336,128]{2,1,0:T(8,128)(2,1)S(1)}, u32[]{:S(2)}, u32[]{:S(2)}) async-start(bf16[8,336,128]{2,1,0:T(8,128)(2,1)} %fusion.2), calls=%async_computation.2 | async-start | bytes 1376256 | tf_op jit(solution)/shard_map/all_to_all | solution.py:279
  138.6 23.4 %collective-permute-start.13 = (bf16[2,112,128]{2,1,0:T(8,128)(2,1)S(1)}, bf16[2,112,128]{2,1,0:T(8,128)(2,1)S(1)}, u32[]{:S(2)}, u32[]{:S(2)}) collective-permute-start(bf16[2,112,128]{2,1,0:T(8,128)(2,1)S(1)} %reduce_sum.34), channel_id=1, source_target_pairs={{0,32},{32,0},{1,33},{33,1},{2,34},{34,2},{3,35},{35,3},{4,36},{36... | collective-permute-start | bytes 172040 | tf_op jit(solution)/shard_map/ppermute | solution.py:208
  160.0 5.2 %collective-permute-start.12 = (bf16[336,128]{1,0:T(8,128)(2,1)S(1)}, bf16[336,128]{1,0:T(8,128)(2,1)S(1)}, u32[]{:S(2)}, u32[]{:S(2)}) collective-permute-start(bf16[336,128]{1,0:T(8,128)(2,1)S(1)} %reduce_sum.33), channel_id=1, source_target_pairs={{0,32},{32,0},{1,33},{33,1},{2,34},{34,2},{3,35},{35,3},{4,36},{36... | collective-permute-start | bytes 258056 | tf_op jit(solution)/shard_map/ppermute | solution.py:208
  166.2 49.8 %all-to-all-start.3 = ((bf16[8,2,208,128]{3,2,1,0:T(8,128)(2,1)}), bf16[8,2,208,128]{3,2,1,0:T(8,128)(2,1)S(1)}, u32[]{:S(2)}, u32[]{:S(2)}) async-start(bf16[8,2,208,128]{3,2,1,0:T(8,128)(2,1)} %broadcast_in_dim.7), calls=%async_computation.3 | async-start | bytes 1703936 | tf_op jit(solution)/shard_map/all_to_all | solution.py:213
  207.2 14.1 %copy-start.1 = (bf16[16,240,128]{2,1,0:T(8,128)(2,1)}, bf16[16,240,128]{2,1,0:T(8,128)(2,1)S(1)}, u32[]{:S(2)}) copy-start(bf16[16,240,128]{2,1,0:T(8,128)(2,1)S(1)} %all-gather.1) | copy-start | bytes 2949124
  207.2 11.1 %collective-permute-start.14 = (bf16[8,2,240,128]{3,2,1,0:T(8,128)(2,1)S(1)}, bf16[8,2,240,128]{3,2,1,0:T(8,128)(2,1)S(1)}, u32[]{:S(2)}, u32[]{:S(2)}) collective-permute-start(bf16[8,2,240,128]{3,2,1,0:T(8,128)(2,1)S(1)} %bitcast.22), channel_id=1, source_target_pairs={{0,16},{16,0},{1,17},{17,1},{2,18},{18,2},{3,19},{19,3},{4,20},{20... | collective-permute-start | bytes 2949128 | tf_op jit(solution)/shard_map/ppermute | solution.py:208
  216.1 5.2 %copy-start.2 = (bf16[8,2,208,128]{3,2,1,0:T(8,128)(2,1)}, bf16[8,2,208,128]{3,2,1,0:T(8,128)(2,1)S(1)}, u32[]{:S(2)}) copy-start(bf16[8,2,208,128]{3,2,1,0:T(8,128)(2,1)S(1)} %all-to-all-done.3.refs_1_) | copy-start | bytes 2555908
  216.1 4.3 %collective-permute-start.15 = (bf16[8,2,208,128]{3,2,1,0:T(8,128)(2,1)S(1)}, bf16[8,2,208,128]{3,2,1,0:T(8,128)(2,1)S(1)}, u32[]{:S(2)}, u32[]{:S(2)}) collective-permute-start(bf16[8,2,208,128]{3,2,1,0:T(8,128)(2,1)S(1)} %all-to-all-done.3.refs_1_), channel_id=1, source_target_pairs={{0,16},{16,0},{1,17},{17,1},{2,18},{18,2},{3,19},{19,3},{4,20},{20... | collective-permute-start | bytes 2555912 | tf_op jit(solution)/shard_map/ppermute | solution.py:208
  218.3 3.1 %copy-start.5 = (bf16[8,2,240,128]{3,2,1,0:T(8,128)(2,1)}, bf16[8,2,240,128]{3,2,1,0:T(8,128)(2,1)S(1)}, u32[]{:S(2)}) copy-start(bf16[8,2,240,128]{3,2,1,0:T(8,128)(2,1)S(1)} %collective-permute-done.14.refs_2_) | copy-start | bytes 2949124
  220.4 0.9 copy-start.7
  229.0 14.7 %all-to-all-start.4 = ((f32[32,2,448]{2,1,0:T(2,128)}), f32[32,2,448]{2,1,0:T(2,128)S(1)}, u32[]{:S(2)}, u32[]{:S(2)}) async-start(f32[32,2,448]{2,1,0:T(2,128)} %broadcast_in_dim.8), calls=%async_computation.4 | async-start | bytes 262144 | tf_op jit(solution)/shard_map/all_to_all | solution.py:213

commit v6 on v5

--- a/solution.py
+++ b/solution.py
@@ -11,8 +11,7 @@
 REP = ("y", "zl", "c")
 F32, BF = jnp.float32, jnp.bfloat16
 NT = (((1,), (1,)), ((), ()))
-CUT = 336
-RING = 240
+CUT = 304
 VMEM_LIMIT = 60 * 1024 * 1024
 TOK = pltpu.VMEM((16, 512, 256), BF)
 ACC = pltpu.VMEM((448, 512), F32)
@@ -151,6 +150,10 @@
     keep_bend.wait()
 
 
+def both_parts(held, held_b, y, rel):
+    return [jnp.concatenate([held[2 * core + rel, y], held_b[core, y, rel]], 0) for core in (0, 1)]
+
+
 def own_kernel(me, source, a0, a1, sent, b0, b1, acc, tok, held, held_b, tok_sems, sems):
     tok_ready = fetched([(source, tok)], tok_sems)
     pairs = [(a, held.at[i]) for i, a in enumerate((a0, a1, sent.at[0], sent.at[1]))]
@@ -161,20 +164,16 @@
         tok_ready(half)
         rows_ready(half)
 
-    def rows_of(y, rel):
-        return [
-            jnp.concatenate([held[2 * core + rel, y], held_b[core, y, rel]], 0) for core in (0, 1)
-        ]
-
-    project(me, tok, rows_of, acc, ready)
+    project(me, tok, functools.partial(both_parts, held, held_b), acc, ready)
 
 
 def mean_kernel(me, source, bend_in, own_in, *refs):
-    sums, acc, bend, own, tok, held, held_b, tok_sems, sems, in_sems = refs[4:]
+    sums, acc, bend, own, tok, held, held_b, tok_sems, sems, in_sems = refs[6:]
     tok_ready = fetched([(source, tok)], tok_sems)
     get_bend = pltpu.make_async_copy(bend_in, bend, in_sems.at[0])
     get_own = pltpu.make_async_copy(own_in, own, in_sems.at[1])
-    pairs = [(a, (held, held_b)[i % 2].at[i // 2]) for i, a in enumerate(refs[:4])]
+    pairs = [(a, held.at[i]) for i, a in enumerate(refs[:4])]
+    pairs += [(b, held_b.at[i]) for i, b in enumerate(refs[4:6])]
     rows_ready = fetched(pairs, sems)
     get_bend.start()
     get_own.start()
@@ -183,12 +182,7 @@
         tok_ready(half)
         rows_ready(half)
 
-    def rows_of(y, rel):
-        return [
-            jnp.concatenate([held[core, y, rel], held_b[core, y, rel]], 0) for core in (0, 1)
-        ]
-
-    project(me, tok, rows_of, acc, ready)
+    project(me, tok, functools.partial(both_parts, held, held_b), acc, ready)
     get_bend.wait()
     get_own.wait()
     c = jnp.zeros((448, 128), F32)
@@ -281,26 +275,20 @@
     other_b = swap(part_b, "zl")
     both_b = total(part_b, other_b[::-1]).astype(BF)
     grad_a = jnp.sum(across_a.astype(F32), axis=0).astype(BF)
-    both_a = jnp.stack([grad_a, swap(grad_a, "zl")])
-    both = jnp.concatenate([both_a, both_b], axis=1)
-    g1 = to_all(both[:, RING:], "y")
-    g0 = lax.all_gather(both[:, :RING], "y", axis=0)
+    u0, both_b = lax.optimization_barrier((to_all(grad_a, "y"), both_b))
+    v0 = to_all(both_b, "y")
+    u1 = swap(u0, "zl")
+    rows = (u0, u1, swap(u0, "c"), swap(u1, "c"), v0, swap(v0, "c"))
     line = call(
         mean_kernel,
         [shape(2, 448, dtype=F32)],
-        (me, tok, bend, own, g0, g1, swap(g0, "c"), swap(g1, "c")),
+        (me, tok, bend, own, *rows),
         flops,
-        [
-            *[ACC] * 3,
-            TOK,
-            pltpu.VMEM((2, 8, 2, RING, 128), BF),
-            pltpu.VMEM((2, 8, 2, 448 - RING, 128), BF),
-            *map(dma, ((1, 2), (4, 2), (2,))),
-        ],
+        [*[ACC] * 3, TOK, *held, *map(dma, ((1, 2), (6, 2), (2,)))],
         True,
     )[0]
     whole = jnp.sum(to_all(line, REP), axis=0)
-    grad = both[0].T
+    grad = jnp.concatenate([grad_a, both_b[0]], axis=0).T
     return grad, whole[0], whole[1] / 31
 
 

time: 246 us -> 234 us (0.951)
  blocking collectives: 60.7 us -> 47.2 us
  starting transfers between devices: 94.1 us -> 99.5 us
  waiting for transfers between devices: 54.4 us -> 51.1 us
    all_gather x1 -> x0, blocking collectives: 37.3 us -> none  [shards(): g0 = lax.all_gather(both[:, :RING], 'y', axis=0)]
    all_to_all x0 -> x1, blocking collectives: none -> 23.9 us  [shards(): across_a = lax.all_to_all(sums_a, 'y', 0, 0, tiled=True)]
    all_to_all x1 -> x0, waiting for transfers between devices: 19.4 us -> none  [shards(): across_a = lax.all_to_all(sums_a, 'y', 0, 0, tiled=True)]
    all_to_all x3 -> x4, waiting for transfers between devices: 8.61 us -> 20.5 us  [to_all(): lax.all_to_all(jnp.broadcast_to(value[None], (count, *value.shape)), axis...]
    ppermute x10 -> x11, waiting for transfers between devices: 11.4 us -> 21.9 us  [swap(): return lax.ppermute(value, axis, ((0, 1), (1, 0)))]
    all_to_all x1, waiting for transfers between devices: 6.37 us -> 0.01 us  [shards(): across_b = lax.all_to_all(sums_b, 'y', 0, 0, tiled=True)]
    all_to_all x3 -> x4, starting transfers between devices: 20 us -> 25.3 us  [to_all(): lax.all_to_all(jnp.broadcast_to(value[None], (count, *value.shape)), axis...]
    ppermute x10 -> x11, starting transfers between devices: 45.7 us -> 50.8 us  [swap(): return lax.ppermute(value, axis, ((0, 1), (1, 0)))]
  transfers between devices with their start and end apart: 21 -> 22, of which waited for: 12 -> 11; matrix products, arithmetic and copies ran while one was open for 2% -> 2% of each run, Pallas kernels for 3% -> 3%
where the time goes in v6:
time: 234 us; the launch traced here: 233 us
  starting transfers between devices  99.5 us (43%)
  waiting for transfers between devices  51.1 us (22%)
  blocking collectives  47.2 us (20%)
  Pallas kernels  22.6 us (10%)
  local copies, waits for them, and re-layouts  6.31 us (3%)
  other arithmetic  5.53 us (2%)
    ppermute x11, starting transfers between devices, swap(): return lax.ppermute(value, axis, ((0, 1), (1, 0)))  50.8 us
    all_to_all x4, starting transfers between devices, to_all(): lax.all_to_all(jnp.broadcast_to(value[None], (count, *value.shape)), axis...  25.3 us
    all_to_all x1, blocking collectives, shards(): across_a = lax.all_to_all(sums_a, 'y', 0, 0, tiled=True)  23.9 us
    all_gather x1, blocking collectives, shards(): w0 = lax.all_gather(gate_weight.T, 'y', axis=0)  23.3 us
    pallas_call x3, Pallas kernels, call(): pl.pallas_call(kernel, out_shape=outs, in_specs=[SM] + [ANY] * (len(opera...  22.6 us
    ppermute x11, waiting for transfers between devices, swap(): return lax.ppermute(value, axis, ((0, 1), (1, 0)))  21.9 us
    all_to_all x4, waiting for transfers between devices, to_all(): lax.all_to_all(jnp.broadcast_to(value[None], (count, *value.shape)), axis...  20.5 us
    ppermute x6, starting transfers between devices, along_x(): return lax.ppermute(value, 'x', [(i, (i + by) % 4) for i in range(4)])  18.1 us
  transfers between devices with their start and end apart: 22, of which 11 were waited for; matrix products, arithmetic and copies ran while one was open for 2% of the time, Pallas kernels for 3%

profile of v6, /device:TPU:1, one launch (start us, length us, event | category | flops | bytes accessed | tf_op | source)
XLA Modules:
  0.0 233.3 jit_solution(10559572304303568227)
XLA Ops:
  0.6 2.0 broadcast_in_dim.8
  2.6 11.0 %all-to-all-start = ((bf16[4,512,256]{2,1,0:T(8,128)(2,1)}), bf16[4,512,256]{2,1,0:T(8,128)(2,1)S(1)}, u32[]{:S(2)}, u32[]{:S(2)}) async-start(bf16[4,512,256]{2,1,0:T(8,128)(2,1)} %broadcast_in_dim.8), calls=%async_computation | async-start | bytes 2097152 | tf_op jit(solution)/shard_map/all_to_all | solution.py:207
  13.6 23.3 %all-gather = bf16[3584,128]{1,0:T(8,128)(2,1)S(1)} all-gather(bf16[448,128]{1,0:T(8,128)(2,1)S(1)} %bitcast.22), channel_id=2, replica_groups=mesh['y'=8,'zl'=2,'c'=2,'zh'=4,'x'=4] {'y'}, dimensions={0}, use_global_device_ids=true | all-gather | bytes 1032192 | tf_op jit(solution)/shard_map/all_gather | solution.py:230
  37.0 4.4 %collective-permute-start.3 = (bf16[2,512,256]{2,1,0:T(8,128)(2,1)S(1)}, bf16[2,512,256]{2,1,0:T(8,128)(2,1)S(1)}, u32[]{:S(2)}, u32[]{:S(2)}) collective-permute-start(bf16[2,512,256]{2,1,0:T(8,128)(2,1)S(1)} %get-tuple-element.47), channel_id=1, source_target_pairs={{0,3},{1,0},{2,1},{3,2},{4,7},{5,4},{6,5},{7,6},{8,11},{9,8},{10,9... | collective-permute-start | bytes 1572872 | tf_op jit(solution)/shard_map/ppermute | solution.py:221
  41.4 1.9 collective-permute-start
  43.3 7.2 %collective-permute-start.4 = (bf16[8,448,128]{2,1,0:T(8,128)(2,1)S(1)}, bf16[8,448,128]{2,1,0:T(8,128)(2,1)S(1)}, u32[]{:S(2)}, u32[]{:S(2)}) collective-permute-start(bf16[8,448,128]{2,1,0:T(8,128)(2,1)S(1)} %bitcast.19), channel_id=1, source_target_pairs={{0,32},{32,0},{1,33},{33,1},{2,34},{34,2},{3,35},{35,3},{4,36},{36... | collective-permute-start | bytes 2752520 | tf_op jit(solution)/shard_map/ppermute | solution.py:202
  50.5 2.1 collective-permute-start.1
  52.6 4.4 %collective-permute-start.2 = (bf16[2,512,256]{2,1,0:T(8,128)(2,1)S(1)}, bf16[2,512,256]{2,1,0:T(8,128)(2,1)S(1)}, u32[]{:S(2)}, u32[]{:S(2)}) collective-permute-start(bf16[2,512,256]{2,1,0:T(8,128)(2,1)S(1)} %get-tuple-element.48), channel_id=1, source_target_pairs={{0,3},{1,0},{2,1},{3,2},{4,7},{5,4},{6,5},{7,6},{8,11},{9,8},{10,9... | collective-permute-start | bytes 1572872 | tf_op jit(solution)/shard_map/ppermute | solution.py:221
  57.0 3.4 %collective-permute-start.6 = (bf16[2,512,256]{2,1,0:T(8,128)(2,1)S(1)}, bf16[2,512,256]{2,1,0:T(8,128)(2,1)S(1)}, u32[]{:S(2)}, u32[]{:S(2)}) collective-permute-start(bf16[2,512,256]{2,1,0:T(8,128)(2,1)S(1)} %collective-permute-done.3.refs_4_), channel_id=1, source_target_pairs={{0,3},{1,0},{2,1},{3,2},{4,7},{5,4},{6,5},{7,6},{8,11},{9,8},{10,9... | collective-permute-start | bytes 1572872 | tf_op jit(solution)/shard_map/ppermute | solution.py:221
  60.4 1.9 collective-permute-start.5
  62.4 5.3 %collective-permute-done.1.refs_3_ = bf16[2,512,256]{2,1,0:T(8,128)(2,1)S(1)} collective-permute-done((bf16[2,512,256]{2,1,0:T(8,128)(2,1)S(1)}, bf16[2,512,256]{2,1,0:T(8,128)(2,1)S(1)}, u32[]{:S(2)}, u32[]{:S(2)}) %collective-permute-start.1) | collective-permute-done | bytes 524320 | tf_op jit(solution)/shard_map/ppermute | solution.py:221
  67.6 7.8 %collective-permute-start.7 = (bf16[8,448,128]{2,1,0:T(8,128)(2,1)S(1)}, bf16[8,448,128]{2,1,0:T(8,128)(2,1)}, u32[]{:S(2)}, u32[]{:S(2)}) collective-permute-start(bf16[8,448,128]{2,1,0:T(8,128)(2,1)S(1)} %bitcast.20), channel_id=1, source_target_pairs={{0,16},{16,0},{1,17},{17,1},{2,18},{18,2},{3,19},{19,3},{4,20},{20... | collective-permute-start | bytes 2752520 | tf_op jit(solution)/shard_map/ppermute | solution.py:202
  75.5 1.6 collective-permute-done.6.refs_7_
  77.1 1.8 collective-permute-done.5.refs_6_
  78.9 5.1 %collective-permute-start.8 = (bf16[8,448,128]{2,1,0:T(8,128)(2,1)S(1)}, bf16[8,448,128]{2,1,0:T(8,128)(2,1)}, u32[]{:S(2)}, u32[]{:S(2)}) collective-permute-start(bf16[8,448,128]{2,1,0:T(8,128)(2,1)S(1)} %collective-permute-done.4.refs_11_), channel_id=1, source_target_pairs={{0,16},{16,0},{1,17},{17,1},{2,18},{18,2},{3,19},{19,3},{4,20},{20... | collective-permute-start | bytes 2752520 | tf_op jit(solution)/shard_map/ppermute | solution.py:202
  84.0 0.6 pad_add_fusion.refs_0_.me
  84.5 1.6 collective-permute-done.8.refs_13_
  86.1 9.6 %shard_map.67 = (bf16[16,512,256]{2,1,0:T(8,128)(2,1)}, f32[448,512]{1,0:T(8,128)}, bf16[8,304,128]{2,1,0:T(8,128)(2,1)}, bf16[8,304,128]{2,1,0:T(8,128)(2,1)}, ...) custom-call(s32[3]{0:T(128)} %pad_add_fusion.refs_0_.me, ...), custom_call_target="tpu_custom_call" | custom-call | flops 3758096384 | bytes 17563660 | tf_op jit(solution)/shard_map/pallas_call | solution.py:27
  95.7 2.3 collective-permute-start.10
  98.0 2.0 collective-permute-start.9
  100.1 2.1 collective-permute-done.9
  102.1 2.2 add_convert_fusion
  104.3 5.3 %all-to-all-start.1 = ((bf16[8,2,144,128]{3,2,1,0:T(8,128)(2,1)}), bf16[8,2,144,128]{3,2,1,0:T(8,128)(2,1)S(1)}, u32[]{:S(2)}, u32[]{:S(2)}) async-start(bf16[8,2,144,128]{3,2,1,0:T(8,128)(2,1)} %add_convert_fusion), calls=%async_computation.1 | async-start | bytes 1179648 | tf_op jit(solution)/shard_map/all_to_all | solution.py:261
  109.6 1.1 fusion
  110.7 8.0 %collective-permute-start.11 = (bf16[8,304,128]{2,1,0:T(8,128)(2,1)}, bf16[8,304,128]{2,1,0:T(8,128)(2,1)S(1)}, u32[]{:S(2)}, u32[]{:S(2)}) collective-permute-start(bf16[8,304,128]{2,1,0:T(8,128)(2,1)} %fusion), channel_id=1, source_target_pairs={{0,32},{32,0},{1,33},{33,1},{2,34},{34,2},{3,35},{35,3},{4,36},{36... | collective-permute-start | bytes 1867784 | tf_op jit(solution)/shard_map/ppermute | solution.py:202
  118.6 6.6 %shard_map.68.own_in = f32[448,512]{1,0:T(8,128)} custom-call(s32[3]{0:T(128)} %pad_add_fusion.refs_0_.me, bf16[16,512,256]{2,1,0:T(8,128)(2,1)} %get-tuple-element.40.source, bf16[8,304,128]{2,1,0:T(8,128)(2,1)} %get-tuple-element.33.a0, bf16[8,304,128]{2,1,0:T(8,128)(2,1)} %get-tuple-element.38.a1, bf16[2,8,304,128]{3,2,1,0:T(8,128)(2,1)} %get-tuple-element.36.sent, ...), custom_call_target="tpu_custom_call" | custom-call | flops 1879048192 | bytes 8781836 | tf_op jit(solution)/shard_map/pallas_call | solution.py:27
  125.2 7.6 %collective-permute-done.11 = bf16[8,304,128]{2,1,0:T(8,128)(2,1)S(1)} collective-permute-done((bf16[8,304,128]{2,1,0:T(8,128)(2,1)}, bf16[8,304,128]{2,1,0:T(8,128)(2,1)S(1)}, u32[]{:S(2)}, u32[]{:S(2)}) %collective-permute-start.11) | collective-permute-done | bytes 622624 | tf_op jit(solution)/shard_map/ppermute | solution.py:202
  133.1 23.9 %all_to_all.30 = bf16[8,304,128]{2,1,0:T(8,128)(2,1)S(1)} all-to-all(bf16[8,304,128]{2,1,0:T(8,128)(2,1)S(1)} %fusion.2), channel_id=1, replica_groups=mesh['y'=8,'zl'=2,'c'=2,'zh'=4,'x'=4] {'y'}, dimensions={0} | all-to-all | bytes 1245184 | tf_op jit(solution)/shard_map/all_to_all | solution.py:273
  157.1 0.9 broadcast_in_dim.9
  158.0 3.5 %all-to-all-start.3 = ((bf16[8,304,128]{2,1,0:T(8,128)(2,1)}), bf16[8,304,128]{2,1,0:T(8,128)(2,1)S(1)}, u32[]{:S(2)}, u32[]{:S(2)}) async-start(bf16[8,304,128]{2,1,0:T(8,128)(2,1)} %broadcast_in_dim.9), calls=%async_computation.3 | async-start | bytes 1245184 | tf_op jit(solution)/shard_map/all_to_all | solution.py:207
  161.6 2.4 %collective-permute-start.12 = (bf16[2,144,128]{2,1,0:T(8,128)(2,1)S(1)}, bf16[2,144,128]{2,1,0:T(8,128)(2,1)S(1)}, u32[]{:S(2)}, u32[]{:S(2)}) collective-permute-start(bf16[2,144,128]{2,1,0:T(8,128)(2,1)S(1)} %reduce_sum.34), channel_id=1, source_target_pairs={{0,32},{32,0},{1,33},{33,1},{2,34},{34,2},{3,35},{35,3},{4,36},{36... | collective-permute-start | bytes 221192 | tf_op jit(solution)/shard_map/ppermute | solution.py:202
  164.0 2.7 %collective-permute-done.12 = bf16[2,144,128]{2,1,0:T(8,128)(2,1)S(1)} collective-permute-done((bf16[2,144,128]{2,1,0:T(8,128)(2,1)S(1)}, bf16[2,144,128]{2,1,0:T(8,128)(2,1)S(1)}, u32[]{:S(2)}, u32[]{:S(2)}) %collective-permute-start.12) | collective-permute-done | bytes 73760 | tf_op jit(solution)/shard_map/ppermute | solution.py:202
  166.7 11.9 %all-to-all-done.3.refs_0_ = bf16[8,304,128]{2,1,0:T(8,128)(2,1)S(1)} async-done(((bf16[8,304,128]{2,1,0:T(8,128)(2,1)}), bf16[8,304,128]{2,1,0:T(8,128)(2,1)S(1)}, u32[]{:S(2)}, u32[]{:S(2)}) %all-to-all-start.3) | async-done | bytes 622624 | tf_op jit(solution)/shard_map/all_to_all | solution.py:207
  178.7 1.1 broadcast_in_dim.10
  179.8 3.5 %all-to-all-start.4 = ((bf16[8,2,144,128]{3,2,1,0:T(8,128)(2,1)}), bf16[8,2,144,128]{3,2,1,0:T(8,128)(2,1)S(1)}, u32[]{:S(2)}, u32[]{:S(2)}) async-start(bf16[8,2,144,128]{3,2,1,0:T(8,128)(2,1)} %broadcast_in_dim.10), calls=%async_computation.4 | async-start | bytes 1179648 | tf_op jit(solution)/shard_map/all_to_all | solution.py:207
  183.3 2.3 collective-permute-start.13
  185.6 5.7 %collective-permute-start.14 = (bf16[8,304,128]{2,1,0:T(8,128)(2,1)S(1)}, bf16[8,304,128]{2,1,0:T(8,128)(2,1)S(1)}, u32[]{:S(2)}, u32[]{:S(2)}) collective-permute-start(bf16[8,304,128]{2,1,0:T(8,128)(2,1)S(1)} %all-to-all-done.3.refs_0_), channel_id=1, source_target_pairs={{0,16},{16,0},{1,17},{17,1},{2,18},{18,2},{3,19},{19,3},{4,20},{20... | collective-permute-start | bytes 1867784 | tf_op jit(solution)/shard_map/ppermute | solution.py:202
  191.3 6.0 %collective-permute-done.13.refs_1_ = bf16[8,304,128]{2,1,0:T(8,128)(2,1)S(1)} collective-permute-done((bf16[8,304,128]{2,1,0:T(8,128)(2,1)S(1)}, bf16[8,304,128]{2,1,0:T(8,128)(2,1)S(1)}, u32[]{:S(2)}, u32[]{:S(2)}) %collective-permute-start.13) | collective-permute-done | bytes 622624 | tf_op jit(solution)/shard_map/ppermute | solution.py:202
  197.4 6.2 %collective-permute-start.15 = (bf16[8,304,128]{2,1,0:T(8,128)(2,1)S(1)}, bf16[8,304,128]{2,1,0:T(8,128)(2,1)S(1)}, u32[]{:S(2)}, u32[]{:S(2)}) collective-permute-start(bf16[8,304,128]{2,1,0:T(8,128)(2,1)S(1)} %collective-permute-done.13.refs_1_), channel_id=1, source_target_pairs={{0,16},{16,0},{1,17},{17,1},{2,18},{18,2},{3,19},{19,3},{4,20},{20... | collective-permute-start | bytes 1867784 | tf_op jit(solution)/shard_map/ppermute | solution.py:202
  203.6 1.9 collective-permute-start.16
  205.5 1.9 collective-permute-done.16.refs_5_
  207.5 0.8 copy-done.9
  208.3 6.5 %shard_map.69 = f32[2,448]{1,0:T(2,128)} custom-call(s32[3]{0:T(128)} %pad_add_fusion.refs_0_.me, bf16[16,512,256]{2,1,0:T(8,128)(2,1)} %get-tuple-element.40.source, f32[448,512]{1,0:T(8,128)} %get-tuple-element.44.bend_in, f32[448,512]{1,0:T(8,128)} %shard_map.68.own_in, bf16[8,304,128]{2,1,0:T(8,128)(2,1)} %copy-done.1, bf16[8,304,128]{2,1,0:T(8,128)(2,1)} %copy-done.6, ...), custom_call_target="tpu_custom_call" | custom-call | flops 1879048192 | bytes 9702924 | tf_op jit(solution)/shard_map/pallas_call | solution.py:27
  214.8 1.4 broadcast_in_dim.11
  216.2 7.3 %all-to-all-start.5 = ((f32[32,2,448]{2,1,0:T(2,128)}), f32[32,2,448]{2,1,0:T(2,128)S(1)}, u32[]{:S(2)}, u32[]{:S(2)}) async-start(f32[32,2,448]{2,1,0:T(2,128)} %broadcast_in_dim.11), calls=%async_computation.5 | async-start | bytes 262144 | tf_op jit(solution)/shard_map/all_to_all | solution.py:207
  223.4 0.7 maximum_bitcast_fusion
  224.1 8.6 %all-to-all-done.5 = f32[32,2,448]{2,1,0:T(2,128)S(1)} async-done(((f32[32,2,448]{2,1,0:T(2,128)}), f32[32,2,448]{2,1,0:T(2,128)S(1)}, u32[]{:S(2)}, u32[]{:S(2)}) %all-to-all-start.5) | async-done | bytes 114720 | tf_op jit(solution)/shard_map/all_to_all | solution.py:207
  232.7 0.6 slice_multiply_fusion
  (53 shorter events, 0.7 us)
Async XLA Ops:
  2.6 11.0 %copy-start.10 = (bf16[128,448]{0,1:T(8,128)(2,1)S(1)}, bf16[128,448]{0,1:T(8,128)(2,1)}, u32[]{:S(2)}) copy-start(bf16[128,448]{0,1:T(8,128)(2,1)} %param.5) | copy-start | bytes 344068
  2.6 34.3 %all-to-all-start = ((bf16[4,512,256]{2,1,0:T(8,128)(2,1)}), bf16[4,512,256]{2,1,0:T(8,128)(2,1)S(1)}, u32[]{:S(2)}, u32[]{:S(2)}) async-start(bf16[4,512,256]{2,1,0:T(8,128)(2,1)} %broadcast_in_dim.8), calls=%async_computation | async-start | bytes 2097152 | tf_op jit(solution)/shard_map/all_to_all | solution.py:207
  36.9 49.2 %copy-start.5 = (bf16[3584,128]{1,0:T(8,128)(2,1)}, bf16[3584,128]{1,0:T(8,128)(2,1)S(1)}, u32[]{:S(2)}) copy-start(bf16[3584,128]{1,0:T(8,128)(2,1)S(1)} %all-gather) | copy-start | bytes 2752516
  36.9 49.2 %copy-start = (bf16[4,512,256]{2,1,0:T(8,128)(2,1)}, bf16[4,512,256]{2,1,0:T(8,128)(2,1)S(1)}, u32[]{:S(2)}) copy-start(bf16[4,512,256]{2,1,0:T(8,128)(2,1)S(1)} %all-to-all-done.refs_1_) | copy-start | bytes 3145732
  37.0 20.0 %collective-permute-start.3 = (bf16[2,512,256]{2,1,0:T(8,128)(2,1)S(1)}, bf16[2,512,256]{2,1,0:T(8,128)(2,1)S(1)}, u32[]{:S(2)}, u32[]{:S(2)}) collective-permute-start(bf16[2,512,256]{2,1,0:T(8,128)(2,1)S(1)} %get-tuple-element.47), channel_id=1, source_target_pairs={{0,3},{1,0},{2,1},{3,2},{4,7},{5,4},{6,5},{7,6},{8,11},{9,8},{10,9... | collective-permute-start | bytes 1572872 | tf_op jit(solution)/shard_map/ppermute | solution.py:221
  41.4 19.0 %collective-permute-start = (bf16[2,512,256]{2,1,0:T(8,128)(2,1)S(1)}, bf16[2,512,256]{2,1,0:T(8,128)(2,1)S(1)}, u32[]{:S(2)}, u32[]{:S(2)}) collective-permute-start(bf16[2,512,256]{2,1,0:T(8,128)(2,1)S(1)} %get-tuple-element.48), channel_id=1, source_target_pairs={{0,1},{1,2},{2,3},{3,0},{4,5},{5,6},{6,7},{7,4},{8,9},{9,10},{10,1... | collective-permute-start | bytes 1572872 | tf_op jit(solution)/shard_map/ppermute | solution.py:221
  43.3 32.1 %collective-permute-start.4 = (bf16[8,448,128]{2,1,0:T(8,128)(2,1)S(1)}, bf16[8,448,128]{2,1,0:T(8,128)(2,1)S(1)}, u32[]{:S(2)}, u32[]{:S(2)}) collective-permute-start(bf16[8,448,128]{2,1,0:T(8,128)(2,1)S(1)} %bitcast.19), channel_id=1, source_target_pairs={{0,32},{32,0},{1,33},{33,1},{2,34},{34,2},{3,35},{35,3},{4,36},{36... | collective-permute-start | bytes 2752520 | tf_op jit(solution)/shard_map/ppermute | solution.py:202
  50.5 17.1 %collective-permute-start.1 = (bf16[2,512,256]{2,1,0:T(8,128)(2,1)S(1)}, bf16[2,512,256]{2,1,0:T(8,128)(2,1)S(1)}, u32[]{:S(2)}, u32[]{:S(2)}) collective-permute-start(bf16[2,512,256]{2,1,0:T(8,128)(2,1)S(1)} %get-tuple-element.47), channel_id=1, source_target_pairs={{0,1},{1,2},{2,3},{3,0},{4,5},{5,6},{6,7},{7,4},{8,9},{9,10},{10,1... | collective-permute-start | bytes 1572872 | tf_op jit(solution)/shard_map/ppermute | solution.py:221
  52.6 15.0 %collective-permute-start.2 = (bf16[2,512,256]{2,1,0:T(8,128)(2,1)S(1)}, bf16[2,512,256]{2,1,0:T(8,128)(2,1)S(1)}, u32[]{:S(2)}, u32[]{:S(2)}) collective-permute-start(bf16[2,512,256]{2,1,0:T(8,128)(2,1)S(1)} %get-tuple-element.48), channel_id=1, source_target_pairs={{0,3},{1,0},{2,1},{3,2},{4,7},{5,4},{6,5},{7,6},{8,11},{9,8},{10,9... | collective-permute-start | bytes 1572872 | tf_op jit(solution)/shard_map/ppermute | solution.py:221
  57.0 29.1 %copy-start.12 = (bf16[2,512,256]{2,1,0:T(8,128)(2,1)}, bf16[2,512,256]{2,1,0:T(8,128)(2,1)S(1)}, u32[]{:S(2)}) copy-start(bf16[2,512,256]{2,1,0:T(8,128)(2,1)S(1)} %collective-permute-done.3.refs_4_) | copy-start | bytes 1572868
  57.0 20.1 %collective-permute-start.6 = (bf16[2,512,256]{2,1,0:T(8,128)(2,1)S(1)}, bf16[2,512,256]{2,1,0:T(8,128)(2,1)S(1)}, u32[]{:S(2)}, u32[]{:S(2)}) collective-permute-start(bf16[2,512,256]{2,1,0:T(8,128)(2,1)S(1)} %collective-permute-done.3.refs_4_), channel_id=1, source_target_pairs={{0,3},{1,0},{2,1},{3,2},{4,7},{5,4},{6,5},{7,6},{8,11},{9,8},{10,9... | collective-permute-start | bytes 1572872 | tf_op jit(solution)/shard_map/ppermute | solution.py:221
  60.4 16.7 %copy-start.13 = (bf16[2,512,256]{2,1,0:T(8,128)(2,1)}, bf16[2,512,256]{2,1,0:T(8,128)(2,1)S(1)}, u32[]{:S(2)}) copy-start(bf16[2,512,256]{2,1,0:T(8,128)(2,1)S(1)} %collective-permute-done.refs_2_) | copy-start | bytes 1572868
  60.4 18.4 %collective-permute-start.5 = (bf16[2,512,256]{2,1,0:T(8,128)(2,1)S(1)}, bf16[2,512,256]{2,1,0:T(8,128)(2,1)S(1)}, u32[]{:S(2)}, u32[]{:S(2)}) collective-permute-start(bf16[2,512,256]{2,1,0:T(8,128)(2,1)S(1)} %collective-permute-done.refs_2_), channel_id=1, source_target_pairs={{0,1},{1,2},{2,3},{3,0},{4,5},{5,6},{6,7},{7,4},{8,9},{9,10},{10,1... | collective-permute-start | bytes 1572872 | tf_op jit(solution)/shard_map/ppermute | solution.py:221
  67.6 11.2 %copy-start.14 = (bf16[2,512,256]{2,1,0:T(8,128)(2,1)}, bf16[2,512,256]{2,1,0:T(8,128)(2,1)S(1)}, u32[]{:S(2)}) copy-start(bf16[2,512,256]{2,1,0:T(8,128)(2,1)S(1)} %collective-permute-done.1.refs_3_) | copy-start | bytes 1572868
  67.6 16.3 %copy-start.15 = (bf16[2,512,256]{2,1,0:T(8,128)(2,1)}, bf16[2,512,256]{2,1,0:T(8,128)(2,1)S(1)}, u32[]{:S(2)}) copy-start(bf16[2,512,256]{2,1,0:T(8,128)(2,1)S(1)} %collective-permute-done.2.refs_5_) | copy-start | bytes 1572868
  67.6 16.9 %collective-permute-start.7 = (bf16[8,448,128]{2,1,0:T(8,128)(2,1)S(1)}, bf16[8,448,128]{2,1,0:T(8,128)(2,1)}, u32[]{:S(2)}, u32[]{:S(2)}) collective-permute-start(bf16[8,448,128]{2,1,0:T(8,128)(2,1)S(1)} %bitcast.20), channel_id=1, source_target_pairs={{0,16},{16,0},{1,17},{17,1},{2,18},{18,2},{3,19},{19,3},{4,20},{20... | collective-permute-start | bytes 2752520 | tf_op jit(solution)/shard_map/ppermute | solution.py:202
  75.5 10.7 %copy-start.11 = (bf16[8,448,128]{2,1,0:T(8,128)(2,1)}, bf16[8,448,128]{2,1,0:T(8,128)(2,1)S(1)}, u32[]{:S(2)}) copy-start(bf16[8,448,128]{2,1,0:T(8,128)(2,1)S(1)} %collective-permute-done.4.refs_11_) | copy-start | bytes 2752516
  77.1 6.8 %copy-start.16 = (bf16[2,512,256]{2,1,0:T(8,128)(2,1)}, bf16[2,512,256]{2,1,0:T(8,128)(2,1)S(1)}, u32[]{:S(2)}) copy-start(bf16[2,512,256]{2,1,0:T(8,128)(2,1)S(1)} %collective-permute-done.6.refs_7_) | copy-start | bytes 1572868
  78.9 5.1 %copy-start.17 = (bf16[2,512,256]{2,1,0:T(8,128)(2,1)}, bf16[2,512,256]{2,1,0:T(8,128)(2,1)S(1)}, u32[]{:S(2)}) copy-start(bf16[2,512,256]{2,1,0:T(8,128)(2,1)S(1)} %collective-permute-done.5.refs_6_) | copy-start | bytes 1572868
  78.9 7.3 %collective-permute-start.8 = (bf16[8,448,128]{2,1,0:T(8,128)(2,1)S(1)}, bf16[8,448,128]{2,1,0:T(8,128)(2,1)}, u32[]{:S(2)}, u32[]{:S(2)}) collective-permute-start(bf16[8,448,128]{2,1,0:T(8,128)(2,1)S(1)} %collective-permute-done.4.refs_11_), channel_id=1, source_target_pairs={{0,16},{16,0},{1,17},{17,1},{2,18},{18,2},{3,19},{19,3},{4,20},{20... | collective-permute-start | bytes 2752520 | tf_op jit(solution)/shard_map/ppermute | solution.py:202
  95.7 8.6 %collective-permute-start.10 = (bf16[2,8,304,128]{3,2,1,0:T(8,128)(2,1)}, bf16[2,8,304,128]{3,2,1,0:T(8,128)(2,1)S(1)}, u32[]{:S(2)}, u32[]{:S(2)}) collective-permute-start(bf16[2,8,304,128]{3,2,1,0:T(8,128)(2,1)} %get-tuple-element.36.sent), channel_id=1, source_target_pairs={{0,16},{16,0},{1,17},{17,1},{2,18},{18,2},{3,19},{19,3},{4,20},{20... | collective-permute-start | bytes 3735560 | tf_op jit(solution)/shard_map/ppermute | solution.py:202
  98.0 4.1 %collective-permute-start.9 = (bf16[8,2,144,128]{3,2,1,0:T(8,128)(2,1)}, bf16[8,2,144,128]{3,2,1,0:T(8,128)(2,1)S(1)}, u32[]{:S(2)}, u32[]{:S(2)}) collective-permute-start(bf16[8,2,144,128]{3,2,1,0:T(8,128)(2,1)} %get-tuple-element.35.b1), channel_id=1, source_target_pairs={{0,16},{16,0},{1,17},{17,1},{2,18},{18,2},{3,19},{19,3},{4,20},{20... | collective-permute-start | bytes 1769480 | tf_op jit(solution)/shard_map/ppermute | solution.py:202
  102.1 7.5 %copy-start.3 = (bf16[8,304,128]{2,1,0:T(8,128)(2,1)S(1)}, bf16[8,304,128]{2,1,0:T(8,128)(2,1)}, u32[]{:S(2)}) copy-start(bf16[8,304,128]{2,1,0:T(8,128)(2,1)} %get-tuple-element.38.a1) | copy-start | bytes 1867780
  104.3 28.8 %all-to-all-start.1 = ((bf16[8,2,144,128]{3,2,1,0:T(8,128)(2,1)}), bf16[8,2,144,128]{3,2,1,0:T(8,128)(2,1)S(1)}, u32[]{:S(2)}, u32[]{:S(2)}) async-start(bf16[8,2,144,128]{3,2,1,0:T(8,128)(2,1)} %add_convert_fusion), calls=%async_computation.1 | async-start | bytes 1179648 | tf_op jit(solution)/shard_map/all_to_all | solution.py:261
  110.7 22.2 %collective-permute-start.11 = (bf16[8,304,128]{2,1,0:T(8,128)(2,1)}, bf16[8,304,128]{2,1,0:T(8,128)(2,1)S(1)}, u32[]{:S(2)}, u32[]{:S(2)}) collective-permute-start(bf16[8,304,128]{2,1,0:T(8,128)(2,1)} %fusion), channel_id=1, source_target_pairs={{0,32},{32,0},{1,33},{33,1},{2,34},{34,2},{3,35},{35,3},{4,36},{36... | collective-permute-start | bytes 1867784 | tf_op jit(solution)/shard_map/ppermute | solution.py:202
  118.6 14.2 %copy-start.2 = (bf16[8,304,128]{2,1,0:T(8,128)(2,1)S(1)}, bf16[8,304,128]{2,1,0:T(8,128)(2,1)}, u32[]{:S(2)}) copy-start(bf16[8,304,128]{2,1,0:T(8,128)(2,1)} %get-tuple-element.33.a0) | copy-start | bytes 1867780
  158.0 20.7 %all-to-all-start.3 = ((bf16[8,304,128]{2,1,0:T(8,128)(2,1)}), bf16[8,304,128]{2,1,0:T(8,128)(2,1)S(1)}, u32[]{:S(2)}, u32[]{:S(2)}) async-start(bf16[8,304,128]{2,1,0:T(8,128)(2,1)} %broadcast_in_dim.9), calls=%async_computation.3 | async-start | bytes 1245184 | tf_op jit(solution)/shard_map/all_to_all | solution.py:207
  161.6 5.1 %collective-permute-start.12 = (bf16[2,144,128]{2,1,0:T(8,128)(2,1)S(1)}, bf16[2,144,128]{2,1,0:T(8,128)(2,1)S(1)}, u32[]{:S(2)}, u32[]{:S(2)}) collective-permute-start(bf16[2,144,128]{2,1,0:T(8,128)(2,1)S(1)} %reduce_sum.34), channel_id=1, source_target_pairs={{0,32},{32,0},{1,33},{33,1},{2,34},{34,2},{3,35},{35,3},{4,36},{36... | collective-permute-start | bytes 221192 | tf_op jit(solution)/shard_map/ppermute | solution.py:202
  178.7 29.6 %copy-start.1 = (bf16[8,304,128]{2,1,0:T(8,128)(2,1)}, bf16[8,304,128]{2,1,0:T(8,128)(2,1)S(1)}, u32[]{:S(2)}) copy-start(bf16[8,304,128]{2,1,0:T(8,128)(2,1)S(1)} %all-to-all-done.3.refs_0_) | copy-start | bytes 1867780
  179.8 23.8 %all-to-all-start.4 = ((bf16[8,2,144,128]{3,2,1,0:T(8,128)(2,1)}), bf16[8,2,144,128]{3,2,1,0:T(8,128)(2,1)S(1)}, u32[]{:S(2)}, u32[]{:S(2)}) async-start(bf16[8,2,144,128]{3,2,1,0:T(8,128)(2,1)} %broadcast_in_dim.10), calls=%async_computation.4 | async-start | bytes 1179648 | tf_op jit(solution)/shard_map/all_to_all | solution.py:207
  183.3 14.0 %collective-permute-start.13 = (bf16[8,304,128]{2,1,0:T(8,128)(2,1)S(1)}, bf16[8,304,128]{2,1,0:T(8,128)(2,1)S(1)}, u32[]{:S(2)}, u32[]{:S(2)}) collective-permute-start(bf16[8,304,128]{2,1,0:T(8,128)(2,1)S(1)} %all-to-all-done.3.refs_0_), channel_id=1, source_target_pairs={{0,32},{32,0},{1,33},{33,1},{2,34},{34,2},{3,35},{35,3},{4,36},{36... | collective-permute-start | bytes 1867784 | tf_op jit(solution)/shard_map/ppermute | solution.py:202
  185.6 19.9 %collective-permute-start.14 = (bf16[8,304,128]{2,1,0:T(8,128)(2,1)S(1)}, bf16[8,304,128]{2,1,0:T(8,128)(2,1)S(1)}, u32[]{:S(2)}, u32[]{:S(2)}) collective-permute-start(bf16[8,304,128]{2,1,0:T(8,128)(2,1)S(1)} %all-to-all-done.3.refs_0_), channel_id=1, source_target_pairs={{0,16},{16,0},{1,17},{17,1},{2,18},{18,2},{3,19},{19,3},{4,20},{20... | collective-permute-start | bytes 1867784 | tf_op jit(solution)/shard_map/ppermute | solution.py:202
  197.3 10.9 %copy-start.6 = (bf16[8,304,128]{2,1,0:T(8,128)(2,1)}, bf16[8,304,128]{2,1,0:T(8,128)(2,1)S(1)}, u32[]{:S(2)}) copy-start(bf16[8,304,128]{2,1,0:T(8,128)(2,1)S(1)} %collective-permute-done.13.refs_1_) | copy-start | bytes 1867780
  197.4 8.2 %collective-permute-start.15 = (bf16[8,304,128]{2,1,0:T(8,128)(2,1)S(1)}, bf16[8,304,128]{2,1,0:T(8,128)(2,1)S(1)}, u32[]{:S(2)}, u32[]{:S(2)}) collective-permute-start(bf16[8,304,128]{2,1,0:T(8,128)(2,1)S(1)} %collective-permute-done.13.refs_1_), channel_id=1, source_target_pairs={{0,16},{16,0},{1,17},{17,1},{2,18},{18,2},{3,19},{19,3},{4,20},{20... | collective-permute-start | bytes 1867784 | tf_op jit(solution)/shard_map/ppermute | solution.py:202
  203.6 4.7 %copy-start.4 = (bf16[8,2,144,128]{3,2,1,0:T(8,128)(2,1)}, bf16[8,2,144,128]{3,2,1,0:T(8,128)(2,1)S(1)}, u32[]{:S(2)}) copy-start(bf16[8,2,144,128]{3,2,1,0:T(8,128)(2,1)S(1)} %all-to-all-done.4.refs_4_) | copy-start | bytes 1769476
  203.6 3.9 %collective-permute-start.16 = (bf16[8,2,144,128]{3,2,1,0:T(8,128)(2,1)S(1)}, bf16[8,2,144,128]{3,2,1,0:T(8,128)(2,1)S(1)}, u32[]{:S(2)}, u32[]{:S(2)}) collective-permute-start(bf16[8,2,144,128]{3,2,1,0:T(8,128)(2,1)S(1)} %all-to-all-done.4.refs_4_), channel_id=1, source_target_pairs={{0,16},{16,0},{1,17},{17,1},{2,18},{18,2},{3,19},{19,3},{4,20},{20... | collective-permute-start | bytes 1769480 | tf_op jit(solution)/shard_map/ppermute | solution.py:202
  205.5 2.8 %copy-start.7 = (bf16[8,304,128]{2,1,0:T(8,128)(2,1)}, bf16[8,304,128]{2,1,0:T(8,128)(2,1)S(1)}, u32[]{:S(2)}) copy-start(bf16[8,304,128]{2,1,0:T(8,128)(2,1)S(1)} %collective-permute-done.14.refs_2_) | copy-start | bytes 1867780
  205.5 2.8 %copy-start.8 = (bf16[8,304,128]{2,1,0:T(8,128)(2,1)}, bf16[8,304,128]{2,1,0:T(8,128)(2,1)S(1)}, u32[]{:S(2)}) copy-start(bf16[8,304,128]{2,1,0:T(8,128)(2,1)S(1)} %collective-permute-done.15.refs_3_) | copy-start | bytes 1867780
  207.5 0.8 copy-start.9
  216.2 16.5 %all-to-all-start.5 = ((f32[32,2,448]{2,1,0:T(2,128)}), f32[32,2,448]{2,1,0:T(2,128)S(1)}, u32[]{:S(2)}, u32[]{:S(2)}) async-start(f32[32,2,448]{2,1,0:T(2,128)} %broadcast_in_dim.11), calls=%async_computation.5 | async-start | bytes 262144 | tf_op jit(solution)/shard_map/all_to_all | solution.py:207

commit v7 on v6

--- a/solution.py
+++ b/solution.py
@@ -70,9 +70,9 @@
 
 
 def first_kernel(*refs):
-    me, t0, p1, p2, m1, m2, f1, f2, up_in, cot_in, w0, w1, w2, w3 = refs[:14]
-    tok_out, bend_out, *outs = refs[14:21]
-    tok, held, up, cot, coeff, bend, acc, own, own_b, tok_sems, w_sems, in_sems, out_sems, sems = refs[21:]
+    me, t0, p1, p2, m1, m2, f1, f2, up_in, cot_in, w0, w1, *other = refs[:16]
+    tok_out, bend_out, *outs = refs[16:23]
+    tok, held, up, cot, coeff, bend, acc, own, own_b, tok_sems, w_sems, in_sems, out_sems, sems = refs[23:]
     mine, first = me[0], me[1] == 0
     sources = ((t0.at[0:2], t0.at[2:4]), (m2, m1), (f1, f2), (p1, p2))
 
@@ -83,7 +83,17 @@
     for z in range(4):
         for d in range(4):
             token_copy(d, z).start()
-    w_ready = fetched([(w, held.at[i]) for i, w in enumerate((w0, w1, w2, w3))], w_sems)
+    def row_copies(half):
+        at = pl.ds(4 * half, 4)
+        own_rows = (w0.at[at], w1.at[at], other[half], other[2 + half])
+        return [
+            pltpu.make_async_copy(w, held.at[i, at], w_sems.at[i, half])
+            for i, w in enumerate(own_rows)
+        ]
+
+    for half in (0, 1):
+        for copy in row_copies(half):
+            copy.start()
     get_up = pltpu.make_async_copy(up_in, up, in_sems.at[0])
     get_cot = pltpu.make_async_copy(cot_in, cot, in_sems.at[1])
     get_up.start()
@@ -93,7 +103,8 @@
         for z in (2 * half, 2 * half + 1):
             for d in range(4):
                 token_copy(d, z).wait()
-        w_ready(half)
+        for copy in row_copies(half):
+            copy.wait()
 
     project(
         me, tok, lambda y, rel: (held[rel, y], held[2 + rel, y]), acc, ready
@@ -194,8 +205,12 @@
         off = own[:, lanes] - mean
         c += b * mean * mean
         s += b * off * off
-    sums[0:1, :] = jnp.sum(c.T, axis=0, keepdims=True)
-    sums[1:2, :] = jnp.sum(s.T, axis=0, keepdims=True)
+    for k, terms in enumerate((c, s)):
+        line = jnp.sum(terms.T, axis=0, keepdims=True)
+        line = jnp.concatenate([line, jnp.zeros((1, 64), F32)], 1)
+        for i in range(4):
+            row = line[:, 128 * i : 128 * i + 128]
+            sums[:, 4 * k + i : 4 * k + i + 1, :] = jnp.broadcast_to(row[None], (32, 1, 128))
 
 
 def swap(value, axis):
@@ -233,9 +248,8 @@
     p1, m1 = along_x(low, 1), along_x(high, -1)
     p2, m2 = along_x(high, 1), along_x(low, -1)
     f1, f2 = along_x(p1, 1), along_x(m1, -1)
-    w1, f1, f2 = lax.optimization_barrier((swap(w0, "zl"), f1, f2))
-    w0, p2, m2 = lax.optimization_barrier((w0, p2, m2))
-    w2, w3 = swap(w0, "c"), swap(w1, "c")
+    w0, w1, p2, m2 = lax.optimization_barrier((w0, swap(w0, "zl"), p2, m2))
+    other = [swap(w[at : at + 4], "c") for w in (w0, w1) for at in (0, 4)]
     tok, bend, a0, a1, sent, b0, sent_b = call(
         first_kernel,
         [
@@ -245,7 +259,7 @@
             shape(2, 8, CUT, 128),
             *[shape(8, 2, rest, 128)] * 2,
         ],
-        (me, t0, p1, p2, m1, m2, f1, f2, up_act.T, cotangent.T, w0, w1, w2, w3),
+        (me, t0, p1, p2, m1, m2, f1, f2, up_act.T, cotangent.T, w0, w1, *other),
         2 * flops,
         [
             TOK,
@@ -281,13 +295,13 @@
     rows = (u0, u1, swap(u0, "c"), swap(u1, "c"), v0, swap(v0, "c"))
     line = call(
         mean_kernel,
-        [shape(2, 448, dtype=F32)],
+        [shape(32, 8, 128, dtype=F32)],
         (me, tok, bend, own, *rows),
         flops,
         [*[ACC] * 3, TOK, *held, *map(dma, ((1, 2), (6, 2), (2,)))],
         True,
     )[0]
-    whole = jnp.sum(to_all(line, REP), axis=0)
+    whole = jnp.sum(lax.all_to_all(line, REP, 0, 0, tiled=True), axis=0).reshape(2, 512)[:, :448]
     grad = jnp.concatenate([grad_a, both_b[0]], axis=0).T
     return grad, whole[0], whole[1] / 31
 

time: 234 us -> 234 us (level)
    all_to_all x4 -> x3, waiting for transfers between devices: 20.5 us -> 11.8 us  [to_all(): lax.all_to_all(jnp.broadcast_to(value[None], (count, *value.shape)), axis...]
    all_to_all x0 -> x1, waiting for transfers between devices: none -> 8.59 us  [shards(): lax.all_to_all(line, REP, 0, 0, tiled=True)]
    all_to_all x0 -> x1, starting transfers between devices: none -> 7.66 us  [shards(): lax.all_to_all(line, REP, 0, 0, tiled=True)]
    all_to_all x4 -> x3, starting transfers between devices: 25.3 us -> 18.1 us  [to_all(): lax.all_to_all(jnp.broadcast_to(value[None], (count, *value.shape)), axis...]
    ppermute x11 -> x13, starting transfers between devices: 50.8 us -> 46.4 us  [swap(): return lax.ppermute(value, axis, ((0, 1), (1, 0)))]
    broadcast_in_dim x4 -> x3, local copies, waits for them, and re-layouts: 5.36 us -> 3.94 us  [to_all(): jnp.broadcast_to(value[None], (count, *value.shape))]
    ppermute x11 -> x13, waiting for transfers between devices: 21.9 us -> 21.4 us  [swap(): return lax.ppermute(value, axis, ((0, 1), (1, 0)))]
  transfers between devices with their start and end apart: 22 -> 24, of which waited for: 11 -> 11; matrix products, arithmetic and copies ran while one was open for 2% -> 3% of each run, Pallas kernels for 3% -> 3%
where the time goes in v7:
time: 234 us; the launch traced here: 233 us
  starting transfers between devices  98.9 us (42%)
  waiting for transfers between devices  52.8 us (23%)
  blocking collectives  45.2 us (19%)
  Pallas kernels  22.7 us (10%)
  local copies, waits for them, and re-layouts  6.69 us (3%)
  other arithmetic  5.52 us (2%)
    ppermute x13, starting transfers between devices, swap(): return lax.ppermute(value, axis, ((0, 1), (1, 0)))  46.4 us
    all_gather x1, blocking collectives, shards(): w0 = lax.all_gather(gate_weight.T, 'y', axis=0)  23.3 us
    pallas_call x3, Pallas kernels, call(): pl.pallas_call(kernel, out_shape=outs, in_specs=[SM] + [ANY] * (len(opera...  22.7 us
    all_to_all x1, blocking collectives, shards(): across_a = lax.all_to_all(sums_a, 'y', 0, 0, tiled=True)  21.8 us
    ppermute x13, waiting for transfers between devices, swap(): return lax.ppermute(value, axis, ((0, 1), (1, 0)))  21.4 us
    ppermute x6, starting transfers between devices, along_x(): return lax.ppermute(value, 'x', [(i, (i + by) % 4) for i in range(4)])  20 us
    all_to_all x3, starting transfers between devices, to_all(): lax.all_to_all(jnp.broadcast_to(value[None], (count, *value.shape)), axis...  18.1 us
    all_to_all x3, waiting for transfers between devices, to_all(): lax.all_to_all(jnp.broadcast_to(value[None], (count, *value.shape)), axis...  11.8 us
  transfers between devices with their start and end apart: 24, of which 11 were waited for; matrix products, arithmetic and copies ran while one was open for 3% of the time, Pallas kernels for 3%

profile of v7, /device:TPU:1, one launch (start us, length us, event | category | flops | bytes accessed | tf_op | source)
XLA Modules:
  0.0 232.8 jit_solution(325546994260231657)
XLA Ops:
  0.6 2.0 broadcast_in_dim.6
  2.6 11.0 %all-to-all-start = ((bf16[4,512,256]{2,1,0:T(8,128)(2,1)}), bf16[4,512,256]{2,1,0:T(8,128)(2,1)S(1)}, u32[]{:S(2)}, u32[]{:S(2)}) async-start(bf16[4,512,256]{2,1,0:T(8,128)(2,1)} %broadcast_in_dim.6), calls=%async_computation | async-start | bytes 2097152 | tf_op jit(solution)/shard_map/all_to_all | solution.py:222
  13.6 23.3 %all-gather = bf16[3584,128]{1,0:T(8,128)(2,1)S(1)} all-gather(bf16[448,128]{1,0:T(8,128)(2,1)S(1)} %bitcast.22), channel_id=2, replica_groups=mesh['y'=8,'zl'=2,'c'=2,'zh'=4,'x'=4] {'y'}, dimensions={0}, use_global_device_ids=true | all-gather | bytes 1032192 | tf_op jit(solution)/shard_map/all_gather | solution.py:245
  37.0 7.2 %collective-permute-start.1 = (bf16[8,448,128]{2,1,0:T(8,128)(2,1)S(1)}, bf16[8,448,128]{2,1,0:T(8,128)(2,1)S(1)}, u32[]{:S(2)}, u32[]{:S(2)}) collective-permute-start(bf16[8,448,128]{2,1,0:T(8,128)(2,1)S(1)} %bitcast.19), channel_id=1, source_target_pairs={{0,32},{32,0},{1,33},{33,1},{2,34},{34,2},{3,35},{35,3},{4,36},{36... | collective-permute-start | bytes 2752520 | tf_op jit(solution)/shard_map/ppermute | solution.py:217
  44.2 4.4 %collective-permute-start.4 = (bf16[2,512,256]{2,1,0:T(8,128)(2,1)S(1)}, bf16[2,512,256]{2,1,0:T(8,128)(2,1)S(1)}, u32[]{:S(2)}, u32[]{:S(2)}) collective-permute-start(bf16[2,512,256]{2,1,0:T(8,128)(2,1)S(1)} %get-tuple-element.43), channel_id=1, source_target_pairs={{0,3},{1,0},{2,1},{3,2},{4,7},{5,4},{6,5},{7,6},{8,11},{9,8},{10,9... | collective-permute-start | bytes 1572872 | tf_op jit(solution)/shard_map/ppermute | solution.py:236
  48.6 1.9 collective-permute-start
  50.5 2.1 collective-permute-start.2
  52.6 4.4 %collective-permute-start.3 = (bf16[2,512,256]{2,1,0:T(8,128)(2,1)S(1)}, bf16[2,512,256]{2,1,0:T(8,128)(2,1)S(1)}, u32[]{:S(2)}, u32[]{:S(2)}) collective-permute-start(bf16[2,512,256]{2,1,0:T(8,128)(2,1)S(1)} %get-tuple-element.44), channel_id=1, source_target_pairs={{0,3},{1,0},{2,1},{3,2},{4,7},{5,4},{6,5},{7,6},{8,11},{9,8},{10,9... | collective-permute-start | bytes 1572872 | tf_op jit(solution)/shard_map/ppermute | solution.py:236
  57.0 1.0 collective-permute-done.4.refs_4_
  58.0 5.3 %collective-permute-start.6 = (bf16[2,512,256]{2,1,0:T(8,128)(2,1)S(1)}, bf16[2,512,256]{2,1,0:T(8,128)(2,1)S(1)}, u32[]{:S(2)}, u32[]{:S(2)}) collective-permute-start(bf16[2,512,256]{2,1,0:T(8,128)(2,1)S(1)} %collective-permute-done.4.refs_4_), channel_id=1, source_target_pairs={{0,3},{1,0},{2,1},{3,2},{4,7},{5,4},{6,5},{7,6},{8,11},{9,8},{10,9... | collective-permute-start | bytes 1572872 | tf_op jit(solution)/shard_map/ppermute | solution.py:236
  63.3 1.9 collective-permute-start.5
  65.2 9.0 %collective-permute-done.2.refs_3_ = bf16[2,512,256]{2,1,0:T(8,128)(2,1)S(1)} collective-permute-done((bf16[2,512,256]{2,1,0:T(8,128)(2,1)S(1)}, bf16[2,512,256]{2,1,0:T(8,128)(2,1)S(1)}, u32[]{:S(2)}, u32[]{:S(2)}) %collective-permute-start.2) | collective-permute-done | bytes 524320 | tf_op jit(solution)/shard_map/ppermute | solution.py:236
  74.3 0.9 fusion.5
  75.2 7.5 %collective-permute-start.8 = (bf16[4,448,128]{2,1,0:T(8,128)(2,1)}, bf16[4,448,128]{2,1,0:T(8,128)(2,1)S(1)}, u32[]{:S(2)}, u32[]{:S(2)}) collective-permute-start(bf16[4,448,128]{2,1,0:T(8,128)(2,1)} %get-tuple-element.47), channel_id=1, source_target_pairs={{0,16},{16,0},{1,17},{17,1},{2,18},{18,2},{3,19},{19,3},{4,20},{20... | collective-permute-start | bytes 1376264 | tf_op jit(solution)/shard_map/ppermute | solution.py:217
  82.8 1.9 collective-permute-start.7
  84.8 2.4 %collective-permute-start.10 = (bf16[4,448,128]{2,1,0:T(8,128)(2,1)S(1)}, bf16[4,448,128]{2,1,0:T(8,128)(2,1)S(1)}, u32[]{:S(2)}, u32[]{:S(2)}) collective-permute-start(bf16[4,448,128]{2,1,0:T(8,128)(2,1)S(1)} %get-tuple-element.45), channel_id=1, source_target_pairs={{0,16},{16,0},{1,17},{17,1},{2,18},{18,2},{3,19},{19,3},{4,20},{20... | collective-permute-start | bytes 1376264 | tf_op jit(solution)/shard_map/ppermute | solution.py:217
  87.2 1.9 collective-permute-start.9
  89.8 1.1 collective-permute-done.9.refs_14_
  91.0 0.8 copy-done.19
  91.7 9.5 %shard_map.67 = (bf16[16,512,256]{2,1,0:T(8,128)(2,1)}, f32[448,512]{1,0:T(8,128)}, bf16[8,304,128]{2,1,0:T(8,128)(2,1)}, bf16[8,304,128]{2,1,0:T(8,128)(2,1)}, ...) custom-call(s32[3]{0:T(128)} %pad_add_fusion.refs_0_.me, ...), custom_call_target="tpu_custom_call" | custom-call | flops 3758096384 | bytes 17563660 | tf_op jit(solution)/shard_map/pallas_call | solution.py:27
  101.3 2.0 collective-permute-start.12
  103.3 2.3 collective-permute-start.11
  105.6 1.8 collective-permute-done.11
  107.5 2.2 add_convert_fusion
  109.6 6.7 %all-to-all-start.1 = ((bf16[8,2,144,128]{3,2,1,0:T(8,128)(2,1)}), bf16[8,2,144,128]{3,2,1,0:T(8,128)(2,1)S(1)}, u32[]{:S(2)}, u32[]{:S(2)}) async-start(bf16[8,2,144,128]{3,2,1,0:T(8,128)(2,1)} %add_convert_fusion), calls=%async_computation.1 | async-start | bytes 1179648 | tf_op jit(solution)/shard_map/all_to_all | solution.py:275
  116.3 1.1 fusion
  117.4 1.9 collective-permute-start.13
  119.3 6.6 %shard_map.68.own_in = f32[448,512]{1,0:T(8,128)} custom-call(s32[3]{0:T(128)} %pad_add_fusion.refs_0_.me, bf16[16,512,256]{2,1,0:T(8,128)(2,1)} %get-tuple-element.36.source, bf16[8,304,128]{2,1,0:T(8,128)(2,1)} %get-tuple-element.29.a0, bf16[8,304,128]{2,1,0:T(8,128)(2,1)} %get-tuple-element.34.a1, bf16[2,8,304,128]{3,2,1,0:T(8,128)(2,1)} %get-tuple-element.32.sent, ...), custom_call_target="tpu_custom_call" | custom-call | flops 1879048192 | bytes 8781836 | tf_op jit(solution)/shard_map/pallas_call | solution.py:27
  125.9 8.5 %collective-permute-done.13 = bf16[8,304,128]{2,1,0:T(8,128)(2,1)S(1)} collective-permute-done((bf16[8,304,128]{2,1,0:T(8,128)(2,1)}, bf16[8,304,128]{2,1,0:T(8,128)(2,1)S(1)}, u32[]{:S(2)}, u32[]{:S(2)}) %collective-permute-start.13) | collective-permute-done | bytes 622624 | tf_op jit(solution)/shard_map/ppermute | solution.py:217
  134.6 1.0 all-to-all-done.1
  135.7 21.8 %all_to_all.30 = bf16[8,304,128]{2,1,0:T(8,128)(2,1)S(1)} all-to-all(bf16[8,304,128]{2,1,0:T(8,128)(2,1)S(1)} %fusion.2), channel_id=1, replica_groups=mesh['y'=8,'zl'=2,'c'=2,'zh'=4,'x'=4] {'y'}, dimensions={0} | all-to-all | bytes 1245184 | tf_op jit(solution)/shard_map/all_to_all | solution.py:287
  157.6 0.9 broadcast_in_dim.7
  158.5 3.5 %all-to-all-start.3 = ((bf16[8,304,128]{2,1,0:T(8,128)(2,1)}), bf16[8,304,128]{2,1,0:T(8,128)(2,1)S(1)}, u32[]{:S(2)}, u32[]{:S(2)}) async-start(bf16[8,304,128]{2,1,0:T(8,128)(2,1)} %broadcast_in_dim.7), calls=%async_computation.3 | async-start | bytes 1245184 | tf_op jit(solution)/shard_map/all_to_all | solution.py:222
  162.2 2.6 %collective-permute-start.14 = (bf16[2,144,128]{2,1,0:T(8,128)(2,1)S(1)}, bf16[2,144,128]{2,1,0:T(8,128)(2,1)S(1)}, u32[]{:S(2)}, u32[]{:S(2)}) collective-permute-start(bf16[2,144,128]{2,1,0:T(8,128)(2,1)S(1)} %reduce_sum.34), channel_id=1, source_target_pairs={{0,32},{32,0},{1,33},{33,1},{2,34},{34,2},{3,35},{35,3},{4,36},{36... | collective-permute-start | bytes 221192 | tf_op jit(solution)/shard_map/ppermute | solution.py:217
  164.8 2.5 %collective-permute-done.14 = bf16[2,144,128]{2,1,0:T(8,128)(2,1)S(1)} collective-permute-done((bf16[2,144,128]{2,1,0:T(8,128)(2,1)S(1)}, bf16[2,144,128]{2,1,0:T(8,128)(2,1)S(1)}, u32[]{:S(2)}, u32[]{:S(2)}) %collective-permute-start.14) | collective-permute-done | bytes 73760 | tf_op jit(solution)/shard_map/ppermute | solution.py:217
  167.3 11.8 %all-to-all-done.3.refs_0_ = bf16[8,304,128]{2,1,0:T(8,128)(2,1)S(1)} async-done(((bf16[8,304,128]{2,1,0:T(8,128)(2,1)}), bf16[8,304,128]{2,1,0:T(8,128)(2,1)S(1)}, u32[]{:S(2)}, u32[]{:S(2)}) %all-to-all-start.3) | async-done | bytes 622624 | tf_op jit(solution)/shard_map/all_to_all | solution.py:222
  179.1 1.0 broadcast_in_dim.8
  180.1 3.5 %all-to-all-start.4 = ((bf16[8,2,144,128]{3,2,1,0:T(8,128)(2,1)}), bf16[8,2,144,128]{3,2,1,0:T(8,128)(2,1)S(1)}, u32[]{:S(2)}, u32[]{:S(2)}) async-start(bf16[8,2,144,128]{3,2,1,0:T(8,128)(2,1)} %broadcast_in_dim.8), calls=%async_computation.4 | async-start | bytes 1179648 | tf_op jit(solution)/shard_map/all_to_all | solution.py:222
  183.6 2.7 %collective-permute-start.15 = (bf16[8,304,128]{2,1,0:T(8,128)(2,1)S(1)}, bf16[8,304,128]{2,1,0:T(8,128)(2,1)S(1)}, u32[]{:S(2)}, u32[]{:S(2)}) collective-permute-start(bf16[8,304,128]{2,1,0:T(8,128)(2,1)S(1)} %all-to-all-done.3.refs_0_), channel_id=1, source_target_pairs={{0,32},{32,0},{1,33},{33,1},{2,34},{34,2},{3,35},{35,3},{4,36},{36... | collective-permute-start | bytes 1867784 | tf_op jit(solution)/shard_map/ppermute | solution.py:217
  186.3 5.7 %collective-permute-start.16 = (bf16[8,304,128]{2,1,0:T(8,128)(2,1)S(1)}, bf16[8,304,128]{2,1,0:T(8,128)(2,1)S(1)}, u32[]{:S(2)}, u32[]{:S(2)}) collective-permute-start(bf16[8,304,128]{2,1,0:T(8,128)(2,1)S(1)} %all-to-all-done.3.refs_0_), channel_id=1, source_target_pairs={{0,16},{16,0},{1,17},{17,1},{2,18},{18,2},{3,19},{19,3},{4,20},{20... | collective-permute-start | bytes 1867784 | tf_op jit(solution)/shard_map/ppermute | solution.py:217
  192.1 5.5 %collective-permute-done.15.refs_1_ = bf16[8,304,128]{2,1,0:T(8,128)(2,1)S(1)} collective-permute-done((bf16[8,304,128]{2,1,0:T(8,128)(2,1)S(1)}, bf16[8,304,128]{2,1,0:T(8,128)(2,1)S(1)}, u32[]{:S(2)}, u32[]{:S(2)}) %collective-permute-start.15) | collective-permute-done | bytes 622624 | tf_op jit(solution)/shard_map/ppermute | solution.py:217
  197.6 6.3 %collective-permute-start.17 = (bf16[8,304,128]{2,1,0:T(8,128)(2,1)S(1)}, bf16[8,304,128]{2,1,0:T(8,128)(2,1)S(1)}, u32[]{:S(2)}, u32[]{:S(2)}) collective-permute-start(bf16[8,304,128]{2,1,0:T(8,128)(2,1)S(1)} %collective-permute-done.15.refs_1_), channel_id=1, source_target_pairs={{0,16},{16,0},{1,17},{17,1},{2,18},{18,2},{3,19},{19,3},{4,20},{20... | collective-permute-start | bytes 1867784 | tf_op jit(solution)/shard_map/ppermute | solution.py:217
  203.9 1.9 collective-permute-start.18
  205.9 1.9 collective-permute-done.18.refs_5_
  207.8 0.8 copy-done.10
  208.6 6.5 %shard_map.69 = f32[32,8,128]{2,1,0:T(8,128)} custom-call(s32[3]{0:T(128)} %pad_add_fusion.refs_0_.me, bf16[16,512,256]{2,1,0:T(8,128)(2,1)} %get-tuple-element.36.source, f32[448,512]{1,0:T(8,128)} %get-tuple-element.40.bend_in, f32[448,512]{1,0:T(8,128)} %shard_map.68.own_in, bf16[8,304,128]{2,1,0:T(8,128)(2,1)} %copy-done.2, ...), custom_call_target="tpu_custom_call" | custom-call | flops 1879048192 | bytes 9830412 | tf_op jit(solution)/shard_map/pallas_call | solution.py:27
  215.2 7.7 %all-to-all-start.5 = ((f32[32,8,128]{2,1,0:T(8,128)}), f32[32,8,128]{2,1,0:T(8,128)S(1)}, u32[]{:S(2)}, u32[]{:S(2)}) async-start(f32[32,8,128]{2,1,0:T(8,128)} %shard_map.69), calls=%async_computation.5 | async-start | bytes 262144 | tf_op jit(solution)/shard_map/all_to_all | solution.py:304
  223.5 8.6 %all-to-all-done.5 = f32[32,8,128]{2,1,0:T(8,128)S(1)} async-done(((f32[32,8,128]{2,1,0:T(8,128)}), f32[32,8,128]{2,1,0:T(8,128)S(1)}, u32[]{:S(2)}, u32[]{:S(2)}) %all-to-all-start.5) | async-done | bytes 131104 | tf_op jit(solution)/shard_map/all_to_all | solution.py:304
  (63 shorter events, 2.6 us)
Async XLA Ops:
  2.6 11.0 %copy-start.11 = (bf16[128,448]{0,1:T(8,128)(2,1)S(1)}, bf16[128,448]{0,1:T(8,128)(2,1)}, u32[]{:S(2)}) copy-start(bf16[128,448]{0,1:T(8,128)(2,1)} %param.5) | copy-start | bytes 344068
  2.6 34.3 %all-to-all-start = ((bf16[4,512,256]{2,1,0:T(8,128)(2,1)}), bf16[4,512,256]{2,1,0:T(8,128)(2,1)S(1)}, u32[]{:S(2)}, u32[]{:S(2)}) async-start(bf16[4,512,256]{2,1,0:T(8,128)(2,1)} %broadcast_in_dim.6), calls=%async_computation | async-start | bytes 2097152 | tf_op jit(solution)/shard_map/all_to_all | solution.py:222
  36.9 38.3 %copy-start.1 = (bf16[3584,128]{1,0:T(8,128)(2,1)}, bf16[3584,128]{1,0:T(8,128)(2,1)S(1)}, u32[]{:S(2)}) copy-start(bf16[3584,128]{1,0:T(8,128)(2,1)S(1)} %all-gather) | copy-start | bytes 2752516
  37.0 38.3 %copy-start = (bf16[4,512,256]{2,1,0:T(8,128)(2,1)}, bf16[4,512,256]{2,1,0:T(8,128)(2,1)S(1)}, u32[]{:S(2)}) copy-start(bf16[4,512,256]{2,1,0:T(8,128)(2,1)S(1)} %all-to-all-done.refs_1_) | copy-start | bytes 3145732
  37.0 37.3 %collective-permute-start.1 = (bf16[8,448,128]{2,1,0:T(8,128)(2,1)S(1)}, bf16[8,448,128]{2,1,0:T(8,128)(2,1)S(1)}, u32[]{:S(2)}, u32[]{:S(2)}) collective-permute-start(bf16[8,448,128]{2,1,0:T(8,128)(2,1)S(1)} %bitcast.19), channel_id=1, source_target_pairs={{0,32},{32,0},{1,33},{33,1},{2,34},{34,2},{3,35},{35,3},{4,36},{36... | collective-permute-start | bytes 2752520 | tf_op jit(solution)/shard_map/ppermute | solution.py:217
  44.2 13.8 %collective-permute-start.4 = (bf16[2,512,256]{2,1,0:T(8,128)(2,1)S(1)}, bf16[2,512,256]{2,1,0:T(8,128)(2,1)S(1)}, u32[]{:S(2)}, u32[]{:S(2)}) collective-permute-start(bf16[2,512,256]{2,1,0:T(8,128)(2,1)S(1)} %get-tuple-element.43), channel_id=1, source_target_pairs={{0,3},{1,0},{2,1},{3,2},{4,7},{5,4},{6,5},{7,6},{8,11},{9,8},{10,9... | collective-permute-start | bytes 1572872 | tf_op jit(solution)/shard_map/ppermute | solution.py:236
  48.6 14.7 %collective-permute-start = (bf16[2,512,256]{2,1,0:T(8,128)(2,1)S(1)}, bf16[2,512,256]{2,1,0:T(8,128)(2,1)}, u32[]{:S(2)}, u32[]{:S(2)}) collective-permute-start(bf16[2,512,256]{2,1,0:T(8,128)(2,1)S(1)} %get-tuple-element.44), channel_id=1, source_target_pairs={{0,1},{1,2},{2,3},{3,0},{4,5},{5,6},{6,7},{7,4},{8,9},{9,10},{10,1... | collective-permute-start | bytes 1572872 | tf_op jit(solution)/shard_map/ppermute | solution.py:236
  50.5 23.7 %collective-permute-start.2 = (bf16[2,512,256]{2,1,0:T(8,128)(2,1)S(1)}, bf16[2,512,256]{2,1,0:T(8,128)(2,1)S(1)}, u32[]{:S(2)}, u32[]{:S(2)}) collective-permute-start(bf16[2,512,256]{2,1,0:T(8,128)(2,1)S(1)} %get-tuple-element.43), channel_id=1, source_target_pairs={{0,1},{1,2},{2,3},{3,0},{4,5},{5,6},{6,7},{7,4},{8,9},{9,10},{10,1... | collective-permute-start | bytes 1572872 | tf_op jit(solution)/shard_map/ppermute | solution.py:236
  52.6 21.6 %collective-permute-start.3 = (bf16[2,512,256]{2,1,0:T(8,128)(2,1)S(1)}, bf16[2,512,256]{2,1,0:T(8,128)(2,1)S(1)}, u32[]{:S(2)}, u32[]{:S(2)}) collective-permute-start(bf16[2,512,256]{2,1,0:T(8,128)(2,1)S(1)} %get-tuple-element.44), channel_id=1, source_target_pairs={{0,3},{1,0},{2,1},{3,2},{4,7},{5,4},{6,5},{7,6},{8,11},{9,8},{10,9... | collective-permute-start | bytes 1572872 | tf_op jit(solution)/shard_map/ppermute | solution.py:236
  58.0 26.8 %copy-start.12 = (bf16[2,512,256]{2,1,0:T(8,128)(2,1)}, bf16[2,512,256]{2,1,0:T(8,128)(2,1)S(1)}, u32[]{:S(2)}) copy-start(bf16[2,512,256]{2,1,0:T(8,128)(2,1)S(1)} %collective-permute-done.4.refs_4_) | copy-start | bytes 1572868
  58.0 29.2 %collective-permute-start.6 = (bf16[2,512,256]{2,1,0:T(8,128)(2,1)S(1)}, bf16[2,512,256]{2,1,0:T(8,128)(2,1)S(1)}, u32[]{:S(2)}, u32[]{:S(2)}) collective-permute-start(bf16[2,512,256]{2,1,0:T(8,128)(2,1)S(1)} %collective-permute-done.4.refs_4_), channel_id=1, source_target_pairs={{0,3},{1,0},{2,1},{3,2},{4,7},{5,4},{6,5},{7,6},{8,11},{9,8},{10,9... | collective-permute-start | bytes 1572872 | tf_op jit(solution)/shard_map/ppermute | solution.py:236
  63.3 26.4 %collective-permute-start.5 = (bf16[2,512,256]{2,1,0:T(8,128)(2,1)}, bf16[2,512,256]{2,1,0:T(8,128)(2,1)}, u32[]{:S(2)}, u32[]{:S(2)}) collective-permute-start(bf16[2,512,256]{2,1,0:T(8,128)(2,1)} %collective-permute-done.refs_2_), channel_id=1, source_target_pairs={{0,1},{1,2},{2,3},{3,0},{4,5},{5,6},{6,7},{7,4},{8,9},{9,10},{10,1... | collective-permute-start | bytes 1572872 | tf_op jit(solution)/shard_map/ppermute | solution.py:236
  74.3 10.5 %copy-start.13 = (bf16[2,512,256]{2,1,0:T(8,128)(2,1)}, bf16[2,512,256]{2,1,0:T(8,128)(2,1)S(1)}, u32[]{:S(2)}) copy-start(bf16[2,512,256]{2,1,0:T(8,128)(2,1)S(1)} %collective-permute-done.2.refs_3_) | copy-start | bytes 1572868
  74.3 10.5 %copy-start.14 = (bf16[2,512,256]{2,1,0:T(8,128)(2,1)}, bf16[2,512,256]{2,1,0:T(8,128)(2,1)S(1)}, u32[]{:S(2)}) copy-start(bf16[2,512,256]{2,1,0:T(8,128)(2,1)S(1)} %collective-permute-done.3.refs_5_) | copy-start | bytes 1572868
  74.3 10.5 %copy-start.6 = (bf16[8,448,128]{2,1,0:T(8,128)(2,1)}, bf16[8,448,128]{2,1,0:T(8,128)(2,1)S(1)}, u32[]{:S(2)}) copy-start(bf16[8,448,128]{2,1,0:T(8,128)(2,1)S(1)} %collective-permute-done.1.refs_11_) | copy-start | bytes 2752516
  75.2 14.5 %collective-permute-start.8 = (bf16[4,448,128]{2,1,0:T(8,128)(2,1)}, bf16[4,448,128]{2,1,0:T(8,128)(2,1)S(1)}, u32[]{:S(2)}, u32[]{:S(2)}) collective-permute-start(bf16[4,448,128]{2,1,0:T(8,128)(2,1)} %get-tuple-element.47), channel_id=1, source_target_pairs={{0,16},{16,0},{1,17},{17,1},{2,18},{18,2},{3,19},{19,3},{4,20},{20... | collective-permute-start | bytes 1376264 | tf_op jit(solution)/shard_map/ppermute | solution.py:217
  82.8 7.0 %collective-permute-start.7 = (bf16[4,448,128]{2,1,0:T(8,128)(2,1)S(1)}, bf16[4,448,128]{2,1,0:T(8,128)(2,1)S(1)}, u32[]{:S(2)}, u32[]{:S(2)}) collective-permute-start(bf16[4,448,128]{2,1,0:T(8,128)(2,1)S(1)} %get-tuple-element.48), channel_id=1, source_target_pairs={{0,16},{16,0},{1,17},{17,1},{2,18},{18,2},{3,19},{19,3},{4,20},{20... | collective-permute-start | bytes 1376264 | tf_op jit(solution)/shard_map/ppermute | solution.py:217
  84.8 5.0 %collective-permute-start.10 = (bf16[4,448,128]{2,1,0:T(8,128)(2,1)S(1)}, bf16[4,448,128]{2,1,0:T(8,128)(2,1)S(1)}, u32[]{:S(2)}, u32[]{:S(2)}) collective-permute-start(bf16[4,448,128]{2,1,0:T(8,128)(2,1)S(1)} %get-tuple-element.45), channel_id=1, source_target_pairs={{0,16},{16,0},{1,17},{17,1},{2,18},{18,2},{3,19},{19,3},{4,20},{20... | collective-permute-start | bytes 1376264 | tf_op jit(solution)/shard_map/ppermute | solution.py:217
  87.2 1.9 copy-start.15
  87.2 3.7 %collective-permute-start.9 = (bf16[4,448,128]{2,1,0:T(8,128)(2,1)S(1)}, bf16[4,448,128]{2,1,0:T(8,128)(2,1)S(1)}, u32[]{:S(2)}, u32[]{:S(2)}) collective-permute-start(bf16[4,448,128]{2,1,0:T(8,128)(2,1)S(1)} %get-tuple-element.46), channel_id=1, source_target_pairs={{0,16},{16,0},{1,17},{17,1},{2,18},{18,2},{3,19},{19,3},{4,20},{20... | collective-permute-start | bytes 1376264 | tf_op jit(solution)/shard_map/ppermute | solution.py:217
  89.8 1.2 copy-start.16
  89.8 1.2 copy-start.17
  89.8 1.2 copy-start.18
  90.9 0.8 copy-start.19
  101.3 8.3 %collective-permute-start.12 = (bf16[2,8,304,128]{3,2,1,0:T(8,128)(2,1)}, bf16[2,8,304,128]{3,2,1,0:T(8,128)(2,1)S(1)}, u32[]{:S(2)}, u32[]{:S(2)}) collective-permute-start(bf16[2,8,304,128]{3,2,1,0:T(8,128)(2,1)} %get-tuple-element.32.sent), channel_id=1, source_target_pairs={{0,16},{16,0},{1,17},{17,1},{2,18},{18,2},{3,19},{19,3},{4,20},{20... | collective-permute-start | bytes 3735560 | tf_op jit(solution)/shard_map/ppermute | solution.py:217
  103.3 4.1 %collective-permute-start.11 = (bf16[8,2,144,128]{3,2,1,0:T(8,128)(2,1)}, bf16[8,2,144,128]{3,2,1,0:T(8,128)(2,1)S(1)}, u32[]{:S(2)}, u32[]{:S(2)}) collective-permute-start(bf16[8,2,144,128]{3,2,1,0:T(8,128)(2,1)} %get-tuple-element.31.b1), channel_id=1, source_target_pairs={{0,16},{16,0},{1,17},{17,1},{2,18},{18,2},{3,19},{19,3},{4,20},{20... | collective-permute-start | bytes 1769480 | tf_op jit(solution)/shard_map/ppermute | solution.py:217
  107.5 8.9 %copy-start.4 = (bf16[8,304,128]{2,1,0:T(8,128)(2,1)S(1)}, bf16[8,304,128]{2,1,0:T(8,128)(2,1)}, u32[]{:S(2)}) copy-start(bf16[8,304,128]{2,1,0:T(8,128)(2,1)} %get-tuple-element.34.a1) | copy-start | bytes 1867780
  109.6 26.1 %all-to-all-start.1 = ((bf16[8,2,144,128]{3,2,1,0:T(8,128)(2,1)}), bf16[8,2,144,128]{3,2,1,0:T(8,128)(2,1)S(1)}, u32[]{:S(2)}, u32[]{:S(2)}) async-start(bf16[8,2,144,128]{3,2,1,0:T(8,128)(2,1)} %add_convert_fusion), calls=%async_computation.1 | async-start | bytes 1179648 | tf_op jit(solution)/shard_map/all_to_all | solution.py:275
  117.4 17.0 %collective-permute-start.13 = (bf16[8,304,128]{2,1,0:T(8,128)(2,1)}, bf16[8,304,128]{2,1,0:T(8,128)(2,1)S(1)}, u32[]{:S(2)}, u32[]{:S(2)}) collective-permute-start(bf16[8,304,128]{2,1,0:T(8,128)(2,1)} %fusion), channel_id=1, source_target_pairs={{0,32},{32,0},{1,33},{33,1},{2,34},{34,2},{3,35},{35,3},{4,36},{36... | collective-permute-start | bytes 1867784 | tf_op jit(solution)/shard_map/ppermute | solution.py:217
  119.3 15.1 %copy-start.3 = (bf16[8,304,128]{2,1,0:T(8,128)(2,1)S(1)}, bf16[8,304,128]{2,1,0:T(8,128)(2,1)}, u32[]{:S(2)}) copy-start(bf16[8,304,128]{2,1,0:T(8,128)(2,1)} %get-tuple-element.29.a0) | copy-start | bytes 1867780
  158.5 20.6 %all-to-all-start.3 = ((bf16[8,304,128]{2,1,0:T(8,128)(2,1)}), bf16[8,304,128]{2,1,0:T(8,128)(2,1)S(1)}, u32[]{:S(2)}, u32[]{:S(2)}) async-start(bf16[8,304,128]{2,1,0:T(8,128)(2,1)} %broadcast_in_dim.7), calls=%async_computation.3 | async-start | bytes 1245184 | tf_op jit(solution)/shard_map/all_to_all | solution.py:222
  162.2 5.1 %collective-permute-start.14 = (bf16[2,144,128]{2,1,0:T(8,128)(2,1)S(1)}, bf16[2,144,128]{2,1,0:T(8,128)(2,1)S(1)}, u32[]{:S(2)}, u32[]{:S(2)}) collective-permute-start(bf16[2,144,128]{2,1,0:T(8,128)(2,1)S(1)} %reduce_sum.34), channel_id=1, source_target_pairs={{0,32},{32,0},{1,33},{33,1},{2,34},{34,2},{3,35},{35,3},{4,36},{36... | collective-permute-start | bytes 221192 | tf_op jit(solution)/shard_map/ppermute | solution.py:217
  179.1 29.5 %copy-start.2 = (bf16[8,304,128]{2,1,0:T(8,128)(2,1)}, bf16[8,304,128]{2,1,0:T(8,128)(2,1)S(1)}, u32[]{:S(2)}) copy-start(bf16[8,304,128]{2,1,0:T(8,128)(2,1)S(1)} %all-to-all-done.3.refs_0_) | copy-start | bytes 1867780
  180.1 23.8 %all-to-all-start.4 = ((bf16[8,2,144,128]{3,2,1,0:T(8,128)(2,1)}), bf16[8,2,144,128]{3,2,1,0:T(8,128)(2,1)S(1)}, u32[]{:S(2)}, u32[]{:S(2)}) async-start(bf16[8,2,144,128]{3,2,1,0:T(8,128)(2,1)} %broadcast_in_dim.8), calls=%async_computation.4 | async-start | bytes 1179648 | tf_op jit(solution)/shard_map/all_to_all | solution.py:222
  183.6 13.9 %collective-permute-start.15 = (bf16[8,304,128]{2,1,0:T(8,128)(2,1)S(1)}, bf16[8,304,128]{2,1,0:T(8,128)(2,1)S(1)}, u32[]{:S(2)}, u32[]{:S(2)}) collective-permute-start(bf16[8,304,128]{2,1,0:T(8,128)(2,1)S(1)} %all-to-all-done.3.refs_0_), channel_id=1, source_target_pairs={{0,32},{32,0},{1,33},{33,1},{2,34},{34,2},{3,35},{35,3},{4,36},{36... | collective-permute-start | bytes 1867784 | tf_op jit(solution)/shard_map/ppermute | solution.py:217
  186.3 19.5 %collective-permute-start.16 = (bf16[8,304,128]{2,1,0:T(8,128)(2,1)S(1)}, bf16[8,304,128]{2,1,0:T(8,128)(2,1)S(1)}, u32[]{:S(2)}, u32[]{:S(2)}) collective-permute-start(bf16[8,304,128]{2,1,0:T(8,128)(2,1)S(1)} %all-to-all-done.3.refs_0_), channel_id=1, source_target_pairs={{0,16},{16,0},{1,17},{17,1},{2,18},{18,2},{3,19},{19,3},{4,20},{20... | collective-permute-start | bytes 1867784 | tf_op jit(solution)/shard_map/ppermute | solution.py:217
  197.6 11.1 %copy-start.7 = (bf16[8,304,128]{2,1,0:T(8,128)(2,1)}, bf16[8,304,128]{2,1,0:T(8,128)(2,1)S(1)}, u32[]{:S(2)}) copy-start(bf16[8,304,128]{2,1,0:T(8,128)(2,1)S(1)} %collective-permute-done.15.refs_1_) | copy-start | bytes 1867780
  197.6 8.3 %collective-permute-start.17 = (bf16[8,304,128]{2,1,0:T(8,128)(2,1)S(1)}, bf16[8,304,128]{2,1,0:T(8,128)(2,1)S(1)}, u32[]{:S(2)}, u32[]{:S(2)}) collective-permute-start(bf16[8,304,128]{2,1,0:T(8,128)(2,1)S(1)} %collective-permute-done.15.refs_1_), channel_id=1, source_target_pairs={{0,16},{16,0},{1,17},{17,1},{2,18},{18,2},{3,19},{19,3},{4,20},{20... | collective-permute-start | bytes 1867784 | tf_op jit(solution)/shard_map/ppermute | solution.py:217
  203.9 4.7 %copy-start.5 = (bf16[8,2,144,128]{3,2,1,0:T(8,128)(2,1)}, bf16[8,2,144,128]{3,2,1,0:T(8,128)(2,1)S(1)}, u32[]{:S(2)}) copy-start(bf16[8,2,144,128]{3,2,1,0:T(8,128)(2,1)S(1)} %all-to-all-done.4.refs_4_) | copy-start | bytes 1769476
  203.9 3.9 %collective-permute-start.18 = (bf16[8,2,144,128]{3,2,1,0:T(8,128)(2,1)S(1)}, bf16[8,2,144,128]{3,2,1,0:T(8,128)(2,1)S(1)}, u32[]{:S(2)}, u32[]{:S(2)}) collective-permute-start(bf16[8,2,144,128]{3,2,1,0:T(8,128)(2,1)S(1)} %all-to-all-done.4.refs_4_), channel_id=1, source_target_pairs={{0,16},{16,0},{1,17},{17,1},{2,18},{18,2},{3,19},{19,3},{4,20},{20... | collective-permute-start | bytes 1769480 | tf_op jit(solution)/shard_map/ppermute | solution.py:217
  205.9 2.8 %copy-start.8 = (bf16[8,304,128]{2,1,0:T(8,128)(2,1)}, bf16[8,304,128]{2,1,0:T(8,128)(2,1)S(1)}, u32[]{:S(2)}) copy-start(bf16[8,304,128]{2,1,0:T(8,128)(2,1)S(1)} %collective-permute-done.16.refs_2_) | copy-start | bytes 1867780
  205.9 2.8 %copy-start.9 = (bf16[8,304,128]{2,1,0:T(8,128)(2,1)}, bf16[8,304,128]{2,1,0:T(8,128)(2,1)S(1)}, u32[]{:S(2)}) copy-start(bf16[8,304,128]{2,1,0:T(8,128)(2,1)S(1)} %collective-permute-done.17.refs_3_) | copy-start | bytes 1867780
  207.8 0.8 copy-start.10
  215.2 16.9 %all-to-all-start.5 = ((f32[32,8,128]{2,1,0:T(8,128)}), f32[32,8,128]{2,1,0:T(8,128)S(1)}, u32[]{:S(2)}, u32[]{:S(2)}) async-start(f32[32,8,128]{2,1,0:T(8,128)} %shard_map.69), calls=%async_computation.5 | async-start | bytes 262144 | tf_op jit(solution)/shard_map/all_to_all | solution.py:304

commit v8 on v6

--- a/solution.py
+++ b/solution.py
@@ -11,7 +11,8 @@
 REP = ("y", "zl", "c")
 F32, BF = jnp.float32, jnp.bfloat16
 NT = (((1,), (1,)), ((), ()))
-CUT = 304
+CUT = 256
+BACK_CUT = 304
 VMEM_LIMIT = 60 * 1024 * 1024
 TOK = pltpu.VMEM((16, 512, 256), BF)
 ACC = pltpu.VMEM((448, 512), F32)
@@ -70,7 +71,7 @@
 
 
 def first_kernel(*refs):
-    me, t0, p1, p2, m1, m2, f1, f2, up_in, cot_in, w0, w1, w2, w3 = refs[:14]
+    me, t0, p1, p2, m1, m2, f1, f2, up_in, cot_in, *weights = refs[:14]
     tok_out, bend_out, *outs = refs[14:21]
     tok, held, up, cot, coeff, bend, acc, own, own_b, tok_sems, w_sems, in_sems, out_sems, sems = refs[21:]
     mine, first = me[0], me[1] == 0
@@ -83,7 +84,7 @@
     for z in range(4):
         for d in range(4):
             token_copy(d, z).start()
-    w_ready = fetched([(w, held.at[i]) for i, w in enumerate((w0, w1, w2, w3))], w_sems)
+    w_ready = fetched([(w, held.at[i]) for i, w in enumerate(weights)], w_sems)
     get_up = pltpu.make_async_copy(up_in, up, in_sems.at[0])
     get_cot = pltpu.make_async_copy(cot_in, cot, in_sems.at[1])
     get_up.start()
@@ -194,8 +195,12 @@
         off = own[:, lanes] - mean
         c += b * mean * mean
         s += b * off * off
-    sums[0:1, :] = jnp.sum(c.T, axis=0, keepdims=True)
-    sums[1:2, :] = jnp.sum(s.T, axis=0, keepdims=True)
+    for k, terms in enumerate((c, s)):
+        line = jnp.sum(terms.T, axis=0, keepdims=True)
+        line = jnp.concatenate([line, jnp.zeros((1, 64), F32)], 1)
+        for i in range(4):
+            row = line[:, 128 * i : 128 * i + 128]
+            sums[:, 4 * k + i : 4 * k + i + 1, :] = jnp.broadcast_to(row[None], (32, 1, 128))
 
 
 def swap(value, axis):
@@ -226,7 +231,10 @@
     flops = 2 * 448 * 512 * 4096
     rest = 448 - CUT
     dma = pltpu.SemaphoreType.DMA
-    held = [pltpu.VMEM((4, 8, CUT, 128), BF), pltpu.VMEM((2, 8, 2, rest, 128), BF)]
+    held, held_back = (
+        [pltpu.VMEM((4, 8, cut, 128), BF), pltpu.VMEM((2, 8, 2, 448 - cut, 128), BF)]
+        for cut in (CUT, BACK_CUT)
+    )
     w0 = lax.all_gather(gate_weight.T, "y", axis=0)
     t0, w0 = lax.optimization_barrier((to_all(tokens, "zh"), w0))
     low, high = t0[:2], t0[2:]
@@ -275,20 +283,22 @@
     other_b = swap(part_b, "zl")
     both_b = total(part_b, other_b[::-1]).astype(BF)
     grad_a = jnp.sum(across_a.astype(F32), axis=0).astype(BF)
-    u0, both_b = lax.optimization_barrier((to_all(grad_a, "y"), both_b))
-    v0 = to_all(both_b, "y")
+    more = BACK_CUT - CUT
+    first = jnp.concatenate([grad_a, both_b[0, :more]])
+    u0, last = lax.optimization_barrier((to_all(first, "y"), both_b[:, more:]))
+    v0 = to_all(last, "y")
     u1 = swap(u0, "zl")
     rows = (u0, u1, swap(u0, "c"), swap(u1, "c"), v0, swap(v0, "c"))
     line = call(
         mean_kernel,
-        [shape(2, 448, dtype=F32)],
+        [shape(32, 8, 128, dtype=F32)],
         (me, tok, bend, own, *rows),
         flops,
-        [*[ACC] * 3, TOK, *held, *map(dma, ((1, 2), (6, 2), (2,)))],
+        [*[ACC] * 3, TOK, *held_back, *map(dma, ((1, 2), (6, 2), (2,)))],
         True,
     )[0]
-    whole = jnp.sum(to_all(line, REP), axis=0)
-    grad = jnp.concatenate([grad_a, both_b[0]], axis=0).T
+    whole = jnp.sum(lax.all_to_all(line, REP, 0, 0, tiled=True), axis=0).reshape(2, 512)[:, :448]
+    grad = jnp.concatenate([first, last[0]], axis=0).T
     return grad, whole[0], whole[1] / 31
 
 

time: 234 us -> 238 us (1.017)
  blocking collectives: 47.2 us -> 23.3 us
  waiting for transfers between devices: 51.1 us -> 65.9 us
  starting transfers between devices: 99.5 us -> 113 us
    all_to_all x1 -> x0, blocking collectives: 23.9 us -> none  [shards(): across_a = lax.all_to_all(sums_a, 'y', 0, 0, tiled=True)]
    all_to_all x0 -> x2, waiting for transfers between devices: none -> 14.1 us  [the longest x1 8.59 us: shards(): lax.all_to_all(line, REP, 0, 0, tiled=True)]
    all_to_all x0 -> x2, starting transfers between devices: none -> 12.1 us  [the longest x1 8.32 us: shards(): lax.all_to_all(line, REP, 0, 0, tiled=True)]
    ppermute x11, starting transfers between devices: 50.8 us -> 59.5 us  [swap(): return lax.ppermute(value, axis, ((0, 1), (1, 0)))]
    all_to_all x4 -> x3, starting transfers between devices: 25.3 us -> 17.9 us  [to_all(): lax.all_to_all(jnp.broadcast_to(value[None], (count, *value.shape)), axis...]
    all_to_all x4 -> x3, waiting for transfers between devices: 20.5 us -> 17.6 us  [to_all(): lax.all_to_all(jnp.broadcast_to(value[None], (count, *value.shape)), axis...]
    all_to_all x1, waiting for transfers between devices: 0.01 us -> 2.56 us  [shards(): across_b = lax.all_to_all(sums_b, 'y', 0, 0, tiled=True)]
    broadcast_in_dim x4 -> x3, local copies, waits for them, and re-layouts: 5.36 us -> 3.99 us  [to_all(): jnp.broadcast_to(value[None], (count, *value.shape))]
  transfers between devices with their start and end apart: 22 -> 23, of which waited for: 11 -> 14; matrix products, arithmetic and copies ran while one was open for 2% -> 2% of each run, Pallas kernels for 3% -> 3%
where the time goes in v8:
time: 238 us; the launch traced here: 237 us
  starting transfers between devices  113 us (47%)
  waiting for transfers between devices  65.9 us (28%)
  blocking collectives  23.3 us (10%)
  Pallas kernels  22.7 us (10%)
  other arithmetic  5.67 us (2%)
  local copies, waits for them, and re-layouts  4.99 us (2%)
    ppermute x11, starting transfers between devices, swap(): return lax.ppermute(value, axis, ((0, 1), (1, 0)))  59.5 us
    all_gather x1, blocking collectives, shards(): w0 = lax.all_gather(gate_weight.T, 'y', axis=0)  23.3 us
    ppermute x11, waiting for transfers between devices, swap(): return lax.ppermute(value, axis, ((0, 1), (1, 0)))  23.1 us
    pallas_call x3, Pallas kernels, call(): pl.pallas_call(kernel, out_shape=outs, in_specs=[SM] + [ANY] * (len(opera...  22.7 us
    ppermute x6, starting transfers between devices, along_x(): return lax.ppermute(value, 'x', [(i, (i + by) % 4) for i in range(4)])  18.1 us
    all_to_all x3, starting transfers between devices, to_all(): lax.all_to_all(jnp.broadcast_to(value[None], (count, *value.shape)), axis...  17.9 us
    all_to_all x3, waiting for transfers between devices, to_all(): lax.all_to_all(jnp.broadcast_to(value[None], (count, *value.shape)), axis...  17.6 us
    ppermute x6, waiting for transfers between devices, along_x(): return lax.ppermute(value, 'x', [(i, (i + by) % 4) for i in range(4)])  8.64 us
  transfers between devices with their start and end apart: 23, of which 14 were waited for; matrix products, arithmetic and copies ran while one was open for 2% of the time, Pallas kernels for 3%

profile of v8, /device:TPU:1, one launch (start us, length us, event | category | flops | bytes accessed | tf_op | source)
XLA Modules:
  0.0 236.6 jit_solution(3684553341672193863)
XLA Ops:
  0.6 2.0 broadcast_in_dim.6
  2.7 10.8 %all-to-all-start = ((bf16[4,512,256]{2,1,0:T(8,128)(2,1)}), bf16[4,512,256]{2,1,0:T(8,128)(2,1)S(1)}, u32[]{:S(2)}, u32[]{:S(2)}) async-start(bf16[4,512,256]{2,1,0:T(8,128)(2,1)} %broadcast_in_dim.6), calls=%async_computation | async-start | bytes 2097152 | tf_op jit(solution)/shard_map/all_to_all | solution.py:212
  13.5 23.3 %all-gather = bf16[3584,128]{1,0:T(8,128)(2,1)S(1)} all-gather(bf16[448,128]{1,0:T(8,128)(2,1)S(1)} %bitcast.24), channel_id=2, replica_groups=mesh['y'=8,'zl'=2,'c'=2,'zh'=4,'x'=4] {'y'}, dimensions={0}, use_global_device_ids=true | all-gather | bytes 1032192 | tf_op jit(solution)/shard_map/all_gather | solution.py:238
  36.9 4.4 %collective-permute-start.3 = (bf16[2,512,256]{2,1,0:T(8,128)(2,1)S(1)}, bf16[2,512,256]{2,1,0:T(8,128)(2,1)S(1)}, u32[]{:S(2)}, u32[]{:S(2)}) collective-permute-start(bf16[2,512,256]{2,1,0:T(8,128)(2,1)S(1)} %get-tuple-element.47), channel_id=1, source_target_pairs={{0,3},{1,0},{2,1},{3,2},{4,7},{5,4},{6,5},{7,6},{8,11},{9,8},{10,9... | collective-permute-start | bytes 1572872 | tf_op jit(solution)/shard_map/ppermute | solution.py:226
  41.3 1.9 collective-permute-start
  43.3 7.2 %collective-permute-start.4 = (bf16[8,448,128]{2,1,0:T(8,128)(2,1)S(1)}, bf16[8,448,128]{2,1,0:T(8,128)(2,1)S(1)}, u32[]{:S(2)}, u32[]{:S(2)}) collective-permute-start(bf16[8,448,128]{2,1,0:T(8,128)(2,1)S(1)} %bitcast.21), channel_id=1, source_target_pairs={{0,32},{32,0},{1,33},{33,1},{2,34},{34,2},{3,35},{35,3},{4,36},{36... | collective-permute-start | bytes 2752520 | tf_op jit(solution)/shard_map/ppermute | solution.py:207
  50.4 2.1 collective-permute-start.1
  52.5 4.4 %collective-permute-start.2 = (bf16[2,512,256]{2,1,0:T(8,128)(2,1)S(1)}, bf16[2,512,256]{2,1,0:T(8,128)(2,1)S(1)}, u32[]{:S(2)}, u32[]{:S(2)}) collective-permute-start(bf16[2,512,256]{2,1,0:T(8,128)(2,1)S(1)} %get-tuple-element.48), channel_id=1, source_target_pairs={{0,3},{1,0},{2,1},{3,2},{4,7},{5,4},{6,5},{7,6},{8,11},{9,8},{10,9... | collective-permute-start | bytes 1572872 | tf_op jit(solution)/shard_map/ppermute | solution.py:226
  57.0 3.4 %collective-permute-start.6 = (bf16[2,512,256]{2,1,0:T(8,128)(2,1)S(1)}, bf16[2,512,256]{2,1,0:T(8,128)(2,1)S(1)}, u32[]{:S(2)}, u32[]{:S(2)}) collective-permute-start(bf16[2,512,256]{2,1,0:T(8,128)(2,1)S(1)} %collective-permute-done.3.refs_4_), channel_id=1, source_target_pairs={{0,3},{1,0},{2,1},{3,2},{4,7},{5,4},{6,5},{7,6},{8,11},{9,8},{10,9... | collective-permute-start | bytes 1572872 | tf_op jit(solution)/shard_map/ppermute | solution.py:226
  60.3 1.9 collective-permute-start.5
  62.3 5.3 %collective-permute-done.1.refs_3_ = bf16[2,512,256]{2,1,0:T(8,128)(2,1)S(1)} collective-permute-done((bf16[2,512,256]{2,1,0:T(8,128)(2,1)S(1)}, bf16[2,512,256]{2,1,0:T(8,128)(2,1)S(1)}, u32[]{:S(2)}, u32[]{:S(2)}) %collective-permute-start.1) | collective-permute-done | bytes 524320 | tf_op jit(solution)/shard_map/ppermute | solution.py:226
  67.5 7.8 %collective-permute-start.7 = (bf16[8,448,128]{2,1,0:T(8,128)(2,1)S(1)}, bf16[8,448,128]{2,1,0:T(8,128)(2,1)}, u32[]{:S(2)}, u32[]{:S(2)}) collective-permute-start(bf16[8,448,128]{2,1,0:T(8,128)(2,1)S(1)} %bitcast.22), channel_id=1, source_target_pairs={{0,16},{16,0},{1,17},{17,1},{2,18},{18,2},{3,19},{19,3},{4,20},{20... | collective-permute-start | bytes 2752520 | tf_op jit(solution)/shard_map/ppermute | solution.py:207
  75.4 1.6 collective-permute-done.6.refs_7_
  77.0 1.8 collective-permute-done.5.refs_6_
  78.8 5.1 %collective-permute-start.8 = (bf16[8,448,128]{2,1,0:T(8,128)(2,1)S(1)}, bf16[8,448,128]{2,1,0:T(8,128)(2,1)}, u32[]{:S(2)}, u32[]{:S(2)}) collective-permute-start(bf16[8,448,128]{2,1,0:T(8,128)(2,1)S(1)} %collective-permute-done.4.refs_11_), channel_id=1, source_target_pairs={{0,16},{16,0},{1,17},{17,1},{2,18},{18,2},{3,19},{19,3},{4,20},{20... | collective-permute-start | bytes 2752520 | tf_op jit(solution)/shard_map/ppermute | solution.py:207
  83.9 0.7 pad_add_fusion.refs_0_.me
  84.6 1.5 collective-permute-done.8.refs_13_
  86.1 9.6 %shard_map.67 = (bf16[16,512,256]{2,1,0:T(8,128)(2,1)}, f32[448,512]{1,0:T(8,128)}, bf16[8,256,128]{2,1,0:T(8,128)(2,1)}, bf16[8,256,128]{2,1,0:T(8,128)(2,1)}, ...) custom-call(s32[3]{0:T(128)} %pad_add_fusion.refs_0_.me, ...), custom_call_target="tpu_custom_call" | custom-call | flops 3758096384 | bytes 17563660 | tf_op jit(solution)/shard_map/pallas_call | solution.py:28
  95.6 2.3 collective-permute-start.9
  97.9 2.0 collective-permute-start.10
  100.0 2.4 add_convert_fusion
  102.7 5.3 %all-to-all-start.1 = ((bf16[8,2,192,128]{3,2,1,0:T(8,128)(2,1)}), bf16[8,2,192,128]{3,2,1,0:T(8,128)(2,1)S(1)}, u32[]{:S(2)}, u32[]{:S(2)}) async-start(bf16[8,2,192,128]{3,2,1,0:T(8,128)(2,1)} %add_convert_fusion), calls=%async_computation.1 | async-start | bytes 1572864 | tf_op jit(solution)/shard_map/all_to_all | solution.py:269
  108.2 8.0 %collective-permute-start.11 = (bf16[8,256,128]{2,1,0:T(8,128)(2,1)S(1)}, bf16[8,256,128]{2,1,0:T(8,128)(2,1)S(1)}, u32[]{:S(2)}, u32[]{:S(2)}) collective-permute-start(bf16[8,256,128]{2,1,0:T(8,128)(2,1)S(1)} %fusion), channel_id=1, source_target_pairs={{0,32},{32,0},{1,33},{33,1},{2,34},{34,2},{3,35},{35,3},{4,36},{36... | collective-permute-start | bytes 1572872 | tf_op jit(solution)/shard_map/ppermute | solution.py:207
  116.2 6.6 %shard_map.68.own_in = f32[448,512]{1,0:T(8,128)} custom-call(s32[3]{0:T(128)} %pad_add_fusion.refs_0_.me, bf16[16,512,256]{2,1,0:T(8,128)(2,1)} %get-tuple-element.40.source, bf16[8,256,128]{2,1,0:T(8,128)(2,1)} %get-tuple-element.33.a0, bf16[8,256,128]{2,1,0:T(8,128)(2,1)} %get-tuple-element.38.a1, bf16[2,8,256,128]{3,2,1,0:T(8,128)(2,1)} %get-tuple-element.36.sent, ...), custom_call_target="tpu_custom_call" | custom-call | flops 1879048192 | bytes 8781836 | tf_op jit(solution)/shard_map/pallas_call | solution.py:28
  122.7 5.3 %collective-permute-done.11 = bf16[8,256,128]{2,1,0:T(8,128)(2,1)S(1)} collective-permute-done((bf16[8,256,128]{2,1,0:T(8,128)(2,1)S(1)}, bf16[8,256,128]{2,1,0:T(8,128)(2,1)S(1)}, u32[]{:S(2)}, u32[]{:S(2)}) %collective-permute-start.11) | collective-permute-done | bytes 524320 | tf_op jit(solution)/shard_map/ppermute | solution.py:207
  128.1 1.0 fusion.2
  129.1 2.6 %all-to-all-done.1 = bf16[8,2,192,128]{3,2,1,0:T(8,128)(2,1)S(1)} async-done(((bf16[8,2,192,128]{3,2,1,0:T(8,128)(2,1)}), bf16[8,2,192,128]{3,2,1,0:T(8,128)(2,1)S(1)}, u32[]{:S(2)}, u32[]{:S(2)}) %all-to-all-start.1) | async-done | bytes 786464 | tf_op jit(solution)/shard_map/all_to_all | solution.py:269
  131.6 3.8 %all-to-all-start.2 = ((bf16[8,256,128]{2,1,0:T(8,128)(2,1)}), bf16[8,256,128]{2,1,0:T(8,128)(2,1)S(1)}, u32[]{:S(2)}, u32[]{:S(2)}) async-start(bf16[8,256,128]{2,1,0:T(8,128)(2,1)} %fusion.2), calls=%async_computation.2 | async-start | bytes 1048576 | tf_op jit(solution)/shard_map/all_to_all | solution.py:281
  135.5 7.7 %collective-permute-start.12 = (bf16[2,192,128]{2,1,0:T(8,128)(2,1)S(1)}, bf16[2,192,128]{2,1,0:T(8,128)(2,1)S(1)}, u32[]{:S(2)}, u32[]{:S(2)}) collective-permute-start(bf16[2,192,128]{2,1,0:T(8,128)(2,1)S(1)} %reduce_sum.34), channel_id=1, source_target_pairs={{0,32},{32,0},{1,33},{33,1},{2,34},{34,2},{3,35},{35,3},{4,36},{36... | collective-permute-start | bytes 294920 | tf_op jit(solution)/shard_map/ppermute | solution.py:207
  143.3 2.7 %collective-permute-done.12 = bf16[2,192,128]{2,1,0:T(8,128)(2,1)S(1)} collective-permute-done((bf16[2,192,128]{2,1,0:T(8,128)(2,1)S(1)}, bf16[2,192,128]{2,1,0:T(8,128)(2,1)S(1)}, u32[]{:S(2)}, u32[]{:S(2)}) %collective-permute-start.12) | collective-permute-done | bytes 98336 | tf_op jit(solution)/shard_map/ppermute | solution.py:207
  146.0 5.5 %all-to-all-done.2 = bf16[8,256,128]{2,1,0:T(8,128)(2,1)S(1)} async-done(((bf16[8,256,128]{2,1,0:T(8,128)(2,1)}), bf16[8,256,128]{2,1,0:T(8,128)(2,1)S(1)}, u32[]{:S(2)}, u32[]{:S(2)}) %all-to-all-start.2) | async-done | bytes 524320 | tf_op jit(solution)/shard_map/all_to_all | solution.py:281
  151.6 0.9 broadcast_in_dim.7
  152.5 3.5 %all-to-all-start.3 = ((bf16[8,304,128]{2,1,0:T(8,128)(2,1)}), bf16[8,304,128]{2,1,0:T(8,128)(2,1)S(1)}, u32[]{:S(2)}, u32[]{:S(2)}) async-start(bf16[8,304,128]{2,1,0:T(8,128)(2,1)} %broadcast_in_dim.7), calls=%async_computation.3 | async-start | bytes 1245184 | tf_op jit(solution)/shard_map/all_to_all | solution.py:212
  156.1 17.6 %all-to-all-done.3.refs_0_ = bf16[8,304,128]{2,1,0:T(8,128)(2,1)S(1)} async-done(((bf16[8,304,128]{2,1,0:T(8,128)(2,1)}), bf16[8,304,128]{2,1,0:T(8,128)(2,1)S(1)}, u32[]{:S(2)}, u32[]{:S(2)}) %all-to-all-start.3) | async-done | bytes 622624 | tf_op jit(solution)/shard_map/all_to_all | solution.py:212
  173.6 1.0 broadcast_in_dim.8
  174.6 3.5 %all-to-all-start.4 = ((bf16[8,2,144,128]{3,2,1,0:T(8,128)(2,1)}), bf16[8,2,144,128]{3,2,1,0:T(8,128)(2,1)S(1)}, u32[]{:S(2)}, u32[]{:S(2)}) async-start(bf16[8,2,144,128]{3,2,1,0:T(8,128)(2,1)} %broadcast_in_dim.8), calls=%async_computation.4 | async-start | bytes 1179648 | tf_op jit(solution)/shard_map/all_to_all | solution.py:212
  178.2 11.9 %collective-permute-start.13 = (bf16[8,304,128]{2,1,0:T(8,128)(2,1)S(1)}, bf16[8,304,128]{2,1,0:T(8,128)(2,1)S(1)}, u32[]{:S(2)}, u32[]{:S(2)}) collective-permute-start(bf16[8,304,128]{2,1,0:T(8,128)(2,1)S(1)} %all-to-all-done.3.refs_0_), channel_id=1, source_target_pairs={{0,32},{32,0},{1,33},{33,1},{2,34},{34,2},{3,35},{35,3},{4,36},{36... | collective-permute-start | bytes 1867784 | tf_op jit(solution)/shard_map/ppermute | solution.py:207
  190.1 2.7 %collective-permute-start.14 = (bf16[8,304,128]{2,1,0:T(8,128)(2,1)S(1)}, bf16[8,304,128]{2,1,0:T(8,128)(2,1)S(1)}, u32[]{:S(2)}, u32[]{:S(2)}) collective-permute-start(bf16[8,304,128]{2,1,0:T(8,128)(2,1)S(1)} %all-to-all-done.3.refs_0_), channel_id=1, source_target_pairs={{0,16},{16,0},{1,17},{17,1},{2,18},{18,2},{3,19},{19,3},{4,20},{20... | collective-permute-start | bytes 1867784 | tf_op jit(solution)/shard_map/ppermute | solution.py:207
  192.8 11.3 %collective-permute-done.13.refs_1_ = bf16[8,304,128]{2,1,0:T(8,128)(2,1)S(1)} collective-permute-done((bf16[8,304,128]{2,1,0:T(8,128)(2,1)S(1)}, bf16[8,304,128]{2,1,0:T(8,128)(2,1)S(1)}, u32[]{:S(2)}, u32[]{:S(2)}) %collective-permute-start.13) | collective-permute-done | bytes 622624 | tf_op jit(solution)/shard_map/ppermute | solution.py:207
  204.1 2.9 %collective-permute-start.15 = (bf16[8,304,128]{2,1,0:T(8,128)(2,1)S(1)}, bf16[8,304,128]{2,1,0:T(8,128)(2,1)S(1)}, u32[]{:S(2)}, u32[]{:S(2)}) collective-permute-start(bf16[8,304,128]{2,1,0:T(8,128)(2,1)S(1)} %collective-permute-done.13.refs_1_), channel_id=1, source_target_pairs={{0,16},{16,0},{1,17},{17,1},{2,18},{18,2},{3,19},{19,3},{4,20},{20... | collective-permute-start | bytes 1867784 | tf_op jit(solution)/shard_map/ppermute | solution.py:207
  207.0 1.9 collective-permute-start.16
  209.0 1.9 collective-permute-done.16.refs_5_
  210.9 0.8 copy-done.9
  211.8 6.5 %shard_map.69 = f32[32,8,128]{2,1,0:T(8,128)} custom-call(s32[3]{0:T(128)} %pad_add_fusion.refs_0_.me, bf16[16,512,256]{2,1,0:T(8,128)(2,1)} %get-tuple-element.40.source, f32[448,512]{1,0:T(8,128)} %get-tuple-element.44.bend_in, f32[448,512]{1,0:T(8,128)} %shard_map.68.own_in, bf16[8,304,128]{2,1,0:T(8,128)(2,1)} %copy-done.1, ...), custom_call_target="tpu_custom_call" | custom-call | flops 1879048192 | bytes 9830412 | tf_op jit(solution)/shard_map/pallas_call | solution.py:28
  218.3 8.3 %all-to-all-start.5 = ((f32[32,8,128]{2,1,0:T(8,128)}), f32[32,8,128]{2,1,0:T(8,128)S(1)}, u32[]{:S(2)}, u32[]{:S(2)}) async-start(f32[32,8,128]{2,1,0:T(8,128)} %shard_map.69), calls=%async_computation.5 | async-start | bytes 262144 | tf_op jit(solution)/shard_map/all_to_all | solution.py:300
  226.7 0.7 maximum_bitcast_fusion
  227.3 8.6 %all-to-all-done.5 = f32[32,8,128]{2,1,0:T(8,128)S(1)} async-done(((f32[32,8,128]{2,1,0:T(8,128)}), f32[32,8,128]{2,1,0:T(8,128)S(1)}, u32[]{:S(2)}, u32[]{:S(2)}) %all-to-all-start.5) | async-done | bytes 131104 | tf_op jit(solution)/shard_map/all_to_all | solution.py:300
  236.0 0.6 slice_multiply_fusion
  (57 shorter events, 0.9 us)
Async XLA Ops:
  0.6 12.9 %copy-start.10 = (bf16[128,448]{0,1:T(8,128)(2,1)S(1)}, bf16[128,448]{0,1:T(8,128)(2,1)}, u32[]{:S(2)}) copy-start(bf16[128,448]{0,1:T(8,128)(2,1)} %param.5) | copy-start | bytes 344068
  2.7 34.2 %all-to-all-start = ((bf16[4,512,256]{2,1,0:T(8,128)(2,1)}), bf16[4,512,256]{2,1,0:T(8,128)(2,1)S(1)}, u32[]{:S(2)}, u32[]{:S(2)}) async-start(bf16[4,512,256]{2,1,0:T(8,128)(2,1)} %broadcast_in_dim.6), calls=%async_computation | async-start | bytes 2097152 | tf_op jit(solution)/shard_map/all_to_all | solution.py:212
  36.8 49.2 %copy-start.5 = (bf16[3584,128]{1,0:T(8,128)(2,1)}, bf16[3584,128]{1,0:T(8,128)(2,1)S(1)}, u32[]{:S(2)}) copy-start(bf16[3584,128]{1,0:T(8,128)(2,1)S(1)} %all-gather) | copy-start | bytes 2752516
  36.9 49.2 %copy-start = (bf16[4,512,256]{2,1,0:T(8,128)(2,1)}, bf16[4,512,256]{2,1,0:T(8,128)(2,1)S(1)}, u32[]{:S(2)}) copy-start(bf16[4,512,256]{2,1,0:T(8,128)(2,1)S(1)} %all-to-all-done.refs_1_) | copy-start | bytes 3145732
  36.9 20.0 %collective-permute-start.3 = (bf16[2,512,256]{2,1,0:T(8,128)(2,1)S(1)}, bf16[2,512,256]{2,1,0:T(8,128)(2,1)S(1)}, u32[]{:S(2)}, u32[]{:S(2)}) collective-permute-start(bf16[2,512,256]{2,1,0:T(8,128)(2,1)S(1)} %get-tuple-element.47), channel_id=1, source_target_pairs={{0,3},{1,0},{2,1},{3,2},{4,7},{5,4},{6,5},{7,6},{8,11},{9,8},{10,9... | collective-permute-start | bytes 1572872 | tf_op jit(solution)/shard_map/ppermute | solution.py:226
  41.3 19.0 %collective-permute-start = (bf16[2,512,256]{2,1,0:T(8,128)(2,1)S(1)}, bf16[2,512,256]{2,1,0:T(8,128)(2,1)S(1)}, u32[]{:S(2)}, u32[]{:S(2)}) collective-permute-start(bf16[2,512,256]{2,1,0:T(8,128)(2,1)S(1)} %get-tuple-element.48), channel_id=1, source_target_pairs={{0,1},{1,2},{2,3},{3,0},{4,5},{5,6},{6,7},{7,4},{8,9},{9,10},{10,1... | collective-permute-start | bytes 1572872 | tf_op jit(solution)/shard_map/ppermute | solution.py:226
  43.3 32.1 %collective-permute-start.4 = (bf16[8,448,128]{2,1,0:T(8,128)(2,1)S(1)}, bf16[8,448,128]{2,1,0:T(8,128)(2,1)S(1)}, u32[]{:S(2)}, u32[]{:S(2)}) collective-permute-start(bf16[8,448,128]{2,1,0:T(8,128)(2,1)S(1)} %bitcast.21), channel_id=1, source_target_pairs={{0,32},{32,0},{1,33},{33,1},{2,34},{34,2},{3,35},{35,3},{4,36},{36... | collective-permute-start | bytes 2752520 | tf_op jit(solution)/shard_map/ppermute | solution.py:207
  50.4 17.1 %collective-permute-start.1 = (bf16[2,512,256]{2,1,0:T(8,128)(2,1)S(1)}, bf16[2,512,256]{2,1,0:T(8,128)(2,1)S(1)}, u32[]{:S(2)}, u32[]{:S(2)}) collective-permute-start(bf16[2,512,256]{2,1,0:T(8,128)(2,1)S(1)} %get-tuple-element.47), channel_id=1, source_target_pairs={{0,1},{1,2},{2,3},{3,0},{4,5},{5,6},{6,7},{7,4},{8,9},{9,10},{10,1... | collective-permute-start | bytes 1572872 | tf_op jit(solution)/shard_map/ppermute | solution.py:226
  52.5 15.0 %collective-permute-start.2 = (bf16[2,512,256]{2,1,0:T(8,128)(2,1)S(1)}, bf16[2,512,256]{2,1,0:T(8,128)(2,1)S(1)}, u32[]{:S(2)}, u32[]{:S(2)}) collective-permute-start(bf16[2,512,256]{2,1,0:T(8,128)(2,1)S(1)} %get-tuple-element.48), channel_id=1, source_target_pairs={{0,3},{1,0},{2,1},{3,2},{4,7},{5,4},{6,5},{7,6},{8,11},{9,8},{10,9... | collective-permute-start | bytes 1572872 | tf_op jit(solution)/shard_map/ppermute | solution.py:226
  56.9 29.1 %copy-start.12 = (bf16[2,512,256]{2,1,0:T(8,128)(2,1)}, bf16[2,512,256]{2,1,0:T(8,128)(2,1)S(1)}, u32[]{:S(2)}) copy-start(bf16[2,512,256]{2,1,0:T(8,128)(2,1)S(1)} %collective-permute-done.3.refs_4_) | copy-start | bytes 1572868
  57.0 20.1 %collective-permute-start.6 = (bf16[2,512,256]{2,1,0:T(8,128)(2,1)S(1)}, bf16[2,512,256]{2,1,0:T(8,128)(2,1)S(1)}, u32[]{:S(2)}, u32[]{:S(2)}) collective-permute-start(bf16[2,512,256]{2,1,0:T(8,128)(2,1)S(1)} %collective-permute-done.3.refs_4_), channel_id=1, source_target_pairs={{0,3},{1,0},{2,1},{3,2},{4,7},{5,4},{6,5},{7,6},{8,11},{9,8},{10,9... | collective-permute-start | bytes 1572872 | tf_op jit(solution)/shard_map/ppermute | solution.py:226
  60.3 16.7 %copy-start.13 = (bf16[2,512,256]{2,1,0:T(8,128)(2,1)}, bf16[2,512,256]{2,1,0:T(8,128)(2,1)S(1)}, u32[]{:S(2)}) copy-start(bf16[2,512,256]{2,1,0:T(8,128)(2,1)S(1)} %collective-permute-done.refs_2_) | copy-start | bytes 1572868
  60.3 18.4 %collective-permute-start.5 = (bf16[2,512,256]{2,1,0:T(8,128)(2,1)S(1)}, bf16[2,512,256]{2,1,0:T(8,128)(2,1)S(1)}, u32[]{:S(2)}, u32[]{:S(2)}) collective-permute-start(bf16[2,512,256]{2,1,0:T(8,128)(2,1)S(1)} %collective-permute-done.refs_2_), channel_id=1, source_target_pairs={{0,1},{1,2},{2,3},{3,0},{4,5},{5,6},{6,7},{7,4},{8,9},{9,10},{10,1... | collective-permute-start | bytes 1572872 | tf_op jit(solution)/shard_map/ppermute | solution.py:226
  67.5 11.2 %copy-start.14 = (bf16[2,512,256]{2,1,0:T(8,128)(2,1)}, bf16[2,512,256]{2,1,0:T(8,128)(2,1)S(1)}, u32[]{:S(2)}) copy-start(bf16[2,512,256]{2,1,0:T(8,128)(2,1)S(1)} %collective-permute-done.1.refs_3_) | copy-start | bytes 1572868
  67.5 16.3 %copy-start.15 = (bf16[2,512,256]{2,1,0:T(8,128)(2,1)}, bf16[2,512,256]{2,1,0:T(8,128)(2,1)S(1)}, u32[]{:S(2)}) copy-start(bf16[2,512,256]{2,1,0:T(8,128)(2,1)S(1)} %collective-permute-done.2.refs_5_) | copy-start | bytes 1572868
  67.5 17.0 %collective-permute-start.7 = (bf16[8,448,128]{2,1,0:T(8,128)(2,1)S(1)}, bf16[8,448,128]{2,1,0:T(8,128)(2,1)}, u32[]{:S(2)}, u32[]{:S(2)}) collective-permute-start(bf16[8,448,128]{2,1,0:T(8,128)(2,1)S(1)} %bitcast.22), channel_id=1, source_target_pairs={{0,16},{16,0},{1,17},{17,1},{2,18},{18,2},{3,19},{19,3},{4,20},{20... | collective-permute-start | bytes 2752520 | tf_op jit(solution)/shard_map/ppermute | solution.py:207
  75.4 10.7 %copy-start.11 = (bf16[8,448,128]{2,1,0:T(8,128)(2,1)}, bf16[8,448,128]{2,1,0:T(8,128)(2,1)S(1)}, u32[]{:S(2)}) copy-start(bf16[8,448,128]{2,1,0:T(8,128)(2,1)S(1)} %collective-permute-done.4.refs_11_) | copy-start | bytes 2752516
  77.0 6.8 %copy-start.16 = (bf16[2,512,256]{2,1,0:T(8,128)(2,1)}, bf16[2,512,256]{2,1,0:T(8,128)(2,1)S(1)}, u32[]{:S(2)}) copy-start(bf16[2,512,256]{2,1,0:T(8,128)(2,1)S(1)} %collective-permute-done.6.refs_7_) | copy-start | bytes 1572868
  78.8 5.1 %copy-start.17 = (bf16[2,512,256]{2,1,0:T(8,128)(2,1)}, bf16[2,512,256]{2,1,0:T(8,128)(2,1)S(1)}, u32[]{:S(2)}) copy-start(bf16[2,512,256]{2,1,0:T(8,128)(2,1)S(1)} %collective-permute-done.5.refs_6_) | copy-start | bytes 1572868
  78.8 7.3 %collective-permute-start.8 = (bf16[8,448,128]{2,1,0:T(8,128)(2,1)S(1)}, bf16[8,448,128]{2,1,0:T(8,128)(2,1)}, u32[]{:S(2)}, u32[]{:S(2)}) collective-permute-start(bf16[8,448,128]{2,1,0:T(8,128)(2,1)S(1)} %collective-permute-done.4.refs_11_), channel_id=1, source_target_pairs={{0,16},{16,0},{1,17},{17,1},{2,18},{18,2},{3,19},{19,3},{4,20},{20... | collective-permute-start | bytes 2752520 | tf_op jit(solution)/shard_map/ppermute | solution.py:207
  95.6 4.4 %collective-permute-start.9 = (bf16[8,2,192,128]{3,2,1,0:T(8,128)(2,1)}, bf16[8,2,192,128]{3,2,1,0:T(8,128)(2,1)S(1)}, u32[]{:S(2)}, u32[]{:S(2)}) collective-permute-start(bf16[8,2,192,128]{3,2,1,0:T(8,128)(2,1)} %get-tuple-element.35.b1), channel_id=1, source_target_pairs={{0,16},{16,0},{1,17},{17,1},{2,18},{18,2},{3,19},{19,3},{4,20},{20... | collective-permute-start | bytes 2359304 | tf_op jit(solution)/shard_map/ppermute | solution.py:207
  97.9 4.8 %collective-permute-start.10 = (bf16[2,8,256,128]{3,2,1,0:T(8,128)(2,1)}, bf16[2,8,256,128]{3,2,1,0:T(8,128)(2,1)S(1)}, u32[]{:S(2)}, u32[]{:S(2)}) collective-permute-start(bf16[2,8,256,128]{3,2,1,0:T(8,128)(2,1)} %get-tuple-element.36.sent), channel_id=1, source_target_pairs={{0,16},{16,0},{1,17},{17,1},{2,18},{18,2},{3,19},{19,3},{4,20},{20... | collective-permute-start | bytes 3145736 | tf_op jit(solution)/shard_map/ppermute | solution.py:207
  100.0 8.0 %copy-start.3 = (bf16[8,256,128]{2,1,0:T(8,128)(2,1)S(1)}, bf16[8,256,128]{2,1,0:T(8,128)(2,1)}, u32[]{:S(2)}) copy-start(bf16[8,256,128]{2,1,0:T(8,128)(2,1)} %get-tuple-element.38.a1) | copy-start | bytes 1572868
  102.7 28.9 %all-to-all-start.1 = ((bf16[8,2,192,128]{3,2,1,0:T(8,128)(2,1)}), bf16[8,2,192,128]{3,2,1,0:T(8,128)(2,1)S(1)}, u32[]{:S(2)}, u32[]{:S(2)}) async-start(bf16[8,2,192,128]{3,2,1,0:T(8,128)(2,1)} %add_convert_fusion), calls=%async_computation.1 | async-start | bytes 1572864 | tf_op jit(solution)/shard_map/all_to_all | solution.py:269
  108.2 19.9 %collective-permute-start.11 = (bf16[8,256,128]{2,1,0:T(8,128)(2,1)S(1)}, bf16[8,256,128]{2,1,0:T(8,128)(2,1)S(1)}, u32[]{:S(2)}, u32[]{:S(2)}) collective-permute-start(bf16[8,256,128]{2,1,0:T(8,128)(2,1)S(1)} %fusion), channel_id=1, source_target_pairs={{0,32},{32,0},{1,33},{33,1},{2,34},{34,2},{3,35},{35,3},{4,36},{36... | collective-permute-start | bytes 1572872 | tf_op jit(solution)/shard_map/ppermute | solution.py:207
  116.2 11.9 %copy-start.4 = (bf16[8,256,128]{2,1,0:T(8,128)(2,1)S(1)}, bf16[8,256,128]{2,1,0:T(8,128)(2,1)}, u32[]{:S(2)}) copy-start(bf16[8,256,128]{2,1,0:T(8,128)(2,1)} %get-tuple-element.33.a0) | copy-start | bytes 1572868
  131.6 19.8 %all-to-all-start.2 = ((bf16[8,256,128]{2,1,0:T(8,128)(2,1)}), bf16[8,256,128]{2,1,0:T(8,128)(2,1)S(1)}, u32[]{:S(2)}, u32[]{:S(2)}) async-start(bf16[8,256,128]{2,1,0:T(8,128)(2,1)} %fusion.2), calls=%async_computation.2 | async-start | bytes 1048576 | tf_op jit(solution)/shard_map/all_to_all | solution.py:281
  135.5 10.5 %collective-permute-start.12 = (bf16[2,192,128]{2,1,0:T(8,128)(2,1)S(1)}, bf16[2,192,128]{2,1,0:T(8,128)(2,1)S(1)}, u32[]{:S(2)}, u32[]{:S(2)}) collective-permute-start(bf16[2,192,128]{2,1,0:T(8,128)(2,1)S(1)} %reduce_sum.34), channel_id=1, source_target_pairs={{0,32},{32,0},{1,33},{33,1},{2,34},{34,2},{3,35},{35,3},{4,36},{36... | collective-permute-start | bytes 294920 | tf_op jit(solution)/shard_map/ppermute | solution.py:207
  152.5 21.1 %all-to-all-start.3 = ((bf16[8,304,128]{2,1,0:T(8,128)(2,1)}), bf16[8,304,128]{2,1,0:T(8,128)(2,1)S(1)}, u32[]{:S(2)}, u32[]{:S(2)}) async-start(bf16[8,304,128]{2,1,0:T(8,128)(2,1)} %broadcast_in_dim.7), calls=%async_computation.3 | async-start | bytes 1245184 | tf_op jit(solution)/shard_map/all_to_all | solution.py:212
  173.6 38.2 %copy-start.1 = (bf16[8,304,128]{2,1,0:T(8,128)(2,1)}, bf16[8,304,128]{2,1,0:T(8,128)(2,1)S(1)}, u32[]{:S(2)}) copy-start(bf16[8,304,128]{2,1,0:T(8,128)(2,1)S(1)} %all-to-all-done.3.refs_0_) | copy-start | bytes 1867780
  174.6 32.4 %all-to-all-start.4 = ((bf16[8,2,144,128]{3,2,1,0:T(8,128)(2,1)}), bf16[8,2,144,128]{3,2,1,0:T(8,128)(2,1)S(1)}, u32[]{:S(2)}, u32[]{:S(2)}) async-start(bf16[8,2,144,128]{3,2,1,0:T(8,128)(2,1)} %broadcast_in_dim.8), calls=%async_computation.4 | async-start | bytes 1179648 | tf_op jit(solution)/shard_map/all_to_all | solution.py:212
  178.2 25.9 %collective-permute-start.13 = (bf16[8,304,128]{2,1,0:T(8,128)(2,1)S(1)}, bf16[8,304,128]{2,1,0:T(8,128)(2,1)S(1)}, u32[]{:S(2)}, u32[]{:S(2)}) collective-permute-start(bf16[8,304,128]{2,1,0:T(8,128)(2,1)S(1)} %all-to-all-done.3.refs_0_), channel_id=1, source_target_pairs={{0,32},{32,0},{1,33},{33,1},{2,34},{34,2},{3,35},{35,3},{4,36},{36... | collective-permute-start | bytes 1867784 | tf_op jit(solution)/shard_map/ppermute | solution.py:207
  190.1 18.8 %collective-permute-start.14 = (bf16[8,304,128]{2,1,0:T(8,128)(2,1)S(1)}, bf16[8,304,128]{2,1,0:T(8,128)(2,1)S(1)}, u32[]{:S(2)}, u32[]{:S(2)}) collective-permute-start(bf16[8,304,128]{2,1,0:T(8,128)(2,1)S(1)} %all-to-all-done.3.refs_0_), channel_id=1, source_target_pairs={{0,16},{16,0},{1,17},{17,1},{2,18},{18,2},{3,19},{19,3},{4,20},{20... | collective-permute-start | bytes 1867784 | tf_op jit(solution)/shard_map/ppermute | solution.py:207
  204.1 7.7 %copy-start.6 = (bf16[8,304,128]{2,1,0:T(8,128)(2,1)}, bf16[8,304,128]{2,1,0:T(8,128)(2,1)S(1)}, u32[]{:S(2)}) copy-start(bf16[8,304,128]{2,1,0:T(8,128)(2,1)S(1)} %collective-permute-done.13.refs_1_) | copy-start | bytes 1867780
  204.1 4.9 %collective-permute-start.15 = (bf16[8,304,128]{2,1,0:T(8,128)(2,1)S(1)}, bf16[8,304,128]{2,1,0:T(8,128)(2,1)S(1)}, u32[]{:S(2)}, u32[]{:S(2)}) collective-permute-start(bf16[8,304,128]{2,1,0:T(8,128)(2,1)S(1)} %collective-permute-done.13.refs_1_), channel_id=1, source_target_pairs={{0,16},{16,0},{1,17},{17,1},{2,18},{18,2},{3,19},{19,3},{4,20},{20... | collective-permute-start | bytes 1867784 | tf_op jit(solution)/shard_map/ppermute | solution.py:207
  207.0 4.8 %copy-start.2 = (bf16[8,2,144,128]{3,2,1,0:T(8,128)(2,1)}, bf16[8,2,144,128]{3,2,1,0:T(8,128)(2,1)S(1)}, u32[]{:S(2)}) copy-start(bf16[8,2,144,128]{3,2,1,0:T(8,128)(2,1)S(1)} %all-to-all-done.4.refs_4_) | copy-start | bytes 1769476
  207.0 3.9 %collective-permute-start.16 = (bf16[8,2,144,128]{3,2,1,0:T(8,128)(2,1)S(1)}, bf16[8,2,144,128]{3,2,1,0:T(8,128)(2,1)S(1)}, u32[]{:S(2)}, u32[]{:S(2)}) collective-permute-start(bf16[8,2,144,128]{3,2,1,0:T(8,128)(2,1)S(1)} %all-to-all-done.4.refs_4_), channel_id=1, source_target_pairs={{0,16},{16,0},{1,17},{17,1},{2,18},{18,2},{3,19},{19,3},{4,20},{20... | collective-permute-start | bytes 1769480 | tf_op jit(solution)/shard_map/ppermute | solution.py:207
  209.0 2.8 %copy-start.7 = (bf16[8,304,128]{2,1,0:T(8,128)(2,1)}, bf16[8,304,128]{2,1,0:T(8,128)(2,1)S(1)}, u32[]{:S(2)}) copy-start(bf16[8,304,128]{2,1,0:T(8,128)(2,1)S(1)} %collective-permute-done.14.refs_2_) | copy-start | bytes 1867780
  209.0 2.8 %copy-start.8 = (bf16[8,304,128]{2,1,0:T(8,128)(2,1)}, bf16[8,304,128]{2,1,0:T(8,128)(2,1)S(1)}, u32[]{:S(2)}) copy-start(bf16[8,304,128]{2,1,0:T(8,128)(2,1)S(1)} %collective-permute-done.15.refs_3_) | copy-start | bytes 1867780
  210.9 0.8 copy-start.9
  218.3 17.6 %all-to-all-start.5 = ((f32[32,8,128]{2,1,0:T(8,128)}), f32[32,8,128]{2,1,0:T(8,128)S(1)}, u32[]{:S(2)}, u32[]{:S(2)}) async-start(f32[32,8,128]{2,1,0:T(8,128)} %shard_map.69), calls=%async_computation.5 | async-start | bytes 262144 | tf_op jit(solution)/shard_map/all_to_all | solution.py:300

commit v9 on v6

--- a/solution.py
+++ b/solution.py
@@ -70,7 +70,7 @@
 
 
 def first_kernel(*refs):
-    me, t0, p1, p2, m1, m2, f1, f2, up_in, cot_in, w0, w1, w2, w3 = refs[:14]
+    me, t0, p1, p2, m1, m2, f1, f2, up_in, cot_in, *weights = refs[:14]
     tok_out, bend_out, *outs = refs[14:21]
     tok, held, up, cot, coeff, bend, acc, own, own_b, tok_sems, w_sems, in_sems, out_sems, sems = refs[21:]
     mine, first = me[0], me[1] == 0
@@ -83,7 +83,7 @@
     for z in range(4):
         for d in range(4):
             token_copy(d, z).start()
-    w_ready = fetched([(w, held.at[i]) for i, w in enumerate((w0, w1, w2, w3))], w_sems)
+    w_ready = fetched([(w, held.at[i]) for i, w in enumerate(weights)], w_sems)
     get_up = pltpu.make_async_copy(up_in, up, in_sems.at[0])
     get_cot = pltpu.make_async_copy(cot_in, cot, in_sems.at[1])
     get_up.start()
@@ -194,8 +194,12 @@
         off = own[:, lanes] - mean
         c += b * mean * mean
         s += b * off * off
-    sums[0:1, :] = jnp.sum(c.T, axis=0, keepdims=True)
-    sums[1:2, :] = jnp.sum(s.T, axis=0, keepdims=True)
+    for k, terms in enumerate((c, s)):
+        line = jnp.sum(terms.T, axis=0, keepdims=True)
+        line = jnp.concatenate([line, jnp.zeros((1, 64), F32)], 1)
+        for i in range(4):
+            row = line[:, 128 * i : 128 * i + 128]
+            sums[:, 4 * k + i : 4 * k + i + 1, :] = jnp.broadcast_to(row[None], (32, 1, 128))
 
 
 def swap(value, axis):
@@ -281,13 +285,13 @@
     rows = (u0, u1, swap(u0, "c"), swap(u1, "c"), v0, swap(v0, "c"))
     line = call(
         mean_kernel,
-        [shape(2, 448, dtype=F32)],
+        [shape(32, 8, 128, dtype=F32)],
         (me, tok, bend, own, *rows),
         flops,
         [*[ACC] * 3, TOK, *held, *map(dma, ((1, 2), (6, 2), (2,)))],
         True,
     )[0]
-    whole = jnp.sum(to_all(line, REP), axis=0)
+    whole = jnp.sum(lax.all_to_all(line, REP, 0, 0, tiled=True), axis=0).reshape(2, 512)[:, :448]
     grad = jnp.concatenate([grad_a, both_b[0]], axis=0).T
     return grad, whole[0], whole[1] / 31
 

time: 234 us -> 233 us (level)
    all_to_all x0 -> x1, waiting for transfers between devices: none -> 8.59 us  [shards(): lax.all_to_all(line, REP, 0, 0, tiled=True)]
    all_to_all x4 -> x3, waiting for transfers between devices: 20.5 us -> 11.9 us  [to_all(): lax.all_to_all(jnp.broadcast_to(value[None], (count, *value.shape)), axis...]
    all_to_all x0 -> x1, starting transfers between devices: none -> 7.26 us  [shards(): lax.all_to_all(line, REP, 0, 0, tiled=True)]
    all_to_all x4 -> x3, starting transfers between devices: 25.3 us -> 18.1 us  [to_all(): lax.all_to_all(jnp.broadcast_to(value[None], (count, *value.shape)), axis...]
    broadcast_in_dim x4 -> x3, local copies, waits for them, and re-layouts: 5.36 us -> 4 us  [to_all(): jnp.broadcast_to(value[None], (count, *value.shape))]
where the time goes in v9:
time: 233 us; the launch traced here: 232 us
  starting transfers between devices  99.6 us (43%)
  waiting for transfers between devices  51.1 us (22%)
  blocking collectives  47.2 us (20%)
  Pallas kernels  22.7 us (10%)
  other arithmetic  5.5 us (2%)
  local copies, waits for them, and re-layouts  4.97 us (2%)
    ppermute x11, starting transfers between devices, swap(): return lax.ppermute(value, axis, ((0, 1), (1, 0)))  50.8 us
    all_to_all x1, blocking collectives, shards(): across_a = lax.all_to_all(sums_a, 'y', 0, 0, tiled=True)  23.9 us
    all_gather x1, blocking collectives, shards(): w0 = lax.all_gather(gate_weight.T, 'y', axis=0)  23.3 us
    pallas_call x3, Pallas kernels, call(): pl.pallas_call(kernel, out_shape=outs, in_specs=[SM] + [ANY] * (len(opera...  22.7 us
    ppermute x11, waiting for transfers between devices, swap(): return lax.ppermute(value, axis, ((0, 1), (1, 0)))  21.9 us
    ppermute x6, starting transfers between devices, along_x(): return lax.ppermute(value, 'x', [(i, (i + by) % 4) for i in range(4)])  18.1 us
    all_to_all x3, starting transfers between devices, to_all(): lax.all_to_all(jnp.broadcast_to(value[None], (count, *value.shape)), axis...  18.1 us
    all_to_all x3, waiting for transfers between devices, to_all(): lax.all_to_all(jnp.broadcast_to(value[None], (count, *value.shape)), axis...  11.9 us
  transfers between devices with their start and end apart: 22, of which 11 were waited for; matrix products, arithmetic and copies ran while one was open for 2% of the time, Pallas kernels for 3%

profile of v9, /device:TPU:1, one launch (start us, length us, event | category | flops | bytes accessed | tf_op | source)
XLA Modules:
  0.0 232.0 jit_solution(8968412739979607107)
XLA Ops:
  0.6 2.0 broadcast_in_dim.6
  2.6 11.0 %all-to-all-start = ((bf16[4,512,256]{2,1,0:T(8,128)(2,1)}), bf16[4,512,256]{2,1,0:T(8,128)(2,1)S(1)}, u32[]{:S(2)}, u32[]{:S(2)}) async-start(bf16[4,512,256]{2,1,0:T(8,128)(2,1)} %broadcast_in_dim.6), calls=%async_computation | async-start | bytes 2097152 | tf_op jit(solution)/shard_map/all_to_all | solution.py:211
  13.6 23.3 %all-gather = bf16[3584,128]{1,0:T(8,128)(2,1)S(1)} all-gather(bf16[448,128]{1,0:T(8,128)(2,1)S(1)} %bitcast.22), channel_id=2, replica_groups=mesh['y'=8,'zl'=2,'c'=2,'zh'=4,'x'=4] {'y'}, dimensions={0}, use_global_device_ids=true | all-gather | bytes 1032192 | tf_op jit(solution)/shard_map/all_gather | solution.py:234
  37.0 4.4 %collective-permute-start.3 = (bf16[2,512,256]{2,1,0:T(8,128)(2,1)S(1)}, bf16[2,512,256]{2,1,0:T(8,128)(2,1)S(1)}, u32[]{:S(2)}, u32[]{:S(2)}) collective-permute-start(bf16[2,512,256]{2,1,0:T(8,128)(2,1)S(1)} %get-tuple-element.47), channel_id=1, source_target_pairs={{0,3},{1,0},{2,1},{3,2},{4,7},{5,4},{6,5},{7,6},{8,11},{9,8},{10,9... | collective-permute-start | bytes 1572872 | tf_op jit(solution)/shard_map/ppermute | solution.py:225
  41.4 1.9 collective-permute-start
  43.3 7.2 %collective-permute-start.4 = (bf16[8,448,128]{2,1,0:T(8,128)(2,1)S(1)}, bf16[8,448,128]{2,1,0:T(8,128)(2,1)S(1)}, u32[]{:S(2)}, u32[]{:S(2)}) collective-permute-start(bf16[8,448,128]{2,1,0:T(8,128)(2,1)S(1)} %bitcast.19), channel_id=1, source_target_pairs={{0,32},{32,0},{1,33},{33,1},{2,34},{34,2},{3,35},{35,3},{4,36},{36... | collective-permute-start | bytes 2752520 | tf_op jit(solution)/shard_map/ppermute | solution.py:206
  50.5 2.1 collective-permute-start.1
  52.6 4.4 %collective-permute-start.2 = (bf16[2,512,256]{2,1,0:T(8,128)(2,1)S(1)}, bf16[2,512,256]{2,1,0:T(8,128)(2,1)S(1)}, u32[]{:S(2)}, u32[]{:S(2)}) collective-permute-start(bf16[2,512,256]{2,1,0:T(8,128)(2,1)S(1)} %get-tuple-element.48), channel_id=1, source_target_pairs={{0,3},{1,0},{2,1},{3,2},{4,7},{5,4},{6,5},{7,6},{8,11},{9,8},{10,9... | collective-permute-start | bytes 1572872 | tf_op jit(solution)/shard_map/ppermute | solution.py:225
  57.0 3.4 %collective-permute-start.6 = (bf16[2,512,256]{2,1,0:T(8,128)(2,1)S(1)}, bf16[2,512,256]{2,1,0:T(8,128)(2,1)S(1)}, u32[]{:S(2)}, u32[]{:S(2)}) collective-permute-start(bf16[2,512,256]{2,1,0:T(8,128)(2,1)S(1)} %collective-permute-done.3.refs_4_), channel_id=1, source_target_pairs={{0,3},{1,0},{2,1},{3,2},{4,7},{5,4},{6,5},{7,6},{8,11},{9,8},{10,9... | collective-permute-start | bytes 1572872 | tf_op jit(solution)/shard_map/ppermute | solution.py:225
  60.4 1.9 collective-permute-start.5
  62.4 5.3 %collective-permute-done.1.refs_3_ = bf16[2,512,256]{2,1,0:T(8,128)(2,1)S(1)} collective-permute-done((bf16[2,512,256]{2,1,0:T(8,128)(2,1)S(1)}, bf16[2,512,256]{2,1,0:T(8,128)(2,1)S(1)}, u32[]{:S(2)}, u32[]{:S(2)}) %collective-permute-start.1) | collective-permute-done | bytes 524320 | tf_op jit(solution)/shard_map/ppermute | solution.py:225
  67.6 7.8 %collective-permute-start.7 = (bf16[8,448,128]{2,1,0:T(8,128)(2,1)S(1)}, bf16[8,448,128]{2,1,0:T(8,128)(2,1)}, u32[]{:S(2)}, u32[]{:S(2)}) collective-permute-start(bf16[8,448,128]{2,1,0:T(8,128)(2,1)S(1)} %bitcast.20), channel_id=1, source_target_pairs={{0,16},{16,0},{1,17},{17,1},{2,18},{18,2},{3,19},{19,3},{4,20},{20... | collective-permute-start | bytes 2752520 | tf_op jit(solution)/shard_map/ppermute | solution.py:206
  75.5 1.6 collective-permute-done.6.refs_7_
  77.1 1.8 collective-permute-done.5.refs_6_
  78.9 5.1 %collective-permute-start.8 = (bf16[8,448,128]{2,1,0:T(8,128)(2,1)S(1)}, bf16[8,448,128]{2,1,0:T(8,128)(2,1)}, u32[]{:S(2)}, u32[]{:S(2)}) collective-permute-start(bf16[8,448,128]{2,1,0:T(8,128)(2,1)S(1)} %collective-permute-done.4.refs_11_), channel_id=1, source_target_pairs={{0,16},{16,0},{1,17},{17,1},{2,18},{18,2},{3,19},{19,3},{4,20},{20... | collective-permute-start | bytes 2752520 | tf_op jit(solution)/shard_map/ppermute | solution.py:206
  84.0 0.6 pad_add_fusion.refs_0_.me
  84.5 1.6 collective-permute-done.8.refs_13_
  86.1 9.6 %shard_map.67 = (bf16[16,512,256]{2,1,0:T(8,128)(2,1)}, f32[448,512]{1,0:T(8,128)}, bf16[8,304,128]{2,1,0:T(8,128)(2,1)}, bf16[8,304,128]{2,1,0:T(8,128)(2,1)}, ...) custom-call(s32[3]{0:T(128)} %pad_add_fusion.refs_0_.me, ...), custom_call_target="tpu_custom_call" | custom-call | flops 3758096384 | bytes 17563660 | tf_op jit(solution)/shard_map/pallas_call | solution.py:27
  95.7 2.3 collective-permute-start.10
  98.0 2.0 collective-permute-start.9
  100.1 2.1 collective-permute-done.9
  102.1 2.2 add_convert_fusion
  104.3 5.3 %all-to-all-start.1 = ((bf16[8,2,144,128]{3,2,1,0:T(8,128)(2,1)}), bf16[8,2,144,128]{3,2,1,0:T(8,128)(2,1)S(1)}, u32[]{:S(2)}, u32[]{:S(2)}) async-start(bf16[8,2,144,128]{3,2,1,0:T(8,128)(2,1)} %add_convert_fusion), calls=%async_computation.1 | async-start | bytes 1179648 | tf_op jit(solution)/shard_map/all_to_all | solution.py:265
  109.6 1.1 fusion
  110.7 8.0 %collective-permute-start.11 = (bf16[8,304,128]{2,1,0:T(8,128)(2,1)}, bf16[8,304,128]{2,1,0:T(8,128)(2,1)S(1)}, u32[]{:S(2)}, u32[]{:S(2)}) collective-permute-start(bf16[8,304,128]{2,1,0:T(8,128)(2,1)} %fusion), channel_id=1, source_target_pairs={{0,32},{32,0},{1,33},{33,1},{2,34},{34,2},{3,35},{35,3},{4,36},{36... | collective-permute-start | bytes 1867784 | tf_op jit(solution)/shard_map/ppermute | solution.py:206
  118.6 6.6 %shard_map.68.own_in = f32[448,512]{1,0:T(8,128)} custom-call(s32[3]{0:T(128)} %pad_add_fusion.refs_0_.me, bf16[16,512,256]{2,1,0:T(8,128)(2,1)} %get-tuple-element.40.source, bf16[8,304,128]{2,1,0:T(8,128)(2,1)} %get-tuple-element.33.a0, bf16[8,304,128]{2,1,0:T(8,128)(2,1)} %get-tuple-element.38.a1, bf16[2,8,304,128]{3,2,1,0:T(8,128)(2,1)} %get-tuple-element.36.sent, ...), custom_call_target="tpu_custom_call" | custom-call | flops 1879048192 | bytes 8781836 | tf_op jit(solution)/shard_map/pallas_call | solution.py:27
  125.2 7.6 %collective-permute-done.11 = bf16[8,304,128]{2,1,0:T(8,128)(2,1)S(1)} collective-permute-done((bf16[8,304,128]{2,1,0:T(8,128)(2,1)}, bf16[8,304,128]{2,1,0:T(8,128)(2,1)S(1)}, u32[]{:S(2)}, u32[]{:S(2)}) %collective-permute-start.11) | collective-permute-done | bytes 622624 | tf_op jit(solution)/shard_map/ppermute | solution.py:206
  132.9 0.2 fusion.2
  133.1 23.9 %all_to_all.30 = bf16[8,304,128]{2,1,0:T(8,128)(2,1)S(1)} all-to-all(bf16[8,304,128]{2,1,0:T(8,128)(2,1)S(1)} %fusion.2), channel_id=1, replica_groups=mesh['y'=8,'zl'=2,'c'=2,'zh'=4,'x'=4] {'y'}, dimensions={0} | all-to-all | bytes 1245184 | tf_op jit(solution)/shard_map/all_to_all | solution.py:277
  157.1 0.9 broadcast_in_dim.7
  158.0 3.5 %all-to-all-start.3 = ((bf16[8,304,128]{2,1,0:T(8,128)(2,1)}), bf16[8,304,128]{2,1,0:T(8,128)(2,1)S(1)}, u32[]{:S(2)}, u32[]{:S(2)}) async-start(bf16[8,304,128]{2,1,0:T(8,128)(2,1)} %broadcast_in_dim.7), calls=%async_computation.3 | async-start | bytes 1245184 | tf_op jit(solution)/shard_map/all_to_all | solution.py:211
  161.6 2.4 %collective-permute-start.12 = (bf16[2,144,128]{2,1,0:T(8,128)(2,1)S(1)}, bf16[2,144,128]{2,1,0:T(8,128)(2,1)S(1)}, u32[]{:S(2)}, u32[]{:S(2)}) collective-permute-start(bf16[2,144,128]{2,1,0:T(8,128)(2,1)S(1)} %reduce_sum.34), channel_id=1, source_target_pairs={{0,32},{32,0},{1,33},{33,1},{2,34},{34,2},{3,35},{35,3},{4,36},{36... | collective-permute-start | bytes 221192 | tf_op jit(solution)/shard_map/ppermute | solution.py:206
  164.0 2.7 %collective-permute-done.12 = bf16[2,144,128]{2,1,0:T(8,128)(2,1)S(1)} collective-permute-done((bf16[2,144,128]{2,1,0:T(8,128)(2,1)S(1)}, bf16[2,144,128]{2,1,0:T(8,128)(2,1)S(1)}, u32[]{:S(2)}, u32[]{:S(2)}) %collective-permute-start.12) | collective-permute-done | bytes 73760 | tf_op jit(solution)/shard_map/ppermute | solution.py:206
  166.7 11.9 %all-to-all-done.3.refs_0_ = bf16[8,304,128]{2,1,0:T(8,128)(2,1)S(1)} async-done(((bf16[8,304,128]{2,1,0:T(8,128)(2,1)}), bf16[8,304,128]{2,1,0:T(8,128)(2,1)S(1)}, u32[]{:S(2)}, u32[]{:S(2)}) %all-to-all-start.3) | async-done | bytes 622624 | tf_op jit(solution)/shard_map/all_to_all | solution.py:211
  178.7 1.1 broadcast_in_dim.8
  179.8 3.5 %all-to-all-start.4 = ((bf16[8,2,144,128]{3,2,1,0:T(8,128)(2,1)}), bf16[8,2,144,128]{3,2,1,0:T(8,128)(2,1)S(1)}, u32[]{:S(2)}, u32[]{:S(2)}) async-start(bf16[8,2,144,128]{3,2,1,0:T(8,128)(2,1)} %broadcast_in_dim.8), calls=%async_computation.4 | async-start | bytes 1179648 | tf_op jit(solution)/shard_map/all_to_all | solution.py:211
  183.3 2.3 collective-permute-start.13
  185.6 5.7 %collective-permute-start.14 = (bf16[8,304,128]{2,1,0:T(8,128)(2,1)S(1)}, bf16[8,304,128]{2,1,0:T(8,128)(2,1)S(1)}, u32[]{:S(2)}, u32[]{:S(2)}) collective-permute-start(bf16[8,304,128]{2,1,0:T(8,128)(2,1)S(1)} %all-to-all-done.3.refs_0_), channel_id=1, source_target_pairs={{0,16},{16,0},{1,17},{17,1},{2,18},{18,2},{3,19},{19,3},{4,20},{20... | collective-permute-start | bytes 1867784 | tf_op jit(solution)/shard_map/ppermute | solution.py:206
  191.3 6.0 %collective-permute-done.13.refs_1_ = bf16[8,304,128]{2,1,0:T(8,128)(2,1)S(1)} collective-permute-done((bf16[8,304,128]{2,1,0:T(8,128)(2,1)S(1)}, bf16[8,304,128]{2,1,0:T(8,128)(2,1)S(1)}, u32[]{:S(2)}, u32[]{:S(2)}) %collective-permute-start.13) | collective-permute-done | bytes 622624 | tf_op jit(solution)/shard_map/ppermute | solution.py:206
  197.4 6.2 %collective-permute-start.15 = (bf16[8,304,128]{2,1,0:T(8,128)(2,1)S(1)}, bf16[8,304,128]{2,1,0:T(8,128)(2,1)S(1)}, u32[]{:S(2)}, u32[]{:S(2)}) collective-permute-start(bf16[8,304,128]{2,1,0:T(8,128)(2,1)S(1)} %collective-permute-done.13.refs_1_), channel_id=1, source_target_pairs={{0,16},{16,0},{1,17},{17,1},{2,18},{18,2},{3,19},{19,3},{4,20},{20... | collective-permute-start | bytes 1867784 | tf_op jit(solution)/shard_map/ppermute | solution.py:206
  203.6 1.9 collective-permute-start.16
  205.5 1.9 collective-permute-done.16.refs_5_
  207.5 0.8 copy-done.9
  208.3 6.5 %shard_map.69 = f32[32,8,128]{2,1,0:T(8,128)} custom-call(s32[3]{0:T(128)} %pad_add_fusion.refs_0_.me, bf16[16,512,256]{2,1,0:T(8,128)(2,1)} %get-tuple-element.40.source, f32[448,512]{1,0:T(8,128)} %get-tuple-element.44.bend_in, f32[448,512]{1,0:T(8,128)} %shard_map.68.own_in, bf16[8,304,128]{2,1,0:T(8,128)(2,1)} %copy-done.1, ...), custom_call_target="tpu_custom_call" | custom-call | flops 1879048192 | bytes 9830412 | tf_op jit(solution)/shard_map/pallas_call | solution.py:27
  214.8 7.3 %all-to-all-start.5 = ((f32[32,8,128]{2,1,0:T(8,128)}), f32[32,8,128]{2,1,0:T(8,128)S(1)}, u32[]{:S(2)}, u32[]{:S(2)}) async-start(f32[32,8,128]{2,1,0:T(8,128)} %shard_map.69), calls=%async_computation.5 | async-start | bytes 262144 | tf_op jit(solution)/shard_map/all_to_all | solution.py:294
  222.1 0.7 maximum_bitcast_fusion
  222.8 8.6 %all-to-all-done.5 = f32[32,8,128]{2,1,0:T(8,128)S(1)} async-done(((f32[32,8,128]{2,1,0:T(8,128)}), f32[32,8,128]{2,1,0:T(8,128)S(1)}, u32[]{:S(2)}, u32[]{:S(2)}) %all-to-all-start.5) | async-done | bytes 131104 | tf_op jit(solution)/shard_map/all_to_all | solution.py:294
  231.4 0.6 slice_multiply_fusion
  (53 shorter events, 0.4 us)
Async XLA Ops:
  2.6 11.0 %copy-start.10 = (bf16[128,448]{0,1:T(8,128)(2,1)S(1)}, bf16[128,448]{0,1:T(8,128)(2,1)}, u32[]{:S(2)}) copy-start(bf16[128,448]{0,1:T(8,128)(2,1)} %param.5) | copy-start | bytes 344068
  2.6 34.3 %all-to-all-start = ((bf16[4,512,256]{2,1,0:T(8,128)(2,1)}), bf16[4,512,256]{2,1,0:T(8,128)(2,1)S(1)}, u32[]{:S(2)}, u32[]{:S(2)}) async-start(bf16[4,512,256]{2,1,0:T(8,128)(2,1)} %broadcast_in_dim.6), calls=%async_computation | async-start | bytes 2097152 | tf_op jit(solution)/shard_map/all_to_all | solution.py:211
  36.9 49.2 %copy-start.5 = (bf16[3584,128]{1,0:T(8,128)(2,1)}, bf16[3584,128]{1,0:T(8,128)(2,1)S(1)}, u32[]{:S(2)}) copy-start(bf16[3584,128]{1,0:T(8,128)(2,1)S(1)} %all-gather) | copy-start | bytes 2752516
  36.9 49.2 %copy-start = (bf16[4,512,256]{2,1,0:T(8,128)(2,1)}, bf16[4,512,256]{2,1,0:T(8,128)(2,1)S(1)}, u32[]{:S(2)}) copy-start(bf16[4,512,256]{2,1,0:T(8,128)(2,1)S(1)} %all-to-all-done.refs_1_) | copy-start | bytes 3145732
  37.0 20.0 %collective-permute-start.3 = (bf16[2,512,256]{2,1,0:T(8,128)(2,1)S(1)}, bf16[2,512,256]{2,1,0:T(8,128)(2,1)S(1)}, u32[]{:S(2)}, u32[]{:S(2)}) collective-permute-start(bf16[2,512,256]{2,1,0:T(8,128)(2,1)S(1)} %get-tuple-element.47), channel_id=1, source_target_pairs={{0,3},{1,0},{2,1},{3,2},{4,7},{5,4},{6,5},{7,6},{8,11},{9,8},{10,9... | collective-permute-start | bytes 1572872 | tf_op jit(solution)/shard_map/ppermute | solution.py:225
  41.4 19.0 %collective-permute-start = (bf16[2,512,256]{2,1,0:T(8,128)(2,1)S(1)}, bf16[2,512,256]{2,1,0:T(8,128)(2,1)S(1)}, u32[]{:S(2)}, u32[]{:S(2)}) collective-permute-start(bf16[2,512,256]{2,1,0:T(8,128)(2,1)S(1)} %get-tuple-element.48), channel_id=1, source_target_pairs={{0,1},{1,2},{2,3},{3,0},{4,5},{5,6},{6,7},{7,4},{8,9},{9,10},{10,1... | collective-permute-start | bytes 1572872 | tf_op jit(solution)/shard_map/ppermute | solution.py:225
  43.3 32.1 %collective-permute-start.4 = (bf16[8,448,128]{2,1,0:T(8,128)(2,1)S(1)}, bf16[8,448,128]{2,1,0:T(8,128)(2,1)S(1)}, u32[]{:S(2)}, u32[]{:S(2)}) collective-permute-start(bf16[8,448,128]{2,1,0:T(8,128)(2,1)S(1)} %bitcast.19), channel_id=1, source_target_pairs={{0,32},{32,0},{1,33},{33,1},{2,34},{34,2},{3,35},{35,3},{4,36},{36... | collective-permute-start | bytes 2752520 | tf_op jit(solution)/shard_map/ppermute | solution.py:206
  50.5 17.1 %collective-permute-start.1 = (bf16[2,512,256]{2,1,0:T(8,128)(2,1)S(1)}, bf16[2,512,256]{2,1,0:T(8,128)(2,1)S(1)}, u32[]{:S(2)}, u32[]{:S(2)}) collective-permute-start(bf16[2,512,256]{2,1,0:T(8,128)(2,1)S(1)} %get-tuple-element.47), channel_id=1, source_target_pairs={{0,1},{1,2},{2,3},{3,0},{4,5},{5,6},{6,7},{7,4},{8,9},{9,10},{10,1... | collective-permute-start | bytes 1572872 | tf_op jit(solution)/shard_map/ppermute | solution.py:225
  52.6 15.0 %collective-permute-start.2 = (bf16[2,512,256]{2,1,0:T(8,128)(2,1)S(1)}, bf16[2,512,256]{2,1,0:T(8,128)(2,1)S(1)}, u32[]{:S(2)}, u32[]{:S(2)}) collective-permute-start(bf16[2,512,256]{2,1,0:T(8,128)(2,1)S(1)} %get-tuple-element.48), channel_id=1, source_target_pairs={{0,3},{1,0},{2,1},{3,2},{4,7},{5,4},{6,5},{7,6},{8,11},{9,8},{10,9... | collective-permute-start | bytes 1572872 | tf_op jit(solution)/shard_map/ppermute | solution.py:225
  57.0 29.1 %copy-start.12 = (bf16[2,512,256]{2,1,0:T(8,128)(2,1)}, bf16[2,512,256]{2,1,0:T(8,128)(2,1)S(1)}, u32[]{:S(2)}) copy-start(bf16[2,512,256]{2,1,0:T(8,128)(2,1)S(1)} %collective-permute-done.3.refs_4_) | copy-start | bytes 1572868
  57.0 20.1 %collective-permute-start.6 = (bf16[2,512,256]{2,1,0:T(8,128)(2,1)S(1)}, bf16[2,512,256]{2,1,0:T(8,128)(2,1)S(1)}, u32[]{:S(2)}, u32[]{:S(2)}) collective-permute-start(bf16[2,512,256]{2,1,0:T(8,128)(2,1)S(1)} %collective-permute-done.3.refs_4_), channel_id=1, source_target_pairs={{0,3},{1,0},{2,1},{3,2},{4,7},{5,4},{6,5},{7,6},{8,11},{9,8},{10,9... | collective-permute-start | bytes 1572872 | tf_op jit(solution)/shard_map/ppermute | solution.py:225
  60.4 16.7 %copy-start.13 = (bf16[2,512,256]{2,1,0:T(8,128)(2,1)}, bf16[2,512,256]{2,1,0:T(8,128)(2,1)S(1)}, u32[]{:S(2)}) copy-start(bf16[2,512,256]{2,1,0:T(8,128)(2,1)S(1)} %collective-permute-done.refs_2_) | copy-start | bytes 1572868
  60.4 18.4 %collective-permute-start.5 = (bf16[2,512,256]{2,1,0:T(8,128)(2,1)S(1)}, bf16[2,512,256]{2,1,0:T(8,128)(2,1)S(1)}, u32[]{:S(2)}, u32[]{:S(2)}) collective-permute-start(bf16[2,512,256]{2,1,0:T(8,128)(2,1)S(1)} %collective-permute-done.refs_2_), channel_id=1, source_target_pairs={{0,1},{1,2},{2,3},{3,0},{4,5},{5,6},{6,7},{7,4},{8,9},{9,10},{10,1... | collective-permute-start | bytes 1572872 | tf_op jit(solution)/shard_map/ppermute | solution.py:225
  67.6 11.2 %copy-start.14 = (bf16[2,512,256]{2,1,0:T(8,128)(2,1)}, bf16[2,512,256]{2,1,0:T(8,128)(2,1)S(1)}, u32[]{:S(2)}) copy-start(bf16[2,512,256]{2,1,0:T(8,128)(2,1)S(1)} %collective-permute-done.1.refs_3_) | copy-start | bytes 1572868
  67.6 16.3 %copy-start.15 = (bf16[2,512,256]{2,1,0:T(8,128)(2,1)}, bf16[2,512,256]{2,1,0:T(8,128)(2,1)S(1)}, u32[]{:S(2)}) copy-start(bf16[2,512,256]{2,1,0:T(8,128)(2,1)S(1)} %collective-permute-done.2.refs_5_) | copy-start | bytes 1572868
  67.6 16.9 %collective-permute-start.7 = (bf16[8,448,128]{2,1,0:T(8,128)(2,1)S(1)}, bf16[8,448,128]{2,1,0:T(8,128)(2,1)}, u32[]{:S(2)}, u32[]{:S(2)}) collective-permute-start(bf16[8,448,128]{2,1,0:T(8,128)(2,1)S(1)} %bitcast.20), channel_id=1, source_target_pairs={{0,16},{16,0},{1,17},{17,1},{2,18},{18,2},{3,19},{19,3},{4,20},{20... | collective-permute-start | bytes 2752520 | tf_op jit(solution)/shard_map/ppermute | solution.py:206
  75.5 10.7 %copy-start.11 = (bf16[8,448,128]{2,1,0:T(8,128)(2,1)}, bf16[8,448,128]{2,1,0:T(8,128)(2,1)S(1)}, u32[]{:S(2)}) copy-start(bf16[8,448,128]{2,1,0:T(8,128)(2,1)S(1)} %collective-permute-done.4.refs_11_) | copy-start | bytes 2752516
  77.1 6.8 %copy-start.16 = (bf16[2,512,256]{2,1,0:T(8,128)(2,1)}, bf16[2,512,256]{2,1,0:T(8,128)(2,1)S(1)}, u32[]{:S(2)}) copy-start(bf16[2,512,256]{2,1,0:T(8,128)(2,1)S(1)} %collective-permute-done.6.refs_7_) | copy-start | bytes 1572868
  78.9 5.1 %copy-start.17 = (bf16[2,512,256]{2,1,0:T(8,128)(2,1)}, bf16[2,512,256]{2,1,0:T(8,128)(2,1)S(1)}, u32[]{:S(2)}) copy-start(bf16[2,512,256]{2,1,0:T(8,128)(2,1)S(1)} %collective-permute-done.5.refs_6_) | copy-start | bytes 1572868
  78.9 7.3 %collective-permute-start.8 = (bf16[8,448,128]{2,1,0:T(8,128)(2,1)S(1)}, bf16[8,448,128]{2,1,0:T(8,128)(2,1)}, u32[]{:S(2)}, u32[]{:S(2)}) collective-permute-start(bf16[8,448,128]{2,1,0:T(8,128)(2,1)S(1)} %collective-permute-done.4.refs_11_), channel_id=1, source_target_pairs={{0,16},{16,0},{1,17},{17,1},{2,18},{18,2},{3,19},{19,3},{4,20},{20... | collective-permute-start | bytes 2752520 | tf_op jit(solution)/shard_map/ppermute | solution.py:206
  95.7 8.6 %collective-permute-start.10 = (bf16[2,8,304,128]{3,2,1,0:T(8,128)(2,1)}, bf16[2,8,304,128]{3,2,1,0:T(8,128)(2,1)S(1)}, u32[]{:S(2)}, u32[]{:S(2)}) collective-permute-start(bf16[2,8,304,128]{3,2,1,0:T(8,128)(2,1)} %get-tuple-element.36.sent), channel_id=1, source_target_pairs={{0,16},{16,0},{1,17},{17,1},{2,18},{18,2},{3,19},{19,3},{4,20},{20... | collective-permute-start | bytes 3735560 | tf_op jit(solution)/shard_map/ppermute | solution.py:206
  98.0 4.1 %collective-permute-start.9 = (bf16[8,2,144,128]{3,2,1,0:T(8,128)(2,1)}, bf16[8,2,144,128]{3,2,1,0:T(8,128)(2,1)S(1)}, u32[]{:S(2)}, u32[]{:S(2)}) collective-permute-start(bf16[8,2,144,128]{3,2,1,0:T(8,128)(2,1)} %get-tuple-element.35.b1), channel_id=1, source_target_pairs={{0,16},{16,0},{1,17},{17,1},{2,18},{18,2},{3,19},{19,3},{4,20},{20... | collective-permute-start | bytes 1769480 | tf_op jit(solution)/shard_map/ppermute | solution.py:206
  102.1 7.5 %copy-start.3 = (bf16[8,304,128]{2,1,0:T(8,128)(2,1)S(1)}, bf16[8,304,128]{2,1,0:T(8,128)(2,1)}, u32[]{:S(2)}) copy-start(bf16[8,304,128]{2,1,0:T(8,128)(2,1)} %get-tuple-element.38.a1) | copy-start | bytes 1867780
  104.3 28.8 %all-to-all-start.1 = ((bf16[8,2,144,128]{3,2,1,0:T(8,128)(2,1)}), bf16[8,2,144,128]{3,2,1,0:T(8,128)(2,1)S(1)}, u32[]{:S(2)}, u32[]{:S(2)}) async-start(bf16[8,2,144,128]{3,2,1,0:T(8,128)(2,1)} %add_convert_fusion), calls=%async_computation.1 | async-start | bytes 1179648 | tf_op jit(solution)/shard_map/all_to_all | solution.py:265
  110.7 22.2 %collective-permute-start.11 = (bf16[8,304,128]{2,1,0:T(8,128)(2,1)}, bf16[8,304,128]{2,1,0:T(8,128)(2,1)S(1)}, u32[]{:S(2)}, u32[]{:S(2)}) collective-permute-start(bf16[8,304,128]{2,1,0:T(8,128)(2,1)} %fusion), channel_id=1, source_target_pairs={{0,32},{32,0},{1,33},{33,1},{2,34},{34,2},{3,35},{35,3},{4,36},{36... | collective-permute-start | bytes 1867784 | tf_op jit(solution)/shard_map/ppermute | solution.py:206
  118.6 14.2 %copy-start.2 = (bf16[8,304,128]{2,1,0:T(8,128)(2,1)S(1)}, bf16[8,304,128]{2,1,0:T(8,128)(2,1)}, u32[]{:S(2)}) copy-start(bf16[8,304,128]{2,1,0:T(8,128)(2,1)} %get-tuple-element.33.a0) | copy-start | bytes 1867780
  158.0 20.7 %all-to-all-start.3 = ((bf16[8,304,128]{2,1,0:T(8,128)(2,1)}), bf16[8,304,128]{2,1,0:T(8,128)(2,1)S(1)}, u32[]{:S(2)}, u32[]{:S(2)}) async-start(bf16[8,304,128]{2,1,0:T(8,128)(2,1)} %broadcast_in_dim.7), calls=%async_computation.3 | async-start | bytes 1245184 | tf_op jit(solution)/shard_map/all_to_all | solution.py:211
  161.6 5.1 %collective-permute-start.12 = (bf16[2,144,128]{2,1,0:T(8,128)(2,1)S(1)}, bf16[2,144,128]{2,1,0:T(8,128)(2,1)S(1)}, u32[]{:S(2)}, u32[]{:S(2)}) collective-permute-start(bf16[2,144,128]{2,1,0:T(8,128)(2,1)S(1)} %reduce_sum.34), channel_id=1, source_target_pairs={{0,32},{32,0},{1,33},{33,1},{2,34},{34,2},{3,35},{35,3},{4,36},{36... | collective-permute-start | bytes 221192 | tf_op jit(solution)/shard_map/ppermute | solution.py:206
  178.7 29.6 %copy-start.1 = (bf16[8,304,128]{2,1,0:T(8,128)(2,1)}, bf16[8,304,128]{2,1,0:T(8,128)(2,1)S(1)}, u32[]{:S(2)}) copy-start(bf16[8,304,128]{2,1,0:T(8,128)(2,1)S(1)} %all-to-all-done.3.refs_0_) | copy-start | bytes 1867780
  179.8 23.8 %all-to-all-start.4 = ((bf16[8,2,144,128]{3,2,1,0:T(8,128)(2,1)}), bf16[8,2,144,128]{3,2,1,0:T(8,128)(2,1)S(1)}, u32[]{:S(2)}, u32[]{:S(2)}) async-start(bf16[8,2,144,128]{3,2,1,0:T(8,128)(2,1)} %broadcast_in_dim.8), calls=%async_computation.4 | async-start | bytes 1179648 | tf_op jit(solution)/shard_map/all_to_all | solution.py:211
  183.3 14.0 %collective-permute-start.13 = (bf16[8,304,128]{2,1,0:T(8,128)(2,1)S(1)}, bf16[8,304,128]{2,1,0:T(8,128)(2,1)S(1)}, u32[]{:S(2)}, u32[]{:S(2)}) collective-permute-start(bf16[8,304,128]{2,1,0:T(8,128)(2,1)S(1)} %all-to-all-done.3.refs_0_), channel_id=1, source_target_pairs={{0,32},{32,0},{1,33},{33,1},{2,34},{34,2},{3,35},{35,3},{4,36},{36... | collective-permute-start | bytes 1867784 | tf_op jit(solution)/shard_map/ppermute | solution.py:206
  185.6 19.9 %collective-permute-start.14 = (bf16[8,304,128]{2,1,0:T(8,128)(2,1)S(1)}, bf16[8,304,128]{2,1,0:T(8,128)(2,1)S(1)}, u32[]{:S(2)}, u32[]{:S(2)}) collective-permute-start(bf16[8,304,128]{2,1,0:T(8,128)(2,1)S(1)} %all-to-all-done.3.refs_0_), channel_id=1, source_target_pairs={{0,16},{16,0},{1,17},{17,1},{2,18},{18,2},{3,19},{19,3},{4,20},{20... | collective-permute-start | bytes 1867784 | tf_op jit(solution)/shard_map/ppermute | solution.py:206
  197.3 10.9 %copy-start.6 = (bf16[8,304,128]{2,1,0:T(8,128)(2,1)}, bf16[8,304,128]{2,1,0:T(8,128)(2,1)S(1)}, u32[]{:S(2)}) copy-start(bf16[8,304,128]{2,1,0:T(8,128)(2,1)S(1)} %collective-permute-done.13.refs_1_) | copy-start | bytes 1867780
  197.4 8.2 %collective-permute-start.15 = (bf16[8,304,128]{2,1,0:T(8,128)(2,1)S(1)}, bf16[8,304,128]{2,1,0:T(8,128)(2,1)S(1)}, u32[]{:S(2)}, u32[]{:S(2)}) collective-permute-start(bf16[8,304,128]{2,1,0:T(8,128)(2,1)S(1)} %collective-permute-done.13.refs_1_), channel_id=1, source_target_pairs={{0,16},{16,0},{1,17},{17,1},{2,18},{18,2},{3,19},{19,3},{4,20},{20... | collective-permute-start | bytes 1867784 | tf_op jit(solution)/shard_map/ppermute | solution.py:206
  203.6 4.7 %copy-start.4 = (bf16[8,2,144,128]{3,2,1,0:T(8,128)(2,1)}, bf16[8,2,144,128]{3,2,1,0:T(8,128)(2,1)S(1)}, u32[]{:S(2)}) copy-start(bf16[8,2,144,128]{3,2,1,0:T(8,128)(2,1)S(1)} %all-to-all-done.4.refs_4_) | copy-start | bytes 1769476
  203.6 3.9 %collective-permute-start.16 = (bf16[8,2,144,128]{3,2,1,0:T(8,128)(2,1)S(1)}, bf16[8,2,144,128]{3,2,1,0:T(8,128)(2,1)S(1)}, u32[]{:S(2)}, u32[]{:S(2)}) collective-permute-start(bf16[8,2,144,128]{3,2,1,0:T(8,128)(2,1)S(1)} %all-to-all-done.4.refs_4_), channel_id=1, source_target_pairs={{0,16},{16,0},{1,17},{17,1},{2,18},{18,2},{3,19},{19,3},{4,20},{20... | collective-permute-start | bytes 1769480 | tf_op jit(solution)/shard_map/ppermute | solution.py:206
  205.5 2.8 %copy-start.7 = (bf16[8,304,128]{2,1,0:T(8,128)(2,1)}, bf16[8,304,128]{2,1,0:T(8,128)(2,1)S(1)}, u32[]{:S(2)}) copy-start(bf16[8,304,128]{2,1,0:T(8,128)(2,1)S(1)} %collective-permute-done.14.refs_2_) | copy-start | bytes 1867780
  205.5 2.8 %copy-start.8 = (bf16[8,304,128]{2,1,0:T(8,128)(2,1)}, bf16[8,304,128]{2,1,0:T(8,128)(2,1)S(1)}, u32[]{:S(2)}) copy-start(bf16[8,304,128]{2,1,0:T(8,128)(2,1)S(1)} %collective-permute-done.15.refs_3_) | copy-start | bytes 1867780
  207.5 0.8 copy-start.9
  214.8 16.5 %all-to-all-start.5 = ((f32[32,8,128]{2,1,0:T(8,128)}), f32[32,8,128]{2,1,0:T(8,128)S(1)}, u32[]{:S(2)}, u32[]{:S(2)}) async-start(f32[32,8,128]{2,1,0:T(8,128)} %shard_map.69), calls=%async_computation.5 | async-start | bytes 262144 | tf_op jit(solution)/shard_map/all_to_all | solution.py:294

commit v10 on v9

--- a/solution.py
+++ b/solution.py
@@ -12,7 +12,7 @@
 F32, BF = jnp.float32, jnp.bfloat16
 NT = (((1,), (1,)), ((), ()))
 CUT = 304
-VMEM_LIMIT = 60 * 1024 * 1024
+VMEM_LIMIT = 54 * 1024 * 1024
 TOK = pltpu.VMEM((16, 512, 256), BF)
 ACC = pltpu.VMEM((448, 512), F32)
 VM = pl.BlockSpec(memory_space=pltpu.VMEM)

time: 233 us -> 232 us (level)
  no operation moved by 1% of the time
where the time goes in v10:
time: 232 us; the launch traced here: 231 us
  starting transfers between devices  99.6 us (43%)
  waiting for transfers between devices  50.9 us (22%)
  blocking collectives  47.2 us (20%)
  Pallas kernels  22.7 us (10%)
  local copies, waits for them, and re-layouts  4.93 us (2%)
  other arithmetic  4.62 us (2%)
    ppermute x11, starting transfers between devices, swap(): return lax.ppermute(value, axis, ((0, 1), (1, 0)))  50.9 us
    all_to_all x1, blocking collectives, shards(): across_a = lax.all_to_all(sums_a, 'y', 0, 0, tiled=True)  23.9 us
    all_gather x1, blocking collectives, shards(): w0 = lax.all_gather(gate_weight.T, 'y', axis=0)  23.3 us
    pallas_call x3, Pallas kernels, call(): pl.pallas_call(kernel, out_shape=outs, in_specs=[SM] + [ANY] * (len(opera...  22.7 us
    ppermute x11, waiting for transfers between devices, swap(): return lax.ppermute(value, axis, ((0, 1), (1, 0)))  21.7 us
    ppermute x6, starting transfers between devices, along_x(): return lax.ppermute(value, 'x', [(i, (i + by) % 4) for i in range(4)])  18.1 us
    all_to_all x3, starting transfers between devices, to_all(): lax.all_to_all(jnp.broadcast_to(value[None], (count, *value.shape)), axis...  18.1 us
    all_to_all x3, waiting for transfers between devices, to_all(): lax.all_to_all(jnp.broadcast_to(value[None], (count, *value.shape)), axis...  11.9 us
  transfers between devices with their start and end apart: 22, of which 11 were waited for; matrix products, arithmetic and copies ran while one was open for 2% of the time, Pallas kernels for 3%

profile of v10, /device:TPU:1, one launch (start us, length us, event | category | flops | bytes accessed | tf_op | source)
XLA Modules:
  0.0 230.9 jit_solution(12533965367705040137)
XLA Ops:
  0.6 2.0 broadcast_in_dim.6
  2.6 11.0 %all-to-all-start = ((bf16[4,512,256]{2,1,0:T(8,128)(2,1)}), bf16[4,512,256]{2,1,0:T(8,128)(2,1)S(1)}, u32[]{:S(2)}, u32[]{:S(2)}) async-start(bf16[4,512,256]{2,1,0:T(8,128)(2,1)} %broadcast_in_dim.6), calls=%async_computation | async-start | bytes 2097152 | tf_op jit(solution)/shard_map/all_to_all | solution.py:211
  13.6 23.3 %all-gather = bf16[3584,128]{1,0:T(8,128)(2,1)S(1)} all-gather(bf16[448,128]{1,0:T(8,128)(2,1)S(1)} %bitcast.22), channel_id=2, replica_groups=mesh['y'=8,'zl'=2,'c'=2,'zh'=4,'x'=4] {'y'}, dimensions={0}, use_global_device_ids=true | all-gather | bytes 1032192 | tf_op jit(solution)/shard_map/all_gather | solution.py:234
  37.0 4.4 %collective-permute-start.3 = (bf16[2,512,256]{2,1,0:T(8,128)(2,1)S(1)}, bf16[2,512,256]{2,1,0:T(8,128)(2,1)S(1)}, u32[]{:S(2)}, u32[]{:S(2)}) collective-permute-start(bf16[2,512,256]{2,1,0:T(8,128)(2,1)S(1)} %get-tuple-element.47), channel_id=1, source_target_pairs={{0,3},{1,0},{2,1},{3,2},{4,7},{5,4},{6,5},{7,6},{8,11},{9,8},{10,9... | collective-permute-start | bytes 1572872 | tf_op jit(solution)/shard_map/ppermute | solution.py:225
  41.4 1.9 collective-permute-start
  43.3 7.2 %collective-permute-start.4 = (bf16[8,448,128]{2,1,0:T(8,128)(2,1)S(1)}, bf16[8,448,128]{2,1,0:T(8,128)(2,1)S(1)}, u32[]{:S(2)}, u32[]{:S(2)}) collective-permute-start(bf16[8,448,128]{2,1,0:T(8,128)(2,1)S(1)} %bitcast.19), channel_id=1, source_target_pairs={{0,32},{32,0},{1,33},{33,1},{2,34},{34,2},{3,35},{35,3},{4,36},{36... | collective-permute-start | bytes 2752520 | tf_op jit(solution)/shard_map/ppermute | solution.py:206
  50.5 2.1 collective-permute-start.1
  52.6 4.4 %collective-permute-start.2 = (bf16[2,512,256]{2,1,0:T(8,128)(2,1)S(1)}, bf16[2,512,256]{2,1,0:T(8,128)(2,1)S(1)}, u32[]{:S(2)}, u32[]{:S(2)}) collective-permute-start(bf16[2,512,256]{2,1,0:T(8,128)(2,1)S(1)} %get-tuple-element.48), channel_id=1, source_target_pairs={{0,3},{1,0},{2,1},{3,2},{4,7},{5,4},{6,5},{7,6},{8,11},{9,8},{10,9... | collective-permute-start | bytes 1572872 | tf_op jit(solution)/shard_map/ppermute | solution.py:225
  57.0 3.4 %collective-permute-start.6 = (bf16[2,512,256]{2,1,0:T(8,128)(2,1)S(1)}, bf16[2,512,256]{2,1,0:T(8,128)(2,1)S(1)}, u32[]{:S(2)}, u32[]{:S(2)}) collective-permute-start(bf16[2,512,256]{2,1,0:T(8,128)(2,1)S(1)} %collective-permute-done.3.refs_4_), channel_id=1, source_target_pairs={{0,3},{1,0},{2,1},{3,2},{4,7},{5,4},{6,5},{7,6},{8,11},{9,8},{10,9... | collective-permute-start | bytes 1572872 | tf_op jit(solution)/shard_map/ppermute | solution.py:225
  60.4 1.9 collective-permute-start.5
  62.4 5.3 %collective-permute-done.1.refs_3_ = bf16[2,512,256]{2,1,0:T(8,128)(2,1)S(1)} collective-permute-done((bf16[2,512,256]{2,1,0:T(8,128)(2,1)S(1)}, bf16[2,512,256]{2,1,0:T(8,128)(2,1)S(1)}, u32[]{:S(2)}, u32[]{:S(2)}) %collective-permute-start.1) | collective-permute-done | bytes 524320 | tf_op jit(solution)/shard_map/ppermute | solution.py:225
  67.6 7.8 %collective-permute-start.7 = (bf16[8,448,128]{2,1,0:T(8,128)(2,1)S(1)}, bf16[8,448,128]{2,1,0:T(8,128)(2,1)}, u32[]{:S(2)}, u32[]{:S(2)}) collective-permute-start(bf16[8,448,128]{2,1,0:T(8,128)(2,1)S(1)} %bitcast.20), channel_id=1, source_target_pairs={{0,16},{16,0},{1,17},{17,1},{2,18},{18,2},{3,19},{19,3},{4,20},{20... | collective-permute-start | bytes 2752520 | tf_op jit(solution)/shard_map/ppermute | solution.py:206
  75.5 1.6 collective-permute-done.6.refs_7_
  77.1 1.8 collective-permute-done.5.refs_6_
  78.9 5.1 %collective-permute-start.8 = (bf16[8,448,128]{2,1,0:T(8,128)(2,1)S(1)}, bf16[8,448,128]{2,1,0:T(8,128)(2,1)}, u32[]{:S(2)}, u32[]{:S(2)}) collective-permute-start(bf16[8,448,128]{2,1,0:T(8,128)(2,1)S(1)} %collective-permute-done.4.refs_11_), channel_id=1, source_target_pairs={{0,16},{16,0},{1,17},{17,1},{2,18},{18,2},{3,19},{19,3},{4,20},{20... | collective-permute-start | bytes 2752520 | tf_op jit(solution)/shard_map/ppermute | solution.py:206
  84.0 0.6 pad_add_fusion.refs_0_.me
  84.5 1.6 collective-permute-done.8.refs_13_
  86.1 9.6 %shard_map.67 = (bf16[16,512,256]{2,1,0:T(8,128)(2,1)}, f32[448,512]{1,0:T(8,128)}, bf16[8,304,128]{2,1,0:T(8,128)(2,1)}, bf16[8,304,128]{2,1,0:T(8,128)(2,1)}, ...) custom-call(s32[3]{0:T(128)} %pad_add_fusion.refs_0_.me, ...), custom_call_target="tpu_custom_call" | custom-call | flops 3758096384 | bytes 17563660 | tf_op jit(solution)/shard_map/pallas_call | solution.py:27
  95.7 2.3 collective-permute-start.10
  98.0 2.0 collective-permute-start.9
  100.1 2.1 collective-permute-done.9
  102.1 2.2 add_convert_fusion
  104.3 5.3 %all-to-all-start.1 = ((bf16[8,2,144,128]{3,2,1,0:T(8,128)(2,1)}), bf16[8,2,144,128]{3,2,1,0:T(8,128)(2,1)S(1)}, u32[]{:S(2)}, u32[]{:S(2)}) async-start(bf16[8,2,144,128]{3,2,1,0:T(8,128)(2,1)} %add_convert_fusion), calls=%async_computation.1 | async-start | bytes 1179648 | tf_op jit(solution)/shard_map/all_to_all | solution.py:265
  109.6 0.2 fusion
  109.8 8.0 %collective-permute-start.11 = (bf16[8,304,128]{2,1,0:T(8,128)(2,1)S(1)}, bf16[8,304,128]{2,1,0:T(8,128)(2,1)S(1)}, u32[]{:S(2)}, u32[]{:S(2)}) collective-permute-start(bf16[8,304,128]{2,1,0:T(8,128)(2,1)S(1)} %fusion), channel_id=1, source_target_pairs={{0,32},{32,0},{1,33},{33,1},{2,34},{34,2},{3,35},{35,3},{4,36},{36... | collective-permute-start | bytes 1867784 | tf_op jit(solution)/shard_map/ppermute | solution.py:206
  117.8 6.6 %shard_map.68.own_in = f32[448,512]{1,0:T(8,128)} custom-call(s32[3]{0:T(128)} %pad_add_fusion.refs_0_.me, bf16[16,512,256]{2,1,0:T(8,128)(2,1)} %get-tuple-element.40.source, bf16[8,304,128]{2,1,0:T(8,128)(2,1)} %get-tuple-element.33.a0, bf16[8,304,128]{2,1,0:T(8,128)(2,1)} %get-tuple-element.38.a1, bf16[2,8,304,128]{3,2,1,0:T(8,128)(2,1)} %get-tuple-element.36.sent, ...), custom_call_target="tpu_custom_call" | custom-call | flops 1879048192 | bytes 8781836 | tf_op jit(solution)/shard_map/pallas_call | solution.py:27
  124.4 7.4 %collective-permute-done.11 = bf16[8,304,128]{2,1,0:T(8,128)(2,1)S(1)} collective-permute-done((bf16[8,304,128]{2,1,0:T(8,128)(2,1)S(1)}, bf16[8,304,128]{2,1,0:T(8,128)(2,1)S(1)}, u32[]{:S(2)}, u32[]{:S(2)}) %collective-permute-start.11) | collective-permute-done | bytes 622624 | tf_op jit(solution)/shard_map/ppermute | solution.py:206
  131.8 0.2 fusion.2
  132.0 23.9 %all_to_all.30 = bf16[8,304,128]{2,1,0:T(8,128)(2,1)S(1)} all-to-all(bf16[8,304,128]{2,1,0:T(8,128)(2,1)S(1)} %fusion.2), channel_id=1, replica_groups=mesh['y'=8,'zl'=2,'c'=2,'zh'=4,'x'=4] {'y'}, dimensions={0} | all-to-all | bytes 1245184 | tf_op jit(solution)/shard_map/all_to_all | solution.py:277
  156.0 0.9 broadcast_in_dim.7
  156.9 3.5 %all-to-all-start.3 = ((bf16[8,304,128]{2,1,0:T(8,128)(2,1)}), bf16[8,304,128]{2,1,0:T(8,128)(2,1)S(1)}, u32[]{:S(2)}, u32[]{:S(2)}) async-start(bf16[8,304,128]{2,1,0:T(8,128)(2,1)} %broadcast_in_dim.7), calls=%async_computation.3 | async-start | bytes 1245184 | tf_op jit(solution)/shard_map/all_to_all | solution.py:211
  160.5 2.4 %collective-permute-start.12 = (bf16[2,144,128]{2,1,0:T(8,128)(2,1)S(1)}, bf16[2,144,128]{2,1,0:T(8,128)(2,1)S(1)}, u32[]{:S(2)}, u32[]{:S(2)}) collective-permute-start(bf16[2,144,128]{2,1,0:T(8,128)(2,1)S(1)} %reduce_sum.34), channel_id=1, source_target_pairs={{0,32},{32,0},{1,33},{33,1},{2,34},{34,2},{3,35},{35,3},{4,36},{36... | collective-permute-start | bytes 221192 | tf_op jit(solution)/shard_map/ppermute | solution.py:206
  162.9 2.7 %collective-permute-done.12 = bf16[2,144,128]{2,1,0:T(8,128)(2,1)S(1)} collective-permute-done((bf16[2,144,128]{2,1,0:T(8,128)(2,1)S(1)}, bf16[2,144,128]{2,1,0:T(8,128)(2,1)S(1)}, u32[]{:S(2)}, u32[]{:S(2)}) %collective-permute-start.12) | collective-permute-done | bytes 73760 | tf_op jit(solution)/shard_map/ppermute | solution.py:206
  165.7 11.9 %all-to-all-done.3.refs_0_ = bf16[8,304,128]{2,1,0:T(8,128)(2,1)S(1)} async-done(((bf16[8,304,128]{2,1,0:T(8,128)(2,1)}), bf16[8,304,128]{2,1,0:T(8,128)(2,1)S(1)}, u32[]{:S(2)}, u32[]{:S(2)}) %all-to-all-start.3) | async-done | bytes 622624 | tf_op jit(solution)/shard_map/all_to_all | solution.py:211
  177.6 1.1 broadcast_in_dim.8
  178.7 3.5 %all-to-all-start.4 = ((bf16[8,2,144,128]{3,2,1,0:T(8,128)(2,1)}), bf16[8,2,144,128]{3,2,1,0:T(8,128)(2,1)S(1)}, u32[]{:S(2)}, u32[]{:S(2)}) async-start(bf16[8,2,144,128]{3,2,1,0:T(8,128)(2,1)} %broadcast_in_dim.8), calls=%async_computation.4 | async-start | bytes 1179648 | tf_op jit(solution)/shard_map/all_to_all | solution.py:211
  182.2 2.3 collective-permute-start.13
  184.5 5.7 %collective-permute-start.14 = (bf16[8,304,128]{2,1,0:T(8,128)(2,1)S(1)}, bf16[8,304,128]{2,1,0:T(8,128)(2,1)S(1)}, u32[]{:S(2)}, u32[]{:S(2)}) collective-permute-start(bf16[8,304,128]{2,1,0:T(8,128)(2,1)S(1)} %all-to-all-done.3.refs_0_), channel_id=1, source_target_pairs={{0,16},{16,0},{1,17},{17,1},{2,18},{18,2},{3,19},{19,3},{4,20},{20... | collective-permute-start | bytes 1867784 | tf_op jit(solution)/shard_map/ppermute | solution.py:206
  190.3 6.0 %collective-permute-done.13.refs_1_ = bf16[8,304,128]{2,1,0:T(8,128)(2,1)S(1)} collective-permute-done((bf16[8,304,128]{2,1,0:T(8,128)(2,1)S(1)}, bf16[8,304,128]{2,1,0:T(8,128)(2,1)S(1)}, u32[]{:S(2)}, u32[]{:S(2)}) %collective-permute-start.13) | collective-permute-done | bytes 622624 | tf_op jit(solution)/shard_map/ppermute | solution.py:206
  196.3 6.2 %collective-permute-start.15 = (bf16[8,304,128]{2,1,0:T(8,128)(2,1)S(1)}, bf16[8,304,128]{2,1,0:T(8,128)(2,1)S(1)}, u32[]{:S(2)}, u32[]{:S(2)}) collective-permute-start(bf16[8,304,128]{2,1,0:T(8,128)(2,1)S(1)} %collective-permute-done.13.refs_1_), channel_id=1, source_target_pairs={{0,16},{16,0},{1,17},{17,1},{2,18},{18,2},{3,19},{19,3},{4,20},{20... | collective-permute-start | bytes 1867784 | tf_op jit(solution)/shard_map/ppermute | solution.py:206
  202.5 1.9 collective-permute-start.16
  204.5 1.9 collective-permute-done.16.refs_5_
  206.4 0.8 copy-done.9
  207.2 6.5 %shard_map.69 = f32[32,8,128]{2,1,0:T(8,128)} custom-call(s32[3]{0:T(128)} %pad_add_fusion.refs_0_.me, bf16[16,512,256]{2,1,0:T(8,128)(2,1)} %get-tuple-element.40.source, f32[448,512]{1,0:T(8,128)} %get-tuple-element.44.bend_in, f32[448,512]{1,0:T(8,128)} %shard_map.68.own_in, bf16[8,304,128]{2,1,0:T(8,128)(2,1)} %copy-done.1, ...), custom_call_target="tpu_custom_call" | custom-call | flops 1879048192 | bytes 9830412 | tf_op jit(solution)/shard_map/pallas_call | solution.py:27
  213.7 7.3 %all-to-all-start.5 = ((f32[32,8,128]{2,1,0:T(8,128)}), f32[32,8,128]{2,1,0:T(8,128)S(1)}, u32[]{:S(2)}, u32[]{:S(2)}) async-start(f32[32,8,128]{2,1,0:T(8,128)} %shard_map.69), calls=%async_computation.5 | async-start | bytes 262144 | tf_op jit(solution)/shard_map/all_to_all | solution.py:294
  221.0 0.7 maximum_bitcast_fusion
  221.7 8.6 %all-to-all-done.5 = f32[32,8,128]{2,1,0:T(8,128)S(1)} async-done(((f32[32,8,128]{2,1,0:T(8,128)}), f32[32,8,128]{2,1,0:T(8,128)S(1)}, u32[]{:S(2)}, u32[]{:S(2)}) %all-to-all-start.5) | async-done | bytes 131104 | tf_op jit(solution)/shard_map/all_to_all | solution.py:294
  230.3 0.6 slice_multiply_fusion
  (53 shorter events, 0.4 us)
Async XLA Ops:
  2.6 11.0 %copy-start.10 = (bf16[128,448]{0,1:T(8,128)(2,1)S(1)}, bf16[128,448]{0,1:T(8,128)(2,1)}, u32[]{:S(2)}) copy-start(bf16[128,448]{0,1:T(8,128)(2,1)} %param.5) | copy-start | bytes 344068
  2.6 34.3 %all-to-all-start = ((bf16[4,512,256]{2,1,0:T(8,128)(2,1)}), bf16[4,512,256]{2,1,0:T(8,128)(2,1)S(1)}, u32[]{:S(2)}, u32[]{:S(2)}) async-start(bf16[4,512,256]{2,1,0:T(8,128)(2,1)} %broadcast_in_dim.6), calls=%async_computation | async-start | bytes 2097152 | tf_op jit(solution)/shard_map/all_to_all | solution.py:211
  36.9 49.2 %copy-start.5 = (bf16[3584,128]{1,0:T(8,128)(2,1)}, bf16[3584,128]{1,0:T(8,128)(2,1)S(1)}, u32[]{:S(2)}) copy-start(bf16[3584,128]{1,0:T(8,128)(2,1)S(1)} %all-gather) | copy-start | bytes 2752516
  36.9 49.2 %copy-start = (bf16[4,512,256]{2,1,0:T(8,128)(2,1)}, bf16[4,512,256]{2,1,0:T(8,128)(2,1)S(1)}, u32[]{:S(2)}) copy-start(bf16[4,512,256]{2,1,0:T(8,128)(2,1)S(1)} %all-to-all-done.refs_1_) | copy-start | bytes 3145732
  37.0 20.0 %collective-permute-start.3 = (bf16[2,512,256]{2,1,0:T(8,128)(2,1)S(1)}, bf16[2,512,256]{2,1,0:T(8,128)(2,1)S(1)}, u32[]{:S(2)}, u32[]{:S(2)}) collective-permute-start(bf16[2,512,256]{2,1,0:T(8,128)(2,1)S(1)} %get-tuple-element.47), channel_id=1, source_target_pairs={{0,3},{1,0},{2,1},{3,2},{4,7},{5,4},{6,5},{7,6},{8,11},{9,8},{10,9... | collective-permute-start | bytes 1572872 | tf_op jit(solution)/shard_map/ppermute | solution.py:225
  41.4 19.0 %collective-permute-start = (bf16[2,512,256]{2,1,0:T(8,128)(2,1)S(1)}, bf16[2,512,256]{2,1,0:T(8,128)(2,1)S(1)}, u32[]{:S(2)}, u32[]{:S(2)}) collective-permute-start(bf16[2,512,256]{2,1,0:T(8,128)(2,1)S(1)} %get-tuple-element.48), channel_id=1, source_target_pairs={{0,1},{1,2},{2,3},{3,0},{4,5},{5,6},{6,7},{7,4},{8,9},{9,10},{10,1... | collective-permute-start | bytes 1572872 | tf_op jit(solution)/shard_map/ppermute | solution.py:225
  43.3 32.1 %collective-permute-start.4 = (bf16[8,448,128]{2,1,0:T(8,128)(2,1)S(1)}, bf16[8,448,128]{2,1,0:T(8,128)(2,1)S(1)}, u32[]{:S(2)}, u32[]{:S(2)}) collective-permute-start(bf16[8,448,128]{2,1,0:T(8,128)(2,1)S(1)} %bitcast.19), channel_id=1, source_target_pairs={{0,32},{32,0},{1,33},{33,1},{2,34},{34,2},{3,35},{35,3},{4,36},{36... | collective-permute-start | bytes 2752520 | tf_op jit(solution)/shard_map/ppermute | solution.py:206
  50.5 17.1 %collective-permute-start.1 = (bf16[2,512,256]{2,1,0:T(8,128)(2,1)S(1)}, bf16[2,512,256]{2,1,0:T(8,128)(2,1)S(1)}, u32[]{:S(2)}, u32[]{:S(2)}) collective-permute-start(bf16[2,512,256]{2,1,0:T(8,128)(2,1)S(1)} %get-tuple-element.47), channel_id=1, source_target_pairs={{0,1},{1,2},{2,3},{3,0},{4,5},{5,6},{6,7},{7,4},{8,9},{9,10},{10,1... | collective-permute-start | bytes 1572872 | tf_op jit(solution)/shard_map/ppermute | solution.py:225
  52.6 15.0 %collective-permute-start.2 = (bf16[2,512,256]{2,1,0:T(8,128)(2,1)S(1)}, bf16[2,512,256]{2,1,0:T(8,128)(2,1)S(1)}, u32[]{:S(2)}, u32[]{:S(2)}) collective-permute-start(bf16[2,512,256]{2,1,0:T(8,128)(2,1)S(1)} %get-tuple-element.48), channel_id=1, source_target_pairs={{0,3},{1,0},{2,1},{3,2},{4,7},{5,4},{6,5},{7,6},{8,11},{9,8},{10,9... | collective-permute-start | bytes 1572872 | tf_op jit(solution)/shard_map/ppermute | solution.py:225
  57.0 29.1 %copy-start.12 = (bf16[2,512,256]{2,1,0:T(8,128)(2,1)}, bf16[2,512,256]{2,1,0:T(8,128)(2,1)S(1)}, u32[]{:S(2)}) copy-start(bf16[2,512,256]{2,1,0:T(8,128)(2,1)S(1)} %collective-permute-done.3.refs_4_) | copy-start | bytes 1572868
  57.0 20.1 %collective-permute-start.6 = (bf16[2,512,256]{2,1,0:T(8,128)(2,1)S(1)}, bf16[2,512,256]{2,1,0:T(8,128)(2,1)S(1)}, u32[]{:S(2)}, u32[]{:S(2)}) collective-permute-start(bf16[2,512,256]{2,1,0:T(8,128)(2,1)S(1)} %collective-permute-done.3.refs_4_), channel_id=1, source_target_pairs={{0,3},{1,0},{2,1},{3,2},{4,7},{5,4},{6,5},{7,6},{8,11},{9,8},{10,9... | collective-permute-start | bytes 1572872 | tf_op jit(solution)/shard_map/ppermute | solution.py:225
  60.4 16.7 %copy-start.13 = (bf16[2,512,256]{2,1,0:T(8,128)(2,1)}, bf16[2,512,256]{2,1,0:T(8,128)(2,1)S(1)}, u32[]{:S(2)}) copy-start(bf16[2,512,256]{2,1,0:T(8,128)(2,1)S(1)} %collective-permute-done.refs_2_) | copy-start | bytes 1572868
  60.4 18.4 %collective-permute-start.5 = (bf16[2,512,256]{2,1,0:T(8,128)(2,1)S(1)}, bf16[2,512,256]{2,1,0:T(8,128)(2,1)S(1)}, u32[]{:S(2)}, u32[]{:S(2)}) collective-permute-start(bf16[2,512,256]{2,1,0:T(8,128)(2,1)S(1)} %collective-permute-done.refs_2_), channel_id=1, source_target_pairs={{0,1},{1,2},{2,3},{3,0},{4,5},{5,6},{6,7},{7,4},{8,9},{9,10},{10,1... | collective-permute-start | bytes 1572872 | tf_op jit(solution)/shard_map/ppermute | solution.py:225
  67.6 11.2 %copy-start.14 = (bf16[2,512,256]{2,1,0:T(8,128)(2,1)}, bf16[2,512,256]{2,1,0:T(8,128)(2,1)S(1)}, u32[]{:S(2)}) copy-start(bf16[2,512,256]{2,1,0:T(8,128)(2,1)S(1)} %collective-permute-done.1.refs_3_) | copy-start | bytes 1572868
  67.6 16.3 %copy-start.15 = (bf16[2,512,256]{2,1,0:T(8,128)(2,1)}, bf16[2,512,256]{2,1,0:T(8,128)(2,1)S(1)}, u32[]{:S(2)}) copy-start(bf16[2,512,256]{2,1,0:T(8,128)(2,1)S(1)} %collective-permute-done.2.refs_5_) | copy-start | bytes 1572868
  67.6 16.9 %collective-permute-start.7 = (bf16[8,448,128]{2,1,0:T(8,128)(2,1)S(1)}, bf16[8,448,128]{2,1,0:T(8,128)(2,1)}, u32[]{:S(2)}, u32[]{:S(2)}) collective-permute-start(bf16[8,448,128]{2,1,0:T(8,128)(2,1)S(1)} %bitcast.20), channel_id=1, source_target_pairs={{0,16},{16,0},{1,17},{17,1},{2,18},{18,2},{3,19},{19,3},{4,20},{20... | collective-permute-start | bytes 2752520 | tf_op jit(solution)/shard_map/ppermute | solution.py:206
  75.5 10.7 %copy-start.11 = (bf16[8,448,128]{2,1,0:T(8,128)(2,1)}, bf16[8,448,128]{2,1,0:T(8,128)(2,1)S(1)}, u32[]{:S(2)}) copy-start(bf16[8,448,128]{2,1,0:T(8,128)(2,1)S(1)} %collective-permute-done.4.refs_11_) | copy-start | bytes 2752516
  77.1 6.8 %copy-start.16 = (bf16[2,512,256]{2,1,0:T(8,128)(2,1)}, bf16[2,512,256]{2,1,0:T(8,128)(2,1)S(1)}, u32[]{:S(2)}) copy-start(bf16[2,512,256]{2,1,0:T(8,128)(2,1)S(1)} %collective-permute-done.6.refs_7_) | copy-start | bytes 1572868
  78.9 5.1 %copy-start.17 = (bf16[2,512,256]{2,1,0:T(8,128)(2,1)}, bf16[2,512,256]{2,1,0:T(8,128)(2,1)S(1)}, u32[]{:S(2)}) copy-start(bf16[2,512,256]{2,1,0:T(8,128)(2,1)S(1)} %collective-permute-done.5.refs_6_) | copy-start | bytes 1572868
  78.9 7.3 %collective-permute-start.8 = (bf16[8,448,128]{2,1,0:T(8,128)(2,1)S(1)}, bf16[8,448,128]{2,1,0:T(8,128)(2,1)}, u32[]{:S(2)}, u32[]{:S(2)}) collective-permute-start(bf16[8,448,128]{2,1,0:T(8,128)(2,1)S(1)} %collective-permute-done.4.refs_11_), channel_id=1, source_target_pairs={{0,16},{16,0},{1,17},{17,1},{2,18},{18,2},{3,19},{19,3},{4,20},{20... | collective-permute-start | bytes 2752520 | tf_op jit(solution)/shard_map/ppermute | solution.py:206
  95.7 8.6 %collective-permute-start.10 = (bf16[2,8,304,128]{3,2,1,0:T(8,128)(2,1)}, bf16[2,8,304,128]{3,2,1,0:T(8,128)(2,1)S(1)}, u32[]{:S(2)}, u32[]{:S(2)}) collective-permute-start(bf16[2,8,304,128]{3,2,1,0:T(8,128)(2,1)} %get-tuple-element.36.sent), channel_id=1, source_target_pairs={{0,16},{16,0},{1,17},{17,1},{2,18},{18,2},{3,19},{19,3},{4,20},{20... | collective-permute-start | bytes 3735560 | tf_op jit(solution)/shard_map/ppermute | solution.py:206
  98.0 4.1 %collective-permute-start.9 = (bf16[8,2,144,128]{3,2,1,0:T(8,128)(2,1)}, bf16[8,2,144,128]{3,2,1,0:T(8,128)(2,1)S(1)}, u32[]{:S(2)}, u32[]{:S(2)}) collective-permute-start(bf16[8,2,144,128]{3,2,1,0:T(8,128)(2,1)} %get-tuple-element.35.b1), channel_id=1, source_target_pairs={{0,16},{16,0},{1,17},{17,1},{2,18},{18,2},{3,19},{19,3},{4,20},{20... | collective-permute-start | bytes 1769480 | tf_op jit(solution)/shard_map/ppermute | solution.py:206
  102.1 7.5 %copy-start.3 = (bf16[8,304,128]{2,1,0:T(8,128)(2,1)S(1)}, bf16[8,304,128]{2,1,0:T(8,128)(2,1)}, u32[]{:S(2)}) copy-start(bf16[8,304,128]{2,1,0:T(8,128)(2,1)} %get-tuple-element.38.a1) | copy-start | bytes 1867780
  104.3 27.7 %all-to-all-start.1 = ((bf16[8,2,144,128]{3,2,1,0:T(8,128)(2,1)}), bf16[8,2,144,128]{3,2,1,0:T(8,128)(2,1)S(1)}, u32[]{:S(2)}, u32[]{:S(2)}) async-start(bf16[8,2,144,128]{3,2,1,0:T(8,128)(2,1)} %add_convert_fusion), calls=%async_computation.1 | async-start | bytes 1179648 | tf_op jit(solution)/shard_map/all_to_all | solution.py:265
  109.8 22.0 %collective-permute-start.11 = (bf16[8,304,128]{2,1,0:T(8,128)(2,1)S(1)}, bf16[8,304,128]{2,1,0:T(8,128)(2,1)S(1)}, u32[]{:S(2)}, u32[]{:S(2)}) collective-permute-start(bf16[8,304,128]{2,1,0:T(8,128)(2,1)S(1)} %fusion), channel_id=1, source_target_pairs={{0,32},{32,0},{1,33},{33,1},{2,34},{34,2},{3,35},{35,3},{4,36},{36... | collective-permute-start | bytes 1867784 | tf_op jit(solution)/shard_map/ppermute | solution.py:206
  117.8 14.0 %copy-start.2 = (bf16[8,304,128]{2,1,0:T(8,128)(2,1)S(1)}, bf16[8,304,128]{2,1,0:T(8,128)(2,1)}, u32[]{:S(2)}) copy-start(bf16[8,304,128]{2,1,0:T(8,128)(2,1)} %get-tuple-element.33.a0) | copy-start | bytes 1867780
  156.9 20.7 %all-to-all-start.3 = ((bf16[8,304,128]{2,1,0:T(8,128)(2,1)}), bf16[8,304,128]{2,1,0:T(8,128)(2,1)S(1)}, u32[]{:S(2)}, u32[]{:S(2)}) async-start(bf16[8,304,128]{2,1,0:T(8,128)(2,1)} %broadcast_in_dim.7), calls=%async_computation.3 | async-start | bytes 1245184 | tf_op jit(solution)/shard_map/all_to_all | solution.py:211
  160.5 5.1 %collective-permute-start.12 = (bf16[2,144,128]{2,1,0:T(8,128)(2,1)S(1)}, bf16[2,144,128]{2,1,0:T(8,128)(2,1)S(1)}, u32[]{:S(2)}, u32[]{:S(2)}) collective-permute-start(bf16[2,144,128]{2,1,0:T(8,128)(2,1)S(1)} %reduce_sum.34), channel_id=1, source_target_pairs={{0,32},{32,0},{1,33},{33,1},{2,34},{34,2},{3,35},{35,3},{4,36},{36... | collective-permute-start | bytes 221192 | tf_op jit(solution)/shard_map/ppermute | solution.py:206
  177.6 28.8 %copy-start.1 = (bf16[8,304,128]{2,1,0:T(8,128)(2,1)}, bf16[8,304,128]{2,1,0:T(8,128)(2,1)S(1)}, u32[]{:S(2)}) copy-start(bf16[8,304,128]{2,1,0:T(8,128)(2,1)S(1)} %all-to-all-done.3.refs_0_) | copy-start | bytes 1867780
  178.7 23.8 %all-to-all-start.4 = ((bf16[8,2,144,128]{3,2,1,0:T(8,128)(2,1)}), bf16[8,2,144,128]{3,2,1,0:T(8,128)(2,1)S(1)}, u32[]{:S(2)}, u32[]{:S(2)}) async-start(bf16[8,2,144,128]{3,2,1,0:T(8,128)(2,1)} %broadcast_in_dim.8), calls=%async_computation.4 | async-start | bytes 1179648 | tf_op jit(solution)/shard_map/all_to_all | solution.py:211
  182.2 14.0 %collective-permute-start.13 = (bf16[8,304,128]{2,1,0:T(8,128)(2,1)S(1)}, bf16[8,304,128]{2,1,0:T(8,128)(2,1)S(1)}, u32[]{:S(2)}, u32[]{:S(2)}) collective-permute-start(bf16[8,304,128]{2,1,0:T(8,128)(2,1)S(1)} %all-to-all-done.3.refs_0_), channel_id=1, source_target_pairs={{0,32},{32,0},{1,33},{33,1},{2,34},{34,2},{3,35},{35,3},{4,36},{36... | collective-permute-start | bytes 1867784 | tf_op jit(solution)/shard_map/ppermute | solution.py:206
  184.5 19.9 %collective-permute-start.14 = (bf16[8,304,128]{2,1,0:T(8,128)(2,1)S(1)}, bf16[8,304,128]{2,1,0:T(8,128)(2,1)S(1)}, u32[]{:S(2)}, u32[]{:S(2)}) collective-permute-start(bf16[8,304,128]{2,1,0:T(8,128)(2,1)S(1)} %all-to-all-done.3.refs_0_), channel_id=1, source_target_pairs={{0,16},{16,0},{1,17},{17,1},{2,18},{18,2},{3,19},{19,3},{4,20},{20... | collective-permute-start | bytes 1867784 | tf_op jit(solution)/shard_map/ppermute | solution.py:206
  196.3 10.1 %copy-start.6 = (bf16[8,304,128]{2,1,0:T(8,128)(2,1)}, bf16[8,304,128]{2,1,0:T(8,128)(2,1)S(1)}, u32[]{:S(2)}) copy-start(bf16[8,304,128]{2,1,0:T(8,128)(2,1)S(1)} %collective-permute-done.13.refs_1_) | copy-start | bytes 1867780
  196.3 8.2 %collective-permute-start.15 = (bf16[8,304,128]{2,1,0:T(8,128)(2,1)S(1)}, bf16[8,304,128]{2,1,0:T(8,128)(2,1)S(1)}, u32[]{:S(2)}, u32[]{:S(2)}) collective-permute-start(bf16[8,304,128]{2,1,0:T(8,128)(2,1)S(1)} %collective-permute-done.13.refs_1_), channel_id=1, source_target_pairs={{0,16},{16,0},{1,17},{17,1},{2,18},{18,2},{3,19},{19,3},{4,20},{20... | collective-permute-start | bytes 1867784 | tf_op jit(solution)/shard_map/ppermute | solution.py:206
  202.5 3.9 %copy-start.4 = (bf16[8,2,144,128]{3,2,1,0:T(8,128)(2,1)}, bf16[8,2,144,128]{3,2,1,0:T(8,128)(2,1)S(1)}, u32[]{:S(2)}) copy-start(bf16[8,2,144,128]{3,2,1,0:T(8,128)(2,1)S(1)} %all-to-all-done.4.refs_4_) | copy-start | bytes 1769476
  202.5 3.9 %collective-permute-start.16 = (bf16[8,2,144,128]{3,2,1,0:T(8,128)(2,1)S(1)}, bf16[8,2,144,128]{3,2,1,0:T(8,128)(2,1)S(1)}, u32[]{:S(2)}, u32[]{:S(2)}) collective-permute-start(bf16[8,2,144,128]{3,2,1,0:T(8,128)(2,1)S(1)} %all-to-all-done.4.refs_4_), channel_id=1, source_target_pairs={{0,16},{16,0},{1,17},{17,1},{2,18},{18,2},{3,19},{19,3},{4,20},{20... | collective-permute-start | bytes 1769480 | tf_op jit(solution)/shard_map/ppermute | solution.py:206
  204.4 2.0 copy-start.7
  204.4 2.0 copy-start.8
  206.4 0.8 copy-start.9
  213.7 16.5 %all-to-all-start.5 = ((f32[32,8,128]{2,1,0:T(8,128)}), f32[32,8,128]{2,1,0:T(8,128)S(1)}, u32[]{:S(2)}, u32[]{:S(2)}) async-start(f32[32,8,128]{2,1,0:T(8,128)} %shard_map.69), calls=%async_computation.5 | async-start | bytes 262144 | tf_op jit(solution)/shard_map/all_to_all | solution.py:294

commit v11 on v10

--- a/solution.py
+++ b/solution.py
@@ -282,7 +282,9 @@
     u0, both_b = lax.optimization_barrier((to_all(grad_a, "y"), both_b))
     v0 = to_all(both_b, "y")
     u1 = swap(u0, "zl")
-    rows = (u0, u1, swap(u0, "c"), swap(u1, "c"), v0, swap(v0, "c"))
+    v1 = swap(v0, "c")
+    u1, v1 = lax.optimization_barrier((u1, v1))
+    rows = (u0, u1, swap(u0, "c"), swap(u1, "c"), v0, v1)
     line = call(
         mean_kernel,
         [shape(32, 8, 128, dtype=F32)],

time: 232 us -> 232 us (level)
  waiting for transfers between devices: 50.9 us -> 58.6 us
  starting transfers between devices: 99.6 us -> 92.2 us
    all_to_all x3, waiting for transfers between devices: 11.9 us -> 25.7 us  [to_all(): lax.all_to_all(jnp.broadcast_to(value[None], (count, *value.shape)), axis...]
    ppermute x11, waiting for transfers between devices: 21.7 us -> 15.4 us  [swap(): return lax.ppermute(value, axis, ((0, 1), (1, 0)))]
    ppermute x11, starting transfers between devices: 50.9 us -> 46.9 us  [swap(): return lax.ppermute(value, axis, ((0, 1), (1, 0)))]
    all_to_all x1, starting transfers between devices: 7.27 us -> 3.89 us  [shards(): lax.all_to_all(line, REP, 0, 0, tiled=True)]
where the time goes in v11:
time: 232 us; the launch traced here: 231 us
  starting transfers between devices  92.2 us (40%)
  waiting for transfers between devices  58.6 us (25%)
  blocking collectives  47.2 us (20%)
  Pallas kernels  22.7 us (10%)
  local copies, waits for them, and re-layouts  4.97 us (2%)
  other arithmetic  4.61 us (2%)
    ppermute x11, starting transfers between devices, swap(): return lax.ppermute(value, axis, ((0, 1), (1, 0)))  46.9 us
    all_to_all x3, waiting for transfers between devices, to_all(): lax.all_to_all(jnp.broadcast_to(value[None], (count, *value.shape)), axis...  25.7 us
    all_to_all x1, blocking collectives, shards(): across_a = lax.all_to_all(sums_a, 'y', 0, 0, tiled=True)  23.9 us
    all_gather x1, blocking collectives, shards(): w0 = lax.all_gather(gate_weight.T, 'y', axis=0)  23.3 us
    pallas_call x3, Pallas kernels, call(): pl.pallas_call(kernel, out_shape=outs, in_specs=[SM] + [ANY] * (len(opera...  22.7 us
    ppermute x6, starting transfers between devices, along_x(): return lax.ppermute(value, 'x', [(i, (i + by) % 4) for i in range(4)])  18.1 us
    all_to_all x3, starting transfers between devices, to_all(): lax.all_to_all(jnp.broadcast_to(value[None], (count, *value.shape)), axis...  18.1 us
    ppermute x11, waiting for transfers between devices, swap(): return lax.ppermute(value, axis, ((0, 1), (1, 0)))  15.4 us
  transfers between devices with their start and end apart: 22, of which 11 were waited for; matrix products, arithmetic and copies ran while one was open for 2% of the time, Pallas kernels for 3%

profile of v11, /device:TPU:1, one launch (start us, length us, event | category | flops | bytes accessed | tf_op | source)
XLA Modules:
  0.0 231.3 jit_solution(6616264414311438987)
XLA Ops:
  0.6 2.0 broadcast_in_dim.6
  2.6 11.0 %all-to-all-start = ((bf16[4,512,256]{2,1,0:T(8,128)(2,1)}), bf16[4,512,256]{2,1,0:T(8,128)(2,1)S(1)}, u32[]{:S(2)}, u32[]{:S(2)}) async-start(bf16[4,512,256]{2,1,0:T(8,128)(2,1)} %broadcast_in_dim.6), calls=%async_computation | async-start | bytes 2097152 | tf_op jit(solution)/shard_map/all_to_all | solution.py:211
  13.6 23.3 %all-gather = bf16[3584,128]{1,0:T(8,128)(2,1)S(1)} all-gather(bf16[448,128]{1,0:T(8,128)(2,1)S(1)} %bitcast.22), channel_id=2, replica_groups=mesh['y'=8,'zl'=2,'c'=2,'zh'=4,'x'=4] {'y'}, dimensions={0}, use_global_device_ids=true | all-gather | bytes 1032192 | tf_op jit(solution)/shard_map/all_gather | solution.py:234
  37.0 4.4 %collective-permute-start.3 = (bf16[2,512,256]{2,1,0:T(8,128)(2,1)S(1)}, bf16[2,512,256]{2,1,0:T(8,128)(2,1)S(1)}, u32[]{:S(2)}, u32[]{:S(2)}) collective-permute-start(bf16[2,512,256]{2,1,0:T(8,128)(2,1)S(1)} %get-tuple-element.51), channel_id=1, source_target_pairs={{0,3},{1,0},{2,1},{3,2},{4,7},{5,4},{6,5},{7,6},{8,11},{9,8},{10,9... | collective-permute-start | bytes 1572872 | tf_op jit(solution)/shard_map/ppermute | solution.py:225
  41.4 1.9 collective-permute-start
  43.3 7.2 %collective-permute-start.4 = (bf16[8,448,128]{2,1,0:T(8,128)(2,1)S(1)}, bf16[8,448,128]{2,1,0:T(8,128)(2,1)S(1)}, u32[]{:S(2)}, u32[]{:S(2)}) collective-permute-start(bf16[8,448,128]{2,1,0:T(8,128)(2,1)S(1)} %bitcast.19), channel_id=1, source_target_pairs={{0,32},{32,0},{1,33},{33,1},{2,34},{34,2},{3,35},{35,3},{4,36},{36... | collective-permute-start | bytes 2752520 | tf_op jit(solution)/shard_map/ppermute | solution.py:206
  50.5 2.1 collective-permute-start.1
  52.6 4.4 %collective-permute-start.2 = (bf16[2,512,256]{2,1,0:T(8,128)(2,1)S(1)}, bf16[2,512,256]{2,1,0:T(8,128)(2,1)S(1)}, u32[]{:S(2)}, u32[]{:S(2)}) collective-permute-start(bf16[2,512,256]{2,1,0:T(8,128)(2,1)S(1)} %get-tuple-element.52), channel_id=1, source_target_pairs={{0,3},{1,0},{2,1},{3,2},{4,7},{5,4},{6,5},{7,6},{8,11},{9,8},{10,9... | collective-permute-start | bytes 1572872 | tf_op jit(solution)/shard_map/ppermute | solution.py:225
  57.0 3.4 %collective-permute-start.6 = (bf16[2,512,256]{2,1,0:T(8,128)(2,1)S(1)}, bf16[2,512,256]{2,1,0:T(8,128)(2,1)S(1)}, u32[]{:S(2)}, u32[]{:S(2)}) collective-permute-start(bf16[2,512,256]{2,1,0:T(8,128)(2,1)S(1)} %collective-permute-done.3.refs_4_), channel_id=1, source_target_pairs={{0,3},{1,0},{2,1},{3,2},{4,7},{5,4},{6,5},{7,6},{8,11},{9,8},{10,9... | collective-permute-start | bytes 1572872 | tf_op jit(solution)/shard_map/ppermute | solution.py:225
  60.4 1.9 collective-permute-start.5
  62.4 5.3 %collective-permute-done.1.refs_3_ = bf16[2,512,256]{2,1,0:T(8,128)(2,1)S(1)} collective-permute-done((bf16[2,512,256]{2,1,0:T(8,128)(2,1)S(1)}, bf16[2,512,256]{2,1,0:T(8,128)(2,1)S(1)}, u32[]{:S(2)}, u32[]{:S(2)}) %collective-permute-start.1) | collective-permute-done | bytes 524320 | tf_op jit(solution)/shard_map/ppermute | solution.py:225
  67.6 7.8 %collective-permute-start.7 = (bf16[8,448,128]{2,1,0:T(8,128)(2,1)S(1)}, bf16[8,448,128]{2,1,0:T(8,128)(2,1)}, u32[]{:S(2)}, u32[]{:S(2)}) collective-permute-start(bf16[8,448,128]{2,1,0:T(8,128)(2,1)S(1)} %bitcast.20), channel_id=1, source_target_pairs={{0,16},{16,0},{1,17},{17,1},{2,18},{18,2},{3,19},{19,3},{4,20},{20... | collective-permute-start | bytes 2752520 | tf_op jit(solution)/shard_map/ppermute | solution.py:206
  75.5 1.6 collective-permute-done.6.refs_7_
  77.1 1.8 collective-permute-done.5.refs_6_
  78.9 5.1 %collective-permute-start.8 = (bf16[8,448,128]{2,1,0:T(8,128)(2,1)S(1)}, bf16[8,448,128]{2,1,0:T(8,128)(2,1)}, u32[]{:S(2)}, u32[]{:S(2)}) collective-permute-start(bf16[8,448,128]{2,1,0:T(8,128)(2,1)S(1)} %collective-permute-done.4.refs_11_), channel_id=1, source_target_pairs={{0,16},{16,0},{1,17},{17,1},{2,18},{18,2},{3,19},{19,3},{4,20},{20... | collective-permute-start | bytes 2752520 | tf_op jit(solution)/shard_map/ppermute | solution.py:206
  84.0 0.6 pad_add_fusion.refs_0_.me
  84.5 1.6 collective-permute-done.8.refs_13_
  86.1 9.6 %shard_map.67 = (bf16[16,512,256]{2,1,0:T(8,128)(2,1)}, f32[448,512]{1,0:T(8,128)}, bf16[8,304,128]{2,1,0:T(8,128)(2,1)}, bf16[8,304,128]{2,1,0:T(8,128)(2,1)}, ...) custom-call(s32[3]{0:T(128)} %pad_add_fusion.refs_0_.me, ...), custom_call_target="tpu_custom_call" | custom-call | flops 3758096384 | bytes 17563660 | tf_op jit(solution)/shard_map/pallas_call | solution.py:27
  95.7 2.3 collective-permute-start.10
  98.0 2.0 collective-permute-start.9
  100.1 2.1 collective-permute-done.9
  102.1 2.2 add_convert_fusion
  104.3 5.3 %all-to-all-start.1 = ((bf16[8,2,144,128]{3,2,1,0:T(8,128)(2,1)}), bf16[8,2,144,128]{3,2,1,0:T(8,128)(2,1)S(1)}, u32[]{:S(2)}, u32[]{:S(2)}) async-start(bf16[8,2,144,128]{3,2,1,0:T(8,128)(2,1)} %add_convert_fusion), calls=%async_computation.1 | async-start | bytes 1179648 | tf_op jit(solution)/shard_map/all_to_all | solution.py:265
  109.6 0.2 fusion
  109.8 8.0 %collective-permute-start.11 = (bf16[8,304,128]{2,1,0:T(8,128)(2,1)S(1)}, bf16[8,304,128]{2,1,0:T(8,128)(2,1)S(1)}, u32[]{:S(2)}, u32[]{:S(2)}) collective-permute-start(bf16[8,304,128]{2,1,0:T(8,128)(2,1)S(1)} %fusion), channel_id=1, source_target_pairs={{0,32},{32,0},{1,33},{33,1},{2,34},{34,2},{3,35},{35,3},{4,36},{36... | collective-permute-start | bytes 1867784 | tf_op jit(solution)/shard_map/ppermute | solution.py:206
  117.8 6.6 %shard_map.68.own_in = f32[448,512]{1,0:T(8,128)} custom-call(s32[3]{0:T(128)} %pad_add_fusion.refs_0_.me, bf16[16,512,256]{2,1,0:T(8,128)(2,1)} %get-tuple-element.42.source, bf16[8,304,128]{2,1,0:T(8,128)(2,1)} %get-tuple-element.35.a0, bf16[8,304,128]{2,1,0:T(8,128)(2,1)} %get-tuple-element.40.a1, bf16[2,8,304,128]{3,2,1,0:T(8,128)(2,1)} %get-tuple-element.38.sent, ...), custom_call_target="tpu_custom_call" | custom-call | flops 1879048192 | bytes 8781836 | tf_op jit(solution)/shard_map/pallas_call | solution.py:27
  124.4 7.4 %collective-permute-done.11 = bf16[8,304,128]{2,1,0:T(8,128)(2,1)S(1)} collective-permute-done((bf16[8,304,128]{2,1,0:T(8,128)(2,1)S(1)}, bf16[8,304,128]{2,1,0:T(8,128)(2,1)S(1)}, u32[]{:S(2)}, u32[]{:S(2)}) %collective-permute-start.11) | collective-permute-done | bytes 622624 | tf_op jit(solution)/shard_map/ppermute | solution.py:206
  131.8 0.2 fusion.2
  132.0 23.9 %all_to_all.30 = bf16[8,304,128]{2,1,0:T(8,128)(2,1)S(1)} all-to-all(bf16[8,304,128]{2,1,0:T(8,128)(2,1)S(1)} %fusion.2), channel_id=1, replica_groups=mesh['y'=8,'zl'=2,'c'=2,'zh'=4,'x'=4] {'y'}, dimensions={0} | all-to-all | bytes 1245184 | tf_op jit(solution)/shard_map/all_to_all | solution.py:277
  156.0 0.9 broadcast_in_dim.7
  156.9 3.5 %all-to-all-start.3 = ((bf16[8,304,128]{2,1,0:T(8,128)(2,1)}), bf16[8,304,128]{2,1,0:T(8,128)(2,1)S(1)}, u32[]{:S(2)}, u32[]{:S(2)}) async-start(bf16[8,304,128]{2,1,0:T(8,128)(2,1)} %broadcast_in_dim.7), calls=%async_computation.3 | async-start | bytes 1245184 | tf_op jit(solution)/shard_map/all_to_all | solution.py:211
  160.5 2.4 %collective-permute-start.12 = (bf16[2,144,128]{2,1,0:T(8,128)(2,1)S(1)}, bf16[2,144,128]{2,1,0:T(8,128)(2,1)S(1)}, u32[]{:S(2)}, u32[]{:S(2)}) collective-permute-start(bf16[2,144,128]{2,1,0:T(8,128)(2,1)S(1)} %reduce_sum.34), channel_id=1, source_target_pairs={{0,32},{32,0},{1,33},{33,1},{2,34},{34,2},{3,35},{35,3},{4,36},{36... | collective-permute-start | bytes 221192 | tf_op jit(solution)/shard_map/ppermute | solution.py:206
  162.9 2.7 %collective-permute-done.12 = bf16[2,144,128]{2,1,0:T(8,128)(2,1)S(1)} collective-permute-done((bf16[2,144,128]{2,1,0:T(8,128)(2,1)S(1)}, bf16[2,144,128]{2,1,0:T(8,128)(2,1)S(1)}, u32[]{:S(2)}, u32[]{:S(2)}) %collective-permute-start.12) | collective-permute-done | bytes 73760 | tf_op jit(solution)/shard_map/ppermute | solution.py:206
  165.7 11.9 %all-to-all-done.3.refs_0_ = bf16[8,304,128]{2,1,0:T(8,128)(2,1)S(1)} async-done(((bf16[8,304,128]{2,1,0:T(8,128)(2,1)}), bf16[8,304,128]{2,1,0:T(8,128)(2,1)S(1)}, u32[]{:S(2)}, u32[]{:S(2)}) %all-to-all-start.3) | async-done | bytes 622624 | tf_op jit(solution)/shard_map/all_to_all | solution.py:211
  177.6 1.0 broadcast_in_dim.8
  178.6 3.5 %all-to-all-start.4 = ((bf16[8,2,144,128]{3,2,1,0:T(8,128)(2,1)}), bf16[8,2,144,128]{3,2,1,0:T(8,128)(2,1)S(1)}, u32[]{:S(2)}, u32[]{:S(2)}) async-start(bf16[8,2,144,128]{3,2,1,0:T(8,128)(2,1)} %broadcast_in_dim.8), calls=%async_computation.4 | async-start | bytes 1179648 | tf_op jit(solution)/shard_map/all_to_all | solution.py:211
  182.2 2.3 collective-permute-start.13
  184.5 13.8 %all-to-all-done.4.refs_4_ = bf16[8,2,144,128]{3,2,1,0:T(8,128)(2,1)S(1)} async-done(((bf16[8,2,144,128]{3,2,1,0:T(8,128)(2,1)}), bf16[8,2,144,128]{3,2,1,0:T(8,128)(2,1)S(1)}, u32[]{:S(2)}, u32[]{:S(2)}) %all-to-all-start.4) | async-done | bytes 589856 | tf_op jit(solution)/shard_map/all_to_all | solution.py:211
  198.3 5.5 %collective-permute-start.14 = (bf16[8,2,144,128]{3,2,1,0:T(8,128)(2,1)S(1)}, bf16[8,2,144,128]{3,2,1,0:T(8,128)(2,1)S(1)}, u32[]{:S(2)}, u32[]{:S(2)}) collective-permute-start(bf16[8,2,144,128]{3,2,1,0:T(8,128)(2,1)S(1)} %all-to-all-done.4.refs_4_), channel_id=1, source_target_pairs={{0,16},{16,0},{1,17},{17,1},{2,18},{18,2},{3,19},{19,3},{4,20},{20... | collective-permute-start | bytes 1769480 | tf_op jit(solution)/shard_map/ppermute | solution.py:206
  203.9 1.9 collective-permute-start.15
  205.8 2.4 %collective-permute-start.16 = (bf16[8,304,128]{2,1,0:T(8,128)(2,1)S(1)}, bf16[8,304,128]{2,1,0:T(8,128)(2,1)S(1)}, u32[]{:S(2)}, u32[]{:S(2)}) collective-permute-start(bf16[8,304,128]{2,1,0:T(8,128)(2,1)S(1)} %collective-permute-done.13.refs_1_), channel_id=1, source_target_pairs={{0,16},{16,0},{1,17},{17,1},{2,18},{18,2},{3,19},{19,3},{4,20},{20... | collective-permute-start | bytes 1867784 | tf_op jit(solution)/shard_map/ppermute | solution.py:206
  208.3 1.6 collective-permute-done.16.refs_3_
  209.9 0.9 copy-done.8
  210.8 6.5 %shard_map.69 = f32[32,8,128]{2,1,0:T(8,128)} custom-call(s32[3]{0:T(128)} %pad_add_fusion.refs_0_.me, bf16[16,512,256]{2,1,0:T(8,128)(2,1)} %get-tuple-element.42.source, f32[448,512]{1,0:T(8,128)} %get-tuple-element.46.bend_in, f32[448,512]{1,0:T(8,128)} %shard_map.68.own_in, bf16[8,304,128]{2,1,0:T(8,128)(2,1)} %copy-done.1, ...), custom_call_target="tpu_custom_call" | custom-call | flops 1879048192 | bytes 9830412 | tf_op jit(solution)/shard_map/pallas_call | solution.py:27
  217.3 3.9 %all-to-all-start.5 = ((f32[32,8,128]{2,1,0:T(8,128)}), f32[32,8,128]{2,1,0:T(8,128)S(1)}, u32[]{:S(2)}, u32[]{:S(2)}) async-start(f32[32,8,128]{2,1,0:T(8,128)} %shard_map.69), calls=%async_computation.5 | async-start | bytes 262144 | tf_op jit(solution)/shard_map/all_to_all | solution.py:296
  221.2 0.7 maximum_bitcast_fusion
  221.9 8.8 %all-to-all-done.5 = f32[32,8,128]{2,1,0:T(8,128)S(1)} async-done(((f32[32,8,128]{2,1,0:T(8,128)}), f32[32,8,128]{2,1,0:T(8,128)S(1)}, u32[]{:S(2)}, u32[]{:S(2)}) %all-to-all-start.5) | async-done | bytes 131104 | tf_op jit(solution)/shard_map/all_to_all | solution.py:296
  230.7 0.6 slice_multiply_fusion
  (53 shorter events, 0.4 us)
Async XLA Ops:
  2.6 11.0 %copy-start.10 = (bf16[128,448]{0,1:T(8,128)(2,1)S(1)}, bf16[128,448]{0,1:T(8,128)(2,1)}, u32[]{:S(2)}) copy-start(bf16[128,448]{0,1:T(8,128)(2,1)} %param.5) | copy-start | bytes 344068
  2.6 34.3 %all-to-all-start = ((bf16[4,512,256]{2,1,0:T(8,128)(2,1)}), bf16[4,512,256]{2,1,0:T(8,128)(2,1)S(1)}, u32[]{:S(2)}, u32[]{:S(2)}) async-start(bf16[4,512,256]{2,1,0:T(8,128)(2,1)} %broadcast_in_dim.6), calls=%async_computation | async-start | bytes 2097152 | tf_op jit(solution)/shard_map/all_to_all | solution.py:211
  36.9 49.2 %copy-start.5 = (bf16[3584,128]{1,0:T(8,128)(2,1)}, bf16[3584,128]{1,0:T(8,128)(2,1)S(1)}, u32[]{:S(2)}) copy-start(bf16[3584,128]{1,0:T(8,128)(2,1)S(1)} %all-gather) | copy-start | bytes 2752516
  36.9 49.2 %copy-start = (bf16[4,512,256]{2,1,0:T(8,128)(2,1)}, bf16[4,512,256]{2,1,0:T(8,128)(2,1)S(1)}, u32[]{:S(2)}) copy-start(bf16[4,512,256]{2,1,0:T(8,128)(2,1)S(1)} %all-to-all-done.refs_1_) | copy-start | bytes 3145732
  37.0 20.0 %collective-permute-start.3 = (bf16[2,512,256]{2,1,0:T(8,128)(2,1)S(1)}, bf16[2,512,256]{2,1,0:T(8,128)(2,1)S(1)}, u32[]{:S(2)}, u32[]{:S(2)}) collective-permute-start(bf16[2,512,256]{2,1,0:T(8,128)(2,1)S(1)} %get-tuple-element.51), channel_id=1, source_target_pairs={{0,3},{1,0},{2,1},{3,2},{4,7},{5,4},{6,5},{7,6},{8,11},{9,8},{10,9... | collective-permute-start | bytes 1572872 | tf_op jit(solution)/shard_map/ppermute | solution.py:225
  41.4 19.0 %collective-permute-start = (bf16[2,512,256]{2,1,0:T(8,128)(2,1)S(1)}, bf16[2,512,256]{2,1,0:T(8,128)(2,1)S(1)}, u32[]{:S(2)}, u32[]{:S(2)}) collective-permute-start(bf16[2,512,256]{2,1,0:T(8,128)(2,1)S(1)} %get-tuple-element.52), channel_id=1, source_target_pairs={{0,1},{1,2},{2,3},{3,0},{4,5},{5,6},{6,7},{7,4},{8,9},{9,10},{10,1... | collective-permute-start | bytes 1572872 | tf_op jit(solution)/shard_map/ppermute | solution.py:225
  43.3 32.1 %collective-permute-start.4 = (bf16[8,448,128]{2,1,0:T(8,128)(2,1)S(1)}, bf16[8,448,128]{2,1,0:T(8,128)(2,1)S(1)}, u32[]{:S(2)}, u32[]{:S(2)}) collective-permute-start(bf16[8,448,128]{2,1,0:T(8,128)(2,1)S(1)} %bitcast.19), channel_id=1, source_target_pairs={{0,32},{32,0},{1,33},{33,1},{2,34},{34,2},{3,35},{35,3},{4,36},{36... | collective-permute-start | bytes 2752520 | tf_op jit(solution)/shard_map/ppermute | solution.py:206
  50.5 17.1 %collective-permute-start.1 = (bf16[2,512,256]{2,1,0:T(8,128)(2,1)S(1)}, bf16[2,512,256]{2,1,0:T(8,128)(2,1)S(1)}, u32[]{:S(2)}, u32[]{:S(2)}) collective-permute-start(bf16[2,512,256]{2,1,0:T(8,128)(2,1)S(1)} %get-tuple-element.51), channel_id=1, source_target_pairs={{0,1},{1,2},{2,3},{3,0},{4,5},{5,6},{6,7},{7,4},{8,9},{9,10},{10,1... | collective-permute-start | bytes 1572872 | tf_op jit(solution)/shard_map/ppermute | solution.py:225
  52.6 15.0 %collective-permute-start.2 = (bf16[2,512,256]{2,1,0:T(8,128)(2,1)S(1)}, bf16[2,512,256]{2,1,0:T(8,128)(2,1)S(1)}, u32[]{:S(2)}, u32[]{:S(2)}) collective-permute-start(bf16[2,512,256]{2,1,0:T(8,128)(2,1)S(1)} %get-tuple-element.52), channel_id=1, source_target_pairs={{0,3},{1,0},{2,1},{3,2},{4,7},{5,4},{6,5},{7,6},{8,11},{9,8},{10,9... | collective-permute-start | bytes 1572872 | tf_op jit(solution)/shard_map/ppermute | solution.py:225
  57.0 29.1 %copy-start.12 = (bf16[2,512,256]{2,1,0:T(8,128)(2,1)}, bf16[2,512,256]{2,1,0:T(8,128)(2,1)S(1)}, u32[]{:S(2)}) copy-start(bf16[2,512,256]{2,1,0:T(8,128)(2,1)S(1)} %collective-permute-done.3.refs_4_) | copy-start | bytes 1572868
  57.0 20.1 %collective-permute-start.6 = (bf16[2,512,256]{2,1,0:T(8,128)(2,1)S(1)}, bf16[2,512,256]{2,1,0:T(8,128)(2,1)S(1)}, u32[]{:S(2)}, u32[]{:S(2)}) collective-permute-start(bf16[2,512,256]{2,1,0:T(8,128)(2,1)S(1)} %collective-permute-done.3.refs_4_), channel_id=1, source_target_pairs={{0,3},{1,0},{2,1},{3,2},{4,7},{5,4},{6,5},{7,6},{8,11},{9,8},{10,9... | collective-permute-start | bytes 1572872 | tf_op jit(solution)/shard_map/ppermute | solution.py:225
  60.4 16.7 %copy-start.13 = (bf16[2,512,256]{2,1,0:T(8,128)(2,1)}, bf16[2,512,256]{2,1,0:T(8,128)(2,1)S(1)}, u32[]{:S(2)}) copy-start(bf16[2,512,256]{2,1,0:T(8,128)(2,1)S(1)} %collective-permute-done.refs_2_) | copy-start | bytes 1572868
  60.4 18.4 %collective-permute-start.5 = (bf16[2,512,256]{2,1,0:T(8,128)(2,1)S(1)}, bf16[2,512,256]{2,1,0:T(8,128)(2,1)S(1)}, u32[]{:S(2)}, u32[]{:S(2)}) collective-permute-start(bf16[2,512,256]{2,1,0:T(8,128)(2,1)S(1)} %collective-permute-done.refs_2_), channel_id=1, source_target_pairs={{0,1},{1,2},{2,3},{3,0},{4,5},{5,6},{6,7},{7,4},{8,9},{9,10},{10,1... | collective-permute-start | bytes 1572872 | tf_op jit(solution)/shard_map/ppermute | solution.py:225
  67.6 11.2 %copy-start.14 = (bf16[2,512,256]{2,1,0:T(8,128)(2,1)}, bf16[2,512,256]{2,1,0:T(8,128)(2,1)S(1)}, u32[]{:S(2)}) copy-start(bf16[2,512,256]{2,1,0:T(8,128)(2,1)S(1)} %collective-permute-done.1.refs_3_) | copy-start | bytes 1572868
  67.6 16.3 %copy-start.15 = (bf16[2,512,256]{2,1,0:T(8,128)(2,1)}, bf16[2,512,256]{2,1,0:T(8,128)(2,1)S(1)}, u32[]{:S(2)}) copy-start(bf16[2,512,256]{2,1,0:T(8,128)(2,1)S(1)} %collective-permute-done.2.refs_5_) | copy-start | bytes 1572868
  67.6 16.9 %collective-permute-start.7 = (bf16[8,448,128]{2,1,0:T(8,128)(2,1)S(1)}, bf16[8,448,128]{2,1,0:T(8,128)(2,1)}, u32[]{:S(2)}, u32[]{:S(2)}) collective-permute-start(bf16[8,448,128]{2,1,0:T(8,128)(2,1)S(1)} %bitcast.20), channel_id=1, source_target_pairs={{0,16},{16,0},{1,17},{17,1},{2,18},{18,2},{3,19},{19,3},{4,20},{20... | collective-permute-start | bytes 2752520 | tf_op jit(solution)/shard_map/ppermute | solution.py:206
  75.5 10.7 %copy-start.11 = (bf16[8,448,128]{2,1,0:T(8,128)(2,1)}, bf16[8,448,128]{2,1,0:T(8,128)(2,1)S(1)}, u32[]{:S(2)}) copy-start(bf16[8,448,128]{2,1,0:T(8,128)(2,1)S(1)} %collective-permute-done.4.refs_11_) | copy-start | bytes 2752516
  77.1 6.8 %copy-start.16 = (bf16[2,512,256]{2,1,0:T(8,128)(2,1)}, bf16[2,512,256]{2,1,0:T(8,128)(2,1)S(1)}, u32[]{:S(2)}) copy-start(bf16[2,512,256]{2,1,0:T(8,128)(2,1)S(1)} %collective-permute-done.6.refs_7_) | copy-start | bytes 1572868
  78.9 5.1 %copy-start.17 = (bf16[2,512,256]{2,1,0:T(8,128)(2,1)}, bf16[2,512,256]{2,1,0:T(8,128)(2,1)S(1)}, u32[]{:S(2)}) copy-start(bf16[2,512,256]{2,1,0:T(8,128)(2,1)S(1)} %collective-permute-done.5.refs_6_) | copy-start | bytes 1572868
  78.9 7.3 %collective-permute-start.8 = (bf16[8,448,128]{2,1,0:T(8,128)(2,1)S(1)}, bf16[8,448,128]{2,1,0:T(8,128)(2,1)}, u32[]{:S(2)}, u32[]{:S(2)}) collective-permute-start(bf16[8,448,128]{2,1,0:T(8,128)(2,1)S(1)} %collective-permute-done.4.refs_11_), channel_id=1, source_target_pairs={{0,16},{16,0},{1,17},{17,1},{2,18},{18,2},{3,19},{19,3},{4,20},{20... | collective-permute-start | bytes 2752520 | tf_op jit(solution)/shard_map/ppermute | solution.py:206
  95.7 8.6 %collective-permute-start.10 = (bf16[2,8,304,128]{3,2,1,0:T(8,128)(2,1)}, bf16[2,8,304,128]{3,2,1,0:T(8,128)(2,1)S(1)}, u32[]{:S(2)}, u32[]{:S(2)}) collective-permute-start(bf16[2,8,304,128]{3,2,1,0:T(8,128)(2,1)} %get-tuple-element.38.sent), channel_id=1, source_target_pairs={{0,16},{16,0},{1,17},{17,1},{2,18},{18,2},{3,19},{19,3},{4,20},{20... | collective-permute-start | bytes 3735560 | tf_op jit(solution)/shard_map/ppermute | solution.py:206
  98.0 4.1 %collective-permute-start.9 = (bf16[8,2,144,128]{3,2,1,0:T(8,128)(2,1)}, bf16[8,2,144,128]{3,2,1,0:T(8,128)(2,1)S(1)}, u32[]{:S(2)}, u32[]{:S(2)}) collective-permute-start(bf16[8,2,144,128]{3,2,1,0:T(8,128)(2,1)} %get-tuple-element.37.b1), channel_id=1, source_target_pairs={{0,16},{16,0},{1,17},{17,1},{2,18},{18,2},{3,19},{19,3},{4,20},{20... | collective-permute-start | bytes 1769480 | tf_op jit(solution)/shard_map/ppermute | solution.py:206
  102.1 7.5 %copy-start.3 = (bf16[8,304,128]{2,1,0:T(8,128)(2,1)S(1)}, bf16[8,304,128]{2,1,0:T(8,128)(2,1)}, u32[]{:S(2)}) copy-start(bf16[8,304,128]{2,1,0:T(8,128)(2,1)} %get-tuple-element.40.a1) | copy-start | bytes 1867780
  104.3 27.7 %all-to-all-start.1 = ((bf16[8,2,144,128]{3,2,1,0:T(8,128)(2,1)}), bf16[8,2,144,128]{3,2,1,0:T(8,128)(2,1)S(1)}, u32[]{:S(2)}, u32[]{:S(2)}) async-start(bf16[8,2,144,128]{3,2,1,0:T(8,128)(2,1)} %add_convert_fusion), calls=%async_computation.1 | async-start | bytes 1179648 | tf_op jit(solution)/shard_map/all_to_all | solution.py:265
  109.8 22.0 %collective-permute-start.11 = (bf16[8,304,128]{2,1,0:T(8,128)(2,1)S(1)}, bf16[8,304,128]{2,1,0:T(8,128)(2,1)S(1)}, u32[]{:S(2)}, u32[]{:S(2)}) collective-permute-start(bf16[8,304,128]{2,1,0:T(8,128)(2,1)S(1)} %fusion), channel_id=1, source_target_pairs={{0,32},{32,0},{1,33},{33,1},{2,34},{34,2},{3,35},{35,3},{4,36},{36... | collective-permute-start | bytes 1867784 | tf_op jit(solution)/shard_map/ppermute | solution.py:206
  117.8 14.0 %copy-start.2 = (bf16[8,304,128]{2,1,0:T(8,128)(2,1)S(1)}, bf16[8,304,128]{2,1,0:T(8,128)(2,1)}, u32[]{:S(2)}) copy-start(bf16[8,304,128]{2,1,0:T(8,128)(2,1)} %get-tuple-element.35.a0) | copy-start | bytes 1867780
  156.9 20.7 %all-to-all-start.3 = ((bf16[8,304,128]{2,1,0:T(8,128)(2,1)}), bf16[8,304,128]{2,1,0:T(8,128)(2,1)S(1)}, u32[]{:S(2)}, u32[]{:S(2)}) async-start(bf16[8,304,128]{2,1,0:T(8,128)(2,1)} %broadcast_in_dim.7), calls=%async_computation.3 | async-start | bytes 1245184 | tf_op jit(solution)/shard_map/all_to_all | solution.py:211
  160.5 5.1 %collective-permute-start.12 = (bf16[2,144,128]{2,1,0:T(8,128)(2,1)S(1)}, bf16[2,144,128]{2,1,0:T(8,128)(2,1)S(1)}, u32[]{:S(2)}, u32[]{:S(2)}) collective-permute-start(bf16[2,144,128]{2,1,0:T(8,128)(2,1)S(1)} %reduce_sum.34), channel_id=1, source_target_pairs={{0,32},{32,0},{1,33},{33,1},{2,34},{34,2},{3,35},{35,3},{4,36},{36... | collective-permute-start | bytes 221192 | tf_op jit(solution)/shard_map/ppermute | solution.py:206
  177.6 32.3 %copy-start.1 = (bf16[8,304,128]{2,1,0:T(8,128)(2,1)}, bf16[8,304,128]{2,1,0:T(8,128)(2,1)S(1)}, u32[]{:S(2)}) copy-start(bf16[8,304,128]{2,1,0:T(8,128)(2,1)S(1)} %all-to-all-done.3.refs_0_) | copy-start | bytes 1867780
  178.6 19.7 %all-to-all-start.4 = ((bf16[8,2,144,128]{3,2,1,0:T(8,128)(2,1)}), bf16[8,2,144,128]{3,2,1,0:T(8,128)(2,1)S(1)}, u32[]{:S(2)}, u32[]{:S(2)}) async-start(bf16[8,2,144,128]{3,2,1,0:T(8,128)(2,1)} %broadcast_in_dim.8), calls=%async_computation.4 | async-start | bytes 1179648 | tf_op jit(solution)/shard_map/all_to_all | solution.py:211
  182.2 23.6 %collective-permute-start.13 = (bf16[8,304,128]{2,1,0:T(8,128)(2,1)S(1)}, bf16[8,304,128]{2,1,0:T(8,128)(2,1)S(1)}, u32[]{:S(2)}, u32[]{:S(2)}) collective-permute-start(bf16[8,304,128]{2,1,0:T(8,128)(2,1)S(1)} %all-to-all-done.3.refs_0_), channel_id=1, source_target_pairs={{0,32},{32,0},{1,33},{33,1},{2,34},{34,2},{3,35},{35,3},{4,36},{36... | collective-permute-start | bytes 1867784 | tf_op jit(solution)/shard_map/ppermute | solution.py:206
  198.3 11.6 %copy-start.4 = (bf16[8,2,144,128]{3,2,1,0:T(8,128)(2,1)}, bf16[8,2,144,128]{3,2,1,0:T(8,128)(2,1)S(1)}, u32[]{:S(2)}) copy-start(bf16[8,2,144,128]{3,2,1,0:T(8,128)(2,1)S(1)} %all-to-all-done.4.refs_4_) | copy-start | bytes 1769476
  198.3 7.5 %collective-permute-start.14 = (bf16[8,2,144,128]{3,2,1,0:T(8,128)(2,1)S(1)}, bf16[8,2,144,128]{3,2,1,0:T(8,128)(2,1)S(1)}, u32[]{:S(2)}, u32[]{:S(2)}) collective-permute-start(bf16[8,2,144,128]{3,2,1,0:T(8,128)(2,1)S(1)} %all-to-all-done.4.refs_4_), channel_id=1, source_target_pairs={{0,16},{16,0},{1,17},{17,1},{2,18},{18,2},{3,19},{19,3},{4,20},{20... | collective-permute-start | bytes 1769480 | tf_op jit(solution)/shard_map/ppermute | solution.py:206
  203.9 4.4 %collective-permute-start.15 = (bf16[8,304,128]{2,1,0:T(8,128)(2,1)S(1)}, bf16[8,304,128]{2,1,0:T(8,128)(2,1)S(1)}, u32[]{:S(2)}, u32[]{:S(2)}) collective-permute-start(bf16[8,304,128]{2,1,0:T(8,128)(2,1)S(1)} %all-to-all-done.3.refs_0_), channel_id=1, source_target_pairs={{0,16},{16,0},{1,17},{17,1},{2,18},{18,2},{3,19},{19,3},{4,20},{20... | collective-permute-start | bytes 1867784 | tf_op jit(solution)/shard_map/ppermute | solution.py:206
  205.8 4.1 %copy-start.6 = (bf16[8,304,128]{2,1,0:T(8,128)(2,1)}, bf16[8,304,128]{2,1,0:T(8,128)(2,1)S(1)}, u32[]{:S(2)}) copy-start(bf16[8,304,128]{2,1,0:T(8,128)(2,1)S(1)} %collective-permute-done.13.refs_1_) | copy-start | bytes 1867780
  205.8 4.1 %copy-start.9 = (bf16[8,2,144,128]{3,2,1,0:T(8,128)(2,1)}, bf16[8,2,144,128]{3,2,1,0:T(8,128)(2,1)S(1)}, u32[]{:S(2)}) copy-start(bf16[8,2,144,128]{3,2,1,0:T(8,128)(2,1)S(1)} %collective-permute-done.14.refs_5_) | copy-start | bytes 1769476
  205.8 4.1 %collective-permute-start.16 = (bf16[8,304,128]{2,1,0:T(8,128)(2,1)S(1)}, bf16[8,304,128]{2,1,0:T(8,128)(2,1)S(1)}, u32[]{:S(2)}, u32[]{:S(2)}) collective-permute-start(bf16[8,304,128]{2,1,0:T(8,128)(2,1)S(1)} %collective-permute-done.13.refs_1_), channel_id=1, source_target_pairs={{0,16},{16,0},{1,17},{17,1},{2,18},{18,2},{3,19},{19,3},{4,20},{20... | collective-permute-start | bytes 1867784 | tf_op jit(solution)/shard_map/ppermute | solution.py:206
  208.3 1.7 copy-start.7
  209.9 0.9 copy-start.8
  217.3 13.4 %all-to-all-start.5 = ((f32[32,8,128]{2,1,0:T(8,128)}), f32[32,8,128]{2,1,0:T(8,128)S(1)}, u32[]{:S(2)}, u32[]{:S(2)}) async-start(f32[32,8,128]{2,1,0:T(8,128)} %shard_map.69), calls=%async_computation.5 | async-start | bytes 262144 | tf_op jit(solution)/shard_map/all_to_all | solution.py:296
